TPU v7x, 32 devices: a whole 2x2x4 slice. The times are simulated.
32 devices in a mesh: groups: 2 (over x), mp: 8 (over z, y), pool: 2 (over core).
Axes of the slice: x: 2, y: 2, z: 4, core: 2. Of those that a mesh axis runs over, the one named last changes fastest.
Arguments:
- states: bfloat16 [4, 512, 8192], P(('groups', 'pool'), 'mp'), parts along dimension 0, may hold values from -6 to 6
- norm_gain: bfloat16 [8192], replicated, may hold values from 0.099609375 to 1.8984375
- w_query: bfloat16 [8192, 8192], P(None, 'mp'), may hold values from -0.0625 to 0.0625
- q_bias: bfloat16 [8192], P('mp'), may hold values from -36 to 36
- w_key: bfloat16 [8192, 1024], P(None, 'mp'), may hold values from -0.0625 to 0.0625
- w_value: bfloat16 [8192, 1024], P(None, 'mp'), may hold values from -0.0625 to 0.0625
- k_bias: bfloat16 [1024], P('mp'), may hold values from -3 to 3
- v_bias: bfloat16 [1024], P('mp'), may hold values from -3 to 3
- w_out: bfloat16 [8192, 8192], P('mp'), may hold values from -0.0625 to 0.0625
- kv_pool: bfloat16 [32, 64, 16, 2048], P(('groups', 'mp', 'pool')), parts along dimension 0, may hold values from -12 to 12
- hit_holder: int32 [4, 256], P('groups'), parts along dimension 0, may hold values from 0 to 15, as said below
- hit_slot: int32 [4, 256], P('groups'), parts along dimension 0, may hold values from 0 to 63
- prefix_len: int32 [4], P('groups'), parts along dimension 0, may hold values from 2048 to 4096, as said below
Outputs:
- attn_out: bfloat16 [4, 512, 8192], P(('groups', 'pool'), 'mp'), parts along dimension 0
- kv_new: bfloat16 [4, 512, 2048], P(('groups', 'pool'), 'mp'), parts along dimension 0
There are 2 independent parts, one for each index of `groups`. A program takes and returns all parts, laid end to end along the dimension named above; an argument that names none is the same for every part. Nothing has to cross between parts.
Inputs may be any that keep to these rules, and one draw needn't show every extreme that they name: `hit_holder`: for each request, at most 32 of its blocks name one holder, and exactly 32 name some holder. `prefix_len`: one request's prefix has exactly 4096 tokens.
All inputs are finite; a program needn't handle non-finite values.
Results may differ from a plain program's by a relative error of at most 0.014.
Values may be sent and summed in bfloat16 or wider, within the bound.
No kernel may reach another device: no remote copies, remote signals or barrier semaphores. Data moves between devices by JAX's collectives and lax.ppermute only.
A program may use at most 192 MiB of HBM per device.

v0:
```python
import math

import jax
import jax.numpy as jnp
from jax import lax
from jax.sharding import PartitionSpec as P

QH = 64
HD = 128


ROPE_BASE = 1000000.0
EPSILON = 1e-06


def rotate(vectors, positions):
    half_dim = vectors.shape[-1] // 2
    frequency = jnp.power(
        jnp.float32(ROPE_BASE), -2.0 * jnp.arange(half_dim, dtype=jnp.float32) / vectors.shape[-1]
    )
    angles = positions.astype(jnp.float32)[:, None] * frequency[None, :]
    cosine = jnp.cos(angles)[:, None, :]
    sine_part = jnp.sin(angles)[:, None, :]
    first_half = vectors[..., :half_dim]
    second = vectors[..., half_dim:]
    return jnp.concatenate(
        [first_half * cosine - second * sine_part, second * cosine + first_half * sine_part], -1
    )


def normalize(states, gain_vec):
    values = states.astype(jnp.float32)
    inv_rms = lax.rsqrt(jnp.mean(values * values, axis=-1, keepdims=True) + EPSILON)
    return (values * inv_rms * gain_vec.astype(jnp.float32)).astype(jnp.bfloat16)


def listing(owned_mask, capacity):
    rank_order = jnp.cumsum(owned_mask.astype(jnp.int32), -1) - 1
    slot_index = jnp.arange(capacity, dtype=jnp.int32)
    return owned_mask[..., None, :] & (rank_order[..., None, :] == slot_index[:, None])


def on_device(
    states,
    norm_gain,
    w_query,
    q_bias,
    w_key,
    w_value,
    k_bias,
    v_bias,
    w_out,
    kv_pool,
    hit_holder,
    hit_slot,
    prefix_len,
):
    n_model = lax.axis_size("mp")
    n_pool = lax.axis_size("pool")
    my_model = lax.axis_index("mp")
    my_pool = lax.axis_index("pool")
    row_count = states.shape[1]
    suffix = row_count * n_model
    q_width = w_query.shape[1]
    q_local = q_width // HD
    kv_local = w_key.shape[1]
    kv_heads = kv_local * n_model // HD
    group_size = QH // kv_heads
    blocks_total = hit_holder.shape[1]
    block_len = kv_pool.shape[2]
    holders = n_model * n_pool
    capacity = 2 * blocks_total // holders
    my_head = my_model * q_local // group_size
    prefix_count = prefix_len[my_pool]
    positions = prefix_count + jnp.arange(suffix, dtype=jnp.int32)
    normed = normalize(states[0], norm_gain)
    piece_rows = lax.all_gather(normed, "mp", axis=0, tiled=True)
    linear = jnp.concatenate(
        [
            jnp.dot(piece_rows, w_query, preferred_element_type=jnp.float32),
            jnp.dot(piece_rows, w_key, preferred_element_type=jnp.float32),
            jnp.dot(piece_rows, w_value, preferred_element_type=jnp.float32),
        ],
        1,
    )
    queries = rotate(
        (linear[:, :q_width] + q_bias.astype(jnp.float32)).reshape(suffix, q_local, HD), positions
    ).astype(jnp.bfloat16)
    key_raw = (linear[:, q_width : q_width + kv_local] + k_bias.astype(jnp.float32)).astype(
        jnp.bfloat16
    )
    value_raw = (linear[:, q_width + kv_local :] + v_bias.astype(jnp.float32)).astype(jnp.bfloat16)
    key_all, value_all = (
        lax.all_gather(key_raw, "mp", axis=1, tiled=True),
        lax.all_gather(value_raw, "mp", axis=1, tiled=True),
    )
    key_head = rotate(
        lax.dynamic_slice_in_dim(key_all, my_head * HD, HD, 1).astype(jnp.float32)[:, None, :],
        positions,
    ).astype(jnp.bfloat16)[:, 0]
    value_head = lax.dynamic_slice_in_dim(value_all, my_head * HD, HD, 1)
    row_start = my_model * row_count
    key_part = (
        lax.dynamic_slice_in_dim(key_all, row_start, row_count, 0)
        .astype(jnp.float32)
        .reshape(row_count, kv_heads, HD)
    )
    key_part = rotate(
        key_part, lax.dynamic_slice_in_dim(positions, row_start, row_count, 0)
    ).astype(jnp.bfloat16)
    value_part = lax.dynamic_slice_in_dim(value_all, row_start, row_count, 0).reshape(
        row_count, kv_heads, HD
    )
    cache_rows = jnp.stack([key_part, value_part], 2).reshape(1, row_count, kv_heads * 2 * HD)
    self_holder = my_model * n_pool + my_pool
    block_ids = jnp.arange(blocks_total, dtype=jnp.int32)
    live_blocks = block_ids[None, :] * block_len < prefix_len[:, None]
    chosen = listing((hit_holder == self_holder) & live_blocks, capacity)
    slot_ids = jnp.sum(jnp.where(chosen, hit_slot[:, None, :], 0), -1)
    pool_blocks = kv_pool[0].reshape(kv_pool.shape[1], block_len, kv_heads, 2 * HD)
    dest_heads = jnp.arange(n_model, dtype=jnp.int32) * q_local // group_size
    outgoing = pool_blocks[slot_ids[None, :, :], :, dest_heads[:, None, None], :]
    arrived = lax.all_to_all(
        outgoing.reshape(holders, capacity, block_len, 2 * HD),
        ("mp", "pool"),
        split_axis=0,
        concat_axis=0,
        tiled=True,
    )
    arrived = arrived.reshape(holders * capacity * block_len, 2 * HD)
    holder_ids = jnp.arange(holders, dtype=jnp.int32)
    mine_live = block_ids * block_len < prefix_count
    sources = listing(
        (hit_holder[my_pool][None, :] == holder_ids[:, None]) & mine_live[None, :], capacity
    )
    filled = jnp.clip(prefix_count - block_ids * block_len, 0, block_len)
    counts = jnp.sum(jnp.where(sources, filled[None, None, :], 0), -1)
    visible = (jnp.arange(block_len, dtype=jnp.int32)[None, None, :] < counts[..., None]).reshape(
        -1
    )
    score_scale = HD ** (-0.5)
    head_queries = queries.transpose(1, 0, 2)
    causal = jnp.arange(suffix)[None, :] <= jnp.arange(suffix)[:, None]
    scores = (
        jnp.einsum("aih,jh->aij", head_queries, key_head, preferred_element_type=jnp.float32)
        * score_scale
    )
    scores = jnp.where(causal[None], scores, -jnp.inf)
    row_peak = jnp.max(scores, -1, keepdims=True)
    weights = jnp.exp(scores - row_peak)
    denominator = jnp.sum(weights, -1, keepdims=True)
    numerator = jnp.einsum(
        "aij,jh->aih", weights.astype(jnp.bfloat16), value_head, preferred_element_type=jnp.float32
    )
    key_count = arrived.shape[0]
    key_span = math.gcd(key_count, 2048)
    keys_blocked = arrived.reshape(key_count // key_span, key_span, 2 * HD)
    visible_blocked = visible.reshape(key_count // key_span, key_span)

    def absorb(carry_state, pair_item):
        old_peak, old_denominator, old_numerator = carry_state
        key_block, seen_mask = pair_item
        block_scores = (
            jnp.einsum(
                "aih,jh->aij", head_queries, key_block[:, :HD], preferred_element_type=jnp.float32
            )
            * score_scale
        )
        block_scores = jnp.where(seen_mask[None, None, :], block_scores, -jnp.inf)
        new_peak = jnp.maximum(old_peak, jnp.max(block_scores, -1, keepdims=True))
        rescale = jnp.exp(old_peak - new_peak)
        block_weights = jnp.exp(block_scores - new_peak)
        new_denominator = old_denominator * rescale + jnp.sum(block_weights, -1, keepdims=True)
        new_numerator = old_numerator * rescale + jnp.einsum(
            "aij,jh->aih",
            block_weights.astype(jnp.bfloat16),
            key_block[:, HD:],
            preferred_element_type=jnp.float32,
        )
        return ((new_peak, new_denominator, new_numerator), None)

    (row_peak, denominator, numerator), _ = lax.scan(
        absorb, (row_peak, denominator, numerator), (keys_blocked, visible_blocked)
    )
    mixed_heads = (
        (numerator / denominator).astype(jnp.bfloat16).transpose(1, 0, 2).reshape(suffix, q_width)
    )
    summed = lax.psum_scatter(
        jnp.dot(mixed_heads, w_out, preferred_element_type=jnp.float32).astype(jnp.bfloat16),
        "mp",
        scatter_dimension=0,
        tiled=True,
    ).astype(jnp.float32)
    return (summed.astype(jnp.bfloat16).reshape(1, row_count, summed.shape[1]), cache_rows)


def solution(mesh):
    placed = (
        P(("groups", "pool"), "mp", None),
        P(),
        P(None, "mp"),
        P("mp"),
        P(None, "mp"),
        P(None, "mp"),
        P("mp"),
        P("mp"),
        P("mp", None),
        P(("groups", "mp", "pool"), None, None, None),
        P("groups", None),
        P("groups", None),
        P("groups"),
    )
    return jax.shard_map(
        on_device,
        mesh=mesh,
        in_specs=placed,
        out_specs=(P(("groups", "pool"), "mp", None), P(("groups", "pool"), "mp", None)),
        check_vma=False,
    )
```

profile of v0, /device:TPU:0, one launch (start us, length us, event | category | flops | bytes accessed | tf_op | source)
XLA Modules:
  0.0 665.6 jit_solution(5312171732272493825)
XLA Ops:
  7.2 1.7 fusion.18
  9.6 2.5 fusion.20
  15.1 3.7 copy.50
  18.7 3.4 copy.41
  22.2 8.7 %gather_fusion = bf16[512,16,256]{2,1,0:T(8,128)(2,1)} fusion(bf16[64,16,8,256]{3,1,2,0:T(8,128)(2,1)} %copy.41, s32[512]{0:T(512)S(1)} %reshape.385), kind=kCustom, calls=%fused_computation | custom fusion | bytes 8392704 | tf_op jit(solution)/shard_map/gather | solution.py:122
  30.8 7.4 %all-to-all-start = ((bf16[16,32,16,256]{3,2,1,0:T(8,128)(2,1)}), bf16[16,32,16,256]{3,2,1,0:T(8,128)(2,1)}, u32[]{:S(2)}, u32[]{:S(2)}) async-start(bf16[16,32,16,256]{3,2,1,0:T(8,128)(2,1)} %bitcast.127), calls=%async_computation | async-start | bytes 8388608 | tf_op jit(solution)/shard_map/all_to_all | solution.py:123
  43.9 175.8 %all-gather.4.cloned.1.call-done = bf16[512,8192]{1,0:T(8,128)(2,1)} async-done(((bf16[64,8192]{1,0:T(8,128)(2,1)}), bf16[512,8192]{1,0:T(8,128)(2,1)}) %all-gather.4.cloned.1.call-update) | async-done | bytes 8388624 | tf_op jit(solution)/shard_map/all_gather | solution.py:77
  219.7 6.4 fusion.21
  226.3 14.4 %add_bitcast_fusion = f32[64,8,8,128]{3,1,2,0:T(8,128)S(1)} fusion(bf16[512,8192]{1,0:T(8,128)(2,1)} %all-gather.4.cloned.1.call-done, bf16[8192,1024]{1,0:T(8,128)(2,1)} %param.17, f32[1024]{0:T(1024)S(1)} %convert_element_type.76), kind=kOutput, calls=%fused_computation.37 | convolution fusion | flops 8590458880 | bytes 27267072 | tf_op jit(solution)/shard_map/dot_general | solution.py:80
  241.3 6.4 fusion.22
  249.8 14.6 %all-gather.6.cloned.1.call-done = bf16[512,1024]{1,0:T(8,128)(2,1)} async-done(((bf16[512,128]{1,0:T(8,128)(2,1)}), bf16[512,1024]{1,0:T(8,128)(2,1)}) %all-gather.6.cloned.1.call-update) | async-done | bytes 1048592 | tf_op jit(solution)/shard_map/all_gather | solution.py:94
  266.6 1.4 fusion.12
  268.1 3.2 copy-done.2
  271.3 1.7 fusion.14
  273.0 32.5 %all-gather.8.cloned.1.call-done = bf16[512,1024]{1,0:T(8,128)(2,1)} async-done(((bf16[512,128]{1,0:T(8,128)(2,1)}), bf16[512,1024]{1,0:T(8,128)(2,1)}) %all-gather.8.cloned.1.call-update) | async-done | bytes 1048592 | tf_op jit(solution)/shard_map/all_gather | solution.py:95
  305.5 6.7 %fusion.15 = f32[8,512,128]{2,1,0:T(8,128)} fusion(f32[8,512,512]{1,2,0:T(8,128)} %copy-done.2, f32[8,512]{1,0:T(8,128)S(1)} %get-tuple-element.74, pred[512,512]{0,1:T(8,128)(4,1)S(1)} %iota_compare_fusion, bf16[512,1024]{1,0:T(8,128)(2,1)} %all-gather.8.cloned.1.call-done, s32[]{:T(128)S(6)} %select_n.61), kind=kOutput, calls=%fused_computation.27 | convolution fusion | flops 545259520 | bytes 10895364 | tf_op jit(solution)/shard_map/aij,jh->aih/dot_general | solution.py:152
  312.3 179.2 %while.14 = (s32[]{:T(128)}, f32[8,512,1]{1,0,2:T(8,128)S(1)}, f32[8,512,1]{1,0,2:T(8,128)S(1)}, f32[8,512,128]{2,1,0:T(8,128)}, pred[4,2048]{1,0:T(4,128)(4,1)S...) while((s32[]{:T(128)}, f32[8,512,1]{1,0,2:T(8,128)S(1)}, ...), condition=%wide.region_12.13_spmd, body=%wide.region_9.12_spmd.sunk | while | flops 4388302848 | bytes 126101664 | solution.py:182
  313.6 12.5 %bitcast_reduce_fusion.2 = (f32[8,512]{1,0:T(8,128)S(1)}, f32[2048,8,512]{2,0,1:T(8,128)}) fusion(pred[2048]{0:T(1024)(128)(4,1)S(1)} %dynamic-slice_reduce_fusion.2, bf16[8,512,128]{2,1,0:T(8,128)(2,1)S(1)} %get-tuple-element.151, bf16[2048,256]{1,0:T(8,128)(2,1)S(1)} %dynamic-slice_bitcast_fusion.3), kind=kOutput, calls=%fused_computation.2.clone.1 | convolution fusion | flops 2172645376 | bytes 35145728 | tf_op jit(solution)/shard_map/while/body/eval_jaxpr/aih,jh->aij/dot_general | solution.py:164
  326.1 14.7 %fusion.74 = f32[8,512]{1,0:T(8,128)S(1)} fusion(f32[2048,8,512]{2,0,1:T(8,128)} %get-tuple-element.127, f32[8,512]{1,0:T(8,128)S(1)} %bitcast.129, pred[2048]{0:T(1024)(128)(4,1)S(1)} %dynamic-slice_reduce_fusion.2), kind=kLoop, calls=%fused_computation.6.clone.1 | loop fusion | flops 33550336 | bytes 33589248 | tf_op jit(solution)/shard_map/while/body/eval_jaxpr/reduce_sum | solution.py:173
  340.9 14.9 %multiply_add_fusion.2 = f32[8,512,128]{2,1,0:T(8,128)S(1)} fusion(f32[8,512,128]{2,1,0:T(8,128)S(1)} %copy-done.3, f32[2048,8,512]{2,0,1:T(8,128)} %get-tuple-element.127, f32[8,512]{1,0:T(8,128)S(1)} %bitcast.130, pred[2048]{0:T(1024)(128)(4,1)S(1)} %dynamic-slice_reduce_fusion.2, f32[8,512]{1,0:T(8,128)S(1)} %get-tuple-element.128, ...), kind=kOutput, calls=%fused_computation.9.clone.1 | convolution fusion | flops 2182086656 | bytes 38307840 | tf_op jit(solution)/shard_map/while/body/eval_jaxpr/aij,jh->aih/dot_general | solution.py:174
  358.4 12.5 %bitcast_reduce_fusion.2 = (f32[8,512]{1,0:T(8,128)S(1)}, f32[2048,8,512]{2,0,1:T(8,128)}) fusion(pred[2048]{0:T(1024)(128)(4,1)S(1)} %dynamic-slice_reduce_fusion.2, bf16[8,512,128]{2,1,0:T(8,128)(2,1)S(1)} %get-tuple-element.151, bf16[2048,256]{1,0:T(8,128)(2,1)S(1)} %dynamic-slice_bitcast_fusion.3), kind=kOutput, calls=%fused_computation.2.clone.1 | convolution fusion | flops 2172645376 | bytes 35145728 | tf_op jit(solution)/shard_map/while/body/eval_jaxpr/aih,jh->aij/dot_general | solution.py:164
  370.9 14.7 %fusion.74 = f32[8,512]{1,0:T(8,128)S(1)} fusion(f32[2048,8,512]{2,0,1:T(8,128)} %get-tuple-element.127, f32[8,512]{1,0:T(8,128)S(1)} %bitcast.129, pred[2048]{0:T(1024)(128)(4,1)S(1)} %dynamic-slice_reduce_fusion.2), kind=kLoop, calls=%fused_computation.6.clone.1 | loop fusion | flops 33550336 | bytes 33589248 | tf_op jit(solution)/shard_map/while/body/eval_jaxpr/reduce_sum | solution.py:173
  385.7 14.9 %multiply_add_fusion.2 = f32[8,512,128]{2,1,0:T(8,128)S(1)} fusion(f32[8,512,128]{2,1,0:T(8,128)S(1)} %copy-done.3, f32[2048,8,512]{2,0,1:T(8,128)} %get-tuple-element.127, f32[8,512]{1,0:T(8,128)S(1)} %bitcast.130, pred[2048]{0:T(1024)(128)(4,1)S(1)} %dynamic-slice_reduce_fusion.2, f32[8,512]{1,0:T(8,128)S(1)} %get-tuple-element.128, ...), kind=kOutput, calls=%fused_computation.9.clone.1 | convolution fusion | flops 2182086656 | bytes 38307840 | tf_op jit(solution)/shard_map/while/body/eval_jaxpr/aij,jh->aih/dot_general | solution.py:174
  403.2 12.5 %bitcast_reduce_fusion.2 = (f32[8,512]{1,0:T(8,128)S(1)}, f32[2048,8,512]{2,0,1:T(8,128)}) fusion(pred[2048]{0:T(1024)(128)(4,1)S(1)} %dynamic-slice_reduce_fusion.2, bf16[8,512,128]{2,1,0:T(8,128)(2,1)S(1)} %get-tuple-element.151, bf16[2048,256]{1,0:T(8,128)(2,1)S(1)} %dynamic-slice_bitcast_fusion.3), kind=kOutput, calls=%fused_computation.2.clone.1 | convolution fusion | flops 2172645376 | bytes 35145728 | tf_op jit(solution)/shard_map/while/body/eval_jaxpr/aih,jh->aij/dot_general | solution.py:164
  415.7 14.7 %fusion.74 = f32[8,512]{1,0:T(8,128)S(1)} fusion(f32[2048,8,512]{2,0,1:T(8,128)} %get-tuple-element.127, f32[8,512]{1,0:T(8,128)S(1)} %bitcast.129, pred[2048]{0:T(1024)(128)(4,1)S(1)} %dynamic-slice_reduce_fusion.2), kind=kLoop, calls=%fused_computation.6.clone.1 | loop fusion | flops 33550336 | bytes 33589248 | tf_op jit(solution)/shard_map/while/body/eval_jaxpr/reduce_sum | solution.py:173
  430.4 14.9 %multiply_add_fusion.2 = f32[8,512,128]{2,1,0:T(8,128)S(1)} fusion(f32[8,512,128]{2,1,0:T(8,128)S(1)} %copy-done.3, f32[2048,8,512]{2,0,1:T(8,128)} %get-tuple-element.127, f32[8,512]{1,0:T(8,128)S(1)} %bitcast.130, pred[2048]{0:T(1024)(128)(4,1)S(1)} %dynamic-slice_reduce_fusion.2, f32[8,512]{1,0:T(8,128)S(1)} %get-tuple-element.128, ...), kind=kOutput, calls=%fused_computation.9.clone.1 | convolution fusion | flops 2182086656 | bytes 38307840 | tf_op jit(solution)/shard_map/while/body/eval_jaxpr/aij,jh->aih/dot_general | solution.py:174
  448.0 12.5 %bitcast_reduce_fusion.2 = (f32[8,512]{1,0:T(8,128)S(1)}, f32[2048,8,512]{2,0,1:T(8,128)}) fusion(pred[2048]{0:T(1024)(128)(4,1)S(1)} %dynamic-slice_reduce_fusion.2, bf16[8,512,128]{2,1,0:T(8,128)(2,1)S(1)} %get-tuple-element.151, bf16[2048,256]{1,0:T(8,128)(2,1)S(1)} %dynamic-slice_bitcast_fusion.3), kind=kOutput, calls=%fused_computation.2.clone.1 | convolution fusion | flops 2172645376 | bytes 35145728 | tf_op jit(solution)/shard_map/while/body/eval_jaxpr/aih,jh->aij/dot_general | solution.py:164
  460.5 14.7 %fusion.74 = f32[8,512]{1,0:T(8,128)S(1)} fusion(f32[2048,8,512]{2,0,1:T(8,128)} %get-tuple-element.127, f32[8,512]{1,0:T(8,128)S(1)} %bitcast.129, pred[2048]{0:T(1024)(128)(4,1)S(1)} %dynamic-slice_reduce_fusion.2), kind=kLoop, calls=%fused_computation.6.clone.1 | loop fusion | flops 33550336 | bytes 33589248 | tf_op jit(solution)/shard_map/while/body/eval_jaxpr/reduce_sum | solution.py:173
  475.2 14.9 %multiply_add_fusion.2 = f32[8,512,128]{2,1,0:T(8,128)S(1)} fusion(f32[8,512,128]{2,1,0:T(8,128)S(1)} %copy-done.3, f32[2048,8,512]{2,0,1:T(8,128)} %get-tuple-element.127, f32[8,512]{1,0:T(8,128)S(1)} %bitcast.130, pred[2048]{0:T(1024)(128)(4,1)S(1)} %dynamic-slice_reduce_fusion.2, f32[8,512]{1,0:T(8,128)S(1)} %get-tuple-element.128, ...), kind=kOutput, calls=%fused_computation.9.clone.1 | convolution fusion | flops 2182086656 | bytes 38307840 | tf_op jit(solution)/shard_map/while/body/eval_jaxpr/aij,jh->aih/dot_general | solution.py:174
  491.4 1.9 copy.42
  493.7 17.4 %convolution_convert_fusion = bf16[512,8192]{1,0:T(8,128)(2,1)} fusion(bf16[512,1024]{0,1:T(8,128)(2,1)S(1)} %bitcast.134, bf16[1024,8192]{1,0:T(8,128)(2,1)} %param.23), kind=kOutput, calls=%fused_computation.21 | convolution fusion | flops 8594128896 | bytes 26214400 | tf_op jit(solution)/shard_map/dot_general | solution.py:189
  514.4 144.7 %reduce-scatter.2.cloned.1.call-done = bf16[64,8192]{1,0:T(8,128)(2,1)} async-done(((bf16[512,8192]{1,0:T(8,128)(2,1)}), bf16[64,8192]{1,0:T(8,128)(2,1)}) %reduce-scatter.2.cloned.1.call-update) | async-done | bytes 1048592 | tf_op jit(solution)/shard_map/reduce_scatter | solution.py:188
  (120 shorter events, 28.3 us)
Async XLA Ops:
  7.2 212.5 %copy-start = (bf16[8192,128]{1,0:T(8,128)(2,1)S(1)}, bf16[8192,128]{1,0:T(8,128)(2,1)}, u32[]{:S(2)}) copy-start(bf16[8192,128]{1,0:T(8,128)(2,1)} %param.19) | copy-start | bytes 6291460
  7.2 212.5 %all-gather.4.cloned.1.call-start = ((), (), s32[]{:S(2)}) async-start(), calls=%async_computation.2 | async-start | bytes 9437184 | tf_op jit(solution)/shard_map/all_gather | solution.py:77
  22.1 16.1 %copy-start.9 = (s32[2]{0:T(128)S(1)}, s32[2]{0:T(128)}, u32[]{:S(2)}) copy-start(s32[2]{0:T(128)} %param.27) | copy-start | bytes 28
  22.1 16.7 %copy-start.11 = (bf16[128]{0:T(256)(128)(2,1)S(1)}, bf16[128]{0:T(256)(128)(2,1)}, u32[]{:S(2)}) copy-start(bf16[128]{0:T(256)(128)(2,1)} %param.21) | copy-start | bytes 772
  22.1 16.7 %copy-start.12 = (bf16[128]{0:T(256)(128)(2,1)S(1)}, bf16[128]{0:T(256)(128)(2,1)}, u32[]{:S(2)}) copy-start(bf16[128]{0:T(256)(128)(2,1)} %param.22) | copy-start | bytes 772
  22.1 16.7 %copy-start.8 = (bf16[1024]{0:T(1024)(128)(2,1)S(1)}, bf16[1024]{0:T(1024)(128)(2,1)}, u32[]{:S(2)}) copy-start(bf16[1024]{0:T(1024)(128)(2,1)} %param.18) | copy-start | bytes 6148
  22.1 17.3 %copy-start.5 = (s32[2,256]{1,0:T(2,128)S(1)}, s32[2,256]{1,0:T(2,128)}, u32[]{:S(2)}) copy-start(s32[2,256]{1,0:T(2,128)} %param.25) | copy-start | bytes 6148
  30.8 281.4 %all-to-all-start = ((bf16[16,32,16,256]{3,2,1,0:T(8,128)(2,1)}), bf16[16,32,16,256]{3,2,1,0:T(8,128)(2,1)}, u32[]{:S(2)}, u32[]{:S(2)}) async-start(bf16[16,32,16,256]{3,2,1,0:T(8,128)(2,1)} %bitcast.127), calls=%async_computation | async-start | bytes 8388608 | tf_op jit(solution)/shard_map/all_to_all | solution.py:123
  38.2 226.2 %all-gather.6.cloned.1.call-start = ((), (), s32[]{:S(2)}) async-start(), calls=%async_computation.3 | async-start | bytes 1179648 | tf_op jit(solution)/shard_map/all_gather | solution.py:94
  42.2 223.2 %copy-start.6 = (f32[64]{0:T(128)}, f32[64]{0:T(128)S(1)}, u32[]{:S(2)}) copy-start(f32[64]{0:T(128)S(1)} %multiply_power_fusion) | copy-start | bytes 772
  226.1 79.4 %all-gather.8.cloned.1.call-start = ((), (), s32[]{:S(2)}) async-start(), calls=%async_computation.4 | async-start | bytes 1179648 | tf_op jit(solution)/shard_map/all_gather | solution.py:95
  226.3 14.9 %copy-start.10 = (bf16[8192,128]{1,0:T(8,128)(2,1)S(1)}, bf16[8192,128]{1,0:T(8,128)(2,1)}, u32[]{:S(2)}) copy-start(bf16[8192,128]{1,0:T(8,128)(2,1)} %param.20) | copy-start | bytes 6291460
  247.7 411.4 %reduce-scatter.2.cloned.1.call-start = ((), (), s32[]{:S(2)}) async-start(), calls=%async_computation.5 | async-start | bytes 9437184 | tf_op jit(solution)/shard_map/reduce_scatter | solution.py:188
  268.0 3.2 copy-start.2
  326.1 14.7 %copy-start.3 = (f32[8,512,128]{2,1,0:T(8,128)S(1)}, f32[8,512,128]{2,1,0:T(8,128)}, u32[]{:S(2)}) copy-start(f32[8,512,128]{2,1,0:T(8,128)} %get-tuple-element.140) | copy-start | bytes 6291460 | tf_op jit(solution)/shard_map/while
  355.8 1.3 copy-start.4
  370.9 14.7 %copy-start.3 = (f32[8,512,128]{2,1,0:T(8,128)S(1)}, f32[8,512,128]{2,1,0:T(8,128)}, u32[]{:S(2)}) copy-start(f32[8,512,128]{2,1,0:T(8,128)} %get-tuple-element.140) | copy-start | bytes 6291460 | tf_op jit(solution)/shard_map/while
  400.6 1.3 copy-start.4
  415.7 14.7 %copy-start.3 = (f32[8,512,128]{2,1,0:T(8,128)S(1)}, f32[8,512,128]{2,1,0:T(8,128)}, u32[]{:S(2)}) copy-start(f32[8,512,128]{2,1,0:T(8,128)} %get-tuple-element.140) | copy-start | bytes 6291460 | tf_op jit(solution)/shard_map/while
  445.3 1.3 copy-start.4
  460.5 14.7 %copy-start.3 = (f32[8,512,128]{2,1,0:T(8,128)S(1)}, f32[8,512,128]{2,1,0:T(8,128)}, u32[]{:S(2)}) copy-start(f32[8,512,128]{2,1,0:T(8,128)} %get-tuple-element.140) | copy-start | bytes 6291460 | tf_op jit(solution)/shard_map/while
  490.1 1.3 copy-start.4
  493.7 165.5 %copy-start.1 = (bf16[8192,128]{1,0:T(8,128)(2,1)S(1)}, bf16[8192,128]{1,0:T(8,128)(2,1)}, u32[]{:S(2)}) copy-start(bf16[8192,128]{1,0:T(8,128)(2,1)} %param.19) | copy-start | bytes 6291460
  511.0 0.7 copy-start.7
Sparse Core Ops, SparseCore 0:
  12.3 207.3 all-gather.3
  226.2 38.1 all-gather.5
  267.1 38.4 all-gather.7
  511.2 147.8 reduce-scatter.1
where the time goes:
time: 667 us; the launch traced here: 666 us
  waiting for transfers between devices  368 us (55%)
  matrix products  162 us (24%)
  other arithmetic  78.6 us (12%)
  local copies, waits for them, and re-layouts  35 us (5%)
  between operations  14.2 us (2%)
  starting transfers between devices  7.69 us (1%)
    all_gather x1, waiting for transfers between devices, on_device(): piece_rows = lax.all_gather(normed, 'mp', axis=0, tiled=True)  176 us
    reduce_scatter x1, waiting for transfers between devices, on_device(): lax.psum_scatter(jnp.dot(mixed_heads, w_out, preferred_element_type=jnp.f...  145 us
    dot_general x4, matrix products, absorb(): jnp.einsum('aij,jh->aih', block_weights.astype(jnp.bfloat16), key_block[:...  59.5 us
    reduce_sum x4, other arithmetic, absorb(): jnp.sum(block_weights, -1, keepdims=True)  58.9 us
    dot_general x4, matrix products, absorb(): jnp.einsum('aih,jh->aij', head_queries, key_block[:, :HD], preferred_elem...  50 us
    all_gather x1, waiting for transfers between devices, on_device(): lax.all_gather(value_raw, 'mp', axis=1, tiled=True)  32.5 us
    dot_general x1, matrix products, on_device(): jnp.dot(mixed_heads, w_out, preferred_element_type=jnp.float32)  17.4 us
    all_gather x1, waiting for transfers between devices, on_device(): lax.all_gather(key_raw, 'mp', axis=1, tiled=True)  14.6 us
  transfers between devices with their start and end apart: 5, of which 4 were waited for; matrix products, arithmetic and copies ran while one was open for 10% of the time, Pallas kernels for 0%

commit v1 on v0

v1 whole, which is shorter than its diff:
```python
import functools
import math

import jax
import jax.numpy as jnp
from jax import lax
from jax.experimental import pallas as pl
from jax.experimental.pallas import tpu as pltpu
from jax.sharding import PartitionSpec as P

QH = 64
HD = 128
ROPE_BASE = 1000000.0
EPSILON = 1e-06
SCORE_SCALE = HD ** (-0.5) * math.log2(math.e)
VMEM_LIMIT = 56 * 1024 * 1024
GATHER_PIECES = 4
ROW_CHUNKS = 4


def angle_tables(positions):
    frequency = jnp.power(
        jnp.float32(ROPE_BASE), -2.0 * jnp.arange(HD // 2, dtype=jnp.float32) / HD
    )
    angles = positions.astype(jnp.float32)[:, None] * frequency[None, :]
    return jnp.cos(angles), jnp.sin(angles)


def rotate(vectors, cosine, sine):
    first_half = vectors[..., : HD // 2]
    second = vectors[..., HD // 2 :]
    cosine = cosine[:, None, :]
    sine = sine[:, None, :]
    return jnp.concatenate(
        [first_half * cosine - second * sine, second * cosine + first_half * sine], -1
    )


def normalize(states, gain_vec):
    values = states.astype(jnp.float32)
    inv_rms = lax.rsqrt(jnp.mean(values * values, axis=-1, keepdims=True) + EPSILON)
    return (values * inv_rms * gain_vec.astype(jnp.float32)).astype(jnp.bfloat16)


def listing(owned_mask, capacity):
    rank_order = jnp.cumsum(owned_mask.astype(jnp.int32), -1) - 1
    slot_index = jnp.arange(capacity, dtype=jnp.int32)
    return owned_mask[..., None, :] & (rank_order[..., None, :] == slot_index[:, None])


def pack_kernel(dest_heads, slots_ref, pool_ref, out_ref):
    requests, capacity = slots_ref.shape

    def place(step, _):
        request = step // capacity
        rank = step % capacity
        block = pool_ref[slots_ref[request, rank]]
        for dest, head in enumerate(dest_heads):
            out_ref[dest, request, rank] = block[:, head * 2 * HD : (head + 1) * 2 * HD]
        return 0

    lax.fori_loop(0, requests * capacity, place, 0)


def pack_blocks(pool, slots, dest_heads):
    block_len = pool.shape[1]
    shape = (len(dest_heads), slots.shape[0], slots.shape[1], block_len, 2 * HD)
    return pl.pallas_call(
        functools.partial(pack_kernel, dest_heads),
        out_shape=jax.ShapeDtypeStruct(shape, jnp.bfloat16),
        in_specs=[
            pl.BlockSpec(memory_space=pltpu.SMEM),
            pl.BlockSpec(memory_space=pltpu.VMEM),
        ],
        out_specs=pl.BlockSpec(memory_space=pltpu.VMEM),
        compiler_params=pltpu.CompilerParams(vmem_limit_bytes=VMEM_LIMIT),
        name="pack_blocks",
    )(slots, pool)


def order_kernel(length_ref, where_ref, arrived_ref, key_ref, value_ref):
    block_len = arrived_ref.shape[1]
    length = length_ref[0]
    first = arrived_ref[where_ref[0]][:1, :HD].astype(jnp.float32)
    row = lax.broadcasted_iota(jnp.int32, (block_len, HD), 0)

    def place(block_id, _):
        block = arrived_ref[where_ref[block_id]].astype(jnp.float32)
        start = pl.multiple_of(block_id * block_len, block_len)
        seen = row + start < length
        rows = pl.ds(start, block_len)
        key_ref[rows, :] = jnp.where(seen, block[:, :HD], first).astype(jnp.bfloat16)
        value_ref[rows, :HD] = jnp.where(seen, block[:, HD:], 0.0).astype(jnp.bfloat16)
        value_ref[rows, HD:] = jnp.where(seen, 1.0, 0.0).astype(jnp.bfloat16)
        return 0

    lax.fori_loop(0, where_ref.shape[0], place, 0)


def order_blocks(arrived, where, length):
    tokens = where.shape[0] * arrived.shape[1]
    return pl.pallas_call(
        order_kernel,
        out_shape=(
            jax.ShapeDtypeStruct((tokens, HD), jnp.bfloat16),
            jax.ShapeDtypeStruct((tokens, 2 * HD), jnp.bfloat16),
        ),
        in_specs=[
            pl.BlockSpec(memory_space=pltpu.SMEM),
            pl.BlockSpec(memory_space=pltpu.SMEM),
            pl.BlockSpec(memory_space=pltpu.VMEM),
        ],
        out_specs=(
            pl.BlockSpec(memory_space=pltpu.VMEM),
            pl.BlockSpec(memory_space=pltpu.VMEM),
        ),
        compiler_params=pltpu.CompilerParams(vmem_limit_bytes=VMEM_LIMIT),
        name="order_blocks",
    )(length, where, arrived)


def dot_keys(queries, keys):
    return lax.dot_general(
        queries, keys, (((1,), (1,)), ((), ())), preferred_element_type=jnp.float32
    )


def attend_kernel(
    span, row_step, chunk, query_ref, key_ref, value_ref, new_key_ref, new_value_ref, out_ref
):
    queries = query_ref[0]
    rows = queries.shape[0]
    spans = key_ref.shape[0] // span
    suffix = new_key_ref.shape[0]
    stride = suffix * row_step // rows
    local = lax.broadcasted_iota(jnp.int32, (rows, suffix), 0)
    token = (local // row_step) * stride + chunk * row_step + local % row_step
    causal = lax.broadcasted_iota(jnp.int32, (rows, suffix), 1) <= token
    scores = jnp.where(causal, dot_keys(queries, new_key_ref[...]), -jnp.inf)
    peak = jnp.max(scores, axis=1, keepdims=True)
    total = None
    values = new_value_ref[...]
    for step in range(spans + 1):
        if step < spans:
            next_scores = dot_keys(queries, key_ref[step * span : (step + 1) * span, :])
            next_peak = jnp.maximum(peak, jnp.max(next_scores, axis=1, keepdims=True))
        weights = jnp.exp2((scores - peak) * SCORE_SCALE).astype(jnp.bfloat16)
        product = jnp.dot(weights, values, preferred_element_type=jnp.float32)
        total = product if total is None else total + product
        if step < spans:
            total = total * jnp.exp2((peak - next_peak) * SCORE_SCALE)
            scores, peak = next_scores, next_peak
            values = value_ref[step * span : (step + 1) * span, :]
    out_ref[...] = (total[:, :HD] / total[:, HD:]).astype(jnp.bfloat16)


def attend(queries, keys, values, new_keys, new_values, row_step, chunk):
    heads, rows, _ = queries.shape
    span = math.gcd(keys.shape[0], 1024)
    whole = lambda array: pl.BlockSpec(array.shape, lambda head: (0, 0))
    count = keys.shape[0] + new_keys.shape[0]
    return pl.pallas_call(
        functools.partial(attend_kernel, span, row_step, chunk),
        grid=(heads,),
        out_shape=jax.ShapeDtypeStruct((rows, heads * HD), jnp.bfloat16),
        in_specs=[
            pl.BlockSpec((1, rows, HD), lambda head: (head, 0, 0)),
            whole(keys),
            whole(values),
            whole(new_keys),
            whole(new_values),
        ],
        out_specs=pl.BlockSpec((rows, HD), lambda head: (0, head)),
        compiler_params=pltpu.CompilerParams(vmem_limit_bytes=VMEM_LIMIT),
        cost_estimate=pl.CostEstimate(
            flops=heads * rows * count * HD * 8,
            bytes_accessed=2 * (count * 3 * HD + 2 * heads * rows * HD),
            transcendentals=heads * rows * count,
        ),
        name="attend",
    )(queries, keys, values, new_keys, new_values)


def on_device(
    n_model,
    n_pool,
    states,
    norm_gain,
    w_query,
    q_bias,
    w_key,
    w_value,
    k_bias,
    v_bias,
    w_out,
    kv_pool,
    hit_holder,
    hit_slot,
    prefix_len,
):
    my_model = lax.axis_index("mp")
    my_pool = lax.axis_index("pool")
    row_count, width = states.shape[1:]
    suffix = row_count * n_model
    q_width = w_query.shape[1]
    q_local = q_width // HD
    kv_local = w_key.shape[1]
    kv_heads = kv_local * n_model // HD
    group_size = QH // kv_heads
    blocks_total = hit_holder.shape[1]
    block_len = kv_pool.shape[2]
    holders = n_model * n_pool
    capacity = 2 * blocks_total // holders
    sharers = HD // kv_local
    dest_heads = tuple(dest * q_local // group_size for dest in range(n_model))

    self_holder = my_model * n_pool + my_pool
    chosen = listing(hit_holder == self_holder, capacity)
    slot_ids = jnp.sum(jnp.where(chosen, hit_slot[:, None, :], 0), -1)
    outgoing = pack_blocks(kv_pool[0], slot_ids, dest_heads)
    arrived = lax.all_to_all(
        outgoing.reshape(holders, capacity * block_len, 2 * HD),
        ("mp", "pool"),
        split_axis=0,
        concat_axis=0,
        tiled=True,
    ).reshape(holders * capacity, block_len, 2 * HD)
    my_holder = hit_holder[my_pool]
    block_ids = jnp.arange(blocks_total, dtype=jnp.int32)
    earlier = (my_holder[:, None] == my_holder[None, :]) & (block_ids[None, :] < block_ids[:, None])
    where = my_holder * capacity + jnp.sum(earlier.astype(jnp.int32), -1)
    prefix_count = prefix_len[my_pool]

    normed = normalize(states[0], norm_gain)
    piece = width // GATHER_PIECES
    query_sum = key_sum = value_sum = None
    for index in range(GATHER_PIECES):
        cols = slice(index * piece, (index + 1) * piece)
        tokens = lax.all_gather(normed[:, cols], "mp", axis=0, tiled=True)
        parts = [
            jnp.dot(tokens, weight[cols], preferred_element_type=jnp.float32)
            for weight in (w_query, w_key, w_value)
        ]
        if index == 0:
            query_sum, key_sum, value_sum = parts
        else:
            query_sum, key_sum, value_sum = (
                query_sum + parts[0],
                key_sum + parts[1],
                value_sum + parts[2],
            )
    positions = prefix_count + jnp.arange(suffix, dtype=jnp.int32)
    cosine, sine = angle_tables(positions)
    queries = rotate(
        (query_sum + q_bias.astype(jnp.float32)).reshape(suffix, q_local, HD), cosine, sine
    ).astype(jnp.bfloat16)
    key_raw = (key_sum + k_bias.astype(jnp.float32)).astype(jnp.bfloat16)
    value_raw = (value_sum + v_bias.astype(jnp.float32)).astype(jnp.bfloat16)
    if sharers > 1:
        together = [
            [first + other for other in range(sharers)] for first in range(0, n_model, sharers)
        ]
        key_raw, value_head = (
            lax.all_gather(part, "mp", axis=1, tiled=True, axis_index_groups=together)
            for part in (key_raw, value_raw)
        )
    else:
        value_head = value_raw
    key_head = rotate(key_raw.astype(jnp.float32)[:, None, :], cosine, sine).astype(jnp.bfloat16)[
        :, 0
    ]

    if sharers > 1:
        first_col = (my_model % sharers) * kv_local
        key_cols = lax.dynamic_slice_in_dim(key_head, first_col, kv_local, 1)
        value_cols = value_raw
    else:
        key_cols, value_cols = key_head, value_head
    pairs = jnp.stack([key_cols, value_cols], 1).reshape(n_model, row_count, 2, kv_local)
    pairs = lax.all_to_all(pairs, "mp", split_axis=0, concat_axis=0, tiled=True)
    cache_rows = (
        pairs.reshape(kv_heads, sharers, row_count, 2, kv_local)
        .transpose(2, 0, 3, 1, 4)
        .reshape(1, row_count, kv_heads * 2 * HD)
    )

    prefix_keys, prefix_values = order_blocks(arrived, where, prefix_count.reshape(1))
    new_values = jnp.concatenate([value_head, jnp.ones_like(value_head)], 1)

    row_step = row_count // ROW_CHUNKS
    by_chunk = queries.reshape(n_model, ROW_CHUNKS, row_step, q_local, HD).transpose(1, 3, 0, 2, 4)
    summed = []
    for chunk in range(ROW_CHUNKS):
        mixed = attend(
            by_chunk[chunk].reshape(q_local, n_model * row_step, HD),
            prefix_keys,
            prefix_values,
            key_head,
            new_values,
            row_step,
            chunk,
        )
        share = jnp.dot(mixed, w_out, preferred_element_type=jnp.float32).astype(jnp.bfloat16)
        summed.append(lax.psum_scatter(share, "mp", scatter_dimension=0, tiled=True))
    return (jnp.concatenate(summed, 0)[None], cache_rows)


def solution(mesh):
    placed = (
        P(("groups", "pool"), "mp", None),
        P(),
        P(None, "mp"),
        P("mp"),
        P(None, "mp"),
        P(None, "mp"),
        P("mp"),
        P("mp"),
        P("mp", None),
        P(("groups", "mp", "pool"), None, None, None),
        P("groups", None),
        P("groups", None),
        P("groups"),
    )
    return jax.shard_map(
        functools.partial(on_device, mesh.shape["mp"], mesh.shape["pool"]),
        mesh=mesh,
        in_specs=placed,
        out_specs=(P(("groups", "pool"), "mp", None), P(("groups", "pool"), "mp", None)),
        check_vma=False,
    )
```

time: 667 us -> 606 us (0.909)
  matrix products: 162 us -> 68.9 us
  other arithmetic: 78.6 us -> 13.5 us
  Pallas kernels: 0 us -> 55.7 us
  waiting for transfers between devices: 368 us -> 423 us
  local copies, waits for them, and re-layouts: 35 us -> 10 us
  blocking collectives: 0 us -> 11.8 us
    dot_general x14 -> x16, matrix products: 162 us -> 68.9 us  [the longest x4 38.5 us: on_device(): jnp.dot(mixed, w_out, preferred_element_type=jnp.float32)]
    reduce_sum x6 -> x1, other arithmetic: 61 us -> 0.18 us  [on_device(): where = my_holder * capacity + jnp.sum(earlier.astype(jnp.int32), -1)]
    pallas_call x0 -> x6, Pallas kernels: none -> 55.7 us  [the longest x4 43.7 us: attend(): pl.pallas_call(functools.partial(attend_kernel, span, row_step, chunk), g...]
    reduce_scatter x1 -> x4, waiting for transfers between devices: 145 us -> 199 us  [on_device(): lax.psum_scatter(share, 'mp', scatter_dimension=0, tiled=True)]
    all_to_all x0 -> x1, blocking collectives: none -> 11.8 us  [on_device(): pairs = lax.all_to_all(pairs, 'mp', split_axis=0, concat_axis=0, tiled=True)]
    gather x1 -> x0, local copies, waits for them, and re-layouts: 8.68 us -> none  [on_device(): pool_blocks[slot_ids[None, :, :], :, dest_heads[:, None, None], :]]
    while x21 -> x0, local copies, waits for them, and re-layouts: 6.99 us -> none
    all_gather x3 -> x4, waiting for transfers between devices: 223 us -> 221 us  [on_device(): tokens = lax.all_gather(normed[:, cols], 'mp', axis=0, tiled=True)]
  transfers between devices with their start and end apart: 5 -> 9, of which waited for: 4 -> 7; matrix products, arithmetic and copies ran while one was open for 10% -> 12% of each run, Pallas kernels for 0% -> 6%
where the time goes in v1:
time: 606 us; the launch traced here: 605 us
  waiting for transfers between devices  423 us (70%)
  matrix products  68.9 us (11%)
  Pallas kernels  55.7 us (9%)
  between operations  14.4 us (2%)
  other arithmetic  13.5 us (2%)
  blocking collectives  11.8 us (2%)
  local copies, waits for them, and re-layouts  10 us (2%)
  starting transfers between devices  8.12 us (1%)
    all_gather x4, waiting for transfers between devices, on_device(): tokens = lax.all_gather(normed[:, cols], 'mp', axis=0, tiled=True)  221 us
    reduce_scatter x4, waiting for transfers between devices, on_device(): lax.psum_scatter(share, 'mp', scatter_dimension=0, tiled=True)  199 us
    pallas_call x4, Pallas kernels, attend(): pl.pallas_call(functools.partial(attend_kernel, span, row_step, chunk), g...  43.7 us
    dot_general x4, matrix products, on_device(): jnp.dot(mixed, w_out, preferred_element_type=jnp.float32)  38.5 us
    dot_general x12, matrix products, on_device(): jnp.dot(tokens, weight[cols], preferred_element_type=jnp.float32)  30.4 us
  transfers between devices with their start and end apart: 9, of which 7 were waited for; matrix products, arithmetic and copies ran while one was open for 12% of the time, Pallas kernels for 6%

profile of v1, /device:TPU:0, one launch (start us, length us, event | category | flops | bytes accessed | tf_op | source)
XLA Modules:
  0.0 605.2 jit_solution(18434525272774656713)
XLA Ops:
  7.2 1.5 fusion.8
  9.5 1.5 fusion.10
  11.0 1.0 fusion.41
  15.9 5.2 pack_blocks.1
  21.2 7.6 %all-to-all-start = ((bf16[16,512,256]{2,1,0:T(8,128)(2,1)}), bf16[16,512,256]{2,1,0:T(8,128)(2,1)}, u32[]{:S(2)}, u32[]{:S(2)}) async-start(bf16[16,512,256]{2,1,0:T(8,128)(2,1)} %bitcast.70), calls=%async_computation | async-start | bytes 8388608 | tf_op jit(solution)/shard_map/all_to_all | solution.py:221
  30.9 1.0 multiply_cosine_fusion.1
  31.9 83.1 %all-gather.7.cloned.1.call-done = bf16[512,2048]{1,0:T(8,128)(2,1)} async-done(((bf16[64,2048]{1,0:T(8,128)(2,1)}), bf16[512,2048]{1,0:T(8,128)(2,1)}) %all-gather.7.cloned.1.call-update) | async-done | bytes 2097168 | tf_op jit(solution)/shard_map/all_gather | solution.py:239
  115.0 5.1 fusion.4
  120.2 51.1 %all-gather.11.cloned.1.call-done = bf16[512,2048]{1,0:T(8,128)(2,1)} async-done(((bf16[64,2048]{1,0:T(8,128)(2,1)}), bf16[512,2048]{1,0:T(8,128)(2,1)}) %all-gather.11.cloned.1.call-update) | async-done | bytes 2097168 | tf_op jit(solution)/shard_map/all_gather | solution.py:239
  171.3 6.5 %fusion = f32[512,1024]{1,0:T(8,128)} fusion(bf16[512,2048]{1,0:T(8,128)(2,1)} %all-gather.11.cloned.1.call-done, bf16[8192,1024]{1,0:T(8,128)(2,1)} %param.15), kind=kOutput, calls=%fused_computation.4 | convolution fusion | flops 2147483648 | bytes 8388608 | tf_op jit(solution)/shard_map/dot_general | solution.py:241
  177.8 43.2 %all-gather.9.cloned.1.call-done = bf16[512,2048]{1,0:T(8,128)(2,1)} async-done(((bf16[64,2048]{1,0:T(8,128)(2,1)}), bf16[512,2048]{1,0:T(8,128)(2,1)}) %all-gather.9.cloned.1.call-update) | async-done | bytes 2097168 | tf_op jit(solution)/shard_map/all_gather | solution.py:239
  220.9 6.5 %fusion.2 = f32[512,1024]{1,0:T(8,128)} fusion(bf16[512,2048]{1,0:T(8,128)(2,1)} %all-gather.9.cloned.1.call-done, bf16[8192,1024]{1,0:T(8,128)(2,1)} %param.15), kind=kOutput, calls=%fused_computation.6 | convolution fusion | flops 2147483648 | bytes 8388608 | tf_op jit(solution)/shard_map/dot_general | solution.py:241
  227.4 43.9 %all-gather.5.cloned.1.call-done = bf16[512,2048]{1,0:T(8,128)(2,1)} async-done(((bf16[64,2048]{1,0:T(8,128)(2,1)}), bf16[512,2048]{1,0:T(8,128)(2,1)}) %all-gather.5.cloned.1.call-update) | async-done | bytes 2097168 | tf_op jit(solution)/shard_map/all_gather | solution.py:239
  271.3 6.4 %add_bitcast_fusion = f32[64,8,8,128]{3,1,2,0:T(8,128)S(1)} fusion(f32[512,1024]{1,0:T(8,128)} %fusion, f32[512,1024]{1,0:T(8,128)} %fusion.2, f32[512,1024]{1,0:T(8,128)S(1)} %fusion.4, bf16[512,2048]{1,0:T(8,128)(2,1)} %all-gather.5.cloned.1.call-done, bf16[8192,1024]{1,0:T(8,128)(2,1)} %param.15, f32[1024]{0:T(1024)S(1)} %convert_element_type.68), kind=kOutput, calls=%fused_computation.19 | convolution fusion | flops 2149580800 | bytes 14684160 | tf_op jit(solution)/shard_map/dot_general | solution.py:241
  280.7 0.9 copy-done.4
  285.5 0.9 fusion.16
  290.0 1.2 fusion.34
  292.0 6.8 %order_blocks.1 = (bf16[4096,128]{1,0:T(8,128)(2,1)}, bf16[4096,256]{1,0:T(8,128)(2,1)}) custom-call(s32[1]{0:T(128)} %dynamic_slice.6.length_ref, s32[256]{0:T(256)} %multiply_add_fusion.where_ref, bf16[512,16,256]{2,1,0:T(8,128)(2,1)} %bitcast.10.arrived_ref), custom_call_target="tpu_custom_call" | custom-call | tf_op jit(solution)/shard_map/order_blocks/pallas_call | solution.py:102
  298.8 10.9 %attend.4 = bf16[128,1024]{1,0:T(8,128)(2,1)} custom-call(bf16[8,128,128]{2,1,0:T(8,128)(2,1)} %bitcast.80, bf16[4096,128]{1,0:T(8,128)(2,1)} %get-tuple-element.4.key_ref, bf16[4096,256]{1,0:T(8,128)(2,1)} %get-tuple-element.5.value_ref, bf16[512,128]{1,0:T(8,128)(2,1)} %pad_maximum_fusion.1.new_key_ref, bf16[512,256]{1,0:T(8,128)(2,1)} %concatenate.47.new_value_ref), custom_call_target="tpu_custom_call" | custom-call | flops 4831838208 | bytes 4063232 | tf_op jit(solution)/shard_map/attend/pallas_call | solution.py:162
  309.7 9.6 %convolution_convert_fusion.3 = bf16[128,8192]{1,0:T(8,128)(2,1)} fusion(bf16[128,1024]{1,0:T(8,128)(2,1)} %attend.4, bf16[1024,8192]{1,0:T(8,128)(2,1)} %param.21), kind=kOutput, calls=%fused_computation.3 | convolution fusion | flops 2148532224 | bytes 19136512 | tf_op jit(solution)/shard_map/dot_general | solution.py:303
  320.0 10.9 %attend.5 = bf16[128,1024]{1,0:T(8,128)(2,1)} custom-call(bf16[8,128,128]{2,1,0:T(8,128)(2,1)} %bitcast.82, bf16[4096,128]{1,0:T(8,128)(2,1)} %get-tuple-element.4.key_ref, bf16[4096,256]{1,0:T(8,128)(2,1)} %get-tuple-element.5.value_ref, bf16[512,128]{1,0:T(8,128)(2,1)} %pad_maximum_fusion.1.new_key_ref, bf16[512,256]{1,0:T(8,128)(2,1)} %concatenate.47.new_value_ref), custom_call_target="tpu_custom_call" | custom-call | flops 4831838208 | bytes 4063232 | tf_op jit(solution)/shard_map/attend/pallas_call | solution.py:162
  331.0 9.7 %convolution_convert_fusion.2 = bf16[128,8192]{1,0:T(8,128)(2,1)} fusion(bf16[128,1024]{1,0:T(8,128)(2,1)} %attend.5, bf16[1024,8192]{1,0:T(8,128)(2,1)} %param.21), kind=kOutput, calls=%fused_computation.2 | convolution fusion | flops 2148532224 | bytes 19136512 | tf_op jit(solution)/shard_map/dot_general | solution.py:303
  341.7 10.9 %attend.6 = bf16[128,1024]{1,0:T(8,128)(2,1)} custom-call(bf16[8,128,128]{2,1,0:T(8,128)(2,1)} %bitcast.83, bf16[4096,128]{1,0:T(8,128)(2,1)} %get-tuple-element.4.key_ref, bf16[4096,256]{1,0:T(8,128)(2,1)} %get-tuple-element.5.value_ref, bf16[512,128]{1,0:T(8,128)(2,1)} %pad_maximum_fusion.1.new_key_ref, bf16[512,256]{1,0:T(8,128)(2,1)} %concatenate.47.new_value_ref), custom_call_target="tpu_custom_call" | custom-call | flops 4831838208 | bytes 4063232 | tf_op jit(solution)/shard_map/attend/pallas_call | solution.py:162
  352.6 9.7 %convolution_convert_fusion.1 = bf16[128,8192]{1,0:T(8,128)(2,1)} fusion(bf16[128,1024]{1,0:T(8,128)(2,1)} %attend.6, bf16[1024,8192]{1,0:T(8,128)(2,1)} %param.21), kind=kOutput, calls=%fused_computation.1 | convolution fusion | flops 2148532224 | bytes 19136512 | tf_op jit(solution)/shard_map/dot_general | solution.py:303
  363.1 11.0 %attend.7 = bf16[128,1024]{1,0:T(8,128)(2,1)} custom-call(bf16[8,128,128]{2,1,0:T(8,128)(2,1)} %bitcast.81, bf16[4096,128]{1,0:T(8,128)(2,1)} %get-tuple-element.4.key_ref, bf16[4096,256]{1,0:T(8,128)(2,1)} %get-tuple-element.5.value_ref, bf16[512,128]{1,0:T(8,128)(2,1)} %pad_maximum_fusion.1.new_key_ref, bf16[512,256]{1,0:T(8,128)(2,1)} %concatenate.47.new_value_ref), custom_call_target="tpu_custom_call" | custom-call | flops 4831838208 | bytes 4063232 | tf_op jit(solution)/shard_map/attend/pallas_call | solution.py:162
  374.0 9.6 %convolution_convert_fusion = bf16[128,8192]{1,0:T(8,128)(2,1)} fusion(bf16[128,1024]{1,0:T(8,128)(2,1)} %attend.7, bf16[1024,8192]{1,0:T(8,128)(2,1)} %param.21), kind=kOutput, calls=%fused_computation | convolution fusion | flops 2148532224 | bytes 19136512 | tf_op jit(solution)/shard_map/dot_general | solution.py:303
  383.8 11.8 %all_to_all.10 = bf16[8,64,2,128]{3,1,2,0:T(8,128)(2,1)S(1)} all-to-all(bf16[8,64,2,128]{3,1,2,0:T(8,128)(2,1)S(1)} %pad_maximum_fusion), channel_id=1, replica_groups=mesh['groups'=2,'mp'=8,'pool'=2] {'mp'}, dimensions={0} | all-to-all | bytes 524288 | tf_op jit(solution)/shard_map/all_to_all | solution.py:280
  395.9 0.9 reshape.221
  396.8 59.1 %reduce-scatter.7.cloned.1.call-done = bf16[16,8192]{1,0:T(8,128)(2,1)} async-done(((bf16[128,8192]{1,0:T(8,128)(2,1)}), bf16[16,8192]{1,0:T(8,128)(2,1)}) %reduce-scatter.7.cloned.1.call-update) | async-done | bytes 262160 | tf_op jit(solution)/shard_map/reduce_scatter | solution.py:304
  455.9 70.1 %reduce-scatter.9.cloned.1.call-done = bf16[16,8192]{1,0:T(8,128)(2,1)} async-done(((bf16[128,8192]{1,0:T(8,128)(2,1)}), bf16[16,8192]{1,0:T(8,128)(2,1)}) %reduce-scatter.9.cloned.1.call-update) | async-done | bytes 262160 | tf_op jit(solution)/shard_map/reduce_scatter | solution.py:304
  526.0 70.1 %reduce-scatter.11.cloned.1.call-done = bf16[16,8192]{1,0:T(8,128)(2,1)} async-done(((bf16[128,8192]{1,0:T(8,128)(2,1)}), bf16[16,8192]{1,0:T(8,128)(2,1)}) %reduce-scatter.11.cloned.1.call-update) | async-done | bytes 262160 | tf_op jit(solution)/shard_map/reduce_scatter | solution.py:304
  596.2 2.2 maximum_bitcast_fusion.1
  (79 shorter events, 20.8 us)
Async XLA Ops:
  7.2 107.8 %all-gather.7.cloned.1.call-start = ((), (), s32[]{:S(2)}) async-start(), calls=%async_computation.7 | async-start | bytes 2359296 | tf_op jit(solution)/shard_map/all_gather | solution.py:239
  11.0 3.1 copy-start.5
  11.0 4.2 copy-start.6
  12.0 159.2 %all-gather.11.cloned.1.call-start = ((), (), s32[]{:S(2)}) async-start(), calls=%async_computation.9 | async-start | bytes 2359296 | tf_op jit(solution)/shard_map/all_gather | solution.py:239
  12.8 208.1 %all-gather.9.cloned.1.call-start = ((), (), s32[]{:S(2)}) async-start(), calls=%async_computation.8 | async-start | bytes 2359296 | tf_op jit(solution)/shard_map/all_gather | solution.py:239
  13.5 257.8 %all-gather.5.cloned.1.call-start = ((), (), s32[]{:S(2)}) async-start(), calls=%async_computation.6 | async-start | bytes 2359296 | tf_op jit(solution)/shard_map/all_gather | solution.py:239
  21.2 7.7 %copy-start.9 = (bf16[128]{0:T(256)(128)(2,1)S(1)}, bf16[128]{0:T(256)(128)(2,1)}, u32[]{:S(2)}) copy-start(bf16[128]{0:T(256)(128)(2,1)} %param.19) | copy-start | bytes 772
  21.2 7.7 %copy-start.10 = (bf16[128]{0:T(256)(128)(2,1)S(1)}, bf16[128]{0:T(256)(128)(2,1)}, u32[]{:S(2)}) copy-start(bf16[128]{0:T(256)(128)(2,1)} %param.20) | copy-start | bytes 772
  21.2 7.7 %copy-start.7 = (bf16[1024]{0:T(1024)(128)(2,1)S(1)}, bf16[1024]{0:T(1024)(128)(2,1)}, u32[]{:S(2)}) copy-start(bf16[1024]{0:T(1024)(128)(2,1)} %param.16) | copy-start | bytes 6148
  21.2 7.7 %copy-start.11 = (s32[2]{0:T(128)S(1)}, s32[2]{0:T(128)}, u32[]{:S(2)}) copy-start(s32[2]{0:T(128)} %param.25) | copy-start | bytes 28
  21.2 270.8 %all-to-all-start = ((bf16[16,512,256]{2,1,0:T(8,128)(2,1)}), bf16[16,512,256]{2,1,0:T(8,128)(2,1)}, u32[]{:S(2)}, u32[]{:S(2)}) async-start(bf16[16,512,256]{2,1,0:T(8,128)(2,1)} %bitcast.70), calls=%async_computation | async-start | bytes 8388608 | tf_op jit(solution)/shard_map/all_to_all | solution.py:221
  28.8 368.0 %reduce-scatter.5.cloned.1.call-start = ((), (), s32[]{:S(2)}) async-start(), calls=%async_computation.10 | async-start | bytes 2359296 | tf_op jit(solution)/shard_map/reduce_scatter | solution.py:304
  279.1 1.6 copy-start.8
  279.7 1.9 copy-start.4
  279.8 2.5 copy-start
  282.3 1.6 copy-start.1
  283.9 1.6 copy-start.2
  285.5 1.7 copy-start.3
  319.2 136.6 %reduce-scatter.7.cloned.1.call-start = ((), (), s32[]{:S(2)}) async-start(), calls=%async_computation.11 | async-start | bytes 2359296 | tf_op jit(solution)/shard_map/reduce_scatter | solution.py:304
  340.7 185.4 %reduce-scatter.9.cloned.1.call-start = ((), (), s32[]{:S(2)}) async-start(), calls=%async_computation.12 | async-start | bytes 2359296 | tf_op jit(solution)/shard_map/reduce_scatter | solution.py:304
  362.3 233.9 %reduce-scatter.11.cloned.1.call-start = ((), (), s32[]{:S(2)}) async-start(), calls=%async_computation.13 | async-start | bytes 2359296 | tf_op jit(solution)/shard_map/reduce_scatter | solution.py:304
Sparse Core Ops, SparseCore 0:
  12.2 102.7 all-gather.6
  117.7 53.5 all-gather.10
  173.4 47.4 all-gather.8
  223.5 47.7 all-gather.4
  319.4 66.1 reduce-scatter.4
  388.9 66.9 reduce-scatter.6
  459.4 66.5 reduce-scatter.8
  529.5 66.5 reduce-scatter.10

commit v2 on v1

--- a/solution.py
+++ b/solution.py
@@ -14,8 +14,9 @@
 EPSILON = 1e-06
 SCORE_SCALE = HD ** (-0.5) * math.log2(math.e)
 VMEM_LIMIT = 56 * 1024 * 1024
-GATHER_PIECES = 4
+GATHER_PIECES = 2
 ROW_CHUNKS = 4
+LINE_MODELS = 8
 
 
 def angle_tables(positions):
@@ -46,6 +47,209 @@
     rank_order = jnp.cumsum(owned_mask.astype(jnp.int32), -1) - 1
     slot_index = jnp.arange(capacity, dtype=jnp.int32)
     return owned_mask[..., None, :] & (rank_order[..., None, :] == slot_index[:, None])
+
+
+def line_gather(own, n_model):
+    length = n_model // 2
+
+    def across(block, low, high):
+        pairs = [(2 * z + y, 2 * z + 1 - y) for z in range(low, high) for y in range(2)]
+        return lax.ppermute(block, "mp", pairs)
+
+    lower, upper = [], []
+    here, there = [own], []
+    rising = falling = own
+    there.append(across(own, 0, length))
+    for step in range(1, length):
+        rising = lax.ppermute(
+            rising,
+            "mp",
+            [(2 * z + y, 2 * z + 2 + y) for z in range(step - 1, length - 1) for y in range(2)],
+        )
+        falling = lax.ppermute(
+            falling,
+            "mp",
+            [(2 * z + y, 2 * z - 2 + y) for z in range(1, length - step + 1) for y in range(2)],
+        )
+        lower.append((rising, across(rising, step, length)))
+        upper.append((falling, across(falling, 0, length - step)))
+    here += [pair[0] for pair in lower] + [pair[0] for pair in upper]
+    there += [pair[1] for pair in lower] + [pair[1] for pair in upper]
+    return here + there
+
+
+def project_kernel(length, first, last, *refs):
+    place_ref = refs[0]
+    n_blocks = 2 * (2 * length - 1) if length else 1
+    blocks = refs[1 : 1 + n_blocks]
+    rest = list(refs[1 + n_blocks :])
+    weights = [rest.pop(0) for _ in range(3)]
+    if not first:
+        partial_ref = rest.pop(0)
+    if last:
+        q_bias_ref, k_bias_ref, v_bias_ref, cos_ref, sin_ref = rest[:5]
+        query_ref, key_ref, value_ref, pair_ref = rest[5:9]
+        rest = rest[9:]
+    else:
+        sum_ref = rest.pop(0)
+    tokens_ref, total_ref, sems = rest
+    step = pl.program_id(0)
+    depth = weights[0].shape[0]
+    q_width = weights[0].shape[1]
+
+    def each_copy(act):
+        if not length:
+            act(pltpu.make_async_copy(blocks[0], tokens_ref, sems.at[0]))
+            return
+        rows = tokens_ref.shape[0] // (2 * length)
+        my_y = place_ref[1]
+        for my_z in range(length):
+
+            @pl.when(place_ref[0] == my_z)
+            def _():
+                for z in range(length):
+                    source = abs(z - my_z) + (length - 1 if z > my_z else 0)
+                    for side in range(2):
+                        y = my_y if side == 0 else 1 - my_y
+                        start = pl.multiple_of((2 * z + y) * rows, rows)
+                        act(
+                            pltpu.make_async_copy(
+                                blocks[side * (2 * length - 1) + source],
+                                tokens_ref.at[pl.ds(start, rows), :],
+                                sems.at[2 * z + side],
+                            )
+                        )
+
+    @pl.when(step == 0)
+    def _():
+        each_copy(lambda copy: copy.start())
+        total_ref[...] = jnp.zeros_like(total_ref) if first else partial_ref[...]
+        each_copy(lambda copy: copy.wait())
+
+    tokens = tokens_ref[:, pl.ds(pl.multiple_of(step * depth, depth), depth)]
+    total_ref[:, :q_width] += jnp.dot(
+        tokens, weights[0][...], preferred_element_type=jnp.float32
+    )
+    both = jnp.concatenate([weights[1][...], weights[2][...]], axis=1)
+    total_ref[:, q_width:] += jnp.dot(tokens, both, preferred_element_type=jnp.float32)
+
+    @pl.when(step == pl.num_programs(0) - 1)
+    def _():
+        if not last:
+            sum_ref[...] = total_ref[...]
+            return
+        cosine, sine = cos_ref[...], sin_ref[...]
+
+        def turned(vectors):
+            return vectors * cosine + pltpu.roll(vectors, HD // 2, 1) * sine
+
+        for head in range(q_width // HD):
+            cols = slice(head * HD, (head + 1) * HD)
+            query = total_ref[:, cols] + q_bias_ref[:, cols].astype(jnp.float32)
+            query_ref[head] = turned(query).astype(jnp.bfloat16)
+        key = total_ref[:, q_width : q_width + HD] + k_bias_ref[...].astype(jnp.float32)
+        key = turned(key.astype(jnp.bfloat16).astype(jnp.float32)).astype(jnp.bfloat16)
+        value = total_ref[:, q_width + HD :] + v_bias_ref[...].astype(jnp.float32)
+        value = value.astype(jnp.bfloat16)
+        key_ref[...] = key
+        value_ref[:, :HD] = value
+        value_ref[:, HD:] = jnp.ones_like(value)
+        pair_ref[:, :HD] = key
+        pair_ref[:, HD:] = value
+
+
+def project(place, blocks, weights, piece, pieces, partial, biases, tables):
+    length = place_length(blocks)
+    width = blocks[0].shape[1]
+    rows = blocks[0].shape[0] * (2 * length if length else 1)
+    depth = math.gcd(width, 1024)
+    steps = width // depth
+    out_width = sum(weight.shape[1] for weight in weights)
+    q_width = weights[0].shape[1]
+    first, last = piece == 0, piece == pieces - 1
+    fixed = lambda array: pl.BlockSpec(array.shape, lambda step: (0,) * len(array.shape))
+    in_specs = [pl.BlockSpec(memory_space=pltpu.SMEM)]
+    in_specs += [pl.BlockSpec(memory_space=pl.ANY)] * len(blocks)
+    in_specs += [
+        pl.BlockSpec((depth, weight.shape[1]), lambda step: (piece * steps + step, 0))
+        for weight in weights
+    ]
+    operands = [place, *blocks, *weights]
+    if not first:
+        operands.append(partial)
+    if last:
+        operands += [*biases, *tables]
+        out_shape = (
+            jax.ShapeDtypeStruct((q_width // HD, rows, HD), jnp.bfloat16),
+            jax.ShapeDtypeStruct((rows, HD), jnp.bfloat16),
+            jax.ShapeDtypeStruct((rows, 2 * HD), jnp.bfloat16),
+            jax.ShapeDtypeStruct((rows, 2 * HD), jnp.bfloat16),
+        )
+        out_specs = tuple(fixed(shape) for shape in out_shape)
+    else:
+        out_shape = jax.ShapeDtypeStruct((rows, out_width), jnp.float32)
+        out_specs = fixed(out_shape)
+    in_specs += [fixed(array) for array in operands[len(in_specs) :]]
+    return pl.pallas_call(
+        functools.partial(project_kernel, length, first, last),
+        grid=(steps,),
+        out_shape=out_shape,
+        in_specs=in_specs,
+        out_specs=out_specs,
+        scratch_shapes=[
+            pltpu.VMEM((rows, width), jnp.bfloat16),
+            pltpu.VMEM((rows, out_width), jnp.float32),
+            pltpu.SemaphoreType.DMA((max(2 * length, 1),)),
+        ],
+        compiler_params=pltpu.CompilerParams(vmem_limit_bytes=VMEM_LIMIT),
+        cost_estimate=pl.CostEstimate(
+            flops=2 * rows * width * out_width,
+            bytes_accessed=2 * width * (rows + out_width) + 4 * rows * out_width,
+            transcendentals=0,
+        ),
+        name="project",
+    )(*operands)
+
+
+def place_length(blocks):
+    return 0 if len(blocks) == 1 else (len(blocks) // 2 + 1) // 2
+
+
+def ring_scatter(shares, n_model, my_model):
+    order = [m for m in range(0, n_model, 2)] + [m for m in range(n_model - 1, 0, -2)]
+    inverse = [order.index(m) for m in range(n_model)]
+    spot = jnp.array(inverse, jnp.int32)[my_model]
+    half = n_model // 2
+    width = shares.shape[-1]
+
+    def share_of(offset):
+        owner = jnp.array(order, jnp.int32)[(spot + offset + n_model) % n_model]
+        return lax.dynamic_index_in_dim(shares, owner, 0, keepdims=False)
+
+    def added(left, right):
+        return (left.astype(jnp.float32) + right.astype(jnp.float32)).astype(jnp.bfloat16)
+
+    def pairs(way):
+        return [(order[i], order[(i + way) % n_model]) for i in range(n_model)]
+
+    far = share_of(half)
+    onward = lax.ppermute(far[:, : width // 2], "mp", pairs(1))
+    back = lax.ppermute(far[:, width // 2 :], "mp", pairs(-1))
+    for distance in range(half - 1, 0, -1):
+        ahead, behind = share_of(distance), share_of(-distance)
+        if distance == half - 1:
+            onward = jnp.concatenate(
+                [added(ahead[:, : width // 2], onward), ahead[:, width // 2 :]], 1
+            )
+            back = jnp.concatenate(
+                [behind[:, : width // 2], added(behind[:, width // 2 :], back)], 1
+            )
+        else:
+            onward, back = added(ahead, onward), added(behind, back)
+        onward = lax.ppermute(onward, "mp", pairs(1))
+        back = lax.ppermute(back, "mp", pairs(-1))
+    own = share_of(0).astype(jnp.float32)
+    return (own + onward.astype(jnp.float32) + back.astype(jnp.float32)).astype(jnp.bfloat16)
 
 
 def pack_kernel(dest_heads, slots_ref, pool_ref, out_ref):
@@ -128,8 +332,8 @@
 def attend_kernel(
     span, row_step, chunk, query_ref, key_ref, value_ref, new_key_ref, new_value_ref, out_ref
 ):
-    queries = query_ref[0]
-    rows = queries.shape[0]
+    rows = out_ref.shape[0]
+    queries = query_ref[0].reshape(rows, HD)
     spans = key_ref.shape[0] // span
     suffix = new_key_ref.shape[0]
     stride = suffix * row_step // rows
@@ -155,7 +359,8 @@
 
 
 def attend(queries, keys, values, new_keys, new_values, row_step, chunk):
-    heads, rows, _ = queries.shape
+    heads, owners = queries.shape[:2]
+    rows = owners * row_step
     span = math.gcd(keys.shape[0], 1024)
     whole = lambda array: pl.BlockSpec(array.shape, lambda head: (0, 0))
     count = keys.shape[0] + new_keys.shape[0]
@@ -164,7 +369,7 @@
         grid=(heads,),
         out_shape=jax.ShapeDtypeStruct((rows, heads * HD), jnp.bfloat16),
         in_specs=[
-            pl.BlockSpec((1, rows, HD), lambda head: (head, 0, 0)),
+            pl.BlockSpec((1, owners, None, row_step, HD), lambda head: (head, 0, chunk, 0, 0)),
             whole(keys),
             whole(values),
             whole(new_keys),
@@ -231,52 +436,48 @@
     where = my_holder * capacity + jnp.sum(earlier.astype(jnp.int32), -1)
     prefix_count = prefix_len[my_pool]
 
-    normed = normalize(states[0], norm_gain)
-    piece = width // GATHER_PIECES
-    query_sum = key_sum = value_sum = None
-    for index in range(GATHER_PIECES):
-        cols = slice(index * piece, (index + 1) * piece)
-        tokens = lax.all_gather(normed[:, cols], "mp", axis=0, tiled=True)
-        parts = [
-            jnp.dot(tokens, weight[cols], preferred_element_type=jnp.float32)
-            for weight in (w_query, w_key, w_value)
-        ]
-        if index == 0:
-            query_sum, key_sum, value_sum = parts
-        else:
-            query_sum, key_sum, value_sum = (
-                query_sum + parts[0],
-                key_sum + parts[1],
-                value_sum + parts[2],
-            )
     positions = prefix_count + jnp.arange(suffix, dtype=jnp.int32)
     cosine, sine = angle_tables(positions)
-    queries = rotate(
-        (query_sum + q_bias.astype(jnp.float32)).reshape(suffix, q_local, HD), cosine, sine
-    ).astype(jnp.bfloat16)
-    key_raw = (key_sum + k_bias.astype(jnp.float32)).astype(jnp.bfloat16)
-    value_raw = (value_sum + v_bias.astype(jnp.float32)).astype(jnp.bfloat16)
-    if sharers > 1:
+    tables = (jnp.concatenate([cosine, cosine], 1), jnp.concatenate([-sine, sine], 1))
+    normed = normalize(states[0], norm_gain)
+    if sharers == 1:
+        pieces = GATHER_PIECES
+        place = jnp.stack([my_model // 2, my_model % 2]).astype(jnp.int32)
+        biases = [bias.reshape(1, -1) for bias in (q_bias, k_bias, v_bias)]
+        weights = (w_query, w_key, w_value)
+        result = None
+        for piece in range(pieces):
+            own = normed[:, piece * width // pieces : (piece + 1) * width // pieces]
+            if n_model == LINE_MODELS:
+                blocks = line_gather(own, n_model)
+            else:
+                blocks = [lax.all_gather(own, "mp", axis=0, tiled=True)]
+            result = project(place, blocks, weights, piece, pieces, result, biases, tables)
+        queries, new_keys, new_values, pairs = result
+        pairs = pairs.reshape(n_model, row_count, 2 * HD)
+    else:
+        tokens = lax.all_gather(normed, "mp", axis=0, tiled=True)
+        linear, key_raw, value_raw = (
+            jnp.dot(tokens, weight, preferred_element_type=jnp.float32) + bias.astype(jnp.float32)
+            for weight, bias in ((w_query, q_bias), (w_key, k_bias), (w_value, v_bias))
+        )
+        queries = rotate(linear.reshape(suffix, q_local, HD), cosine, sine)
+        queries = queries.astype(jnp.bfloat16).transpose(1, 0, 2)
+        key_raw, value_raw = key_raw.astype(jnp.bfloat16), value_raw.astype(jnp.bfloat16)
         together = [
             [first + other for other in range(sharers)] for first in range(0, n_model, sharers)
         ]
-        key_raw, value_head = (
+        key_whole, value_whole = (
             lax.all_gather(part, "mp", axis=1, tiled=True, axis_index_groups=together)
             for part in (key_raw, value_raw)
         )
-    else:
-        value_head = value_raw
-    key_head = rotate(key_raw.astype(jnp.float32)[:, None, :], cosine, sine).astype(jnp.bfloat16)[
-        :, 0
-    ]
-
-    if sharers > 1:
+        new_keys = rotate(key_whole.astype(jnp.float32)[:, None, :], cosine, sine)
+        new_keys = new_keys.astype(jnp.bfloat16)[:, 0]
+        new_values = jnp.concatenate([value_whole, jnp.ones_like(value_whole)], 1)
         first_col = (my_model % sharers) * kv_local
-        key_cols = lax.dynamic_slice_in_dim(key_head, first_col, kv_local, 1)
-        value_cols = value_raw
-    else:
-        key_cols, value_cols = key_head, value_head
-    pairs = jnp.stack([key_cols, value_cols], 1).reshape(n_model, row_count, 2, kv_local)
+        key_cols = lax.dynamic_slice_in_dim(new_keys, first_col, kv_local, 1)
+        pairs = jnp.stack([key_cols, value_raw], 1).reshape(n_model, row_count, 2 * kv_local)
+
     pairs = lax.all_to_all(pairs, "mp", split_axis=0, concat_axis=0, tiled=True)
     cache_rows = (
         pairs.reshape(kv_heads, sharers, row_count, 2, kv_local)
@@ -285,23 +486,17 @@
     )
 
     prefix_keys, prefix_values = order_blocks(arrived, where, prefix_count.reshape(1))
-    new_values = jnp.concatenate([value_head, jnp.ones_like(value_head)], 1)
-
-    row_step = row_count // ROW_CHUNKS
-    by_chunk = queries.reshape(n_model, ROW_CHUNKS, row_step, q_local, HD).transpose(1, 3, 0, 2, 4)
+
+    row_step = max(row_count // ROW_CHUNKS, 16)
+    by_chunk = queries.reshape(q_local, n_model, row_count // row_step, row_step, HD)
     summed = []
-    for chunk in range(ROW_CHUNKS):
+    for chunk in range(row_count // row_step):
         mixed = attend(
-            by_chunk[chunk].reshape(q_local, n_model * row_step, HD),
-            prefix_keys,
-            prefix_values,
-            key_head,
-            new_values,
-            row_step,
-            chunk,
+            by_chunk, prefix_keys, prefix_values, new_keys, new_values, row_step, chunk
         )
         share = jnp.dot(mixed, w_out, preferred_element_type=jnp.float32).astype(jnp.bfloat16)
-        summed.append(lax.psum_scatter(share, "mp", scatter_dimension=0, tiled=True))
+        share = share.reshape(n_model, row_step, share.shape[1])
+        summed.append(ring_scatter(share, n_model, my_model))
     return (jnp.concatenate(summed, 0)[None], cache_rows)
 
 

time: 606 us -> 416 us (0.69)
  waiting for transfers between devices: 423 us -> 150 us
  starting transfers between devices: 8.12 us -> 122 us
  matrix products: 68.9 us -> 21.2 us
  Pallas kernels: 55.7 us -> 81.6 us
  blocking collectives: 11.8 us -> 0 us
  between operations: 14.4 us -> 22 us
    all_gather x4 -> x0, waiting for transfers between devices: 221 us -> none  [on_device(): tokens = lax.all_gather(normed[:, cols], 'mp', axis=0, tiled=True)]
    reduce_scatter x4 -> x0, waiting for transfers between devices: 199 us -> none  [on_device(): lax.psum_scatter(share, 'mp', scatter_dimension=0, tiled=True)]
    ppermute x0 -> x58, starting transfers between devices: none -> 107 us  [the longest x14 29.9 us: across(): return lax.ppermute(block, 'mp', pairs)]
    ppermute x0 -> x58, waiting for transfers between devices: none -> 94.9 us  [the longest x6 32.9 us: line_gather(): lax.ppermute(falling, 'mp', [(2 * z + y, 2 * z - 2 + y) for z in range(1,...]
    all_to_all x1, waiting for transfers between devices: 0.01 us -> 54.1 us  [on_device(): lax.all_to_all(outgoing.reshape(holders, capacity * block_len, 2 * HD), (...]
    dot_general x12 -> x0, matrix products: 30.4 us -> none  [on_device(): jnp.dot(tokens, weight[cols], preferred_element_type=jnp.float32)]
    pallas_call x0 -> x2, Pallas kernels: none -> 25.5 us  [project(): pl.pallas_call(functools.partial(project_kernel, length, first, last), gr...]
    dot_general x4, matrix products: 38.5 us -> 21.2 us  [on_device(): jnp.dot(mixed, w_out, preferred_element_type=jnp.float32)]
  transfers between devices with their start and end apart: 9 -> 60, of which waited for: 7 -> 26; matrix products, arithmetic and copies ran while one was open for 12% -> 6% of each run, Pallas kernels for 6% -> 4%
where the time goes in v2:
time: 416 us; the launch traced here: 415 us
  waiting for transfers between devices  150 us (36%)
  starting transfers between devices  122 us (29%)
  Pallas kernels  81.6 us (20%)
  between operations  22 us (5%)
  matrix products  21.2 us (5%)
  other arithmetic  12.4 us (3%)
  local copies, waits for them, and re-layouts  5.29 us (1%)
    all_to_all x1, waiting for transfers between devices, on_device(): lax.all_to_all(outgoing.reshape(holders, capacity * block_len, 2 * HD), (...  54.1 us
    pallas_call x4, Pallas kernels, attend(): pl.pallas_call(functools.partial(attend_kernel, span, row_step, chunk), g...  44 us
    ppermute x6, waiting for transfers between devices, line_gather(): lax.ppermute(falling, 'mp', [(2 * z + y, 2 * z - 2 + y) for z in range(1,...  32.9 us
    ppermute x12, waiting for transfers between devices, ring_scatter(): onward = lax.ppermute(onward, 'mp', pairs(1))  32.7 us
    ppermute x14, starting transfers between devices, across(): return lax.ppermute(block, 'mp', pairs)  29.9 us
    pallas_call x2, Pallas kernels, project(): pl.pallas_call(functools.partial(project_kernel, length, first, last), gr...  25.5 us
    ppermute x12, waiting for transfers between devices, ring_scatter(): back = lax.ppermute(back, 'mp', pairs(-1))  23 us
    dot_general x4, matrix products, on_device(): jnp.dot(mixed, w_out, preferred_element_type=jnp.float32)  21.2 us
  transfers between devices with their start and end apart: 60, of which 26 were waited for; matrix products, arithmetic and copies ran while one was open for 6% of the time, Pallas kernels for 4%

profile of v2, /device:TPU:0, one launch (start us, length us, event | category | flops | bytes accessed | tf_op | source)
XLA Modules:
  0.0 414.5 jit_solution(1808315721760961694)
XLA Ops:
  4.6 5.0 %collective-permute-start.13 = (bf16[64,4096]{1,0:T(8,128)(2,1)S(1)}, bf16[64,4096]{1,0:T(8,128)(2,1)S(1)}, u32[]{:S(2)}, u32[]{:S(2)}) collective-permute-start(bf16[64,4096]{1,0:T(8,128)(2,1)S(1)} %get-tuple-element.36.refs_1_), channel_id=1, source_target_pairs={{0,4},{2,6},{4,8},{6,10},{8,12},{10,14},{1,5},{3,7},{5,9},{7,11},{... | collective-permute-start | bytes 1572872 | tf_op jit(solution)/shard_map/ppermute | solution.py:64
  13.7 5.2 %collective-permute-start = (bf16[64,4096]{1,0:T(8,128)(2,1)S(1)}, bf16[64,4096]{1,0:T(8,128)(2,1)S(1)}, u32[]{:S(2)}, u32[]{:S(2)}) collective-permute-start(bf16[64,4096]{1,0:T(8,128)(2,1)S(1)} %get-tuple-element.37.refs_1_), channel_id=1, source_target_pairs={{0,4},{2,6},{4,8},{6,10},{8,12},{10,14},{1,5},{3,7},{5,9},{7,11},{... | collective-permute-start | bytes 1572872 | tf_op jit(solution)/shard_map/ppermute | solution.py:64
  28.3 9.2 %collective-permute-done.3.refs_5_ = bf16[64,4096]{1,0:T(8,128)(2,1)S(1)} collective-permute-done((bf16[64,4096]{1,0:T(8,128)(2,1)S(1)}, bf16[64,4096]{1,0:T(8,128)(2,1)S(1)}, u32[]{:S(2)}, u32[]{:S(2)}) %collective-permute-start.3) | collective-permute-done | bytes 524320 | tf_op jit(solution)/shard_map/ppermute | solution.py:69
  38.2 3.4 collective-permute-start.23
  44.5 4.4 %collective-permute-done.17.refs_6_ = bf16[64,4096]{1,0:T(8,128)(2,1)} collective-permute-done((bf16[64,4096]{1,0:T(8,128)(2,1)S(1)}, bf16[64,4096]{1,0:T(8,128)(2,1)}, u32[]{:S(2)}, u32[]{:S(2)}) %collective-permute-start.17) | collective-permute-done | bytes 524320 | tf_op jit(solution)/shard_map/ppermute | solution.py:69
  48.9 3.4 collective-permute-start.10
  55.1 3.6 collective-permute-done.4.refs_6_
  59.3 3.4 collective-permute-start.24
  65.6 12.8 %collective-permute-done.18.refs_7_ = bf16[64,4096]{1,0:T(8,128)(2,1)} collective-permute-done((bf16[64,4096]{1,0:T(8,128)(2,1)}, bf16[64,4096]{1,0:T(8,128)(2,1)}, u32[]{:S(2)}, u32[]{:S(2)}) %collective-permute-start.18) | collective-permute-done | bytes 524320 | tf_op jit(solution)/shard_map/ppermute | solution.py:69
  100.3 12.1 %project.2.refs_18_ = f32[512,1280]{1,0:T(8,128)} custom-call(s32[2]{0:T(128)} %pad_add_fusion.refs_0_, bf16[64,4096]{1,0:T(8,128)(2,1)} %copy-done.1, bf16[64,4096]{1,0:T(8,128)(2,1)} %copy-done.5, bf16[64,4096]{1,0:T(8,128)(2,1)} %copy-done.8, bf16[64,4096]{1,0:T(8,128)(2,1)} %collective-permute-done.15.refs_4_, bf16[64,4096]{1,0:T(8,128)(2,1)} %copy-done.6, ...), custom_call_target="tpu_custom_call" | custom-call | flops 5368709120 | bytes 17301504 | tf_op jit(solution)/shard_map/project/pallas_call | solution.py:193
  114.1 13.4 %project.3 = (bf16[8,512,128]{2,1,0:T(8,128)(2,1)}, bf16[512,128]{1,0:T(8,128)(2,1)}, bf16[512,256]{1,0:T(8,128)(2,1)}, bf16[512,256]{1,0:T(8,128)(2,1)}) custom-call(s32[2]{0:T(128)} %pad_add_fusion.refs_0_, bf16[64,4096]{1,0:T(8,128)(2,1)} %copy-done, bf16[64,4096]{1,0:T(8,128)(2,1)} %copy-done.3, bf16[64,4096]{1,0:T(8,128)(2,1)} %collective-permute-done.1.refs_3_, ...), custom_call_target="tpu_custom_call" | custom-call | flops 5368709120 | bytes 17301504 | tf_op jit(solution)/shard_map/project/pallas_call | solution.py:193
  127.5 10.0 %all-to-all-start.1 = ((bf16[8,64,256]{2,1,0:T(8,128)(2,1)}), bf16[8,64,256]{2,1,0:T(8,128)(2,1)S(1)}, u32[]{:S(2)}, u32[]{:S(2)}) async-start(bf16[8,64,256]{2,1,0:T(8,128)(2,1)} %bitcast.165), calls=%async_computation.1 | async-start | bytes 524288 | tf_op jit(solution)/shard_map/all_to_all | solution.py:481
  139.3 5.3 %pack_blocks.1 = bf16[8,2,32,16,256]{4,3,2,1,0:T(8,128)(2,1)} custom-call(s32[2,32]{1,0:T(2,128)} %select_reduce_fusion.slots_ref, bf16[64,16,2048]{2,1,0:T(8,128)(2,1)} %bitcast.163), custom_call_target="tpu_custom_call" | custom-call | tf_op jit(solution)/shard_map/pack_blocks/pallas_call | solution.py:272
  145.7 5.2 %all-to-all-start = ((bf16[16,512,256]{2,1,0:T(8,128)(2,1)}), bf16[16,512,256]{2,1,0:T(8,128)(2,1)}, u32[]{:S(2)}, u32[]{:S(2)}) async-start(bf16[16,512,256]{2,1,0:T(8,128)(2,1)} %bitcast.142), calls=%async_computation | async-start | bytes 8388608 | tf_op jit(solution)/shard_map/all_to_all | solution.py:426
  174.5 54.1 %all-to-all-done = bf16[16,512,256]{2,1,0:T(8,128)(2,1)} async-done(((bf16[16,512,256]{2,1,0:T(8,128)(2,1)}), bf16[16,512,256]{2,1,0:T(8,128)(2,1)}, u32[]{:S(2)}, u32[]{:S(2)}) %all-to-all-start) | async-done | bytes 4194336 | tf_op jit(solution)/shard_map/all_to_all | solution.py:426
  228.6 6.8 %order_blocks.1 = (bf16[4096,128]{1,0:T(8,128)(2,1)}, bf16[4096,256]{1,0:T(8,128)(2,1)}) custom-call(s32[1]{0:T(128)} %dynamic_slice.211.length_ref, s32[256]{0:T(256)} %multiply_add_fusion.where_ref, bf16[512,16,256]{2,1,0:T(8,128)(2,1)} %bitcast.11.arrived_ref), custom_call_target="tpu_custom_call" | custom-call | tf_op jit(solution)/shard_map/order_blocks/pallas_call | solution.py:306
  235.5 11.0 %attend.4 = bf16[128,1024]{1,0:T(8,128)(2,1)} custom-call(bf16[8,8,4,16,128]{4,3,2,1,0:T(8,128)(2,1)} %bitcast.172, bf16[4096,128]{1,0:T(8,128)(2,1)} %get-tuple-element.9.key_ref, bf16[4096,256]{1,0:T(8,128)(2,1)} %get-tuple-element.10.value_ref, bf16[512,128]{1,0:T(8,128)(2,1)} %get-tuple-element.11.new_key_ref, ...), custom_call_target="tpu_custom_call" | custom-call | flops 4831838208 | bytes 4063232 | tf_op jit(solution)/shard_map/attend/pallas_call | solution.py:367
  246.4 11.0 %attend.5 = bf16[128,1024]{1,0:T(8,128)(2,1)} custom-call(bf16[8,8,4,16,128]{4,3,2,1,0:T(8,128)(2,1)} %bitcast.173, bf16[4096,128]{1,0:T(8,128)(2,1)} %get-tuple-element.9.key_ref, bf16[4096,256]{1,0:T(8,128)(2,1)} %get-tuple-element.10.value_ref, bf16[512,128]{1,0:T(8,128)(2,1)} %get-tuple-element.11.new_key_ref, ...), custom_call_target="tpu_custom_call" | custom-call | flops 4831838208 | bytes 4063232 | tf_op jit(solution)/shard_map/attend/pallas_call | solution.py:367
  257.4 11.0 %attend.6 = bf16[128,1024]{1,0:T(8,128)(2,1)} custom-call(bf16[8,8,4,16,128]{4,3,2,1,0:T(8,128)(2,1)} %bitcast.174, bf16[4096,128]{1,0:T(8,128)(2,1)} %get-tuple-element.9.key_ref, bf16[4096,256]{1,0:T(8,128)(2,1)} %get-tuple-element.10.value_ref, bf16[512,128]{1,0:T(8,128)(2,1)} %get-tuple-element.11.new_key_ref, ...), custom_call_target="tpu_custom_call" | custom-call | flops 4831838208 | bytes 4063232 | tf_op jit(solution)/shard_map/attend/pallas_call | solution.py:367
  268.4 11.0 %attend.7 = bf16[128,1024]{1,0:T(8,128)(2,1)} custom-call(bf16[8,8,4,16,128]{4,3,2,1,0:T(8,128)(2,1)} %bitcast.175, bf16[4096,128]{1,0:T(8,128)(2,1)} %get-tuple-element.9.key_ref, bf16[4096,256]{1,0:T(8,128)(2,1)} %get-tuple-element.10.value_ref, bf16[512,128]{1,0:T(8,128)(2,1)} %get-tuple-element.11.new_key_ref, ...), custom_call_target="tpu_custom_call" | custom-call | flops 4831838208 | bytes 4063232 | tf_op jit(solution)/shard_map/attend/pallas_call | solution.py:367
  279.4 8.3 %convolution_convert_fusion.3 = bf16[128,8192]{1,0:T(8,128)(2,1)S(1)} fusion(bf16[128,1024]{1,0:T(8,128)(2,1)S(1)} %copy-done.16, bf16[1024,8192]{1,0:T(8,128)(2,1)} %param.57), kind=kOutput, calls=%fused_computation.3 | convolution fusion | flops 2148532224 | bytes 19136512 | tf_op jit(solution)/shard_map/dot_general | solution.py:497
  287.8 6.2 %collective-permute-start.30 = (bf16[16,4096]{1,0:T(8,128)(2,1)S(1)}, bf16[16,4096]{1,0:T(8,128)(2,1)S(1)}, u32[]{:S(2)}, u32[]{:S(2)}) collective-permute-start(bf16[16,4096]{1,0:T(8,128)(2,1)S(1)} %get-tuple-element.39), channel_id=1, source_target_pairs={{0,2},{4,0},{8,4},{12,8},{14,12},{10,14},{6,10},{2,6},{1,3},{5,1},... | collective-permute-start | bytes 393224 | tf_op jit(solution)/shard_map/ppermute | solution.py:237
  294.1 8.9 %collective-permute-start.26 = (bf16[16,4096]{1,0:T(8,128)(2,1)S(1)}, bf16[16,4096]{1,0:T(8,128)(2,1)S(1)}, u32[]{:S(2)}, u32[]{:S(2)}) collective-permute-start(bf16[16,4096]{1,0:T(8,128)(2,1)S(1)} %get-tuple-element.38), channel_id=1, source_target_pairs={{0,4},{4,8},{8,12},{12,14},{14,10},{10,6},{6,2},{2,0},{1,5},{5,9},... | collective-permute-start | bytes 393224 | tf_op jit(solution)/shard_map/ppermute | solution.py:236
  303.0 8.1 %convolution_convert_fusion.2 = bf16[128,8192]{1,0:T(8,128)(2,1)S(1)} fusion(bf16[128,1024]{1,0:T(8,128)(2,1)S(1)} %copy-done.15, bf16[1024,8192]{1,0:T(8,128)(2,1)} %param.57), kind=kOutput, calls=%fused_computation.2 | convolution fusion | flops 2148532224 | bytes 19136512 | tf_op jit(solution)/shard_map/dot_general | solution.py:497
  338.3 4.2 %collective-permute-done.35 = bf16[16,8192]{1,0:T(8,128)(2,1)S(1)} collective-permute-done((bf16[16,8192]{1,0:T(8,128)(2,1)S(1)}, bf16[16,8192]{1,0:T(8,128)(2,1)S(1)}, u32[]{:S(2)}, u32[]{:S(2)}) %collective-permute-start.35) | collective-permute-done | bytes 262176 | tf_op jit(solution)/shard_map/ppermute | solution.py:249
  348.0 6.1 %collective-permute-done.51 = bf16[16,8192]{1,0:T(8,128)(2,1)S(1)} collective-permute-done((bf16[16,8192]{1,0:T(8,128)(2,1)S(1)}, bf16[16,8192]{1,0:T(8,128)(2,1)S(1)}, u32[]{:S(2)}, u32[]{:S(2)}) %collective-permute-start.51) | collective-permute-done | bytes 262176 | tf_op jit(solution)/shard_map/ppermute | solution.py:249
  356.4 7.0 %collective-permute-done.28 = bf16[16,8192]{1,0:T(8,128)(2,1)S(1)} collective-permute-done((bf16[16,8192]{1,0:T(8,128)(2,1)S(1)}, bf16[16,8192]{1,0:T(8,128)(2,1)S(1)}, u32[]{:S(2)}, u32[]{:S(2)}) %collective-permute-start.28) | collective-permute-done | bytes 262176 | tf_op jit(solution)/shard_map/ppermute | solution.py:249
  371.2 3.4 collective-permute-done.44
  376.8 3.4 collective-permute-done.52
  388.2 4.0 collective-permute-done.56
  395.1 6.3 %collective-permute-done.33 = bf16[16,8192]{1,0:T(8,128)(2,1)S(1)} collective-permute-done((bf16[16,8192]{1,0:T(8,128)(2,1)S(1)}, bf16[16,8192]{1,0:T(8,128)(2,1)S(1)}, u32[]{:S(2)}, u32[]{:S(2)}) %collective-permute-start.33) | collective-permute-done | bytes 262176 | tf_op jit(solution)/shard_map/ppermute | solution.py:250
  407.2 3.4 collective-permute-done.49
  (232 shorter events, 121.9 us)
Async XLA Ops:
  4.6 17.2 %collective-permute-start.13 = (bf16[64,4096]{1,0:T(8,128)(2,1)S(1)}, bf16[64,4096]{1,0:T(8,128)(2,1)S(1)}, u32[]{:S(2)}, u32[]{:S(2)}) collective-permute-start(bf16[64,4096]{1,0:T(8,128)(2,1)S(1)} %get-tuple-element.36.refs_1_), channel_id=1, source_target_pairs={{0,4},{2,6},{4,8},{6,10},{8,12},{10,14},{1,5},{3,7},{5,9},{7,11},{... | collective-permute-start | bytes 1572872 | tf_op jit(solution)/shard_map/ppermute | solution.py:64
  9.5 16.7 %collective-permute-start.16 = (bf16[64,4096]{1,0:T(8,128)(2,1)S(1)}, bf16[64,4096]{1,0:T(8,128)(2,1)S(1)}, u32[]{:S(2)}, u32[]{:S(2)}) collective-permute-start(bf16[64,4096]{1,0:T(8,128)(2,1)S(1)} %get-tuple-element.36.refs_1_), channel_id=1, source_target_pairs={{4,0},{6,2},{8,4},{10,6},{12,8},{14,10},{5,1},{7,3},{9,5},{11,7},{... | collective-permute-start | bytes 1572872 | tf_op jit(solution)/shard_map/ppermute | solution.py:69
  12.4 25.1 %collective-permute-start.3 = (bf16[64,4096]{1,0:T(8,128)(2,1)S(1)}, bf16[64,4096]{1,0:T(8,128)(2,1)S(1)}, u32[]{:S(2)}, u32[]{:S(2)}) collective-permute-start(bf16[64,4096]{1,0:T(8,128)(2,1)S(1)} %get-tuple-element.37.refs_1_), channel_id=1, source_target_pairs={{4,0},{6,2},{8,4},{10,6},{12,8},{14,10},{5,1},{7,3},{9,5},{11,7},{... | collective-permute-start | bytes 1572872 | tf_op jit(solution)/shard_map/ppermute | solution.py:69
  13.7 24.5 %collective-permute-start = (bf16[64,4096]{1,0:T(8,128)(2,1)S(1)}, bf16[64,4096]{1,0:T(8,128)(2,1)S(1)}, u32[]{:S(2)}, u32[]{:S(2)}) collective-permute-start(bf16[64,4096]{1,0:T(8,128)(2,1)S(1)} %get-tuple-element.37.refs_1_), channel_id=1, source_target_pairs={{0,4},{2,6},{4,8},{6,10},{8,12},{10,14},{1,5},{3,7},{5,9},{7,11},{... | collective-permute-start | bytes 1572872 | tf_op jit(solution)/shard_map/ppermute | solution.py:64
  21.8 19.8 %collective-permute-start.6 = (bf16[64,4096]{1,0:T(8,128)(2,1)S(1)}, bf16[64,4096]{1,0:T(8,128)(2,1)S(1)}, u32[]{:S(2)}, u32[]{:S(2)}) collective-permute-start(bf16[64,4096]{1,0:T(8,128)(2,1)S(1)} %get-tuple-element.37.refs_1_), channel_id=1, source_target_pairs={{0,2},{2,0},{4,6},{6,4},{8,10},{10,8},{12,14},{14,12},{1,3},{3,1},... | collective-permute-start | bytes 1572872 | tf_op jit(solution)/shard_map/ppermute | solution.py:57
  26.3 16.7 %collective-permute-start.14 = (bf16[64,4096]{1,0:T(8,128)(2,1)S(1)}, bf16[64,4096]{1,0:T(8,128)(2,1)S(1)}, u32[]{:S(2)}, u32[]{:S(2)}) collective-permute-start(bf16[64,4096]{1,0:T(8,128)(2,1)S(1)} %collective-permute-done.13.refs_2_), channel_id=1, source_target_pairs={{4,8},{6,10},{8,12},{10,14},{5,9},{7,11},{9,13},{11,15},{20,24},{2... | collective-permute-start | bytes 1572872 | tf_op jit(solution)/shard_map/ppermute | solution.py:64
  27.0 21.9 %collective-permute-start.17 = (bf16[64,4096]{1,0:T(8,128)(2,1)S(1)}, bf16[64,4096]{1,0:T(8,128)(2,1)}, u32[]{:S(2)}, u32[]{:S(2)}) collective-permute-start(bf16[64,4096]{1,0:T(8,128)(2,1)S(1)} %collective-permute-done.16.refs_5_), channel_id=1, source_target_pairs={{4,0},{6,2},{8,4},{10,6},{5,1},{7,3},{9,5},{11,7},{20,16},{22,18},... | collective-permute-start | bytes 1572872 | tf_op jit(solution)/shard_map/ppermute | solution.py:69
  41.7 16.9 %collective-permute-start.4 = (bf16[64,4096]{1,0:T(8,128)(2,1)S(1)}, bf16[64,4096]{1,0:T(8,128)(2,1)}, u32[]{:S(2)}, u32[]{:S(2)}) collective-permute-start(bf16[64,4096]{1,0:T(8,128)(2,1)S(1)} %collective-permute-done.3.refs_5_), channel_id=1, source_target_pairs={{4,0},{6,2},{8,4},{10,6},{5,1},{7,3},{9,5},{11,7},{20,16},{22,18},... | collective-permute-start | bytes 1572872 | tf_op jit(solution)/shard_map/ppermute | solution.py:69
  43.0 16.3 %collective-permute-start.1 = (bf16[64,4096]{1,0:T(8,128)(2,1)S(1)}, bf16[64,4096]{1,0:T(8,128)(2,1)}, u32[]{:S(2)}, u32[]{:S(2)}) collective-permute-start(bf16[64,4096]{1,0:T(8,128)(2,1)S(1)} %collective-permute-done.refs_2_), channel_id=1, source_target_pairs={{4,8},{6,10},{8,12},{10,14},{5,9},{7,11},{9,13},{11,15},{20,24},{2... | collective-permute-start | bytes 1572872 | tf_op jit(solution)/shard_map/ppermute | solution.py:64
  53.8 24.7 %collective-permute-start.18 = (bf16[64,4096]{1,0:T(8,128)(2,1)}, bf16[64,4096]{1,0:T(8,128)(2,1)}, u32[]{:S(2)}, u32[]{:S(2)}) collective-permute-start(bf16[64,4096]{1,0:T(8,128)(2,1)} %collective-permute-done.17.refs_6_), channel_id=1, source_target_pairs={{4,0},{6,2},{5,1},{7,3},{20,16},{22,18},{21,17},{23,19}} | collective-permute-start | bytes 1572872 | tf_op jit(solution)/shard_map/ppermute | solution.py:69
  58.6 21.3 %collective-permute-start.21 = (bf16[64,4096]{1,0:T(8,128)(2,1)S(1)}, bf16[64,4096]{1,0:T(8,128)(2,1)S(1)}, u32[]{:S(2)}, u32[]{:S(2)}) collective-permute-start(bf16[64,4096]{1,0:T(8,128)(2,1)S(1)} %collective-permute-done.14.refs_3_), channel_id=1, source_target_pairs={{8,10},{10,8},{12,14},{14,12},{9,11},{11,9},{13,15},{15,13},{24,26... | collective-permute-start | bytes 1572872 | tf_op jit(solution)/shard_map/ppermute | solution.py:57
  59.3 28.2 %collective-permute-start.24 = (bf16[64,4096]{1,0:T(8,128)(2,1)}, bf16[64,4096]{1,0:T(8,128)(2,1)}, u32[]{:S(2)}, u32[]{:S(2)}) collective-permute-start(bf16[64,4096]{1,0:T(8,128)(2,1)} %collective-permute-done.17.refs_6_), channel_id=1, source_target_pairs={{0,2},{2,0},{4,6},{6,4},{1,3},{3,1},{5,7},{7,5},{16,18},{18,16},{2... | collective-permute-start | bytes 1572872 | tf_op jit(solution)/shard_map/ppermute | solution.py:57
  62.8 26.3 %collective-permute-start.5 = (bf16[64,4096]{1,0:T(8,128)(2,1)}, bf16[64,4096]{1,0:T(8,128)(2,1)}, u32[]{:S(2)}, u32[]{:S(2)}) collective-permute-start(bf16[64,4096]{1,0:T(8,128)(2,1)} %collective-permute-done.4.refs_6_), channel_id=1, source_target_pairs={{4,0},{6,2},{5,1},{7,3},{20,16},{22,18},{21,17},{23,19}} | collective-permute-start | bytes 1572872 | tf_op jit(solution)/shard_map/ppermute | solution.py:69
  64.1 27.4 %collective-permute-start.2 = (bf16[64,4096]{1,0:T(8,128)(2,1)}, bf16[64,4096]{1,0:T(8,128)(2,1)}, u32[]{:S(2)}, u32[]{:S(2)}) collective-permute-start(bf16[64,4096]{1,0:T(8,128)(2,1)} %collective-permute-done.1.refs_3_), channel_id=1, source_target_pairs={{8,12},{10,14},{9,13},{11,15},{24,28},{26,30},{25,29},{27,31}} | collective-permute-start | bytes 1572872 | tf_op jit(solution)/shard_map/ppermute | solution.py:64
  80.7 16.9 %collective-permute-start.25 = (bf16[64,4096]{1,0:T(8,128)(2,1)}, bf16[64,4096]{1,0:T(8,128)(2,1)}, u32[]{:S(2)}, u32[]{:S(2)}) collective-permute-start(bf16[64,4096]{1,0:T(8,128)(2,1)} %collective-permute-done.18.refs_7_), channel_id=1, source_target_pairs={{0,2},{2,0},{1,3},{3,1},{16,18},{18,16},{17,19},{19,17}} | collective-permute-start | bytes 1572872 | tf_op jit(solution)/shard_map/ppermute | solution.py:57
  87.5 24.9 %collective-permute-start.7 = (bf16[64,4096]{1,0:T(8,128)(2,1)S(1)}, bf16[64,4096]{1,0:T(8,128)(2,1)}, u32[]{:S(2)}, u32[]{:S(2)}) collective-permute-start(bf16[64,4096]{1,0:T(8,128)(2,1)S(1)} %collective-permute-done.refs_2_), channel_id=1, source_target_pairs={{4,6},{6,4},{8,10},{10,8},{12,14},{14,12},{5,7},{7,5},{9,11},{11,9... | collective-permute-start | bytes 1572872 | tf_op jit(solution)/shard_map/ppermute | solution.py:57
  89.1 23.4 %collective-permute-start.11 = (bf16[64,4096]{1,0:T(8,128)(2,1)}, bf16[64,4096]{1,0:T(8,128)(2,1)}, u32[]{:S(2)}, u32[]{:S(2)}) collective-permute-start(bf16[64,4096]{1,0:T(8,128)(2,1)} %collective-permute-done.4.refs_6_), channel_id=1, source_target_pairs={{0,2},{2,0},{4,6},{6,4},{1,3},{3,1},{5,7},{7,5},{16,18},{18,16},{2... | collective-permute-start | bytes 1572872 | tf_op jit(solution)/shard_map/ppermute | solution.py:57
  91.5 20.9 %collective-permute-start.8 = (bf16[64,4096]{1,0:T(8,128)(2,1)}, bf16[64,4096]{1,0:T(8,128)(2,1)}, u32[]{:S(2)}, u32[]{:S(2)}) collective-permute-start(bf16[64,4096]{1,0:T(8,128)(2,1)} %collective-permute-done.1.refs_3_), channel_id=1, source_target_pairs={{8,10},{10,8},{12,14},{14,12},{9,11},{11,9},{13,15},{15,13},{24,26... | collective-permute-start | bytes 1572872 | tf_op jit(solution)/shard_map/ppermute | solution.py:57
  93.0 21.1 %collective-permute-start.12 = (bf16[64,4096]{1,0:T(8,128)(2,1)}, bf16[64,4096]{1,0:T(8,128)(2,1)}, u32[]{:S(2)}, u32[]{:S(2)}) collective-permute-start(bf16[64,4096]{1,0:T(8,128)(2,1)} %collective-permute-done.5.refs_7_), channel_id=1, source_target_pairs={{0,2},{2,0},{1,3},{3,1},{16,18},{18,16},{17,19},{19,17}} | collective-permute-start | bytes 1572872 | tf_op jit(solution)/shard_map/ppermute | solution.py:57
  97.6 16.5 %collective-permute-start.9 = (bf16[64,4096]{1,0:T(8,128)(2,1)}, bf16[64,4096]{1,0:T(8,128)(2,1)}, u32[]{:S(2)}, u32[]{:S(2)}) collective-permute-start(bf16[64,4096]{1,0:T(8,128)(2,1)} %collective-permute-done.2.refs_4_), channel_id=1, source_target_pairs={{12,14},{14,12},{13,15},{15,13},{28,30},{30,28},{29,31},{31,29}} | collective-permute-start | bytes 1572872 | tf_op jit(solution)/shard_map/ppermute | solution.py:57
  127.5 18.2 %all-to-all-start.1 = ((bf16[8,64,256]{2,1,0:T(8,128)(2,1)}), bf16[8,64,256]{2,1,0:T(8,128)(2,1)S(1)}, u32[]{:S(2)}, u32[]{:S(2)}) async-start(bf16[8,64,256]{2,1,0:T(8,128)(2,1)} %bitcast.165), calls=%async_computation.1 | async-start | bytes 524288 | tf_op jit(solution)/shard_map/all_to_all | solution.py:481
  145.7 82.9 %all-to-all-start = ((bf16[16,512,256]{2,1,0:T(8,128)(2,1)}), bf16[16,512,256]{2,1,0:T(8,128)(2,1)}, u32[]{:S(2)}, u32[]{:S(2)}) async-start(bf16[16,512,256]{2,1,0:T(8,128)(2,1)} %bitcast.142), calls=%async_computation | async-start | bytes 8388608 | tf_op jit(solution)/shard_map/all_to_all | solution.py:426
  287.8 34.4 %collective-permute-start.30 = (bf16[16,4096]{1,0:T(8,128)(2,1)S(1)}, bf16[16,4096]{1,0:T(8,128)(2,1)S(1)}, u32[]{:S(2)}, u32[]{:S(2)}) collective-permute-start(bf16[16,4096]{1,0:T(8,128)(2,1)S(1)} %get-tuple-element.39), channel_id=1, source_target_pairs={{0,2},{4,0},{8,4},{12,8},{14,12},{10,14},{6,10},{2,6},{1,3},{5,1},... | collective-permute-start | bytes 393224 | tf_op jit(solution)/shard_map/ppermute | solution.py:237
  294.1 29.4 %collective-permute-start.26 = (bf16[16,4096]{1,0:T(8,128)(2,1)S(1)}, bf16[16,4096]{1,0:T(8,128)(2,1)S(1)}, u32[]{:S(2)}, u32[]{:S(2)}) collective-permute-start(bf16[16,4096]{1,0:T(8,128)(2,1)S(1)} %get-tuple-element.38), channel_id=1, source_target_pairs={{0,4},{4,8},{8,12},{12,14},{14,10},{10,6},{6,2},{2,0},{1,5},{5,9},... | collective-permute-start | bytes 393224 | tf_op jit(solution)/shard_map/ppermute | solution.py:236
  325.8 29.0 %collective-permute-start.31 = (bf16[16,8192]{1,0:T(8,128)(2,1)S(1)}, bf16[16,8192]{1,0:T(8,128)(2,1)S(1)}, u32[]{:S(2)}, u32[]{:S(2)}) collective-permute-start(bf16[16,8192]{1,0:T(8,128)(2,1)S(1)} %pad_maximum_fusion.3), channel_id=1, source_target_pairs={{0,2},{4,0},{8,4},{12,8},{14,12},{10,14},{6,10},{2,6},{1,3},{5,1},... | collective-permute-start | bytes 786440 | tf_op jit(solution)/shard_map/ppermute | solution.py:250
  328.4 35.7 %collective-permute-start.39 = (bf16[16,8192]{1,0:T(8,128)(2,1)S(1)}, bf16[16,8192]{1,0:T(8,128)(2,1)S(1)}, u32[]{:S(2)}, u32[]{:S(2)}) collective-permute-start(bf16[16,8192]{1,0:T(8,128)(2,1)S(1)} %pad_maximum_fusion.5), channel_id=1, source_target_pairs={{0,2},{4,0},{8,4},{12,8},{14,12},{10,14},{6,10},{2,6},{1,3},{5,1},... | collective-permute-start | bytes 786440 | tf_op jit(solution)/shard_map/ppermute | solution.py:250
  332.0 38.8 %collective-permute-start.47 = (bf16[16,8192]{1,0:T(8,128)(2,1)S(1)}, bf16[16,8192]{1,0:T(8,128)(2,1)S(1)}, u32[]{:S(2)}, u32[]{:S(2)}) collective-permute-start(bf16[16,8192]{1,0:T(8,128)(2,1)S(1)} %pad_maximum_fusion.7), channel_id=1, source_target_pairs={{0,2},{4,0},{8,4},{12,8},{14,12},{10,14},{6,10},{2,6},{1,3},{5,1},... | collective-permute-start | bytes 786440 | tf_op jit(solution)/shard_map/ppermute | solution.py:250
  342.4 33.9 %collective-permute-start.55 = (bf16[16,8192]{1,0:T(8,128)(2,1)S(1)}, bf16[16,8192]{1,0:T(8,128)(2,1)S(1)}, u32[]{:S(2)}, u32[]{:S(2)}) collective-permute-start(bf16[16,8192]{1,0:T(8,128)(2,1)S(1)} %pad_maximum_fusion.9), channel_id=1, source_target_pairs={{0,2},{4,0},{8,4},{12,8},{14,12},{10,14},{6,10},{2,6},{1,3},{5,1},... | collective-permute-start | bytes 786440 | tf_op jit(solution)/shard_map/ppermute | solution.py:250
  370.8 23.2 %collective-permute-start.29 = (bf16[16,8192]{1,0:T(8,128)(2,1)S(1)}, bf16[16,8192]{1,0:T(8,128)(2,1)S(1)}, u32[]{:S(2)}, u32[]{:S(2)}) collective-permute-start(bf16[16,8192]{1,0:T(8,128)(2,1)S(1)} %get-tuple-element.16), channel_id=1, source_target_pairs={{0,4},{4,8},{8,12},{12,14},{14,10},{10,6},{6,2},{2,0},{1,5},{5,9},... | collective-permute-start | bytes 786440 | tf_op jit(solution)/shard_map/ppermute | solution.py:249
  376.4 26.9 %collective-permute-start.37 = (bf16[16,8192]{1,0:T(8,128)(2,1)S(1)}, bf16[16,8192]{1,0:T(8,128)(2,1)S(1)}, u32[]{:S(2)}, u32[]{:S(2)}) collective-permute-start(bf16[16,8192]{1,0:T(8,128)(2,1)S(1)} %get-tuple-element.21), channel_id=1, source_target_pairs={{0,4},{4,8},{8,12},{12,14},{14,10},{10,6},{6,2},{2,0},{1,5},{5,9},... | collective-permute-start | bytes 786440 | tf_op jit(solution)/shard_map/ppermute | solution.py:249
  382.0 25.2 %collective-permute-start.45 = (bf16[16,8192]{1,0:T(8,128)(2,1)S(1)}, bf16[16,8192]{1,0:T(8,128)(2,1)S(1)}, u32[]{:S(2)}, u32[]{:S(2)}) collective-permute-start(bf16[16,8192]{1,0:T(8,128)(2,1)S(1)} %get-tuple-element.26), channel_id=1, source_target_pairs={{0,4},{4,8},{8,12},{12,14},{14,10},{10,6},{6,2},{2,0},{1,5},{5,9},... | collective-permute-start | bytes 786440 | tf_op jit(solution)/shard_map/ppermute | solution.py:249
  388.1 22.6 %collective-permute-start.53 = (bf16[16,8192]{1,0:T(8,128)(2,1)S(1)}, bf16[16,8192]{1,0:T(8,128)(2,1)S(1)}, u32[]{:S(2)}, u32[]{:S(2)}) collective-permute-start(bf16[16,8192]{1,0:T(8,128)(2,1)S(1)} %get-tuple-element.31), channel_id=1, source_target_pairs={{0,4},{4,8},{8,12},{12,14},{14,10},{10,6},{6,2},{2,0},{1,5},{5,9},... | collective-permute-start | bytes 786440 | tf_op jit(solution)/shard_map/ppermute | solution.py:249
  (55 other events, 1365.7 us)

commit v3 on v2

--- a/solution.py
+++ b/solution.py
@@ -14,6 +14,7 @@
 EPSILON = 1e-06
 SCORE_SCALE = HD ** (-0.5) * math.log2(math.e)
 VMEM_LIMIT = 56 * 1024 * 1024
+ATTEND_VMEM = 28 * 1024 * 1024
 GATHER_PIECES = 2
 ROW_CHUNKS = 4
 LINE_MODELS = 8
@@ -376,7 +377,7 @@
             whole(new_values),
         ],
         out_specs=pl.BlockSpec((rows, HD), lambda head: (0, head)),
-        compiler_params=pltpu.CompilerParams(vmem_limit_bytes=VMEM_LIMIT),
+        compiler_params=pltpu.CompilerParams(vmem_limit_bytes=ATTEND_VMEM),
         cost_estimate=pl.CostEstimate(
             flops=heads * rows * count * HD * 8,
             bytes_accessed=2 * (count * 3 * HD + 2 * heads * rows * HD),
@@ -452,6 +453,10 @@
                 blocks = line_gather(own, n_model)
             else:
                 blocks = [lax.all_gather(own, "mp", axis=0, tiled=True)]
+            if piece == pieces - 1:
+                (prefix_keys, prefix_values), blocks[0] = lax.optimization_barrier(
+                    (order_blocks(arrived, where, prefix_count.reshape(1)), blocks[0])
+                )
             result = project(place, blocks, weights, piece, pieces, result, biases, tables)
         queries, new_keys, new_values, pairs = result
         pairs = pairs.reshape(n_model, row_count, 2 * HD)
@@ -477,15 +482,7 @@
         first_col = (my_model % sharers) * kv_local
         key_cols = lax.dynamic_slice_in_dim(new_keys, first_col, kv_local, 1)
         pairs = jnp.stack([key_cols, value_raw], 1).reshape(n_model, row_count, 2 * kv_local)
-
-    pairs = lax.all_to_all(pairs, "mp", split_axis=0, concat_axis=0, tiled=True)
-    cache_rows = (
-        pairs.reshape(kv_heads, sharers, row_count, 2, kv_local)
-        .transpose(2, 0, 3, 1, 4)
-        .reshape(1, row_count, kv_heads * 2 * HD)
-    )
-
-    prefix_keys, prefix_values = order_blocks(arrived, where, prefix_count.reshape(1))
+        prefix_keys, prefix_values = order_blocks(arrived, where, prefix_count.reshape(1))
 
     row_step = max(row_count // ROW_CHUNKS, 16)
     by_chunk = queries.reshape(q_local, n_model, row_count // row_step, row_step, HD)
@@ -495,8 +492,15 @@
             by_chunk, prefix_keys, prefix_values, new_keys, new_values, row_step, chunk
         )
         share = jnp.dot(mixed, w_out, preferred_element_type=jnp.float32).astype(jnp.bfloat16)
+        share, by_chunk, pairs = lax.optimization_barrier((share, by_chunk, pairs))
         share = share.reshape(n_model, row_step, share.shape[1])
         summed.append(ring_scatter(share, n_model, my_model))
+    pairs = lax.all_to_all(pairs, "mp", split_axis=0, concat_axis=0, tiled=True)
+    cache_rows = (
+        pairs.reshape(kv_heads, sharers, row_count, 2, kv_local)
+        .transpose(2, 0, 3, 1, 4)
+        .reshape(1, row_count, kv_heads * 2 * HD)
+    )
     return (jnp.concatenate(summed, 0)[None], cache_rows)
 
 

time: 416 us -> 421 us (1.012)
  other arithmetic: 12.4 us -> 29 us
  starting transfers between devices: 122 us -> 107 us
  local copies, waits for them, and re-layouts: 5.29 us -> 20.1 us
  Pallas kernels: 81.6 us -> 71.6 us
  matrix products: 21.2 us -> 16.9 us
    ppermute x6, waiting for transfers between devices: 2.9 us -> 66.1 us  [line_gather(): lax.ppermute(rising, 'mp', [(2 * z + y, 2 * z + 2 + y) for z in range(ste...]
    all_to_all x1, waiting for transfers between devices: 54.1 us -> 0.01 us  [on_device(): lax.all_to_all(outgoing.reshape(holders, capacity * block_len, 2 * HD), (...]
    ppermute x6, waiting for transfers between devices: 32.9 us -> 50.8 us  [line_gather(): lax.ppermute(falling, 'mp', [(2 * z + y, 2 * z - 2 + y) for z in range(1,...]
    convert_element_type x20, other arithmetic: 1.32 us -> 15.7 us  [added(): (left.astype(jnp.float32) + right.astype(jnp.float32)).astype(jnp.bfloat16)]
    ppermute x12, waiting for transfers between devices: 32.7 us -> 18.6 us  [ring_scatter(): onward = lax.ppermute(onward, 'mp', pairs(1))]
    pallas_call x4, Pallas kernels: 44 us -> 33.3 us  [attend(): pl.pallas_call(functools.partial(attend_kernel, span, row_step, chunk), g...]
    ppermute x12, starting transfers between devices: 10.4 us -> 21 us  [ring_scatter(): onward = lax.ppermute(onward, 'mp', pairs(1))]
    ppermute x4, starting transfers between devices: 12.4 us -> 4.49 us  [ring_scatter(): back = lax.ppermute(far[:, width // 2:], 'mp', pairs(-1))]
  transfers between devices with their start and end apart: 60 -> 60, of which waited for: 26 -> 19; matrix products, arithmetic and copies ran while one was open for 6% -> 11% of each run, Pallas kernels for 4% -> 10%
where the time goes in v3:
time: 421 us; the launch traced here: 420 us
  waiting for transfers between devices  153 us (36%)
  starting transfers between devices  107 us (25%)
  Pallas kernels  71.6 us (17%)
  other arithmetic  29 us (7%)
  between operations  21.9 us (5%)
  local copies, waits for them, and re-layouts  20.1 us (5%)
  matrix products  16.9 us (4%)
    ppermute x6, waiting for transfers between devices, line_gather(): lax.ppermute(rising, 'mp', [(2 * z + y, 2 * z + 2 + y) for z in range(ste...  66.1 us
    ppermute x6, waiting for transfers between devices, line_gather(): lax.ppermute(falling, 'mp', [(2 * z + y, 2 * z - 2 + y) for z in range(1,...  50.8 us
    pallas_call x4, Pallas kernels, attend(): pl.pallas_call(functools.partial(attend_kernel, span, row_step, chunk), g...  33.3 us
    ppermute x14, starting transfers between devices, across(): return lax.ppermute(block, 'mp', pairs)  30.3 us
    pallas_call x2, Pallas kernels, project(): pl.pallas_call(functools.partial(project_kernel, length, first, last), gr...  26.3 us
    ppermute x12, starting transfers between devices, ring_scatter(): onward = lax.ppermute(onward, 'mp', pairs(1))  21 us
    ppermute x12, waiting for transfers between devices, ring_scatter(): onward = lax.ppermute(onward, 'mp', pairs(1))  18.6 us
    ppermute x12, waiting for transfers between devices, ring_scatter(): back = lax.ppermute(back, 'mp', pairs(-1))  17.4 us
  transfers between devices with their start and end apart: 60, of which 19 were waited for; matrix products, arithmetic and copies ran while one was open for 11% of the time, Pallas kernels for 10%

profile of v3, /device:TPU:0, one launch (start us, length us, event | category | flops | bytes accessed | tf_op | source)
XLA Modules:
  0.0 419.6 jit_solution(4623967356370557757)
XLA Ops:
  3.8 5.3 %pack_blocks.1 = bf16[8,2,32,16,256]{4,3,2,1,0:T(8,128)(2,1)} custom-call(s32[2,32]{1,0:T(2,128)} %select_reduce_fusion.slots_ref, bf16[64,16,2048]{2,1,0:T(8,128)(2,1)} %bitcast.167), custom_call_target="tpu_custom_call" | custom-call | tf_op jit(solution)/shard_map/pack_blocks/pallas_call | solution.py:273
  9.1 7.6 %all-to-all-start = ((bf16[16,512,256]{2,1,0:T(8,128)(2,1)}), bf16[16,512,256]{2,1,0:T(8,128)(2,1)}, u32[]{:S(2)}, u32[]{:S(2)}) async-start(bf16[16,512,256]{2,1,0:T(8,128)(2,1)} %bitcast.146), calls=%async_computation | async-start | bytes 8388608 | tf_op jit(solution)/shard_map/all_to_all | solution.py:427
  17.5 3.8 collective-permute-start.13
  25.4 5.2 %collective-permute-start = (bf16[64,4096]{1,0:T(8,128)(2,1)S(1)}, bf16[64,4096]{1,0:T(8,128)(2,1)S(1)}, u32[]{:S(2)}, u32[]{:S(2)}) collective-permute-start(bf16[64,4096]{1,0:T(8,128)(2,1)S(1)} %get-tuple-element.24.refs_1_), channel_id=1, source_target_pairs={{0,4},{2,6},{4,8},{6,10},{8,12},{10,14},{1,5},{3,7},{5,9},{7,11},{... | collective-permute-start | bytes 1572872 | tf_op jit(solution)/shard_map/ppermute | solution.py:65
  30.6 66.1 %collective-permute-done.13.refs_2_ = bf16[64,4096]{1,0:T(8,128)(2,1)S(1)} collective-permute-done((bf16[64,4096]{1,0:T(8,128)(2,1)S(1)}, bf16[64,4096]{1,0:T(8,128)(2,1)S(1)}, u32[]{:S(2)}, u32[]{:S(2)}) %collective-permute-start.13) | collective-permute-done | bytes 524320 | tf_op jit(solution)/shard_map/ppermute | solution.py:65
  96.8 2.8 collective-permute-start.6
  102.4 7.3 %collective-permute-done.3.refs_5_ = bf16[64,4096]{1,0:T(8,128)(2,1)S(1)} collective-permute-done((bf16[64,4096]{1,0:T(8,128)(2,1)S(1)}, bf16[64,4096]{1,0:T(8,128)(2,1)S(1)}, u32[]{:S(2)}, u32[]{:S(2)}) %collective-permute-start.3) | collective-permute-done | bytes 524320 | tf_op jit(solution)/shard_map/ppermute | solution.py:70
  110.4 3.5 collective-permute-start.23
  116.7 23.6 %collective-permute-done.17.refs_6_ = bf16[64,4096]{1,0:T(8,128)(2,1)} collective-permute-done((bf16[64,4096]{1,0:T(8,128)(2,1)S(1)}, bf16[64,4096]{1,0:T(8,128)(2,1)}, u32[]{:S(2)}, u32[]{:S(2)}) %collective-permute-start.17) | collective-permute-done | bytes 524320 | tf_op jit(solution)/shard_map/ppermute | solution.py:70
  140.3 2.6 collective-permute-start.10
  145.7 7.0 %collective-permute-done.4.refs_6_ = bf16[64,4096]{1,0:T(8,128)(2,1)S(1)} collective-permute-done((bf16[64,4096]{1,0:T(8,128)(2,1)S(1)}, bf16[64,4096]{1,0:T(8,128)(2,1)S(1)}, u32[]{:S(2)}, u32[]{:S(2)}) %collective-permute-start.4) | collective-permute-done | bytes 524320 | tf_op jit(solution)/shard_map/ppermute | solution.py:70
  157.3 3.4 collective-permute-start.24
  163.4 8.9 %collective-permute-done.18.refs_7_ = bf16[64,4096]{1,0:T(8,128)(2,1)} collective-permute-done((bf16[64,4096]{1,0:T(8,128)(2,1)}, bf16[64,4096]{1,0:T(8,128)(2,1)}, u32[]{:S(2)}, u32[]{:S(2)}) %collective-permute-start.18) | collective-permute-done | bytes 524320 | tf_op jit(solution)/shard_map/ppermute | solution.py:70
  173.8 3.4 collective-permute-start.25
  179.7 4.0 collective-permute-done.5.refs_7_
  183.6 3.4 collective-permute-start.11
  215.1 12.2 %project.2.refs_18_ = f32[512,1280]{1,0:T(8,128)} custom-call(s32[2]{0:T(128)} %pad_add_fusion.refs_0_, bf16[64,4096]{1,0:T(8,128)(2,1)} %copy-done.14, bf16[64,4096]{1,0:T(8,128)(2,1)} %copy-done.21, bf16[64,4096]{1,0:T(8,128)(2,1)} %collective-permute-done.14.refs_3_, bf16[64,4096]{1,0:T(8,128)(2,1)} %collective-permute-done.15.refs_4_, ...), custom_call_target="tpu_custom_call" | custom-call | flops 5368709120 | bytes 17301504 | tf_op jit(solution)/shard_map/project/pallas_call | solution.py:194
  227.3 6.7 %order_blocks.1 = (bf16[4096,128]{1,0:T(8,128)(2,1)}, bf16[4096,256]{1,0:T(8,128)(2,1)}) custom-call(s32[1]{0:T(128)} %dynamic_slice.211.length_ref, s32[256]{0:T(256)} %multiply_add_fusion.where_ref, bf16[512,16,256]{2,1,0:T(8,128)(2,1)} %bitcast.5.arrived_ref), custom_call_target="tpu_custom_call" | custom-call | tf_op jit(solution)/shard_map/order_blocks/pallas_call | solution.py:307
  234.9 14.1 %project.3 = (bf16[8,512,128]{2,1,0:T(8,128)(2,1)}, bf16[512,128]{1,0:T(8,128)(2,1)}, bf16[512,256]{1,0:T(8,128)(2,1)}, bf16[512,256]{1,0:T(8,128)(2,1)}) custom-call(s32[2]{0:T(128)} %pad_add_fusion.refs_0_, bf16[64,4096]{1,0:T(8,128)(2,1)} %copy-done.13, bf16[64,4096]{1,0:T(8,128)(2,1)} %copy-done.19, bf16[64,4096]{1,0:T(8,128)(2,1)} %collective-permute-done.1.refs_3_, ...), custom_call_target="tpu_custom_call" | custom-call | flops 5368709120 | bytes 17301504 | tf_op jit(solution)/shard_map/project/pallas_call | solution.py:194
  252.1 8.3 %attend.4 = bf16[128,1024]{1,0:T(8,128)(2,1)S(1)} custom-call(bf16[8,8,4,16,128]{4,3,2,1,0:T(8,128)(2,1)S(1)} %bitcast.140, bf16[4096,128]{1,0:T(8,128)(2,1)S(1)} %copy-done.1, bf16[4096,256]{1,0:T(8,128)(2,1)S(1)} %copy-done, bf16[512,128]{1,0:T(8,128)(2,1)S(1)} %copy-done.6, bf16[512,256]{1,0:T(8,128)(2,1)S(1)} %copy-done.4), custom_call_target="tpu_custom_call" | custom-call | flops 4831838208 | bytes 4063232 | tf_op jit(solution)/shard_map/attend/pallas_call | solution.py:368
  260.4 8.3 %convolution_convert_fusion.3 = bf16[128,8192]{1,0:T(8,128)(2,1)S(1)} fusion(bf16[128,1024]{1,0:T(8,128)(2,1)S(1)} %attend.4, bf16[1024,8192]{1,0:T(8,128)(2,1)} %param.57), kind=kOutput, calls=%fused_computation.3 | convolution fusion | flops 2148532224 | bytes 19136512 | tf_op jit(solution)/shard_map/dot_general | solution.py:494
  272.3 8.4 %attend.5 = bf16[128,1024]{1,0:T(8,128)(2,1)S(1)} custom-call(bf16[8,8,4,16,128]{4,3,2,1,0:T(8,128)(2,1)S(1)} %bitcast.141, bf16[4096,128]{1,0:T(8,128)(2,1)S(1)} %copy-done.1, bf16[4096,256]{1,0:T(8,128)(2,1)S(1)} %copy-done, bf16[512,128]{1,0:T(8,128)(2,1)S(1)} %copy-done.7, bf16[512,256]{1,0:T(8,128)(2,1)S(1)} %copy-done.5), custom_call_target="tpu_custom_call" | custom-call | flops 4831838208 | bytes 4063232 | tf_op jit(solution)/shard_map/attend/pallas_call | solution.py:368
  286.7 8.3 %attend.6 = bf16[128,1024]{1,0:T(8,128)(2,1)S(1)} custom-call(bf16[8,8,4,16,128]{4,3,2,1,0:T(8,128)(2,1)S(1)} %bitcast.142, bf16[4096,128]{1,0:T(8,128)(2,1)S(1)} %copy-done.1, bf16[4096,256]{1,0:T(8,128)(2,1)S(1)} %copy-done, bf16[512,128]{1,0:T(8,128)(2,1)S(1)} %copy-done.7, bf16[512,256]{1,0:T(8,128)(2,1)S(1)} %copy-done.5), custom_call_target="tpu_custom_call" | custom-call | flops 4831838208 | bytes 4063232 | tf_op jit(solution)/shard_map/attend/pallas_call | solution.py:368
  295.1 3.8 convolution_convert_fusion.1
  302.2 8.3 %attend.7 = bf16[128,1024]{1,0:T(8,128)(2,1)S(1)} custom-call(bf16[8,8,4,16,128]{4,3,2,1,0:T(8,128)(2,1)S(1)} %bitcast.143, bf16[4096,128]{1,0:T(8,128)(2,1)S(1)} %copy-done.1, bf16[4096,256]{1,0:T(8,128)(2,1)S(1)} %copy-done, bf16[512,128]{1,0:T(8,128)(2,1)S(1)} %copy-done.7, bf16[512,256]{1,0:T(8,128)(2,1)S(1)} %copy-done.5), custom_call_target="tpu_custom_call" | custom-call | flops 4831838208 | bytes 4063232 | tf_op jit(solution)/shard_map/attend/pallas_call | solution.py:368
  318.4 4.4 %all-to-all-start.1 = ((bf16[8,64,256]{2,1,0:T(8,128)(2,1)}), bf16[8,64,256]{2,1,0:T(8,128)(2,1)}, u32[]{:S(2)}, u32[]{:S(2)}) async-start(bf16[8,64,256]{2,1,0:T(8,128)(2,1)} %bitcast.169), calls=%async_computation.1 | async-start | bytes 524288 | tf_op jit(solution)/shard_map/all_to_all | solution.py:498
  339.8 3.8 collective-permute-done.27
  356.0 5.0 %collective-permute-done.51 = bf16[16,8192]{1,0:T(8,128)(2,1)S(1)} collective-permute-done((bf16[16,8192]{1,0:T(8,128)(2,1)S(1)}, bf16[16,8192]{1,0:T(8,128)(2,1)S(1)}, u32[]{:S(2)}, u32[]{:S(2)}) %collective-permute-start.51) | collective-permute-done | bytes 262176 | tf_op jit(solution)/shard_map/ppermute | solution.py:250
  392.4 4.9 %collective-permute-done.48 = bf16[16,8192]{1,0:T(8,128)(2,1)S(1)} collective-permute-done((bf16[16,8192]{1,0:T(8,128)(2,1)S(1)}, bf16[16,8192]{1,0:T(8,128)(2,1)S(1)}, u32[]{:S(2)}, u32[]{:S(2)}) %collective-permute-start.48) | collective-permute-done | bytes 262176 | tf_op jit(solution)/shard_map/ppermute | solution.py:251
  399.1 3.8 collective-permute-done.56
  405.6 3.6 collective-permute-done.33
  415.7 2.7 collective-permute-done.57
  (264 shorter events, 133.5 us)
Async XLA Ops:
  9.1 218.2 %all-to-all-start = ((bf16[16,512,256]{2,1,0:T(8,128)(2,1)}), bf16[16,512,256]{2,1,0:T(8,128)(2,1)}, u32[]{:S(2)}, u32[]{:S(2)}) async-start(bf16[16,512,256]{2,1,0:T(8,128)(2,1)} %bitcast.146), calls=%async_computation | async-start | bytes 8388608 | tf_op jit(solution)/shard_map/all_to_all | solution.py:427
  17.5 79.3 %collective-permute-start.13 = (bf16[64,4096]{1,0:T(8,128)(2,1)S(1)}, bf16[64,4096]{1,0:T(8,128)(2,1)S(1)}, u32[]{:S(2)}, u32[]{:S(2)}) collective-permute-start(bf16[64,4096]{1,0:T(8,128)(2,1)S(1)} %get-tuple-element.64.refs_1_), channel_id=1, source_target_pairs={{0,4},{2,6},{4,8},{6,10},{8,12},{10,14},{1,5},{3,7},{5,9},{7,11},{... | collective-permute-start | bytes 1572872 | tf_op jit(solution)/shard_map/ppermute | solution.py:65
  21.3 78.3 %collective-permute-start.16 = (bf16[64,4096]{1,0:T(8,128)(2,1)S(1)}, bf16[64,4096]{1,0:T(8,128)(2,1)S(1)}, u32[]{:S(2)}, u32[]{:S(2)}) collective-permute-start(bf16[64,4096]{1,0:T(8,128)(2,1)S(1)} %get-tuple-element.64.refs_1_), channel_id=1, source_target_pairs={{4,0},{6,2},{8,4},{10,6},{12,8},{14,10},{5,1},{7,3},{9,5},{11,7},{... | collective-permute-start | bytes 1572872 | tf_op jit(solution)/shard_map/ppermute | solution.py:70
  22.6 78.5 %collective-permute-start.19 = (bf16[64,4096]{1,0:T(8,128)(2,1)S(1)}, bf16[64,4096]{1,0:T(8,128)(2,1)S(1)}, u32[]{:S(2)}, u32[]{:S(2)}) collective-permute-start(bf16[64,4096]{1,0:T(8,128)(2,1)S(1)} %get-tuple-element.64.refs_1_), channel_id=1, source_target_pairs={{0,2},{2,0},{4,6},{6,4},{8,10},{10,8},{12,14},{14,12},{1,3},{3,1},... | collective-permute-start | bytes 1572872 | tf_op jit(solution)/shard_map/ppermute | solution.py:58
  24.1 85.5 %collective-permute-start.3 = (bf16[64,4096]{1,0:T(8,128)(2,1)S(1)}, bf16[64,4096]{1,0:T(8,128)(2,1)S(1)}, u32[]{:S(2)}, u32[]{:S(2)}) collective-permute-start(bf16[64,4096]{1,0:T(8,128)(2,1)S(1)} %get-tuple-element.24.refs_1_), channel_id=1, source_target_pairs={{4,0},{6,2},{8,4},{10,6},{12,8},{14,10},{5,1},{7,3},{9,5},{11,7},{... | collective-permute-start | bytes 1572872 | tf_op jit(solution)/shard_map/ppermute | solution.py:70
  25.4 84.9 %collective-permute-start = (bf16[64,4096]{1,0:T(8,128)(2,1)S(1)}, bf16[64,4096]{1,0:T(8,128)(2,1)S(1)}, u32[]{:S(2)}, u32[]{:S(2)}) collective-permute-start(bf16[64,4096]{1,0:T(8,128)(2,1)S(1)} %get-tuple-element.24.refs_1_), channel_id=1, source_target_pairs={{0,4},{2,6},{4,8},{6,10},{8,12},{10,14},{1,5},{3,7},{5,9},{7,11},{... | collective-permute-start | bytes 1572872 | tf_op jit(solution)/shard_map/ppermute | solution.py:65
  101.1 39.3 %collective-permute-start.17 = (bf16[64,4096]{1,0:T(8,128)(2,1)S(1)}, bf16[64,4096]{1,0:T(8,128)(2,1)}, u32[]{:S(2)}, u32[]{:S(2)}) collective-permute-start(bf16[64,4096]{1,0:T(8,128)(2,1)S(1)} %collective-permute-done.16.refs_5_), channel_id=1, source_target_pairs={{4,0},{6,2},{8,4},{10,6},{5,1},{7,3},{9,5},{11,7},{20,16},{22,18},... | collective-permute-start | bytes 1572872 | tf_op jit(solution)/shard_map/ppermute | solution.py:70
  109.7 33.2 %collective-permute-start.20 = (bf16[64,4096]{1,0:T(8,128)(2,1)S(1)}, bf16[64,4096]{1,0:T(8,128)(2,1)S(1)}, u32[]{:S(2)}, u32[]{:S(2)}) collective-permute-start(bf16[64,4096]{1,0:T(8,128)(2,1)S(1)} %collective-permute-done.13.refs_2_), channel_id=1, source_target_pairs={{4,6},{6,4},{8,10},{10,8},{12,14},{14,12},{5,7},{7,5},{9,11},{11,9... | collective-permute-start | bytes 1572872 | tf_op jit(solution)/shard_map/ppermute | solution.py:58
  110.4 34.1 %collective-permute-start.23 = (bf16[64,4096]{1,0:T(8,128)(2,1)S(1)}, bf16[64,4096]{1,0:T(8,128)(2,1)S(1)}, u32[]{:S(2)}, u32[]{:S(2)}) collective-permute-start(bf16[64,4096]{1,0:T(8,128)(2,1)S(1)} %collective-permute-done.16.refs_5_), channel_id=1, source_target_pairs={{0,2},{2,0},{4,6},{6,4},{8,10},{10,8},{1,3},{3,1},{5,7},{7,5},{9,1... | collective-permute-start | bytes 1572872 | tf_op jit(solution)/shard_map/ppermute | solution.py:58
  113.9 38.8 %collective-permute-start.4 = (bf16[64,4096]{1,0:T(8,128)(2,1)S(1)}, bf16[64,4096]{1,0:T(8,128)(2,1)S(1)}, u32[]{:S(2)}, u32[]{:S(2)}) collective-permute-start(bf16[64,4096]{1,0:T(8,128)(2,1)S(1)} %collective-permute-done.3.refs_5_), channel_id=1, source_target_pairs={{4,0},{6,2},{8,4},{10,6},{5,1},{7,3},{9,5},{11,7},{20,16},{22,18},... | collective-permute-start | bytes 1572872 | tf_op jit(solution)/shard_map/ppermute | solution.py:70
  115.2 42.0 %collective-permute-start.1 = (bf16[64,4096]{1,0:T(8,128)(2,1)S(1)}, bf16[64,4096]{1,0:T(8,128)(2,1)}, u32[]{:S(2)}, u32[]{:S(2)}) collective-permute-start(bf16[64,4096]{1,0:T(8,128)(2,1)S(1)} %collective-permute-done.refs_2_), channel_id=1, source_target_pairs={{4,8},{6,10},{8,12},{10,14},{5,9},{7,11},{9,13},{11,15},{20,24},{2... | collective-permute-start | bytes 1572872 | tf_op jit(solution)/shard_map/ppermute | solution.py:65
  144.5 27.8 %collective-permute-start.18 = (bf16[64,4096]{1,0:T(8,128)(2,1)}, bf16[64,4096]{1,0:T(8,128)(2,1)}, u32[]{:S(2)}, u32[]{:S(2)}) collective-permute-start(bf16[64,4096]{1,0:T(8,128)(2,1)} %collective-permute-done.17.refs_6_), channel_id=1, source_target_pairs={{4,0},{6,2},{5,1},{7,3},{20,16},{22,18},{21,17},{23,19}} | collective-permute-start | bytes 1572872 | tf_op jit(solution)/shard_map/ppermute | solution.py:70
  160.6 23.0 %collective-permute-start.5 = (bf16[64,4096]{1,0:T(8,128)(2,1)}, bf16[64,4096]{1,0:T(8,128)(2,1)}, u32[]{:S(2)}, u32[]{:S(2)}) collective-permute-start(bf16[64,4096]{1,0:T(8,128)(2,1)} %copy-done.24), channel_id=1, source_target_pairs={{4,0},{6,2},{5,1},{7,3},{20,16},{22,18},{21,17},{23,19}} | collective-permute-start | bytes 1572872 | tf_op jit(solution)/shard_map/ppermute | solution.py:70
  162.0 25.1 %collective-permute-start.2 = (bf16[64,4096]{1,0:T(8,128)(2,1)}, bf16[64,4096]{1,0:T(8,128)(2,1)}, u32[]{:S(2)}, u32[]{:S(2)}) collective-permute-start(bf16[64,4096]{1,0:T(8,128)(2,1)} %collective-permute-done.1.refs_3_), channel_id=1, source_target_pairs={{8,12},{10,14},{9,13},{11,15},{24,28},{26,30},{25,29},{27,31}} | collective-permute-start | bytes 1572872 | tf_op jit(solution)/shard_map/ppermute | solution.py:65
  179.0 55.0 %collective-permute-start.7 = (bf16[64,4096]{1,0:T(8,128)(2,1)S(1)}, bf16[64,4096]{1,0:T(8,128)(2,1)S(1)}, u32[]{:S(2)}, u32[]{:S(2)}) collective-permute-start(bf16[64,4096]{1,0:T(8,128)(2,1)S(1)} %collective-permute-done.refs_2_), channel_id=1, source_target_pairs={{4,6},{6,4},{8,10},{10,8},{12,14},{14,12},{5,7},{7,5},{9,11},{11,9... | collective-permute-start | bytes 1572872 | tf_op jit(solution)/shard_map/ppermute | solution.py:58
  183.6 50.4 %collective-permute-start.11 = (bf16[64,4096]{1,0:T(8,128)(2,1)}, bf16[64,4096]{1,0:T(8,128)(2,1)}, u32[]{:S(2)}, u32[]{:S(2)}) collective-permute-start(bf16[64,4096]{1,0:T(8,128)(2,1)} %copy-done.24), channel_id=1, source_target_pairs={{0,2},{2,0},{4,6},{6,4},{1,3},{3,1},{5,7},{7,5},{16,18},{18,16},{2... | collective-permute-start | bytes 1572872 | tf_op jit(solution)/shard_map/ppermute | solution.py:58
  187.0 47.0 %collective-permute-start.8 = (bf16[64,4096]{1,0:T(8,128)(2,1)}, bf16[64,4096]{1,0:T(8,128)(2,1)}, u32[]{:S(2)}, u32[]{:S(2)}) collective-permute-start(bf16[64,4096]{1,0:T(8,128)(2,1)} %collective-permute-done.1.refs_3_), channel_id=1, source_target_pairs={{8,10},{10,8},{12,14},{14,12},{9,11},{11,9},{13,15},{15,13},{24,26... | collective-permute-start | bytes 1572872 | tf_op jit(solution)/shard_map/ppermute | solution.py:58
  188.5 45.6 %collective-permute-start.12 = (bf16[64,4096]{1,0:T(8,128)(2,1)}, bf16[64,4096]{1,0:T(8,128)(2,1)}, u32[]{:S(2)}, u32[]{:S(2)}) collective-permute-start(bf16[64,4096]{1,0:T(8,128)(2,1)} %collective-permute-done.5.refs_7_), channel_id=1, source_target_pairs={{0,2},{2,0},{1,3},{3,1},{16,18},{18,16},{17,19},{19,17}} | collective-permute-start | bytes 1572872 | tf_op jit(solution)/shard_map/ppermute | solution.py:58
  191.0 43.1 %collective-permute-start.9 = (bf16[64,4096]{1,0:T(8,128)(2,1)}, bf16[64,4096]{1,0:T(8,128)(2,1)}, u32[]{:S(2)}, u32[]{:S(2)}) collective-permute-start(bf16[64,4096]{1,0:T(8,128)(2,1)} %collective-permute-done.2.refs_4_), channel_id=1, source_target_pairs={{12,14},{14,12},{13,15},{15,13},{28,30},{30,28},{29,31},{31,29}} | collective-permute-start | bytes 1572872 | tf_op jit(solution)/shard_map/ppermute | solution.py:58
  269.5 53.2 %collective-permute-start.30 = (bf16[16,4096]{1,0:T(8,128)(2,1)}, bf16[16,4096]{1,0:T(8,128)(2,1)}, u32[]{:S(2)}, u32[]{:S(2)}) collective-permute-start(bf16[16,4096]{1,0:T(8,128)(2,1)} %get-tuple-element.67), channel_id=1, source_target_pairs={{0,2},{4,0},{8,4},{12,8},{14,12},{10,14},{6,10},{2,6},{1,3},{5,1},... | collective-permute-start | bytes 393224 | tf_op jit(solution)/shard_map/ppermute | solution.py:238
  271.7 55.8 %collective-permute-start.26 = (bf16[16,4096]{1,0:T(8,128)(2,1)}, bf16[16,4096]{1,0:T(8,128)(2,1)}, u32[]{:S(2)}, u32[]{:S(2)}) collective-permute-start(bf16[16,4096]{1,0:T(8,128)(2,1)} %get-tuple-element.66), channel_id=1, source_target_pairs={{0,4},{4,8},{8,12},{12,14},{14,10},{10,6},{6,2},{2,0},{1,5},{5,9},... | collective-permute-start | bytes 393224 | tf_op jit(solution)/shard_map/ppermute | solution.py:237
  284.0 45.5 %collective-permute-start.38 = (bf16[16,4096]{1,0:T(8,128)(2,1)}, bf16[16,4096]{1,0:T(8,128)(2,1)}, u32[]{:S(2)}, u32[]{:S(2)}) collective-permute-start(bf16[16,4096]{1,0:T(8,128)(2,1)} %get-tuple-element.69), channel_id=1, source_target_pairs={{0,2},{4,0},{8,4},{12,8},{14,12},{10,14},{6,10},{2,6},{1,3},{5,1},... | collective-permute-start | bytes 393224 | tf_op jit(solution)/shard_map/ppermute | solution.py:238
  286.2 47.1 %collective-permute-start.34 = (bf16[16,4096]{1,0:T(8,128)(2,1)}, bf16[16,4096]{1,0:T(8,128)(2,1)}, u32[]{:S(2)}, u32[]{:S(2)}) collective-permute-start(bf16[16,4096]{1,0:T(8,128)(2,1)} %get-tuple-element.68), channel_id=1, source_target_pairs={{0,4},{4,8},{8,12},{12,14},{14,10},{10,6},{6,2},{2,0},{1,5},{5,9},... | collective-permute-start | bytes 393224 | tf_op jit(solution)/shard_map/ppermute | solution.py:237
  300.7 33.6 %collective-permute-start.46 = (bf16[16,4096]{1,0:T(8,128)(2,1)}, bf16[16,4096]{1,0:T(8,128)(2,1)}, u32[]{:S(2)}, u32[]{:S(2)}) collective-permute-start(bf16[16,4096]{1,0:T(8,128)(2,1)} %get-tuple-element.71), channel_id=1, source_target_pairs={{0,2},{4,0},{8,4},{12,8},{14,12},{10,14},{6,10},{2,6},{1,3},{5,1},... | collective-permute-start | bytes 393224 | tf_op jit(solution)/shard_map/ppermute | solution.py:238
  318.4 46.8 %all-to-all-start.1 = ((bf16[8,64,256]{2,1,0:T(8,128)(2,1)}), bf16[8,64,256]{2,1,0:T(8,128)(2,1)}, u32[]{:S(2)}, u32[]{:S(2)}) async-start(bf16[8,64,256]{2,1,0:T(8,128)(2,1)} %bitcast.169), calls=%async_computation.1 | async-start | bytes 524288 | tf_op jit(solution)/shard_map/all_to_all | solution.py:498
  333.3 34.0 %collective-permute-start.31 = (bf16[16,8192]{1,0:T(8,128)(2,1)}, bf16[16,8192]{1,0:T(8,128)(2,1)}, u32[]{:S(2)}, u32[]{:S(2)}) collective-permute-start(bf16[16,8192]{1,0:T(8,128)(2,1)} %pad_maximum_fusion.3), channel_id=1, source_target_pairs={{0,2},{4,0},{8,4},{12,8},{14,12},{10,14},{6,10},{2,6},{1,3},{5,1},... | collective-permute-start | bytes 786440 | tf_op jit(solution)/shard_map/ppermute | solution.py:251
  337.3 36.9 %collective-permute-start.39 = (bf16[16,8192]{1,0:T(8,128)(2,1)}, bf16[16,8192]{1,0:T(8,128)(2,1)}, u32[]{:S(2)}, u32[]{:S(2)}) collective-permute-start(bf16[16,8192]{1,0:T(8,128)(2,1)} %pad_maximum_fusion.5), channel_id=1, source_target_pairs={{0,2},{4,0},{8,4},{12,8},{14,12},{10,14},{6,10},{2,6},{1,3},{5,1},... | collective-permute-start | bytes 786440 | tf_op jit(solution)/shard_map/ppermute | solution.py:251
  339.6 39.4 %collective-permute-start.47 = (bf16[16,8192]{1,0:T(8,128)(2,1)S(1)}, bf16[16,8192]{1,0:T(8,128)(2,1)}, u32[]{:S(2)}, u32[]{:S(2)}) collective-permute-start(bf16[16,8192]{1,0:T(8,128)(2,1)S(1)} %pad_maximum_fusion.7), channel_id=1, source_target_pairs={{0,2},{4,0},{8,4},{12,8},{14,12},{10,14},{6,10},{2,6},{1,3},{5,1},... | collective-permute-start | bytes 786440 | tf_op jit(solution)/shard_map/ppermute | solution.py:251
  347.4 37.0 %collective-permute-start.55 = (bf16[16,8192]{1,0:T(8,128)(2,1)S(1)}, bf16[16,8192]{1,0:T(8,128)(2,1)S(1)}, u32[]{:S(2)}, u32[]{:S(2)}) collective-permute-start(bf16[16,8192]{1,0:T(8,128)(2,1)S(1)} %pad_maximum_fusion.9), channel_id=1, source_target_pairs={{0,2},{4,0},{8,4},{12,8},{14,12},{10,14},{6,10},{2,6},{1,3},{5,1},... | collective-permute-start | bytes 786440 | tf_op jit(solution)/shard_map/ppermute | solution.py:251
  379.0 24.9 %collective-permute-start.29 = (bf16[16,8192]{1,0:T(8,128)(2,1)S(1)}, bf16[16,8192]{1,0:T(8,128)(2,1)S(1)}, u32[]{:S(2)}, u32[]{:S(2)}) collective-permute-start(bf16[16,8192]{1,0:T(8,128)(2,1)S(1)} %get-tuple-element.44), channel_id=1, source_target_pairs={{0,4},{4,8},{8,12},{12,14},{14,10},{10,6},{6,2},{2,0},{1,5},{5,9},... | collective-permute-start | bytes 786440 | tf_op jit(solution)/shard_map/ppermute | solution.py:250
  384.5 25.9 %collective-permute-start.37 = (bf16[16,8192]{1,0:T(8,128)(2,1)S(1)}, bf16[16,8192]{1,0:T(8,128)(2,1)S(1)}, u32[]{:S(2)}, u32[]{:S(2)}) collective-permute-start(bf16[16,8192]{1,0:T(8,128)(2,1)S(1)} %get-tuple-element.49), channel_id=1, source_target_pairs={{0,4},{4,8},{8,12},{12,14},{14,10},{10,6},{6,2},{2,0},{1,5},{5,9},... | collective-permute-start | bytes 786440 | tf_op jit(solution)/shard_map/ppermute | solution.py:250
  389.1 24.0 %collective-permute-start.45 = (bf16[16,8192]{1,0:T(8,128)(2,1)S(1)}, bf16[16,8192]{1,0:T(8,128)(2,1)S(1)}, u32[]{:S(2)}, u32[]{:S(2)}) collective-permute-start(bf16[16,8192]{1,0:T(8,128)(2,1)S(1)} %get-tuple-element.54), channel_id=1, source_target_pairs={{0,4},{4,8},{8,12},{12,14},{14,10},{10,6},{6,2},{2,0},{1,5},{5,9},... | collective-permute-start | bytes 786440 | tf_op jit(solution)/shard_map/ppermute | solution.py:250
  (71 other events, 2425.5 us)

commit v4 on v1

v4 whole, which is shorter than its diff:
```python
import functools
import math

import jax
import jax.numpy as jnp
from jax import lax
from jax.experimental import pallas as pl
from jax.experimental.pallas import tpu as pltpu
from jax.sharding import PartitionSpec as P

QH = 64
HD = 128
ROPE_BASE = 1000000.0
EPSILON = 1e-06
SCORE_SCALE = HD ** (-0.5) * math.log2(math.e)
VMEM_LIMIT = 56 * 1024 * 1024
ATTEND_VMEM = 28 * 1024 * 1024
ROW_STEP = 32
LINE_MODELS = 8


def angle_tables(positions):
    frequency = jnp.power(
        jnp.float32(ROPE_BASE), -2.0 * jnp.arange(HD // 2, dtype=jnp.float32) / HD
    )
    angles = positions.astype(jnp.float32)[:, None] * frequency[None, :]
    return jnp.cos(angles), jnp.sin(angles)


def rotate(vectors, cosine, sine):
    first_half = vectors[..., : HD // 2]
    second = vectors[..., HD // 2 :]
    cosine = cosine[:, None, :]
    sine = sine[:, None, :]
    return jnp.concatenate(
        [first_half * cosine - second * sine, second * cosine + first_half * sine], -1
    )


def normalize(states, gain_vec):
    values = states.astype(jnp.float32)
    inv_rms = lax.rsqrt(jnp.mean(values * values, axis=-1, keepdims=True) + EPSILON)
    return (values * inv_rms * gain_vec.astype(jnp.float32)).astype(jnp.bfloat16)


def listing(owned_mask, capacity):
    rank_order = jnp.cumsum(owned_mask.astype(jnp.int32), -1) - 1
    slot_index = jnp.arange(capacity, dtype=jnp.int32)
    return owned_mask[..., None, :] & (rank_order[..., None, :] == slot_index[:, None])


def line_gather(own, upper_half, middle):
    def swap(block, mask):
        return lax.ppermute(block, "mp", [(index, index ^ mask) for index in range(LINE_MODELS)])

    def cross(block):
        return lax.ppermute(
            block,
            "mp",
            [(index, index ^ 6 if 2 <= index < 6 else index) for index in range(LINE_MODELS)],
        )

    beside = swap(own, 2)
    over = cross(own)
    own_y = swap(own, 1)
    over_beside = cross(beside)
    over_passed = swap(over, 2)
    beside_y = swap(beside, 1)
    far_first = jnp.where(middle, over, over_passed)
    far_first_y = swap(far_first, 1)
    far_second = jnp.where(middle, over_beside, swap(over_beside, 2))
    far_second_y = swap(far_second, 1)
    return [own, beside, own_y, beside_y], [far_first, far_second, far_first_y, far_second_y]


def project_kernel(starts_ref, *refs):
    n_blocks = starts_ref.shape[0]
    blocks = refs[:n_blocks]
    weights = refs[n_blocks : n_blocks + 3]
    q_bias_ref, k_bias_ref, v_bias_ref, cos_ref, sin_ref = refs[n_blocks + 3 : n_blocks + 8]
    query_ref, key_ref, value_ref, pair_ref, tokens_ref, total_ref, sems = refs[n_blocks + 8 :]
    step = pl.program_id(0)
    depth, q_width = weights[0].shape
    rows = blocks[0].shape[0]

    @pl.when(step == 0)
    def _():
        copies = [
            pltpu.make_async_copy(
                block,
                tokens_ref.at[pl.ds(pl.multiple_of(starts_ref[index], rows), rows), :],
                sems.at[index],
            )
            for index, block in enumerate(blocks)
        ]
        for copy in copies:
            copy.start()
        total_ref[...] = jnp.zeros_like(total_ref)
        for copy in copies:
            copy.wait()

    tokens = tokens_ref[:, pl.ds(pl.multiple_of(step * depth, depth), depth)]
    total_ref[:, :q_width] += jnp.dot(
        tokens, weights[0][...], preferred_element_type=jnp.float32
    )
    both = jnp.concatenate([weights[1][...], weights[2][...]], axis=1)
    total_ref[:, q_width:] += jnp.dot(tokens, both, preferred_element_type=jnp.float32)

    @pl.when(step == pl.num_programs(0) - 1)
    def _():
        cosine, sine = cos_ref[...], sin_ref[...]

        def turned(vectors):
            return vectors * cosine + pltpu.roll(vectors, HD // 2, 1) * sine

        for head in range(q_width // HD):
            cols = slice(head * HD, (head + 1) * HD)
            query = total_ref[:, cols] + q_bias_ref[:, cols].astype(jnp.float32)
            query_ref[head] = turned(query).astype(jnp.bfloat16)
        key = total_ref[:, q_width : q_width + HD] + k_bias_ref[...].astype(jnp.float32)
        key = turned(key.astype(jnp.bfloat16).astype(jnp.float32)).astype(jnp.bfloat16)
        value = total_ref[:, q_width + HD :] + v_bias_ref[...].astype(jnp.float32)
        value = value.astype(jnp.bfloat16)
        key_ref[...] = key
        value_ref[:, :HD] = value
        value_ref[:, HD:] = jnp.ones_like(value)
        pair_ref[:, :HD] = key
        pair_ref[:, HD:] = value


def project(starts, blocks, weights, biases, tables):
    width = blocks[0].shape[1]
    rows = sum(block.shape[0] for block in blocks)
    depth = math.gcd(width, 1024)
    q_width = weights[0].shape[1]
    out_width = q_width + 2 * HD
    fixed = lambda array: pl.BlockSpec(array.shape, lambda step: (0,) * len(array.shape))
    in_specs = [pl.BlockSpec(memory_space=pltpu.SMEM)]
    in_specs += [pl.BlockSpec(memory_space=pl.ANY)] * len(blocks)
    in_specs += [pl.BlockSpec((depth, weight.shape[1]), lambda step: (step, 0)) for weight in weights]
    in_specs += [fixed(array) for array in (*biases, *tables)]
    out_shape = (
        jax.ShapeDtypeStruct((q_width // HD, rows, HD), jnp.bfloat16),
        jax.ShapeDtypeStruct((rows, HD), jnp.bfloat16),
        jax.ShapeDtypeStruct((rows, 2 * HD), jnp.bfloat16),
        jax.ShapeDtypeStruct((rows, 2 * HD), jnp.bfloat16),
    )
    return pl.pallas_call(
        project_kernel,
        grid=(width // depth,),
        out_shape=out_shape,
        in_specs=in_specs,
        out_specs=tuple(fixed(shape) for shape in out_shape),
        scratch_shapes=[
            pltpu.VMEM((rows, width), jnp.bfloat16),
            pltpu.VMEM((rows, out_width), jnp.float32),
            pltpu.SemaphoreType.DMA((len(blocks),)),
        ],
        compiler_params=pltpu.CompilerParams(vmem_limit_bytes=ATTEND_VMEM),
        cost_estimate=pl.CostEstimate(
            flops=2 * rows * width * out_width,
            bytes_accessed=2 * width * (rows + out_width) + 4 * rows * out_width,
            transcendentals=0,
        ),
        name="project",
    )(starts, *blocks, *weights, *biases, *tables)


class RingScatter:
    def __init__(self, shares, n_model, my_model, first, way):
        order = [m for m in range(0, n_model, 2)] + [m for m in range(n_model - 1, 0, -2)]
        self.order = order
        self.n_model = n_model
        self.way = way
        spot = jnp.array([order.index(m) for m in range(n_model)], jnp.int32)[my_model]
        self.shares, self.spot, self.first = shares, spot, first
        self.distance = {way: n_model // 2, -way: n_model // 2 - 1}
        self.moving = {}

    def share_of(self, offset):
        table = jnp.array(self.order, jnp.int32)
        owner = table[(self.spot + offset + self.n_model) % self.n_model]
        owner = (owner - self.first + self.n_model) % self.n_model
        return lax.dynamic_index_in_dim(self.shares, owner, 0, keepdims=False)

    def advance(self):
        started = []
        for way in (self.way, -self.way):
            if not self.distance[way]:
                continue
            block = self.share_of(way * self.distance[way])
            if way in self.moving:
                arrived = self.moving[way].astype(jnp.float32)
                block = (block.astype(jnp.float32) + arrived).astype(jnp.bfloat16)
            started.append(way)
            self.moving[way] = block
            self.distance[way] -= 1
        return started

    def send(self, started):
        for way in started:
            pairs = [
                (self.order[i], self.order[(i + way) % self.n_model]) for i in range(self.n_model)
            ]
            self.moving[way] = lax.ppermute(self.moving[way], "mp", pairs)

    def step(self, *held):
        started = self.advance()
        blocks, held = lax.optimization_barrier(([self.moving[way] for way in started], held))
        for way, block in zip(started, blocks):
            self.moving[way] = block
        self.send(started)
        return held

    def finish(self):
        while any(self.distance.values()):
            self.send(self.advance())
        total = self.share_of(0).astype(jnp.float32)
        for way in (1, -1):
            total = total + self.moving[way].astype(jnp.float32)
        return total.astype(jnp.bfloat16)


def pack_kernel(slots_ref, heads_ref, pool_ref, *out_refs):
    capacity = slots_ref.shape[1]
    dests = heads_ref.shape[0]

    def place(rank, _):
        for listed, out_ref in enumerate(out_refs):
            slot = slots_ref[listed, rank]
            for dest in range(dests):
                first = pl.multiple_of(heads_ref[dest] * 2 * HD, 2 * HD)
                out_ref[dest, rank] = pool_ref[slot, :, pl.ds(first, 2 * HD)]
        return 0

    lax.fori_loop(0, capacity, place, 0)


def pack_blocks(pool, slots, heads):
    shape = (heads.shape[0], slots.shape[1], pool.shape[1], 2 * HD)
    return pl.pallas_call(
        pack_kernel,
        out_shape=[jax.ShapeDtypeStruct(shape, jnp.bfloat16)] * slots.shape[0],
        in_specs=[
            pl.BlockSpec(memory_space=pltpu.SMEM),
            pl.BlockSpec(memory_space=pltpu.SMEM),
            pl.BlockSpec(memory_space=pltpu.VMEM),
        ],
        out_specs=[pl.BlockSpec(memory_space=pltpu.VMEM)] * slots.shape[0],
        compiler_params=pltpu.CompilerParams(vmem_limit_bytes=VMEM_LIMIT),
        name="pack_blocks",
    )(slots, heads, pool)


def merge_kernel(kept_ref, got_ref, *refs):
    *out_refs, sems = refs
    copies = []
    for dest, out_ref in enumerate(out_refs):
        for side, source in enumerate((kept_ref, got_ref)):
            copies.append(
                pltpu.make_async_copy(source.at[dest], out_ref.at[side], sems.at[dest, side])
            )
    for copy in copies:
        copy.start()
    for copy in copies:
        copy.wait()


def merge_blocks(kept, got):
    dests = kept.shape[0]
    shape = jax.ShapeDtypeStruct((2, *kept.shape[1:]), kept.dtype)
    return pl.pallas_call(
        merge_kernel,
        out_shape=[shape] * dests,
        in_specs=[pl.BlockSpec(memory_space=pl.ANY)] * 2,
        out_specs=[pl.BlockSpec(memory_space=pl.ANY)] * dests,
        scratch_shapes=[pltpu.SemaphoreType.DMA((dests, 2))],
        name="merge_blocks",
    )(kept, got)


def order_kernel(length_ref, where_ref, *refs):
    *arrived_refs, key_ref, value_ref, held_ref, sems = refs
    block_len = held_ref.shape[1]
    count = held_ref.shape[0] // len(arrived_refs)
    copies = [
        pltpu.make_async_copy(
            arrived, held_ref.at[index * count : (index + 1) * count], sems.at[index]
        )
        for index, arrived in enumerate(arrived_refs)
    ]
    for copy in copies:
        copy.start()
    for copy in copies:
        copy.wait()
    length = length_ref[0]
    first = held_ref[where_ref[0]][:1, :HD].astype(jnp.float32)
    row = lax.broadcasted_iota(jnp.int32, (block_len, HD), 0)

    def place(block_id, _):
        block = held_ref[where_ref[block_id]].astype(jnp.float32)
        start = pl.multiple_of(block_id * block_len, block_len)
        seen = row + start < length
        rows = pl.ds(start, block_len)
        key_ref[rows, :] = jnp.where(seen, block[:, :HD], first).astype(jnp.bfloat16)
        value_ref[rows, :HD] = jnp.where(seen, block[:, HD:], 0.0).astype(jnp.bfloat16)
        value_ref[rows, HD:] = jnp.where(seen, 1.0, 0.0).astype(jnp.bfloat16)
        return 0

    lax.fori_loop(0, where_ref.shape[0], place, 0, unroll=8)


def order_blocks(arrived, where, length):
    count, block_len, _ = arrived[0].shape
    tokens = where.shape[0] * block_len
    return pl.pallas_call(
        order_kernel,
        out_shape=(
            jax.ShapeDtypeStruct((tokens, HD), jnp.bfloat16),
            jax.ShapeDtypeStruct((tokens, 2 * HD), jnp.bfloat16),
        ),
        in_specs=[pl.BlockSpec(memory_space=pltpu.SMEM)] * 2
        + [pl.BlockSpec(memory_space=pl.ANY)] * len(arrived),
        out_specs=(
            pl.BlockSpec(memory_space=pltpu.VMEM),
            pl.BlockSpec(memory_space=pltpu.VMEM),
        ),
        scratch_shapes=[
            pltpu.VMEM((len(arrived) * count, block_len, 2 * HD), jnp.bfloat16),
            pltpu.SemaphoreType.DMA((len(arrived),)),
        ],
        compiler_params=pltpu.CompilerParams(vmem_limit_bytes=ATTEND_VMEM),
        name="order_blocks",
    )(length, where, *arrived)


def dot_keys(queries, keys):
    return lax.dot_general(
        queries, keys, (((1,), (1,)), ((), ())), preferred_element_type=jnp.float32
    )


def attend_kernel(span, row_step, chunk, half_ref, *refs):
    query_refs, (key_ref, value_ref), new_key_refs, new_value_refs, out_ref = (
        refs[:2],
        refs[2:4],
        refs[4:6],
        refs[6:8],
        refs[8],
    )
    rows = out_ref.shape[0]
    half = new_key_refs[0].shape[0]
    queries = jnp.concatenate([ref[0].reshape(rows // 2, HD) for ref in query_refs], 0)
    spans = key_ref.shape[0] // span
    stride = 2 * half * row_step // rows
    turn = half_ref[0] * half
    local = lax.broadcasted_iota(jnp.int32, (rows, half), 0)
    token = (local // row_step) * stride + chunk * row_step + local % row_step
    token = lax.rem(token + turn, 2 * half)
    column = lax.broadcasted_iota(jnp.int32, (rows, half), 1)
    parts = []
    for side, ref in enumerate(new_key_refs):
        causal = column + lax.rem(turn + side * half, 2 * half) <= token
        parts.append(jnp.where(causal, dot_keys(queries, ref[...]), -jnp.inf))
    scores = jnp.concatenate(parts, 1)
    peak = jnp.max(scores, axis=1, keepdims=True)
    total = None
    values = jnp.concatenate([ref[...] for ref in new_value_refs], 0)
    for step in range(spans + 1):
        if step < spans:
            next_scores = dot_keys(queries, key_ref[step * span : (step + 1) * span, :])
            next_peak = jnp.maximum(peak, jnp.max(next_scores, axis=1, keepdims=True))
        weights = jnp.exp2((scores - peak) * SCORE_SCALE).astype(jnp.bfloat16)
        product = jnp.dot(weights, values, preferred_element_type=jnp.float32)
        total = product if total is None else total + product
        if step < spans:
            total = total * jnp.exp2((peak - next_peak) * SCORE_SCALE)
            scores, peak = next_scores, next_peak
            values = value_ref[step * span : (step + 1) * span, :]
    out_ref[...] = (total[:, :HD] / total[:, HD:]).astype(jnp.bfloat16)


def attend(half, queries, prefix, new_keys, new_values, row_step, chunk, first_head, heads):
    owners = queries[0].shape[1]
    rows = 2 * owners * row_step
    span = math.gcd(prefix[0].shape[0], 1024)
    whole = lambda array: pl.BlockSpec(array.shape, lambda head: (0, 0))
    count = prefix[0].shape[0] + 2 * new_keys[0].shape[0]
    query_spec = pl.BlockSpec(
        (1, owners, None, row_step, HD), lambda head: (first_head + head, 0, chunk, 0, 0)
    )
    fixed = (*prefix, *new_keys, *new_values)
    return pl.pallas_call(
        functools.partial(attend_kernel, span, row_step, chunk),
        grid=(heads,),
        out_shape=jax.ShapeDtypeStruct((rows, heads * HD), jnp.bfloat16),
        in_specs=[pl.BlockSpec(memory_space=pltpu.SMEM), query_spec, query_spec]
        + [whole(array) for array in fixed],
        out_specs=pl.BlockSpec((rows, HD), lambda head: (0, head)),
        compiler_params=pltpu.CompilerParams(vmem_limit_bytes=ATTEND_VMEM),
        cost_estimate=pl.CostEstimate(
            flops=heads * rows * count * HD * 8,
            bytes_accessed=2 * (count * 3 * HD + 2 * heads * rows * HD),
            transcendentals=heads * rows * count,
        ),
        name="attend",
    )(half, *queries, *fixed)


def on_device(
    n_model,
    n_pool,
    states,
    norm_gain,
    w_query,
    q_bias,
    w_key,
    w_value,
    k_bias,
    v_bias,
    w_out,
    kv_pool,
    hit_holder,
    hit_slot,
    prefix_len,
):
    my_model = lax.axis_index("mp")
    my_pool = lax.axis_index("pool")
    row_count = states.shape[1]
    suffix = row_count * n_model
    q_width = w_query.shape[1]
    q_local = q_width // HD
    kv_local = w_key.shape[1]
    kv_heads = kv_local * n_model // HD
    group_size = QH // kv_heads
    blocks_total = hit_holder.shape[1]
    block_len = kv_pool.shape[2]
    holders = n_model * n_pool
    capacity = 2 * blocks_total // holders
    sharers = HD // kv_local

    lined = n_model == LINE_MODELS

    self_holder = my_model * n_pool + my_pool
    chosen = listing(hit_holder == self_holder, capacity)
    slot_ids = jnp.sum(jnp.where(chosen, hit_slot[:, None, :], 0), -1)
    models = jnp.arange(n_model, dtype=jnp.int32)
    my_holder = hit_holder[my_pool]
    if lined:
        slot_ids = jnp.where(my_pool == 0, slot_ids, slot_ids[::-1])
        kept, given = pack_blocks(kv_pool[0], slot_ids, (models ^ my_model) * q_local // group_size)
        got = lax.ppermute(given, "pool", [(0, 1), (1, 0)])
        outgoing = merge_blocks(kept, got)
        arrived = [
            lax.ppermute(block, "mp", [(index, index ^ apart) for index in range(n_model)])
            if apart
            else block
            for apart, block in enumerate(outgoing)
        ]
        arrived = [block.reshape(-1, block_len, 2 * HD) for block in arrived]
        from_holder = ((my_holder // n_pool) ^ my_model) * n_pool + (my_holder % n_pool ^ my_pool)
    else:
        outgoing = jnp.stack(pack_blocks(kv_pool[0], slot_ids, models * q_local // group_size), 1)
        outgoing = outgoing.reshape(holders, capacity * block_len, 2 * HD)
        arrived = lax.all_to_all(outgoing, ("mp", "pool"), split_axis=0, concat_axis=0, tiled=True)
        arrived = [arrived.reshape(holders * capacity, block_len, 2 * HD)]
        from_holder = my_holder
    block_ids = jnp.arange(blocks_total, dtype=jnp.int32)
    earlier = (my_holder[:, None] == my_holder[None, :]) & (block_ids[None, :] < block_ids[:, None])
    where = from_holder * capacity + jnp.sum(earlier.astype(jnp.int32), -1)
    prefix_count = prefix_len[my_pool]

    upper_half = (my_model // (n_model // 2)).astype(jnp.int32) if lined else jnp.int32(0)
    half_rows = suffix // 2
    order = (jnp.arange(suffix, dtype=jnp.int32) + upper_half * half_rows) % suffix
    cosine, sine = angle_tables(prefix_count + order)
    cosine, sine = jnp.concatenate([cosine, cosine], 1), jnp.concatenate([-sine, sine], 1)
    normed = normalize(states[0], norm_gain)
    halves = [slice(0, half_rows), slice(half_rows, suffix)]
    biases = [bias.reshape(1, -1) for bias in (q_bias, k_bias, v_bias)]
    weights = (w_query, w_key, w_value)
    if lined:
        my_z, my_y = my_model // 2, my_model % 2
        middle = (my_z == 1) | (my_z == 2)
        near, far = line_gather(normed, upper_half, middle)
        results = []
        for blocks, inner in ((near, my_z % 2), (far, upper_half)):
            starts = jnp.stack(
                [
                    2 * (inner ^ other) + (my_y ^ side)
                    for side in range(2)
                    for other in range(2)
                ]
            )
            table = [part[halves[len(results)]] for part in (cosine, sine)]
            results.append(
                project(starts.astype(jnp.int32) * row_count, blocks, weights, biases, table)
            )
        queries, new_keys, new_values, pairs = zip(*results)
        pairs = jnp.where(
            upper_half == 0, jnp.concatenate(pairs, 0), jnp.concatenate(pairs[::-1], 0)
        ).reshape(n_model, row_count, 2 * HD)
    else:
        tokens = lax.all_gather(normed, "mp", axis=0, tiled=True)
        linear, key_raw, value_raw = (
            jnp.dot(tokens, weight, preferred_element_type=jnp.float32) + bias.astype(jnp.float32)
            for weight, bias in zip(weights, biases)
        )
        cosine, sine = cosine[:, : HD // 2], sine[:, HD // 2 :]
        queries = rotate(linear.reshape(suffix, q_local, HD), cosine, sine)
        queries = queries.astype(jnp.bfloat16).transpose(1, 0, 2)
        key_raw, value_raw = key_raw.astype(jnp.bfloat16), value_raw.astype(jnp.bfloat16)
        together = [
            [first + other for other in range(sharers)] for first in range(0, n_model, sharers)
        ]
        key_whole, value_whole = (
            lax.all_gather(part, "mp", axis=1, tiled=True, axis_index_groups=together)
            for part in (key_raw, value_raw)
        )
        key_whole = rotate(key_whole.astype(jnp.float32)[:, None, :], cosine, sine)
        key_whole = key_whole.astype(jnp.bfloat16)[:, 0]
        value_ones = jnp.concatenate([value_whole, jnp.ones_like(value_whole)], 1)
        first_col = (my_model % sharers) * kv_local
        key_cols = lax.dynamic_slice_in_dim(key_whole, first_col, kv_local, 1)
        pairs = jnp.stack([key_cols, value_raw], 1).reshape(n_model, row_count, 2 * kv_local)
        queries = [queries[:, part] for part in halves]
        new_keys = [key_whole[part] for part in halves]
        new_values = [value_ones[part] for part in halves]

    prefix = order_blocks(arrived, where, prefix_count.reshape(1))

    row_step = min(row_count, ROW_STEP)
    chunks = row_count // row_step
    queries = [
        part.reshape(q_local, n_model // 2, chunks, row_step, HD) for part in queries
    ]
    half_index = upper_half.reshape(1)
    scatters = []
    for chunk in range(chunks):
        calls = 1 if chunk == 0 else 2
        heads = q_local // calls
        mixed = []
        for call in range(calls):
            mixed.append(
                attend(
                    half_index,
                    queries,
                    prefix,
                    new_keys,
                    new_values,
                    row_step,
                    chunk,
                    call * heads,
                    heads,
                )
            )
            for scatter in scatters:
                queries, mixed = scatter.step(queries, mixed)
        mixed = jnp.concatenate(mixed, 1)
        share = jnp.dot(mixed, w_out, preferred_element_type=jnp.float32).astype(jnp.bfloat16)
        share = share.reshape(n_model, row_step, share.shape[1])
        scatters.append(
            RingScatter(
                share, n_model, my_model, upper_half * (n_model // 2), 1 if chunk % 2 == 0 else -1
            )
        )
        queries, pairs = scatters[-1].step(queries, pairs)
    pairs = lax.all_to_all(pairs, "mp", split_axis=0, concat_axis=0, tiled=True)
    cache_rows = (
        pairs.reshape(kv_heads, sharers, row_count, 2, kv_local)
        .transpose(2, 0, 3, 1, 4)
        .reshape(1, row_count, kv_heads * 2 * HD)
    )
    return (jnp.concatenate([scatter.finish() for scatter in scatters], 0)[None], cache_rows)


def solution(mesh):
    placed = (
        P(("groups", "pool"), "mp", None),
        P(),
        P(None, "mp"),
        P("mp"),
        P(None, "mp"),
        P(None, "mp"),
        P("mp"),
        P("mp"),
        P("mp", None),
        P(("groups", "mp", "pool"), None, None, None),
        P("groups", None),
        P("groups", None),
        P("groups"),
    )
    return jax.shard_map(
        functools.partial(on_device, mesh.shape["mp"], mesh.shape["pool"]),
        mesh=mesh,
        in_specs=placed,
        out_specs=(P(("groups", "pool"), "mp", None), P(("groups", "pool"), "mp", None)),
        check_vma=False,
    )
```

time: 606 us -> 479 us (0.79)
  waiting for transfers between devices: 423 us -> 122 us
  Pallas kernels: 55.7 us -> 184 us
  starting transfers between devices: 8.12 us -> 76.1 us
  matrix products: 68.9 us -> 21.8 us
  local copies, waits for them, and re-layouts: 10 us -> 31.3 us
  other arithmetic: 13.5 us -> 27.9 us
  blocking collectives: 11.8 us -> 0 us
    all_gather x4 -> x0, waiting for transfers between devices: 221 us -> none  [on_device(): tokens = lax.all_gather(normed[:, cols], 'mp', axis=0, tiled=True)]
    reduce_scatter x4 -> x0, waiting for transfers between devices: 199 us -> none  [on_device(): lax.psum_scatter(share, 'mp', scatter_dimension=0, tiled=True)]
    pallas_call x1 -> x4, Pallas kernels: 5.24 us -> 154 us  [the longest x1 128 us: merge_blocks(): pl.pallas_call(merge_kernel, out_shape=[shape] * dests, in_specs=[pl.Bloc...]
    ppermute x0 -> x31, waiting for transfers between devices: none -> 112 us  [the longest x7 40.3 us: on_device(): lax.ppermute(block, 'mp', [(index, index ^ apart) for index in range(n_mo...]
    ppermute x0 -> x31, starting transfers between devices: none -> 71.2 us  [the longest x7 34.6 us: swap(): lax.ppermute(block, 'mp', [(index, index ^ mask) for index in range(LINE_...]
    dot_general x12 -> x0, matrix products: 30.4 us -> none  [on_device(): jnp.dot(tokens, weight[cols], preferred_element_type=jnp.float32)]
    unnamed x26 -> x97, local copies, waits for them, and re-layouts: 3.25 us -> 25.5 us
    pallas_call x4 -> x3, Pallas kernels: 43.7 us -> 26.3 us  [attend(): pl.pallas_call(functools.partial(attend_kernel, span, row_step, chunk), g...]
  transfers between devices with their start and end apart: 9 -> 32, of which waited for: 7 -> 10; matrix products, arithmetic and copies ran while one was open for 12% -> 4% of each run, Pallas kernels for 6% -> 33%
where the time goes in v4:
time: 479 us; the launch traced here: 477 us
  Pallas kernels  184 us (38%)
  waiting for transfers between devices  122 us (25%)
  starting transfers between devices  76.1 us (16%)
  local copies, waits for them, and re-layouts  31.3 us (7%)
  other arithmetic  27.9 us (6%)
  matrix products  21.8 us (5%)
  between operations  13.7 us (3%)
    pallas_call x1, Pallas kernels, merge_blocks(): pl.pallas_call(merge_kernel, out_shape=[shape] * dests, in_specs=[pl.Bloc...  128 us
    ppermute x7, waiting for transfers between devices, on_device(): lax.ppermute(block, 'mp', [(index, index ^ apart) for index in range(n_mo...  40.3 us
    ppermute x7, waiting for transfers between devices, swap(): lax.ppermute(block, 'mp', [(index, index ^ mask) for index in range(LINE_...  38.8 us
    ppermute x7, starting transfers between devices, swap(): lax.ppermute(block, 'mp', [(index, index ^ mask) for index in range(LINE_...  34.6 us
    ppermute x14, waiting for transfers between devices, send(): self.moving[way] = lax.ppermute(self.moving[way], 'mp', pairs)  32.9 us
    pallas_call x3, Pallas kernels, attend(): pl.pallas_call(functools.partial(attend_kernel, span, row_step, chunk), g...  26.3 us
    unnamed x97, local copies, waits for them, and re-layouts  25.5 us
    dot_general x2, matrix products, on_device(): jnp.dot(mixed, w_out, preferred_element_type=jnp.float32)  21.8 us
  transfers between devices with their start and end apart: 32, of which 10 were waited for; matrix products, arithmetic and copies ran while one was open for 4% of the time, Pallas kernels for 33%

profile of v4, /device:TPU:0, one launch (start us, length us, event | category | flops | bytes accessed | tf_op | source)
XLA Modules:
  0.0 477.1 jit_solution(4325129764468451107)
XLA Ops:
  4.4 5.1 %pack_blocks.1 = (bf16[8,32,16,256]{3,2,1,0:T(8,128)(2,1)}, bf16[8,32,16,256]{3,2,1,0:T(8,128)(2,1)}) custom-call(s32[2,32]{1,0:T(2,128)} %broadcast_select_fusion.2.slots_ref, s32[8]{0:T(128)} %and_select_fusion.heads_ref, bf16[64,16,2048]{2,1,0:T(8,128)(2,1)} %bitcast.124), custom_call_target="tpu_custom_call" | custom-call | tf_op jit(solution)/shard_map/pack_blocks/pallas_call | solution.py:241
  12.2 4.5 collective-permute-start
  16.7 24.0 %collective-permute-start.4 = (bf16[64,8192]{1,0:T(8,128)(2,1)}, bf16[64,8192]{1,0:T(8,128)(2,1)}, u32[]{:S(2)}, u32[]{:S(2)}) collective-permute-start(bf16[64,8192]{1,0:T(8,128)(2,1)} %collective-permute-done.3), channel_id=1, source_target_pairs={{0,4},{2,6},{4,0},{6,2},{8,12},{10,14},{12,8},{14,10},{1,5},{3,7},... | collective-permute-start | bytes 3145736 | tf_op jit(solution)/shard_map/ppermute | solution.py:54
  40.7 9.4 %collective-permute-start.5 = (bf16[64,8192]{1,0:T(8,128)(2,1)}, bf16[64,8192]{1,0:T(8,128)(2,1)}, u32[]{:S(2)}, u32[]{:S(2)}) collective-permute-start(bf16[64,8192]{1,0:T(8,128)(2,1)} %collective-permute-done.refs_1_), channel_id=1, source_target_pairs={{0,0},{2,2},{4,8},{6,10},{8,4},{10,6},{12,12},{14,14},{1,1},{3,3},... | collective-permute-start | bytes 3145736 | tf_op jit(solution)/shard_map/ppermute | solution.py:57
  56.1 128.3 %merge_blocks.1 = (bf16[2,32,16,256]{3,2,1,0:T(8,128)(2,1)}, bf16[2,32,16,256]{3,2,1,0:T(8,128)(2,1)}, bf16[2,32,16,256]{3,2,1,0:T(8,128)(2,1)}, bf16[2,32,16,25...) custom-call(bf16[8,32,16,256]{3,2,1,0:T(8,128)(2,1)} %get-tuple-elem, ...), custom_call_target="tpu_custom_call" | custom-call | tf_op jit(solution)/shard_map/merge_blocks/pallas_call | solution.py:272
  188.1 2.3 broadcast_select_fusion.1.refs_0_
  190.5 38.8 %collective-permute-done.6 = bf16[64,8192]{1,0:T(8,128)(2,1)S(1)} collective-permute-done((bf16[64,8192]{1,0:T(8,128)(2,1)}, bf16[64,8192]{1,0:T(8,128)(2,1)S(1)}, u32[]{:S(2)}, u32[]{:S(2)}) %collective-permute-start.6) | collective-permute-done | bytes 1048608 | tf_op jit(solution)/shard_map/ppermute | solution.py:54
  236.2 3.4 collective-permute-start.14
  241.7 2.4 collective-permute-start.15
  244.0 39.1 %collective-permute-done.13 = bf16[2,32,16,256]{3,2,1,0:T(8,128)(2,1)S(1)} collective-permute-done((bf16[2,32,16,256]{3,2,1,0:T(8,128)(2,1)}, bf16[2,32,16,256]{3,2,1,0:T(8,128)(2,1)S(1)}, u32[]{:S(2)}, u32[]{:S(2)}) %collective-permute-start.13) | collective-permute-done | bytes 524320 | tf_op jit(solution)/shard_map/ppermute | solution.py:455
  296.8 5.8 %copy-done = bf16[8192,1024]{1,0:T(8,128)(2,1)S(1)} copy-done((bf16[8192,1024]{1,0:T(8,128)(2,1)S(1)}, bf16[8192,1024]{1,0:T(8,128)(2,1)}, u32[]{:S(2)}) %copy-start) | copy-done | bytes 16777240
  305.7 10.3 %project.2 = (bf16[8,256,128]{2,1,0:T(8,128)(2,1)S(1)}, bf16[256,128]{1,0:T(8,128)(2,1)S(1)}, bf16[256,256]{1,0:T(8,128)(2,1)S(1)}, bf16[256,256]{1,0:T(8,128)(2,1)S(1)}) custom-call(s32[4]{0:T(128)S(1)} %copy-done.18, bf16[64,8192]{1,0:T(8,128)(2,1)S(1)} %fusion.2.refs_0_, bf16[64,8192]{1,0:T(8,128)(2,1)} %collective-permute-done.refs_1_, ...), custom_call_target="tpu_custom_call" | custom-call | flops 5368709120 | bytes 26476544 | tf_op jit(solution)/shard_map/project/pallas_call | solution.py:148
  316.2 4.0 order_blocks.1
  320.2 6.5 %copy-done.1 = bf16[8192,1024]{1,0:T(8,128)(2,1)S(1)} copy-done((bf16[8192,1024]{1,0:T(8,128)(2,1)S(1)}, bf16[8192,1024]{1,0:T(8,128)(2,1)}, u32[]{:S(2)}) %copy-start.1) | copy-done | bytes 16777240
  326.7 10.4 %project.3 = (bf16[8,256,128]{2,1,0:T(8,128)(2,1)S(1)}, bf16[256,128]{1,0:T(8,128)(2,1)S(1)}, bf16[256,256]{1,0:T(8,128)(2,1)S(1)}, bf16[256,256]{1,0:T(8,128)(2,1)S(1)}) custom-call(s32[4]{0:T(128)S(1)} %copy-done.17, bf16[64,8192]{1,0:T(8,128)(2,1)} %broadcast_select_fusion.1.refs_0_, bf16[64,8192]{1,0:T(8,128)(2,1)} %broadcast_select_fusion.refs_1_, ...), custom_call_target="tpu_custom_call" | custom-call | flops 5368709120 | bytes 26476544 | tf_op jit(solution)/shard_map/project/pallas_call | solution.py:148
  337.1 13.1 %attend.3 = bf16[256,1024]{1,0:T(8,128)(2,1)S(1)} custom-call(s32[1]{0:T(128)} %bitcast.half_ref, bf16[8,4,2,32,128]{4,3,2,1,0:T(8,128)(2,1)S(1)} %bitcast.118, bf16[8,4,2,32,128]{4,3,2,1,0:T(8,128)(2,1)S(1)} %bitcast.121, bf16[4096,128]{1,0:T(8,128)(2,1)S(1)} %get-tuple-element.51.refs_2_, bf16[4096,256]{1,0:T(8,128)(2,1)S(1)} %get-tuple-element.52.refs_3_, ...), custom_call_target="tpu_custom_call" | custom-call | flops 9663676416 | bytes 4587520 | tf_op jit(solution)/shard_map/attend/pallas_call | solution.py:393
  350.2 10.7 %convolution_convert_fusion.1 = bf16[256,8192]{1,0:T(8,128)(2,1)S(1)} fusion(bf16[256,1024]{1,0:T(8,128)(2,1)S(1)} %attend.3, bf16[1024,8192]{1,0:T(8,128)(2,1)} %param.39), kind=kOutput, calls=%fused_computation.1 | convolution fusion | flops 4297064448 | bytes 21495808 | tf_op jit(solution)/shard_map/dot_general | solution.py:560
  364.0 2.0 collective-permute-start.18
  370.4 6.6 %attend.4 = bf16[256,512]{1,0:T(8,128)(2,1)S(1)} custom-call(s32[1]{0:T(128)} %bitcast.half_ref, bf16[8,4,2,32,128]{4,3,2,1,0:T(8,128)(2,1)S(1)} %bitcast.119, bf16[8,4,2,32,128]{4,3,2,1,0:T(8,128)(2,1)S(1)} %bitcast.122, bf16[4096,128]{1,0:T(8,128)(2,1)S(1)} %get-tuple-element.51.refs_2_, bf16[4096,256]{1,0:T(8,128)(2,1)S(1)} %copy-done.20, ...), custom_call_target="tpu_custom_call" | custom-call | flops 4831838208 | bytes 4063232 | tf_op jit(solution)/shard_map/attend/pallas_call | solution.py:393
  377.7 2.8 fusion.11
  386.4 6.6 %attend.5 = bf16[256,512]{1,0:T(8,128)(2,1)S(1)} custom-call(s32[1]{0:T(128)} %bitcast.half_ref, bf16[8,4,2,32,128]{4,3,2,1,0:T(8,128)(2,1)S(1)} %bitcast.120, bf16[8,4,2,32,128]{4,3,2,1,0:T(8,128)(2,1)S(1)} %bitcast.123, bf16[4096,128]{1,0:T(8,128)(2,1)S(1)} %get-tuple-element.51.refs_2_, bf16[4096,256]{1,0:T(8,128)(2,1)S(1)} %copy-done.20, ...), custom_call_target="tpu_custom_call" | custom-call | flops 4831838208 | bytes 4063232 | tf_op jit(solution)/shard_map/attend/pallas_call | solution.py:393
  394.8 11.1 %convolution_convert_fusion = bf16[256,8192]{1,0:T(8,128)(2,1)S(1)} fusion(bf16[1024,8192]{1,0:T(8,128)(2,1)} %param.39, bf16[256,512]{1,0:T(8,128)(2,1)S(1)} %attend.5, bf16[256,512]{1,0:T(8,128)(2,1)S(1)} %copy-done.34), kind=kOutput, calls=%fused_computation | convolution fusion | flops 4298113024 | bytes 21495808 | tf_op jit(solution)/shard_map/dot_general | solution.py:560
  408.1 8.4 %collective-permute-done.24 = bf16[32,8192]{1,0:T(8,128)(2,1)S(1)} collective-permute-done((bf16[32,8192]{1,0:T(8,128)(2,1)S(1)}, bf16[32,8192]{1,0:T(8,128)(2,1)S(1)}, u32[]{:S(2)}, u32[]{:S(2)}) %collective-permute-start.24) | collective-permute-done | bytes 524320 | tf_op jit(solution)/shard_map/ppermute | solution.py:205
  419.2 10.5 %collective-permute-done.25 = bf16[32,8192]{1,0:T(8,128)(2,1)S(1)} collective-permute-done((bf16[32,8192]{1,0:T(8,128)(2,1)S(1)}, bf16[32,8192]{1,0:T(8,128)(2,1)S(1)}, u32[]{:S(2)}, u32[]{:S(2)}) %collective-permute-start.25) | collective-permute-done | bytes 524320 | tf_op jit(solution)/shard_map/ppermute | solution.py:205
  429.7 2.4 fusion.7
  432.1 4.9 %all-to-all-start = ((bf16[8,64,256]{2,1,0:T(8,128)(2,1)}), bf16[8,64,256]{2,1,0:T(8,128)(2,1)S(1)}, u32[]{:S(2)}, u32[]{:S(2)}) async-start(bf16[8,64,256]{2,1,0:T(8,128)(2,1)} %bitcast.45), calls=%async_computation | async-start | bytes 524288 | tf_op jit(solution)/shard_map/all_to_all | solution.py:568
  437.7 2.1 collective-permute-start.21
  439.9 9.9 %all-to-all-done = bf16[8,64,256]{2,1,0:T(8,128)(2,1)S(1)} async-done(((bf16[8,64,256]{2,1,0:T(8,128)(2,1)}), bf16[8,64,256]{2,1,0:T(8,128)(2,1)S(1)}, u32[]{:S(2)}, u32[]{:S(2)}) %all-to-all-start) | async-done | bytes 262176 | tf_op jit(solution)/shard_map/all_to_all | solution.py:568
  455.0 2.5 collective-permute-start.22
  459.3 5.1 %collective-permute-done.29 = bf16[32,8192]{1,0:T(8,128)(2,1)S(1)} collective-permute-done((bf16[32,8192]{1,0:T(8,128)(2,1)S(1)}, bf16[32,8192]{1,0:T(8,128)(2,1)S(1)}, u32[]{:S(2)}, u32[]{:S(2)}) %collective-permute-start.29) | collective-permute-done | bytes 524320 | tf_op jit(solution)/shard_map/ppermute | solution.py:205
  466.9 3.4 collective-permute-done.26
  470.3 4.5 collective-permute-done.30
  (184 shorter events, 62.6 us)
Async XLA Ops:
  9.5 46.6 %collective-permute-start.9 = (bf16[8,32,16,256]{3,2,1,0:T(8,128)(2,1)}, bf16[8,32,16,256]{3,2,1,0:T(8,128)(2,1)}, u32[]{:S(2)}, u32[]{:S(2)}) collective-permute-start(bf16[8,32,16,256]{3,2,1,0:T(8,128)(2,1)} %get-tuple-element.42), channel_id=1, source_target_pairs={{0,1},{1,0},{2,3},{3,2},{4,5},{5,4},{6,7},{7,6},{8,9},{9,8},{10,11... | collective-permute-start | bytes 6291464 | tf_op jit(solution)/shard_map/ppermute | solution.py:452
  10.6 6.1 %collective-permute-start.3 = (bf16[64,8192]{1,0:T(8,128)(2,1)S(1)}, bf16[64,8192]{1,0:T(8,128)(2,1)}, u32[]{:S(2)}, u32[]{:S(2)}) collective-permute-start(bf16[64,8192]{1,0:T(8,128)(2,1)S(1)} %fusion.2.refs_0_), channel_id=1, source_target_pairs={{0,0},{2,2},{4,8},{6,10},{8,4},{10,6},{12,12},{14,14},{1,1},{3,3},... | collective-permute-start | bytes 3145736 | tf_op jit(solution)/shard_map/ppermute | solution.py:57
  12.2 28.5 %collective-permute-start = (bf16[64,8192]{1,0:T(8,128)(2,1)S(1)}, bf16[64,8192]{1,0:T(8,128)(2,1)}, u32[]{:S(2)}, u32[]{:S(2)}) collective-permute-start(bf16[64,8192]{1,0:T(8,128)(2,1)S(1)} %fusion.2.refs_0_), channel_id=1, source_target_pairs={{0,4},{2,6},{4,0},{6,2},{8,12},{10,14},{12,8},{14,10},{1,5},{3,7},... | collective-permute-start | bytes 3145736 | tf_op jit(solution)/shard_map/ppermute | solution.py:54
  16.7 169.4 %collective-permute-start.4 = (bf16[64,8192]{1,0:T(8,128)(2,1)}, bf16[64,8192]{1,0:T(8,128)(2,1)}, u32[]{:S(2)}, u32[]{:S(2)}) collective-permute-start(bf16[64,8192]{1,0:T(8,128)(2,1)} %collective-permute-done.3), channel_id=1, source_target_pairs={{0,4},{2,6},{4,0},{6,2},{8,12},{10,14},{12,8},{14,10},{1,5},{3,7},... | collective-permute-start | bytes 3145736 | tf_op jit(solution)/shard_map/ppermute | solution.py:54
  40.7 145.4 %collective-permute-start.5 = (bf16[64,8192]{1,0:T(8,128)(2,1)}, bf16[64,8192]{1,0:T(8,128)(2,1)}, u32[]{:S(2)}, u32[]{:S(2)}) collective-permute-start(bf16[64,8192]{1,0:T(8,128)(2,1)} %collective-permute-done.refs_1_), channel_id=1, source_target_pairs={{0,0},{2,2},{4,8},{6,10},{8,4},{10,6},{12,12},{14,14},{1,1},{3,3},... | collective-permute-start | bytes 3145736 | tf_op jit(solution)/shard_map/ppermute | solution.py:57
  50.2 140.3 %collective-permute-start.1 = (bf16[64,8192]{1,0:T(8,128)(2,1)S(1)}, bf16[64,8192]{1,0:T(8,128)(2,1)}, u32[]{:S(2)}, u32[]{:S(2)}) collective-permute-start(bf16[64,8192]{1,0:T(8,128)(2,1)S(1)} %fusion.2.refs_0_), channel_id=1, source_target_pairs={{0,2},{2,0},{4,6},{6,4},{8,10},{10,8},{12,14},{14,12},{1,3},{3,1},... | collective-permute-start | bytes 3145736 | tf_op jit(solution)/shard_map/ppermute | solution.py:54
  55.6 175.5 %collective-permute-start.2 = (bf16[64,8192]{1,0:T(8,128)(2,1)}, bf16[64,8192]{1,0:T(8,128)(2,1)}, u32[]{:S(2)}, u32[]{:S(2)}) collective-permute-start(bf16[64,8192]{1,0:T(8,128)(2,1)} %collective-permute-done.refs_1_), channel_id=1, source_target_pairs={{0,2},{2,0},{4,6},{6,4},{8,10},{10,8},{12,14},{14,12},{1,3},{3,1},... | collective-permute-start | bytes 3145736 | tf_op jit(solution)/shard_map/ppermute | solution.py:54
  184.5 47.1 %collective-permute-start.10 = (bf16[2,32,16,256]{3,2,1,0:T(8,128)(2,1)}, bf16[2,32,16,256]{3,2,1,0:T(8,128)(2,1)S(1)}, u32[]{:S(2)}, u32[]{:S(2)}) collective-permute-start(bf16[2,32,16,256]{3,2,1,0:T(8,128)(2,1)} %get-tuple-element.44), channel_id=1, source_target_pairs={{0,2},{2,0},{4,6},{6,4},{8,10},{10,8},{12,14},{14,12},{1,3},{3,1},... | collective-permute-start | bytes 1572872 | tf_op jit(solution)/shard_map/ppermute | solution.py:455
  186.1 49.3 %collective-permute-start.11 = (bf16[2,32,16,256]{3,2,1,0:T(8,128)(2,1)}, bf16[2,32,16,256]{3,2,1,0:T(8,128)(2,1)S(1)}, u32[]{:S(2)}, u32[]{:S(2)}) collective-permute-start(bf16[2,32,16,256]{3,2,1,0:T(8,128)(2,1)} %get-tuple-element.45), channel_id=1, source_target_pairs={{0,4},{2,6},{4,0},{6,2},{8,12},{10,14},{12,8},{14,10},{1,5},{3,7},... | collective-permute-start | bytes 1572872 | tf_op jit(solution)/shard_map/ppermute | solution.py:455
  186.1 43.1 %collective-permute-start.6 = (bf16[64,8192]{1,0:T(8,128)(2,1)}, bf16[64,8192]{1,0:T(8,128)(2,1)S(1)}, u32[]{:S(2)}, u32[]{:S(2)}) collective-permute-start(bf16[64,8192]{1,0:T(8,128)(2,1)} %collective-permute-done.5), channel_id=1, source_target_pairs={{0,4},{2,6},{4,0},{6,2},{8,12},{10,14},{12,8},{14,10},{1,5},{3,7},... | collective-permute-start | bytes 3145736 | tf_op jit(solution)/shard_map/ppermute | solution.py:54
  190.5 50.4 %collective-permute-start.12 = (bf16[2,32,16,256]{3,2,1,0:T(8,128)(2,1)}, bf16[2,32,16,256]{3,2,1,0:T(8,128)(2,1)S(1)}, u32[]{:S(2)}, u32[]{:S(2)}) collective-permute-start(bf16[2,32,16,256]{3,2,1,0:T(8,128)(2,1)} %get-tuple-element.46), channel_id=1, source_target_pairs={{0,6},{2,4},{4,2},{6,0},{8,14},{10,12},{12,10},{14,8},{1,7},{3,5},... | collective-permute-start | bytes 1572872 | tf_op jit(solution)/shard_map/ppermute | solution.py:455
  229.3 53.9 %collective-permute-start.13 = (bf16[2,32,16,256]{3,2,1,0:T(8,128)(2,1)}, bf16[2,32,16,256]{3,2,1,0:T(8,128)(2,1)S(1)}, u32[]{:S(2)}, u32[]{:S(2)}) collective-permute-start(bf16[2,32,16,256]{3,2,1,0:T(8,128)(2,1)} %get-tuple-element.47), channel_id=1, source_target_pairs={{0,8},{2,10},{4,12},{6,14},{8,0},{10,2},{12,4},{14,6},{1,9},{3,11}... | collective-permute-start | bytes 1572872 | tf_op jit(solution)/shard_map/ppermute | solution.py:455
  231.1 89.1 %collective-permute-start.7 = (bf16[64,8192]{1,0:T(8,128)(2,1)}, bf16[64,8192]{1,0:T(8,128)(2,1)}, u32[]{:S(2)}, u32[]{:S(2)}) collective-permute-start(bf16[64,8192]{1,0:T(8,128)(2,1)} %broadcast_select_fusion.1.refs_0_), channel_id=1, source_target_pairs={{0,2},{2,0},{4,6},{6,4},{8,10},{10,8},{12,14},{14,12},{1,3},{3,1},... | collective-permute-start | bytes 3145736 | tf_op jit(solution)/shard_map/ppermute | solution.py:54
  232.4 87.8 %collective-permute-start.8 = (bf16[64,8192]{1,0:T(8,128)(2,1)}, bf16[64,8192]{1,0:T(8,128)(2,1)}, u32[]{:S(2)}, u32[]{:S(2)}) collective-permute-start(bf16[64,8192]{1,0:T(8,128)(2,1)} %broadcast_select_fusion.refs_1_), channel_id=1, source_target_pairs={{0,2},{2,0},{4,6},{6,4},{8,10},{10,8},{12,14},{14,12},{1,3},{3,1},... | collective-permute-start | bytes 3145736 | tf_op jit(solution)/shard_map/ppermute | solution.py:54
  236.2 79.8 %collective-permute-start.14 = (bf16[2,32,16,256]{3,2,1,0:T(8,128)(2,1)}, bf16[2,32,16,256]{3,2,1,0:T(8,128)(2,1)}, u32[]{:S(2)}, u32[]{:S(2)}) collective-permute-start(bf16[2,32,16,256]{3,2,1,0:T(8,128)(2,1)} %get-tuple-element.48), channel_id=1, source_target_pairs={{0,10},{2,8},{4,14},{6,12},{8,2},{10,0},{12,6},{14,4},{1,11},{3,9}... | collective-permute-start | bytes 1572872 | tf_op jit(solution)/shard_map/ppermute | solution.py:455
  241.7 74.4 %collective-permute-start.15 = (bf16[2,32,16,256]{3,2,1,0:T(8,128)(2,1)}, bf16[2,32,16,256]{3,2,1,0:T(8,128)(2,1)}, u32[]{:S(2)}, u32[]{:S(2)}) collective-permute-start(bf16[2,32,16,256]{3,2,1,0:T(8,128)(2,1)} %get-tuple-element.49), channel_id=1, source_target_pairs={{0,12},{2,14},{4,8},{6,10},{8,4},{10,6},{12,0},{14,2},{1,13},{3,15... | collective-permute-start | bytes 1572872 | tf_op jit(solution)/shard_map/ppermute | solution.py:455
  284.0 32.1 %collective-permute-start.16 = (bf16[2,32,16,256]{3,2,1,0:T(8,128)(2,1)}, bf16[2,32,16,256]{3,2,1,0:T(8,128)(2,1)}, u32[]{:S(2)}, u32[]{:S(2)}) collective-permute-start(bf16[2,32,16,256]{3,2,1,0:T(8,128)(2,1)} %get-tuple-element.50), channel_id=1, source_target_pairs={{0,14},{2,12},{4,10},{6,8},{8,6},{10,4},{12,2},{14,0},{1,15},{3,13... | collective-permute-start | bytes 1572872 | tf_op jit(solution)/shard_map/ppermute | solution.py:455
  364.0 13.6 %collective-permute-start.17 = (bf16[32,8192]{1,0:T(8,128)(2,1)}, bf16[32,8192]{1,0:T(8,128)(2,1)}, u32[]{:S(2)}, u32[]{:S(2)}) collective-permute-start(bf16[32,8192]{1,0:T(8,128)(2,1)} %get-tuple-element.59), channel_id=1, source_target_pairs={{0,4},{4,8},{8,12},{12,14},{14,10},{10,6},{6,2},{2,0},{1,5},{5,9},... | collective-permute-start | bytes 1572872 | tf_op jit(solution)/shard_map/ppermute | solution.py:205
  364.0 13.6 %collective-permute-start.18 = (bf16[32,8192]{1,0:T(8,128)(2,1)}, bf16[32,8192]{1,0:T(8,128)(2,1)}, u32[]{:S(2)}, u32[]{:S(2)}) collective-permute-start(bf16[32,8192]{1,0:T(8,128)(2,1)} %get-tuple-element.60), channel_id=1, source_target_pairs={{0,2},{4,0},{8,4},{12,8},{14,12},{10,14},{6,10},{2,6},{1,3},{5,1},... | collective-permute-start | bytes 1572872 | tf_op jit(solution)/shard_map/ppermute | solution.py:205
  380.4 12.6 %collective-permute-start.19 = (bf16[32,8192]{1,0:T(8,128)(2,1)}, bf16[32,8192]{1,0:T(8,128)(2,1)}, u32[]{:S(2)}, u32[]{:S(2)}) collective-permute-start(bf16[32,8192]{1,0:T(8,128)(2,1)} %get-tuple-element.63), channel_id=1, source_target_pairs={{0,4},{4,8},{8,12},{12,14},{14,10},{10,6},{6,2},{2,0},{1,5},{5,9},... | collective-permute-start | bytes 1572872 | tf_op jit(solution)/shard_map/ppermute | solution.py:205
  380.4 12.6 %collective-permute-start.20 = (bf16[32,8192]{1,0:T(8,128)(2,1)}, bf16[32,8192]{1,0:T(8,128)(2,1)}, u32[]{:S(2)}, u32[]{:S(2)}) collective-permute-start(bf16[32,8192]{1,0:T(8,128)(2,1)} %get-tuple-element.64), channel_id=1, source_target_pairs={{0,2},{4,0},{8,4},{12,8},{14,12},{10,14},{6,10},{2,6},{1,3},{5,1},... | collective-permute-start | bytes 1572872 | tf_op jit(solution)/shard_map/ppermute | solution.py:205
  406.0 10.5 %collective-permute-start.24 = (bf16[32,8192]{1,0:T(8,128)(2,1)S(1)}, bf16[32,8192]{1,0:T(8,128)(2,1)S(1)}, u32[]{:S(2)}, u32[]{:S(2)}) collective-permute-start(bf16[32,8192]{1,0:T(8,128)(2,1)S(1)} %get-tuple-element.73), channel_id=1, source_target_pairs={{0,4},{4,8},{8,12},{12,14},{14,10},{10,6},{6,2},{2,0},{1,5},{5,9},... | collective-permute-start | bytes 1572872 | tf_op jit(solution)/shard_map/ppermute | solution.py:205
  406.1 13.1 %collective-permute-start.27 = (bf16[32,8192]{1,0:T(8,128)(2,1)S(1)}, bf16[32,8192]{1,0:T(8,128)(2,1)S(1)}, u32[]{:S(2)}, u32[]{:S(2)}) collective-permute-start(bf16[32,8192]{1,0:T(8,128)(2,1)S(1)} %get-tuple-element.74), channel_id=1, source_target_pairs={{0,2},{4,0},{8,4},{12,8},{14,12},{10,14},{6,10},{2,6},{1,3},{5,1},... | collective-permute-start | bytes 1572872 | tf_op jit(solution)/shard_map/ppermute | solution.py:205
  416.7 13.0 %collective-permute-start.25 = (bf16[32,8192]{1,0:T(8,128)(2,1)S(1)}, bf16[32,8192]{1,0:T(8,128)(2,1)S(1)}, u32[]{:S(2)}, u32[]{:S(2)}) collective-permute-start(bf16[32,8192]{1,0:T(8,128)(2,1)S(1)} %fusion.6), channel_id=1, source_target_pairs={{0,4},{4,8},{8,12},{12,14},{14,10},{10,6},{6,2},{2,0},{1,5},{5,9},... | collective-permute-start | bytes 1572872 | tf_op jit(solution)/shard_map/ppermute | solution.py:205
  432.1 18.8 %collective-permute-start.28 = (bf16[32,8192]{1,0:T(8,128)(2,1)}, bf16[32,8192]{1,0:T(8,128)(2,1)S(1)}, u32[]{:S(2)}, u32[]{:S(2)}) collective-permute-start(bf16[32,8192]{1,0:T(8,128)(2,1)} %get-tuple-element.79), channel_id=1, source_target_pairs={{0,2},{4,0},{8,4},{12,8},{14,12},{10,14},{6,10},{2,6},{1,3},{5,1},... | collective-permute-start | bytes 1572872 | tf_op jit(solution)/shard_map/ppermute | solution.py:205
  432.1 17.7 %all-to-all-start = ((bf16[8,64,256]{2,1,0:T(8,128)(2,1)}), bf16[8,64,256]{2,1,0:T(8,128)(2,1)S(1)}, u32[]{:S(2)}, u32[]{:S(2)}) async-start(bf16[8,64,256]{2,1,0:T(8,128)(2,1)} %bitcast.45), calls=%async_computation | async-start | bytes 524288 | tf_op jit(solution)/shard_map/all_to_all | solution.py:568
  437.7 16.1 %collective-permute-start.21 = (bf16[32,8192]{1,0:T(8,128)(2,1)S(1)}, bf16[32,8192]{1,0:T(8,128)(2,1)S(1)}, u32[]{:S(2)}, u32[]{:S(2)}) collective-permute-start(bf16[32,8192]{1,0:T(8,128)(2,1)S(1)} %get-tuple-element.68), channel_id=1, source_target_pairs={{0,4},{4,8},{8,12},{12,14},{14,10},{10,6},{6,2},{2,0},{1,5},{5,9},... | collective-permute-start | bytes 1572872 | tf_op jit(solution)/shard_map/ppermute | solution.py:205
  439.8 25.9 %collective-permute-start.23 = (bf16[32,8192]{1,0:T(8,128)(2,1)S(1)}, bf16[32,8192]{1,0:T(8,128)(2,1)S(1)}, u32[]{:S(2)}, u32[]{:S(2)}) collective-permute-start(bf16[32,8192]{1,0:T(8,128)(2,1)S(1)} %get-tuple-element.69), channel_id=1, source_target_pairs={{0,2},{4,0},{8,4},{12,8},{14,12},{10,14},{6,10},{2,6},{1,3},{5,1},... | collective-permute-start | bytes 1572872 | tf_op jit(solution)/shard_map/ppermute | solution.py:205
  452.1 12.3 %collective-permute-start.29 = (bf16[32,8192]{1,0:T(8,128)(2,1)S(1)}, bf16[32,8192]{1,0:T(8,128)(2,1)S(1)}, u32[]{:S(2)}, u32[]{:S(2)}) collective-permute-start(bf16[32,8192]{1,0:T(8,128)(2,1)S(1)} %fusion.4), channel_id=1, source_target_pairs={{0,2},{4,0},{8,4},{12,8},{14,12},{10,14},{6,10},{2,6},{1,3},{5,1},... | collective-permute-start | bytes 1572872 | tf_op jit(solution)/shard_map/ppermute | solution.py:205
  455.0 10.7 %collective-permute-start.22 = (bf16[32,8192]{1,0:T(8,128)(2,1)S(1)}, bf16[32,8192]{1,0:T(8,128)(2,1)S(1)}, u32[]{:S(2)}, u32[]{:S(2)}) collective-permute-start(bf16[32,8192]{1,0:T(8,128)(2,1)S(1)} %fusion.14), channel_id=1, source_target_pairs={{0,4},{4,8},{8,12},{12,14},{14,10},{10,6},{6,2},{2,0},{1,5},{5,9},... | collective-permute-start | bytes 1572872 | tf_op jit(solution)/shard_map/ppermute | solution.py:205
  457.5 12.8 %collective-permute-start.26 = (bf16[32,8192]{1,0:T(8,128)(2,1)}, bf16[32,8192]{1,0:T(8,128)(2,1)S(1)}, u32[]{:S(2)}, u32[]{:S(2)}) collective-permute-start(bf16[32,8192]{1,0:T(8,128)(2,1)} %get-tuple-element.78), channel_id=1, source_target_pairs={{0,4},{4,8},{8,12},{12,14},{14,10},{10,6},{6,2},{2,0},{1,5},{5,9},... | collective-permute-start | bytes 1572872 | tf_op jit(solution)/shard_map/ppermute | solution.py:205
  465.6 9.2 %collective-permute-start.30 = (bf16[32,8192]{1,0:T(8,128)(2,1)S(1)}, bf16[32,8192]{1,0:T(8,128)(2,1)S(1)}, u32[]{:S(2)}, u32[]{:S(2)}) collective-permute-start(bf16[32,8192]{1,0:T(8,128)(2,1)S(1)} %fusion.5), channel_id=1, source_target_pairs={{0,2},{4,0},{8,4},{12,8},{14,12},{10,14},{6,10},{2,6},{1,3},{5,1},... | collective-permute-start | bytes 1572872 | tf_op jit(solution)/shard_map/ppermute | solution.py:205
  (48 other events, 1084.8 us)

commit v5 on v4

--- a/solution.py
+++ b/solution.py
@@ -17,6 +17,7 @@
 ATTEND_VMEM = 28 * 1024 * 1024
 ROW_STEP = 32
 LINE_MODELS = 8
+IN_FLIGHT = 4
 
 
 def angle_tables(positions):
@@ -49,28 +50,55 @@
     return owned_mask[..., None, :] & (rank_order[..., None, :] == slot_index[:, None])
 
 
-def line_gather(own, upper_half, middle):
-    def swap(block, mask):
-        return lax.ppermute(block, "mp", [(index, index ^ mask) for index in range(LINE_MODELS)])
-
-    def cross(block):
-        return lax.ppermute(
-            block,
-            "mp",
-            [(index, index ^ 6 if 2 <= index < 6 else index) for index in range(LINE_MODELS)],
-        )
-
-    beside = swap(own, 2)
-    over = cross(own)
-    own_y = swap(own, 1)
-    over_beside = cross(beside)
-    over_passed = swap(over, 2)
-    beside_y = swap(beside, 1)
+def swap(block, mask):
+    return lax.ppermute(block, "mp", [(index, index ^ mask) for index in range(LINE_MODELS)])
+
+
+def cross(block):
+    pairs = []
+    for index in range(LINE_MODELS):
+        for core in range(2):
+            if 2 <= index < 6:
+                pairs.append((index * 2 + core, (index ^ 6) * 2 + core))
+            else:
+                pairs.append((index * 2 + core, index * 2 + 1 - core))
+    return lax.ppermute(block, ("mp", "pool"), pairs)
+
+
+def gather_and_exchange(own, outgoing, middle):
+    done = []
+    arrived = {0: outgoing[0]}
+
+    def go(block, move):
+        if len(done) >= IN_FLIGHT:
+            block, done[-IN_FLIGHT] = lax.optimization_barrier((block, done[-IN_FLIGHT]))
+        done.append(move(block))
+        return done[-1]
+
+    def exchange(apart):
+        arrived[apart] = go(outgoing[apart], lambda block: swap(block, apart))
+
+    along = lambda block: swap(block, 2)
+    across = lambda block: swap(block, 1)
+    beside = go(own, along)
+    over = go(own, cross)
+    own_y = go(own, across)
+    over_beside = go(beside, cross)
+    over_passed = go(over, along)
+    beside_y = go(beside, across)
+    exchange(4)
+    over_beside_passed = go(over_beside, along)
     far_first = jnp.where(middle, over, over_passed)
-    far_first_y = swap(far_first, 1)
-    far_second = jnp.where(middle, over_beside, swap(over_beside, 2))
-    far_second_y = swap(far_second, 1)
-    return [own, beside, own_y, beside_y], [far_first, far_second, far_first_y, far_second_y]
+    far_first_y = go(far_first, across)
+    exchange(6)
+    far_second = jnp.where(middle, over_beside, over_beside_passed)
+    far_second_y = go(far_second, across)
+    for apart in (5, 2, 7, 3, 1):
+        exchange(apart)
+    near = [own, beside, own_y, beside_y]
+    far = [far_first, far_second, far_first_y, far_second_y]
+    near[0], far[0] = lax.optimization_barrier((own, far_first, far_second_y))[:2]
+    return near, far, [arrived[apart] for apart in range(LINE_MODELS)]
 
 
 def project_kernel(starts_ref, *refs):
@@ -221,74 +249,66 @@
         return total.astype(jnp.bfloat16)
 
 
-def pack_kernel(slots_ref, heads_ref, pool_ref, *out_refs):
-    capacity = slots_ref.shape[1]
-    dests = heads_ref.shape[0]
-
+def pick_kernel(slots_ref, pool_ref, out_ref):
     def place(rank, _):
-        for listed, out_ref in enumerate(out_refs):
-            slot = slots_ref[listed, rank]
-            for dest in range(dests):
-                first = pl.multiple_of(heads_ref[dest] * 2 * HD, 2 * HD)
-                out_ref[dest, rank] = pool_ref[slot, :, pl.ds(first, 2 * HD)]
+        out_ref[rank] = pool_ref[slots_ref[rank]]
         return 0
 
-    lax.fori_loop(0, capacity, place, 0)
-
-
-def pack_blocks(pool, slots, heads):
-    shape = (heads.shape[0], slots.shape[1], pool.shape[1], 2 * HD)
+    lax.fori_loop(0, slots_ref.shape[0], place, 0)
+
+
+def pick_blocks(pool, slots):
     return pl.pallas_call(
-        pack_kernel,
-        out_shape=[jax.ShapeDtypeStruct(shape, jnp.bfloat16)] * slots.shape[0],
+        pick_kernel,
+        out_shape=jax.ShapeDtypeStruct((*slots.shape, *pool.shape[1:]), pool.dtype),
         in_specs=[
-            pl.BlockSpec(memory_space=pltpu.SMEM),
             pl.BlockSpec(memory_space=pltpu.SMEM),
             pl.BlockSpec(memory_space=pltpu.VMEM),
         ],
-        out_specs=[pl.BlockSpec(memory_space=pltpu.VMEM)] * slots.shape[0],
-        compiler_params=pltpu.CompilerParams(vmem_limit_bytes=VMEM_LIMIT),
+        out_specs=pl.BlockSpec(memory_space=pltpu.VMEM),
+        compiler_params=pltpu.CompilerParams(vmem_limit_bytes=ATTEND_VMEM),
+        name="pick_blocks",
+    )(slots, pool)
+
+
+def pack_kernel(lists, slots_ref, heads_ref, *refs):
+    sources, out_refs = refs[: len(lists)], refs[len(lists) :]
+
+    def place(rank, _):
+        for listed, source_ref in zip(lists, sources):
+            slot = slots_ref[listed, rank]
+            for dest, out_ref in enumerate(out_refs):
+                first = pl.multiple_of(heads_ref[dest] * 2 * HD, 2 * HD)
+                out_ref[listed, rank] = source_ref[slot, :, pl.ds(first, 2 * HD)]
+        return 0
+
+    lax.fori_loop(0, slots_ref.shape[1], place, 0)
+
+
+def pack_blocks(sources, slots, heads):
+    dests = heads.shape[0]
+    block_len = sources[0].shape[1]
+    shape = jax.ShapeDtypeStruct((*slots.shape, block_len, 2 * HD), jnp.bfloat16)
+    return pl.pallas_call(
+        functools.partial(pack_kernel, range(len(sources))),
+        out_shape=[shape] * dests,
+        in_specs=[pl.BlockSpec(memory_space=pltpu.SMEM)] * 2
+        + [pl.BlockSpec(memory_space=pltpu.VMEM)] * len(sources),
+        out_specs=[pl.BlockSpec(memory_space=pltpu.VMEM)] * dests,
+        compiler_params=pltpu.CompilerParams(vmem_limit_bytes=ATTEND_VMEM),
         name="pack_blocks",
-    )(slots, heads, pool)
-
-
-def merge_kernel(kept_ref, got_ref, *refs):
-    *out_refs, sems = refs
-    copies = []
-    for dest, out_ref in enumerate(out_refs):
-        for side, source in enumerate((kept_ref, got_ref)):
-            copies.append(
-                pltpu.make_async_copy(source.at[dest], out_ref.at[side], sems.at[dest, side])
-            )
-    for copy in copies:
-        copy.start()
-    for copy in copies:
-        copy.wait()
-
-
-def merge_blocks(kept, got):
-    dests = kept.shape[0]
-    shape = jax.ShapeDtypeStruct((2, *kept.shape[1:]), kept.dtype)
-    return pl.pallas_call(
-        merge_kernel,
-        out_shape=[shape] * dests,
-        in_specs=[pl.BlockSpec(memory_space=pl.ANY)] * 2,
-        out_specs=[pl.BlockSpec(memory_space=pl.ANY)] * dests,
-        scratch_shapes=[pltpu.SemaphoreType.DMA((dests, 2))],
-        name="merge_blocks",
-    )(kept, got)
+    )(slots, heads, *sources)
 
 
 def order_kernel(length_ref, where_ref, *refs):
     *arrived_refs, key_ref, value_ref, held_ref, sems = refs
     block_len = held_ref.shape[1]
-    count = held_ref.shape[0] // len(arrived_refs)
-    copies = [
-        pltpu.make_async_copy(
-            arrived, held_ref.at[index * count : (index + 1) * count], sems.at[index]
-        )
-        for index, arrived in enumerate(arrived_refs)
-    ]
+    copies = []
+    begin = 0
+    for index, source in enumerate(arrived_refs):
+        end = begin + source.shape[0]
+        copies.append(pltpu.make_async_copy(source, held_ref.at[begin:end], sems.at[index]))
+        begin = end
     for copy in copies:
         copy.start()
     for copy in copies:
@@ -311,7 +331,8 @@
 
 
 def order_blocks(arrived, where, length):
-    count, block_len, _ = arrived[0].shape
+    count = sum(array.shape[-3] for array in arrived)
+    block_len = arrived[0].shape[-2]
     tokens = where.shape[0] * block_len
     return pl.pallas_call(
         order_kernel,
@@ -326,7 +347,7 @@
             pl.BlockSpec(memory_space=pltpu.VMEM),
         ),
         scratch_shapes=[
-            pltpu.VMEM((len(arrived) * count, block_len, 2 * HD), jnp.bfloat16),
+            pltpu.VMEM((count, block_len, 2 * HD), jnp.bfloat16),
             pltpu.SemaphoreType.DMA((len(arrived),)),
         ],
         compiler_params=pltpu.CompilerParams(vmem_limit_bytes=ATTEND_VMEM),
@@ -405,6 +426,35 @@
         ),
         name="attend",
     )(half, *queries, *fixed)
+
+
+def output_kernel(mixed_ref, weight_ref, out_ref):
+    out_ref[...] = jnp.dot(
+        mixed_ref[...], weight_ref[...], preferred_element_type=jnp.float32
+    ).astype(jnp.bfloat16)
+
+
+def output_product(mixed, weight):
+    rows, depth = mixed.shape
+    width = weight.shape[1]
+    tile = math.gcd(width, 1024)
+    return pl.pallas_call(
+        output_kernel,
+        grid=(width // tile,),
+        out_shape=jax.ShapeDtypeStruct((rows, width), jnp.bfloat16),
+        in_specs=[
+            pl.BlockSpec((rows, depth), lambda col: (0, 0)),
+            pl.BlockSpec((depth, tile), lambda col: (0, col)),
+        ],
+        out_specs=pl.BlockSpec((rows, tile), lambda col: (0, col)),
+        compiler_params=pltpu.CompilerParams(vmem_limit_bytes=ATTEND_VMEM),
+        cost_estimate=pl.CostEstimate(
+            flops=2 * rows * depth * width,
+            bytes_accessed=2 * (rows * depth + depth * width + rows * width),
+            transcendentals=0,
+        ),
+        name="output_product",
+    )(mixed, weight)
 
 
 def on_device(
@@ -446,43 +496,41 @@
     slot_ids = jnp.sum(jnp.where(chosen, hit_slot[:, None, :], 0), -1)
     models = jnp.arange(n_model, dtype=jnp.int32)
     my_holder = hit_holder[my_pool]
+    prefix_count = prefix_len[my_pool]
+    block_ids = jnp.arange(blocks_total, dtype=jnp.int32)
+    earlier = (my_holder[:, None] == my_holder[None, :]) & (block_ids[None, :] < block_ids[:, None])
+    rank = jnp.sum(earlier.astype(jnp.int32), -1)
+    normed = normalize(states[0], norm_gain)
     if lined:
-        slot_ids = jnp.where(my_pool == 0, slot_ids, slot_ids[::-1])
-        kept, given = pack_blocks(kv_pool[0], slot_ids, (models ^ my_model) * q_local // group_size)
-        got = lax.ppermute(given, "pool", [(0, 1), (1, 0)])
-        outgoing = merge_blocks(kept, got)
-        arrived = [
-            lax.ppermute(block, "mp", [(index, index ^ apart) for index in range(n_model)])
-            if apart
-            else block
-            for apart, block in enumerate(outgoing)
-        ]
+        mine, others = (
+            lax.dynamic_index_in_dim(slot_ids, pool, 0, keepdims=False)
+            for pool in (my_pool, 1 - my_pool)
+        )
+        pool_blocks = kv_pool[0]
+        got = lax.ppermute(pick_blocks(pool_blocks, others), "pool", [(0, 1), (1, 0)])
+        slots = jnp.stack([mine, jnp.arange(capacity, dtype=jnp.int32)])
+        outgoing = pack_blocks((pool_blocks, got), slots, (models ^ my_model) * q_local // group_size)
+        my_z, my_y = my_model // 2, my_model % 2
+        near, far, arrived = gather_and_exchange(normed, outgoing, (my_z == 1) | (my_z == 2))
         arrived = [block.reshape(-1, block_len, 2 * HD) for block in arrived]
-        from_holder = ((my_holder // n_pool) ^ my_model) * n_pool + (my_holder % n_pool ^ my_pool)
+        distance = (my_holder // n_pool) ^ my_model
+        where = (distance * n_pool + (my_holder % n_pool ^ my_pool)) * capacity + rank
     else:
-        outgoing = jnp.stack(pack_blocks(kv_pool[0], slot_ids, models * q_local // group_size), 1)
-        outgoing = outgoing.reshape(holders, capacity * block_len, 2 * HD)
+        outgoing = pack_blocks((kv_pool[0],) * 2, slot_ids, models * q_local // group_size)
+        outgoing = jnp.stack(outgoing).reshape(holders, capacity * block_len, 2 * HD)
         arrived = lax.all_to_all(outgoing, ("mp", "pool"), split_axis=0, concat_axis=0, tiled=True)
         arrived = [arrived.reshape(holders * capacity, block_len, 2 * HD)]
-        from_holder = my_holder
-    block_ids = jnp.arange(blocks_total, dtype=jnp.int32)
-    earlier = (my_holder[:, None] == my_holder[None, :]) & (block_ids[None, :] < block_ids[:, None])
-    where = from_holder * capacity + jnp.sum(earlier.astype(jnp.int32), -1)
-    prefix_count = prefix_len[my_pool]
+        where = my_holder * capacity + rank
 
     upper_half = (my_model // (n_model // 2)).astype(jnp.int32) if lined else jnp.int32(0)
     half_rows = suffix // 2
     order = (jnp.arange(suffix, dtype=jnp.int32) + upper_half * half_rows) % suffix
     cosine, sine = angle_tables(prefix_count + order)
     cosine, sine = jnp.concatenate([cosine, cosine], 1), jnp.concatenate([-sine, sine], 1)
-    normed = normalize(states[0], norm_gain)
     halves = [slice(0, half_rows), slice(half_rows, suffix)]
     biases = [bias.reshape(1, -1) for bias in (q_bias, k_bias, v_bias)]
     weights = (w_query, w_key, w_value)
     if lined:
-        my_z, my_y = my_model // 2, my_model % 2
-        middle = (my_z == 1) | (my_z == 2)
-        near, far = line_gather(normed, upper_half, middle)
         results = []
         for blocks, inner in ((near, my_z % 2), (far, upper_half)):
             starts = jnp.stack(
@@ -557,15 +605,17 @@
             for scatter in scatters:
                 queries, mixed = scatter.step(queries, mixed)
         mixed = jnp.concatenate(mixed, 1)
-        share = jnp.dot(mixed, w_out, preferred_element_type=jnp.float32).astype(jnp.bfloat16)
+        if chunk == 0:
+            pairs = lax.all_to_all(pairs, "mp", split_axis=0, concat_axis=0, tiled=True)
+            mixed, pairs = lax.optimization_barrier((mixed, pairs))
+        share = output_product(mixed, w_out)
         share = share.reshape(n_model, row_step, share.shape[1])
         scatters.append(
             RingScatter(
                 share, n_model, my_model, upper_half * (n_model // 2), 1 if chunk % 2 == 0 else -1
             )
         )
-        queries, pairs = scatters[-1].step(queries, pairs)
-    pairs = lax.all_to_all(pairs, "mp", split_axis=0, concat_axis=0, tiled=True)
+        queries = scatters[-1].step(queries)[0]
     cache_rows = (
         pairs.reshape(kv_heads, sharers, row_count, 2, kv_local)
         .transpose(2, 0, 3, 1, 4)

time: 479 us -> 361 us (0.75)
  Pallas kernels: 184 us -> 68.6 us
  waiting for transfers between devices: 122 us -> 97.8 us
  starting transfers between devices: 76.1 us -> 100 us
  matrix products: 21.8 us -> 0 us
  local copies, waits for them, and re-layouts: 31.3 us -> 50 us
    pallas_call x2 -> x4, Pallas kernels: 133 us -> 18.5 us  [the longest x2 14.1 us: output_product(): pl.pallas_call(output_kernel, grid=(width // tile,), out_shape=jax.ShapeD...]
    ppermute x7 -> x14, starting transfers between devices: 34.6 us -> 77 us  [swap(): lax.ppermute(block, 'mp', [(index, index ^ mask) for index in range(LINE_...]
    ppermute x10 -> x3, waiting for transfers between devices: 40.3 us -> 0.01 us  [the longest x2 0.01 us: cross(): return lax.ppermute(block, ('mp', 'pool'), pairs)]
    dot_general x2 -> x0, matrix products: 21.8 us -> none  [on_device(): jnp.dot(mixed, w_out, preferred_element_type=jnp.float32)]
    ppermute x10 -> x3, starting transfers between devices: 21.5 us -> 0.57 us  [the longest x2 0.5 us: cross(): return lax.ppermute(block, ('mp', 'pool'), pairs)]
    unnamed x97 -> x89, local copies, waits for them, and re-layouts: 25.5 us -> 44.6 us
    ppermute x7 -> x14, waiting for transfers between devices: 38.8 us -> 53.2 us  [swap(): lax.ppermute(block, 'mp', [(index, index ^ mask) for index in range(LINE_...]
    ppermute x14, waiting for transfers between devices: 32.9 us -> 44.6 us  [send(): self.moving[way] = lax.ppermute(self.moving[way], 'mp', pairs)]
  transfers between devices with their start and end apart: 32 -> 32, of which waited for: 10 -> 10; matrix products, arithmetic and copies ran while one was open for 4% -> 6% of each run, Pallas kernels for 33% -> 15%
where the time goes in v5:
time: 361 us; the launch traced here: 359 us
  starting transfers between devices  100 us (28%)
  waiting for transfers between devices  97.8 us (27%)
  Pallas kernels  68.6 us (19%)
  local copies, waits for them, and re-layouts  50 us (14%)
  other arithmetic  29 us (8%)
  between operations  13.2 us (4%)
    ppermute x14, starting transfers between devices, swap(): lax.ppermute(block, 'mp', [(index, index ^ mask) for index in range(LINE_...  77 us
    ppermute x14, waiting for transfers between devices, swap(): lax.ppermute(block, 'mp', [(index, index ^ mask) for index in range(LINE_...  53.2 us
    ppermute x14, waiting for transfers between devices, send(): self.moving[way] = lax.ppermute(self.moving[way], 'mp', pairs)  44.6 us
    unnamed x89, local copies, waits for them, and re-layouts  44.6 us
    pallas_call x3, Pallas kernels, attend(): pl.pallas_call(functools.partial(attend_kernel, span, row_step, chunk), g...  26.3 us
    pallas_call x2, Pallas kernels, project(): pl.pallas_call(project_kernel, grid=(width // depth,), out_shape=out_shap...  19.7 us
    ppermute x14, starting transfers between devices, send(): self.moving[way] = lax.ppermute(self.moving[way], 'mp', pairs)  17.6 us
    pallas_call x2, Pallas kernels, output_product(): pl.pallas_call(output_kernel, grid=(width // tile,), out_shape=jax.ShapeD...  14.1 us
  transfers between devices with their start and end apart: 32, of which 10 were waited for; matrix products, arithmetic and copies ran while one was open for 6% of the time, Pallas kernels for 15%

profile of v5, /device:TPU:0, one launch (start us, length us, event | category | flops | bytes accessed | tf_op | source)
XLA Modules:
  0.0 358.9 jit_solution(2267501223317157313)
XLA Ops:
  4.5 3.1 collective-permute-start.1
  13.8 17.0 %collective-permute-done.1.refs_1_ = bf16[64,8192]{1,0:T(8,128)(2,1)} collective-permute-done((bf16[64,8192]{1,0:T(8,128)(2,1)S(1)}, bf16[64,8192]{1,0:T(8,128)(2,1)}, u32[]{:S(2)}, u32[]{:S(2)}) %collective-permute-start.1) | collective-permute-done | bytes 1048608 | tf_op jit(solution)/shard_map/ppermute | solution.py:54
  32.5 8.1 %collective-permute-start.2 = (bf16[64,8192]{1,0:T(8,128)(2,1)}, bf16[64,8192]{1,0:T(8,128)(2,1)}, u32[]{:S(2)}, u32[]{:S(2)}) collective-permute-start(bf16[64,8192]{1,0:T(8,128)(2,1)} %collective-permute-done), channel_id=1, source_target_pairs={{0,4},{2,6},{4,0},{6,2},{8,12},{10,14},{12,8},{14,10},{1,5},{3,7},... | collective-permute-start | bytes 3145736 | tf_op jit(solution)/shard_map/ppermute | solution.py:54
  42.9 19.9 %collective-permute-start.4 = (bf16[64,8192]{1,0:T(8,128)(2,1)}, bf16[64,8192]{1,0:T(8,128)(2,1)S(1)}, u32[]{:S(2)}, u32[]{:S(2)}) collective-permute-start(bf16[64,8192]{1,0:T(8,128)(2,1)} %collective-permute-done.3), channel_id=1, source_target_pairs={{0,4},{2,6},{4,0},{6,2},{8,12},{10,14},{12,8},{14,10},{1,5},{3,7},... | collective-permute-start | bytes 3145736 | tf_op jit(solution)/shard_map/ppermute | solution.py:54
  65.0 3.6 %pack_blocks.1 = (bf16[2,32,16,256]{3,2,1,0:T(8,128)(2,1)S(1)}, bf16[2,32,16,256]{3,2,1,0:T(8,128)(2,1)S(1)}, bf16[2,32,16,256]{3,2,1,0:T(8,128)(2,1)S(1)}, bf16...) custom-call(s32[2,32]{1,0:T(2,128)S(1)} %pad_add_fusion.slots_ref, ...), custom_call_target="tpu_custom_call" | custom-call | tf_op jit(solution)/shard_map/pack_blocks/pallas_call | solution.py:292
  70.0 2.7 broadcast_select_fusion.1.refs_0_
  74.3 23.2 %collective-permute-done.4 = bf16[64,8192]{1,0:T(8,128)(2,1)S(1)} collective-permute-done((bf16[64,8192]{1,0:T(8,128)(2,1)}, bf16[64,8192]{1,0:T(8,128)(2,1)S(1)}, u32[]{:S(2)}, u32[]{:S(2)}) %collective-permute-start.4) | collective-permute-done | bytes 1048608 | tf_op jit(solution)/shard_map/ppermute | solution.py:54
  103.6 2.5 collective-permute-start.15
  117.1 3.6 collective-permute-done.15
  120.6 2.4 collective-permute-start.16
  123.1 31.4 %collective-permute-start.13 = (bf16[2,32,16,256]{3,2,1,0:T(8,128)(2,1)}, bf16[2,32,16,256]{3,2,1,0:T(8,128)(2,1)}, u32[]{:S(2)}, u32[]{:S(2)}) collective-permute-start(bf16[2,32,16,256]{3,2,1,0:T(8,128)(2,1)} %copy-done.25), channel_id=1, source_target_pairs={{0,4},{2,6},{4,0},{6,2},{8,12},{10,14},{12,8},{14,10},{1,5},{3,7},... | collective-permute-start | bytes 1572872 | tf_op jit(solution)/shard_map/ppermute | solution.py:54
  154.4 9.3 %collective-permute-done.11 = bf16[2,32,16,256]{3,2,1,0:T(8,128)(2,1)} collective-permute-done((bf16[2,32,16,256]{3,2,1,0:T(8,128)(2,1)}, bf16[2,32,16,256]{3,2,1,0:T(8,128)(2,1)}, u32[]{:S(2)}, u32[]{:S(2)}) %collective-permute-start.11) | collective-permute-done | bytes 524320 | tf_op jit(solution)/shard_map/ppermute | solution.py:54
  165.3 5.8 %copy-done = bf16[8192,1024]{1,0:T(8,128)(2,1)S(1)} copy-done((bf16[8192,1024]{1,0:T(8,128)(2,1)S(1)}, bf16[8192,1024]{1,0:T(8,128)(2,1)}, u32[]{:S(2)}) %copy-start) | copy-done | bytes 16777240
  173.9 9.6 %project.2 = (bf16[8,256,128]{2,1,0:T(8,128)(2,1)S(1)}, bf16[256,128]{1,0:T(8,128)(2,1)S(1)}, bf16[256,256]{1,0:T(8,128)(2,1)S(1)}, bf16[256,256]{1,0:T(8,128)(2,1)S(1)}) custom-call(s32[4]{0:T(128)S(1)} %add_multiply_fusion.starts_ref, bf16[64,8192]{1,0:T(8,128)(2,1)S(1)} %fusion.2.refs_0_, bf16[64,8192]{1,0:T(8,128)(2,1)} %collective-permute-done.1.refs_1_, ...), custom_call_target="tpu_custom_call" | custom-call | flops 5368709120 | bytes 26476544 | tf_op jit(solution)/shard_map/project/pallas_call | solution.py:176
  184.3 5.8 %copy-done.1 = bf16[8192,1024]{1,0:T(8,128)(2,1)S(1)} copy-done((bf16[8192,1024]{1,0:T(8,128)(2,1)S(1)}, bf16[8192,1024]{1,0:T(8,128)(2,1)}, u32[]{:S(2)}) %copy-start.1) | copy-done | bytes 16777240
  190.0 10.1 %project.3 = (bf16[8,256,128]{2,1,0:T(8,128)(2,1)S(1)}, bf16[256,128]{1,0:T(8,128)(2,1)S(1)}, bf16[256,256]{1,0:T(8,128)(2,1)S(1)}, bf16[256,256]{1,0:T(8,128)(2,1)S(1)}) custom-call(s32[4]{0:T(128)S(1)} %add_multiply_fusion.1.starts_ref, bf16[64,8192]{1,0:T(8,128)(2,1)} %broadcast_select_fusion.1.refs_0_, bf16[64,8192]{1,0:T(8,128)(2,1)} %broadcast_select_fusion.refs_1_, ...), custom_call_target="tpu_custom_call" | custom-call | flops 5368709120 | bytes 26476544 | tf_op jit(solution)/shard_map/project/pallas_call | solution.py:176
  201.7 5.1 %all-to-all-start = ((bf16[8,64,256]{2,1,0:T(8,128)(2,1)}), bf16[8,64,256]{2,1,0:T(8,128)(2,1)}, u32[]{:S(2)}, u32[]{:S(2)}) async-start(bf16[8,64,256]{2,1,0:T(8,128)(2,1)} %bitcast.27), calls=%async_computation | async-start | bytes 524288 | tf_op jit(solution)/shard_map/all_to_all | solution.py:609
  206.9 4.0 %order_blocks.1 = (bf16[4096,128]{1,0:T(8,128)(2,1)S(1)}, bf16[4096,256]{1,0:T(8,128)(2,1)S(1)}) custom-call(s32[1]{0:T(128)} %dynamic_slice.118.length_ref, s32[256]{0:T(256)S(1)} %multiply_add_fusion.where_ref, bf16[64,16,256]{2,1,0:T(8,128)(2,1)S(1)} %bitcast.121, bf16[64,16,256]{2,1,0:T(8,128)(2,1)} %bitcast.20.refs_1_, ...), custom_call_target="tpu_custom_call" | custom-call | tf_op jit(solution)/shard_map/order_blocks/pallas_call | solution.py:337
  210.9 13.1 %attend.3.mixed_ref = bf16[256,1024]{1,0:T(8,128)(2,1)S(1)} custom-call(s32[1]{0:T(128)} %bitcast.half_ref, bf16[8,4,2,32,128]{4,3,2,1,0:T(8,128)(2,1)S(1)} %bitcast.127, bf16[8,4,2,32,128]{4,3,2,1,0:T(8,128)(2,1)S(1)} %bitcast.130, bf16[4096,128]{1,0:T(8,128)(2,1)S(1)} %get-tuple-element.75.refs_2_, bf16[4096,256]{1,0:T(8,128)(2,1)S(1)} %get-tuple-element.76.refs_3_, ...), custom_call_target="tpu_custom_call" | custom-call | flops 9663676416 | bytes 4587520 | tf_op jit(solution)/shard_map/attend/pallas_call | solution.py:414
  226.3 5.8 %copy-done.2 = bf16[1024,8192]{1,0:T(8,128)(2,1)S(1)} copy-done((bf16[1024,8192]{1,0:T(8,128)(2,1)S(1)}, bf16[1024,8192]{1,0:T(8,128)(2,1)}, u32[]{:S(2)}) %copy-start.2) | copy-done | bytes 16777240
  232.1 7.0 %output_product.2 = bf16[256,8192]{1,0:T(8,128)(2,1)S(1)} custom-call(bf16[256,1024]{1,0:T(8,128)(2,1)S(1)} %attend.3.mixed_ref, bf16[1024,8192]{1,0:T(8,128)(2,1)S(1)} %copy-done.2), custom_call_target="tpu_custom_call" | custom-call | flops 4294967296 | bytes 21495808 | tf_op jit(solution)/shard_map/output_product/pallas_call | solution.py:441
  249.0 6.6 %attend.4 = bf16[256,512]{1,0:T(8,128)(2,1)S(1)} custom-call(s32[1]{0:T(128)} %bitcast.half_ref, bf16[8,4,2,32,128]{4,3,2,1,0:T(8,128)(2,1)S(1)} %bitcast.128, bf16[8,4,2,32,128]{4,3,2,1,0:T(8,128)(2,1)S(1)} %bitcast.131, bf16[4096,128]{1,0:T(8,128)(2,1)S(1)} %copy-done.21, bf16[4096,256]{1,0:T(8,128)(2,1)S(1)} %copy-done.19, ...), custom_call_target="tpu_custom_call" | custom-call | flops 4831838208 | bytes 4063232 | tf_op jit(solution)/shard_map/attend/pallas_call | solution.py:414
  255.6 2.8 fusion.11
  266.5 6.6 %attend.5 = bf16[256,512]{1,0:T(8,128)(2,1)S(1)} custom-call(s32[1]{0:T(128)} %bitcast.half_ref, bf16[8,4,2,32,128]{4,3,2,1,0:T(8,128)(2,1)S(1)} %bitcast.129, bf16[8,4,2,32,128]{4,3,2,1,0:T(8,128)(2,1)S(1)} %bitcast.132, bf16[4096,128]{1,0:T(8,128)(2,1)S(1)} %copy-done.22, bf16[4096,256]{1,0:T(8,128)(2,1)S(1)} %copy-done.19, ...), custom_call_target="tpu_custom_call" | custom-call | flops 4831838208 | bytes 4063232 | tf_op jit(solution)/shard_map/attend/pallas_call | solution.py:414
  275.1 5.8 %copy-done.3 = bf16[1024,8192]{1,0:T(8,128)(2,1)S(1)} copy-done((bf16[1024,8192]{1,0:T(8,128)(2,1)S(1)}, bf16[1024,8192]{1,0:T(8,128)(2,1)}, u32[]{:S(2)}) %copy-start.3) | copy-done | bytes 16777240
  280.8 7.0 %output_product.3 = bf16[256,8192]{1,0:T(8,128)(2,1)S(1)} custom-call(bf16[256,1024]{1,0:T(8,128)(2,1)S(1)} %pad_maximum_fusion.mixed_ref, bf16[1024,8192]{1,0:T(8,128)(2,1)S(1)} %copy-done.3), custom_call_target="tpu_custom_call" | custom-call | flops 4294967296 | bytes 21495808 | tf_op jit(solution)/shard_map/output_product/pallas_call | solution.py:441
  290.1 10.7 %collective-permute-done.24 = bf16[32,8192]{1,0:T(8,128)(2,1)S(1)} collective-permute-done((bf16[32,8192]{1,0:T(8,128)(2,1)S(1)}, bf16[32,8192]{1,0:T(8,128)(2,1)S(1)}, u32[]{:S(2)}, u32[]{:S(2)}) %collective-permute-start.24) | collective-permute-done | bytes 524320 | tf_op jit(solution)/shard_map/ppermute | solution.py:233
  303.9 6.5 %collective-permute-done.25 = bf16[32,8192]{1,0:T(8,128)(2,1)S(1)} collective-permute-done((bf16[32,8192]{1,0:T(8,128)(2,1)S(1)}, bf16[32,8192]{1,0:T(8,128)(2,1)S(1)}, u32[]{:S(2)}, u32[]{:S(2)}) %collective-permute-start.25) | collective-permute-done | bytes 524320 | tf_op jit(solution)/shard_map/ppermute | solution.py:233
  319.5 8.3 %collective-permute-done.28 = bf16[32,8192]{1,0:T(8,128)(2,1)S(1)} collective-permute-done((bf16[32,8192]{1,0:T(8,128)(2,1)}, bf16[32,8192]{1,0:T(8,128)(2,1)S(1)}, u32[]{:S(2)}, u32[]{:S(2)}) %collective-permute-start.28) | collective-permute-done | bytes 524320 | tf_op jit(solution)/shard_map/ppermute | solution.py:233
  331.0 2.4 collective-permute-done.21
  335.5 10.8 %collective-permute-done.29 = bf16[32,8192]{1,0:T(8,128)(2,1)S(1)} collective-permute-done((bf16[32,8192]{1,0:T(8,128)(2,1)S(1)}, bf16[32,8192]{1,0:T(8,128)(2,1)S(1)}, u32[]{:S(2)}, u32[]{:S(2)}) %collective-permute-start.29) | collective-permute-done | bytes 524320 | tf_op jit(solution)/shard_map/ppermute | solution.py:233
  350.7 5.9 %collective-permute-done.30 = bf16[32,8192]{1,0:T(8,128)(2,1)S(1)} collective-permute-done((bf16[32,8192]{1,0:T(8,128)(2,1)S(1)}, bf16[32,8192]{1,0:T(8,128)(2,1)S(1)}, u32[]{:S(2)}, u32[]{:S(2)}) %collective-permute-start.30) | collective-permute-done | bytes 524320 | tf_op jit(solution)/shard_map/ppermute | solution.py:233
  (178 shorter events, 79.2 us)
Async XLA Ops:
  4.5 26.4 %collective-permute-start.1 = (bf16[64,8192]{1,0:T(8,128)(2,1)S(1)}, bf16[64,8192]{1,0:T(8,128)(2,1)}, u32[]{:S(2)}, u32[]{:S(2)}) collective-permute-start(bf16[64,8192]{1,0:T(8,128)(2,1)S(1)} %fusion.2.refs_0_), channel_id=1, source_target_pairs={{0,4},{2,6},{4,0},{6,2},{8,12},{10,14},{12,8},{14,10},{1,5},{3,7},... | collective-permute-start | bytes 3145736 | tf_op jit(solution)/shard_map/ppermute | solution.py:54
  13.2 49.6 %collective-permute-start.5 = (bf16[32,16,2048]{2,1,0:T(8,128)(2,1)S(1)}, bf16[32,16,2048]{2,1,0:T(8,128)(2,1)}, u32[]{:S(2)}, u32[]{:S(2)}) collective-permute-start(bf16[32,16,2048]{2,1,0:T(8,128)(2,1)S(1)} %pick_blocks.1), channel_id=1, source_target_pairs={{0,1},{1,0},{2,3},{3,2},{4,5},{5,4},{6,7},{7,6},{8,9},{9,8},{10,11... | collective-permute-start | bytes 6291464 | tf_op jit(solution)/shard_map/ppermute | solution.py:510
  13.3 19.2 %collective-permute-start = (bf16[64,8192]{1,0:T(8,128)(2,1)S(1)}, bf16[64,8192]{1,0:T(8,128)(2,1)}, u32[]{:S(2)}, u32[]{:S(2)}) collective-permute-start(bf16[64,8192]{1,0:T(8,128)(2,1)S(1)} %fusion.2.refs_0_), channel_id=1, source_target_pairs={{0,1},{1,0},{2,3},{3,2},{4,8},{5,9},{6,10},{7,11},{8,4},{9,5},{10,... | collective-permute-start | bytes 3145736 | tf_op jit(solution)/shard_map/ppermute | solution.py:65
  30.8 12.1 %collective-permute-start.3 = (bf16[64,8192]{1,0:T(8,128)(2,1)}, bf16[64,8192]{1,0:T(8,128)(2,1)}, u32[]{:S(2)}, u32[]{:S(2)}) collective-permute-start(bf16[64,8192]{1,0:T(8,128)(2,1)} %collective-permute-done.1.refs_1_), channel_id=1, source_target_pairs={{0,1},{1,0},{2,3},{3,2},{4,8},{5,9},{6,10},{7,11},{8,4},{9,5},{10,... | collective-permute-start | bytes 3145736 | tf_op jit(solution)/shard_map/ppermute | solution.py:65
  30.8 37.9 %collective-permute-start.6 = (bf16[64,8192]{1,0:T(8,128)(2,1)S(1)}, bf16[64,8192]{1,0:T(8,128)(2,1)}, u32[]{:S(2)}, u32[]{:S(2)}) collective-permute-start(bf16[64,8192]{1,0:T(8,128)(2,1)S(1)} %fusion.2.refs_0_), channel_id=1, source_target_pairs={{0,2},{2,0},{4,6},{6,4},{8,10},{10,8},{12,14},{14,12},{1,3},{3,1},... | collective-permute-start | bytes 3145736 | tf_op jit(solution)/shard_map/ppermute | solution.py:54
  32.5 37.5 %collective-permute-start.2 = (bf16[64,8192]{1,0:T(8,128)(2,1)}, bf16[64,8192]{1,0:T(8,128)(2,1)}, u32[]{:S(2)}, u32[]{:S(2)}) collective-permute-start(bf16[64,8192]{1,0:T(8,128)(2,1)} %collective-permute-done), channel_id=1, source_target_pairs={{0,4},{2,6},{4,0},{6,2},{8,12},{10,14},{12,8},{14,10},{1,5},{3,7},... | collective-permute-start | bytes 3145736 | tf_op jit(solution)/shard_map/ppermute | solution.py:54
  41.3 61.3 %collective-permute-start.9 = (bf16[64,8192]{1,0:T(8,128)(2,1)}, bf16[64,8192]{1,0:T(8,128)(2,1)S(1)}, u32[]{:S(2)}, u32[]{:S(2)}) collective-permute-start(bf16[64,8192]{1,0:T(8,128)(2,1)} %collective-permute-done.1.refs_1_), channel_id=1, source_target_pairs={{0,2},{2,0},{4,6},{6,4},{8,10},{10,8},{12,14},{14,12},{1,3},{3,1},... | collective-permute-start | bytes 3145736 | tf_op jit(solution)/shard_map/ppermute | solution.py:54
  42.9 54.5 %collective-permute-start.4 = (bf16[64,8192]{1,0:T(8,128)(2,1)}, bf16[64,8192]{1,0:T(8,128)(2,1)S(1)}, u32[]{:S(2)}, u32[]{:S(2)}) collective-permute-start(bf16[64,8192]{1,0:T(8,128)(2,1)} %collective-permute-done.3), channel_id=1, source_target_pairs={{0,4},{2,6},{4,0},{6,2},{8,12},{10,14},{12,8},{14,10},{1,5},{3,7},... | collective-permute-start | bytes 3145736 | tf_op jit(solution)/shard_map/ppermute | solution.py:54
  68.8 29.8 %collective-permute-start.7 = (bf16[2,32,16,256]{3,2,1,0:T(8,128)(2,1)S(1)}, bf16[2,32,16,256]{3,2,1,0:T(8,128)(2,1)S(1)}, u32[]{:S(2)}, u32[]{:S(2)}) collective-permute-start(bf16[2,32,16,256]{3,2,1,0:T(8,128)(2,1)S(1)} %get-tuple-element.54), channel_id=1, source_target_pairs={{0,8},{2,10},{4,12},{6,14},{8,0},{10,2},{12,4},{14,6},{1,9},{3,11}... | collective-permute-start | bytes 1572872 | tf_op jit(solution)/shard_map/ppermute | solution.py:54
  72.7 50.3 %collective-permute-start.10 = (bf16[64,8192]{1,0:T(8,128)(2,1)}, bf16[64,8192]{1,0:T(8,128)(2,1)}, u32[]{:S(2)}, u32[]{:S(2)}) collective-permute-start(bf16[64,8192]{1,0:T(8,128)(2,1)} %broadcast_select_fusion.1.refs_0_), channel_id=1, source_target_pairs={{0,2},{2,0},{4,6},{6,4},{8,10},{10,8},{12,14},{14,12},{1,3},{3,1},... | collective-permute-start | bytes 3145736 | tf_op jit(solution)/shard_map/ppermute | solution.py:54
  98.6 66.7 %collective-permute-start.8 = (bf16[64,8192]{1,0:T(8,128)(2,1)}, bf16[64,8192]{1,0:T(8,128)(2,1)}, u32[]{:S(2)}, u32[]{:S(2)}) collective-permute-start(bf16[64,8192]{1,0:T(8,128)(2,1)} %broadcast_select_fusion.refs_1_), channel_id=1, source_target_pairs={{0,2},{2,0},{4,6},{6,4},{8,10},{10,8},{12,14},{14,12},{1,3},{3,1},... | collective-permute-start | bytes 3145736 | tf_op jit(solution)/shard_map/ppermute | solution.py:54
  103.6 17.0 %collective-permute-start.15 = (bf16[2,32,16,256]{3,2,1,0:T(8,128)(2,1)}, bf16[2,32,16,256]{3,2,1,0:T(8,128)(2,1)}, u32[]{:S(2)}, u32[]{:S(2)}) collective-permute-start(bf16[2,32,16,256]{3,2,1,0:T(8,128)(2,1)} %get-tuple-element.72), channel_id=1, source_target_pairs={{0,12},{2,14},{4,8},{6,10},{8,4},{10,6},{12,0},{14,2},{1,13},{3,15... | collective-permute-start | bytes 1572872 | tf_op jit(solution)/shard_map/ppermute | solution.py:54
  106.1 57.7 %collective-permute-start.11 = (bf16[2,32,16,256]{3,2,1,0:T(8,128)(2,1)}, bf16[2,32,16,256]{3,2,1,0:T(8,128)(2,1)}, u32[]{:S(2)}, u32[]{:S(2)}) collective-permute-start(bf16[2,32,16,256]{3,2,1,0:T(8,128)(2,1)} %get-tuple-element.65), channel_id=1, source_target_pairs={{0,10},{2,8},{4,14},{6,12},{8,2},{10,0},{12,6},{14,4},{1,11},{3,9}... | collective-permute-start | bytes 1572872 | tf_op jit(solution)/shard_map/ppermute | solution.py:54
  120.6 86.2 %collective-permute-start.16 = (bf16[2,32,16,256]{3,2,1,0:T(8,128)(2,1)}, bf16[2,32,16,256]{3,2,1,0:T(8,128)(2,1)}, u32[]{:S(2)}, u32[]{:S(2)}) collective-permute-start(bf16[2,32,16,256]{3,2,1,0:T(8,128)(2,1)} %copy-done.26), channel_id=1, source_target_pairs={{0,14},{2,12},{4,10},{6,8},{8,6},{10,4},{12,2},{14,0},{1,15},{3,13... | collective-permute-start | bytes 1572872 | tf_op jit(solution)/shard_map/ppermute | solution.py:54
  123.1 83.8 %collective-permute-start.13 = (bf16[2,32,16,256]{3,2,1,0:T(8,128)(2,1)}, bf16[2,32,16,256]{3,2,1,0:T(8,128)(2,1)}, u32[]{:S(2)}, u32[]{:S(2)}) collective-permute-start(bf16[2,32,16,256]{3,2,1,0:T(8,128)(2,1)} %copy-done.25), channel_id=1, source_target_pairs={{0,4},{2,6},{4,0},{6,2},{8,12},{10,14},{12,8},{14,10},{1,5},{3,7},... | collective-permute-start | bytes 1572872 | tf_op jit(solution)/shard_map/ppermute | solution.py:54
  163.8 43.1 %collective-permute-start.12 = (bf16[2,32,16,256]{3,2,1,0:T(8,128)(2,1)}, bf16[2,32,16,256]{3,2,1,0:T(8,128)(2,1)}, u32[]{:S(2)}, u32[]{:S(2)}) collective-permute-start(bf16[2,32,16,256]{3,2,1,0:T(8,128)(2,1)} %copy-done.24), channel_id=1, source_target_pairs={{0,2},{2,0},{4,6},{6,4},{8,10},{10,8},{12,14},{14,12},{1,3},{3,1},... | collective-permute-start | bytes 1572872 | tf_op jit(solution)/shard_map/ppermute | solution.py:54
  165.3 41.6 %collective-permute-start.14 = (bf16[2,32,16,256]{3,2,1,0:T(8,128)(2,1)}, bf16[2,32,16,256]{3,2,1,0:T(8,128)(2,1)}, u32[]{:S(2)}, u32[]{:S(2)}) collective-permute-start(bf16[2,32,16,256]{3,2,1,0:T(8,128)(2,1)} %copy-done.23), channel_id=1, source_target_pairs={{0,6},{2,4},{4,2},{6,0},{8,14},{10,12},{12,10},{14,8},{1,7},{3,5},... | collective-permute-start | bytes 1572872 | tf_op jit(solution)/shard_map/ppermute | solution.py:54
  201.7 24.6 %all-to-all-start = ((bf16[8,64,256]{2,1,0:T(8,128)(2,1)}), bf16[8,64,256]{2,1,0:T(8,128)(2,1)}, u32[]{:S(2)}, u32[]{:S(2)}) async-start(bf16[8,64,256]{2,1,0:T(8,128)(2,1)} %bitcast.27), calls=%async_computation | async-start | bytes 524288 | tf_op jit(solution)/shard_map/all_to_all | solution.py:609
  242.2 13.3 %collective-permute-start.18 = (bf16[32,8192]{1,0:T(8,128)(2,1)}, bf16[32,8192]{1,0:T(8,128)(2,1)}, u32[]{:S(2)}, u32[]{:S(2)}) collective-permute-start(bf16[32,8192]{1,0:T(8,128)(2,1)} %get-tuple-element.85), channel_id=1, source_target_pairs={{0,2},{4,0},{8,4},{12,8},{14,12},{10,14},{6,10},{2,6},{1,3},{5,1},... | collective-permute-start | bytes 1572872 | tf_op jit(solution)/shard_map/ppermute | solution.py:233
  244.3 11.3 %collective-permute-start.17 = (bf16[32,8192]{1,0:T(8,128)(2,1)}, bf16[32,8192]{1,0:T(8,128)(2,1)}, u32[]{:S(2)}, u32[]{:S(2)}) collective-permute-start(bf16[32,8192]{1,0:T(8,128)(2,1)} %get-tuple-element.84), channel_id=1, source_target_pairs={{0,4},{4,8},{8,12},{12,14},{14,10},{10,6},{6,2},{2,0},{1,5},{5,9},... | collective-permute-start | bytes 1572872 | tf_op jit(solution)/shard_map/ppermute | solution.py:233
  258.4 14.8 %collective-permute-start.20 = (bf16[32,8192]{1,0:T(8,128)(2,1)}, bf16[32,8192]{1,0:T(8,128)(2,1)}, u32[]{:S(2)}, u32[]{:S(2)}) collective-permute-start(bf16[32,8192]{1,0:T(8,128)(2,1)} %get-tuple-element.89), channel_id=1, source_target_pairs={{0,2},{4,0},{8,4},{12,8},{14,12},{10,14},{6,10},{2,6},{1,3},{5,1},... | collective-permute-start | bytes 1572872 | tf_op jit(solution)/shard_map/ppermute | solution.py:233
  260.4 12.8 %collective-permute-start.19 = (bf16[32,8192]{1,0:T(8,128)(2,1)}, bf16[32,8192]{1,0:T(8,128)(2,1)}, u32[]{:S(2)}, u32[]{:S(2)}) collective-permute-start(bf16[32,8192]{1,0:T(8,128)(2,1)} %get-tuple-element.88), channel_id=1, source_target_pairs={{0,4},{4,8},{8,12},{12,14},{14,10},{10,6},{6,2},{2,0},{1,5},{5,9},... | collective-permute-start | bytes 1572872 | tf_op jit(solution)/shard_map/ppermute | solution.py:233
  288.0 12.8 %collective-permute-start.24 = (bf16[32,8192]{1,0:T(8,128)(2,1)S(1)}, bf16[32,8192]{1,0:T(8,128)(2,1)S(1)}, u32[]{:S(2)}, u32[]{:S(2)}) collective-permute-start(bf16[32,8192]{1,0:T(8,128)(2,1)S(1)} %get-tuple-element.97), channel_id=1, source_target_pairs={{0,4},{4,8},{8,12},{12,14},{14,10},{10,6},{6,2},{2,0},{1,5},{5,9},... | collective-permute-start | bytes 1572872 | tf_op jit(solution)/shard_map/ppermute | solution.py:233
  290.0 14.0 %collective-permute-start.27 = (bf16[32,8192]{1,0:T(8,128)(2,1)S(1)}, bf16[32,8192]{1,0:T(8,128)(2,1)S(1)}, u32[]{:S(2)}, u32[]{:S(2)}) collective-permute-start(bf16[32,8192]{1,0:T(8,128)(2,1)S(1)} %get-tuple-element.98), channel_id=1, source_target_pairs={{0,2},{4,0},{8,4},{12,8},{14,12},{10,14},{6,10},{2,6},{1,3},{5,1},... | collective-permute-start | bytes 1572872 | tf_op jit(solution)/shard_map/ppermute | solution.py:233
  300.9 9.6 %collective-permute-start.25 = (bf16[32,8192]{1,0:T(8,128)(2,1)S(1)}, bf16[32,8192]{1,0:T(8,128)(2,1)S(1)}, u32[]{:S(2)}, u32[]{:S(2)}) collective-permute-start(bf16[32,8192]{1,0:T(8,128)(2,1)S(1)} %fusion.6), channel_id=1, source_target_pairs={{0,4},{4,8},{8,12},{12,14},{14,10},{10,6},{6,2},{2,0},{1,5},{5,9},... | collective-permute-start | bytes 1572872 | tf_op jit(solution)/shard_map/ppermute | solution.py:233
  312.7 15.1 %collective-permute-start.28 = (bf16[32,8192]{1,0:T(8,128)(2,1)}, bf16[32,8192]{1,0:T(8,128)(2,1)S(1)}, u32[]{:S(2)}, u32[]{:S(2)}) collective-permute-start(bf16[32,8192]{1,0:T(8,128)(2,1)} %get-tuple-element.103), channel_id=1, source_target_pairs={{0,2},{4,0},{8,4},{12,8},{14,12},{10,14},{6,10},{2,6},{1,3},{5,1},... | collective-permute-start | bytes 1572872 | tf_op jit(solution)/shard_map/ppermute | solution.py:233
  317.5 32.0 %collective-permute-start.23 = (bf16[32,8192]{1,0:T(8,128)(2,1)S(1)}, bf16[32,8192]{1,0:T(8,128)(2,1)S(1)}, u32[]{:S(2)}, u32[]{:S(2)}) collective-permute-start(bf16[32,8192]{1,0:T(8,128)(2,1)S(1)} %get-tuple-element.94), channel_id=1, source_target_pairs={{0,2},{4,0},{8,4},{12,8},{14,12},{10,14},{6,10},{2,6},{1,3},{5,1},... | collective-permute-start | bytes 1572872 | tf_op jit(solution)/shard_map/ppermute | solution.py:233
  318.8 14.6 %collective-permute-start.21 = (bf16[32,8192]{1,0:T(8,128)(2,1)S(1)}, bf16[32,8192]{1,0:T(8,128)(2,1)S(1)}, u32[]{:S(2)}, u32[]{:S(2)}) collective-permute-start(bf16[32,8192]{1,0:T(8,128)(2,1)S(1)} %get-tuple-element.93), channel_id=1, source_target_pairs={{0,4},{4,8},{8,12},{12,14},{14,10},{10,6},{6,2},{2,0},{1,5},{5,9},... | collective-permute-start | bytes 1572872 | tf_op jit(solution)/shard_map/ppermute | solution.py:233
  328.9 17.3 %collective-permute-start.29 = (bf16[32,8192]{1,0:T(8,128)(2,1)S(1)}, bf16[32,8192]{1,0:T(8,128)(2,1)S(1)}, u32[]{:S(2)}, u32[]{:S(2)}) collective-permute-start(bf16[32,8192]{1,0:T(8,128)(2,1)S(1)} %fusion.4), channel_id=1, source_target_pairs={{0,2},{4,0},{8,4},{12,8},{14,12},{10,14},{6,10},{2,6},{1,3},{5,1},... | collective-permute-start | bytes 1572872 | tf_op jit(solution)/shard_map/ppermute | solution.py:233
  334.6 14.9 %collective-permute-start.22 = (bf16[32,8192]{1,0:T(8,128)(2,1)S(1)}, bf16[32,8192]{1,0:T(8,128)(2,1)S(1)}, u32[]{:S(2)}, u32[]{:S(2)}) collective-permute-start(bf16[32,8192]{1,0:T(8,128)(2,1)S(1)} %fusion.14), channel_id=1, source_target_pairs={{0,4},{4,8},{8,12},{12,14},{14,10},{10,6},{6,2},{2,0},{1,5},{5,9},... | collective-permute-start | bytes 1572872 | tf_op jit(solution)/shard_map/ppermute | solution.py:233
  335.4 15.3 %collective-permute-start.26 = (bf16[32,8192]{1,0:T(8,128)(2,1)S(1)}, bf16[32,8192]{1,0:T(8,128)(2,1)S(1)}, u32[]{:S(2)}, u32[]{:S(2)}) collective-permute-start(bf16[32,8192]{1,0:T(8,128)(2,1)S(1)} %get-tuple-element.102), channel_id=1, source_target_pairs={{0,4},{4,8},{8,12},{12,14},{14,10},{10,6},{6,2},{2,0},{1,5},{5,9},... | collective-permute-start | bytes 1572872 | tf_op jit(solution)/shard_map/ppermute | solution.py:233
  347.4 9.2 %collective-permute-start.30 = (bf16[32,8192]{1,0:T(8,128)(2,1)S(1)}, bf16[32,8192]{1,0:T(8,128)(2,1)S(1)}, u32[]{:S(2)}, u32[]{:S(2)}) collective-permute-start(bf16[32,8192]{1,0:T(8,128)(2,1)S(1)} %fusion.5), channel_id=1, source_target_pairs={{0,2},{4,0},{8,4},{12,8},{14,12},{10,14},{6,10},{2,6},{1,3},{5,1},... | collective-permute-start | bytes 1572872 | tf_op jit(solution)/shard_map/ppermute | solution.py:233
  (44 other events, 834.4 us)

commit v6 on v5

--- a/solution.py
+++ b/solution.py
@@ -15,9 +15,8 @@
 SCORE_SCALE = HD ** (-0.5) * math.log2(math.e)
 VMEM_LIMIT = 56 * 1024 * 1024
 ATTEND_VMEM = 28 * 1024 * 1024
-ROW_STEP = 32
+COLUMN_CHUNKS = 2
 LINE_MODELS = 8
-IN_FLIGHT = 4
 
 
 def angle_tables(positions):
@@ -66,38 +65,36 @@
 
 
 def gather_and_exchange(own, outgoing, middle):
-    done = []
     arrived = {0: outgoing[0]}
 
-    def go(block, move):
-        if len(done) >= IN_FLIGHT:
-            block, done[-IN_FLIGHT] = lax.optimization_barrier((block, done[-IN_FLIGHT]))
-        done.append(move(block))
-        return done[-1]
-
-    def exchange(apart):
-        arrived[apart] = go(outgoing[apart], lambda block: swap(block, apart))
-
-    along = lambda block: swap(block, 2)
-    across = lambda block: swap(block, 1)
-    beside = go(own, along)
-    over = go(own, cross)
-    own_y = go(own, across)
-    over_beside = go(beside, cross)
-    over_passed = go(over, along)
-    beside_y = go(beside, across)
-    exchange(4)
-    over_beside_passed = go(over_beside, along)
+    def after(block, *events):
+        return lax.optimization_barrier((block, events))[0]
+
+    def exchange(apart, *events):
+        block = after(outgoing[apart], *events) if events else outgoing[apart]
+        arrived[apart] = swap(block, apart)
+
+    beside = swap(own, 2)
+    over = cross(own)
+    own_y = swap(own, 1)
+    exchange(6)
+    beside = after(beside, outgoing[6])
+    over_beside = cross(beside)
+    over_passed = swap(over, 2)
+    beside_y = swap(beside, 1)
+    exchange(4, over)
+    over_beside_passed = swap(over_beside, 2)
     far_first = jnp.where(middle, over, over_passed)
-    far_first_y = go(far_first, across)
-    exchange(6)
+    far_first_y = swap(far_first, 1)
+    exchange(5, arrived[6], over_beside)
+    exchange(2, over_passed, beside_y)
     far_second = jnp.where(middle, over_beside, over_beside_passed)
-    far_second_y = go(far_second, across)
-    for apart in (5, 2, 7, 3, 1):
-        exchange(apart)
-    near = [own, beside, own_y, beside_y]
-    far = [far_first, far_second, far_first_y, far_second_y]
-    near[0], far[0] = lax.optimization_barrier((own, far_first, far_second_y))[:2]
+    far_second_y = swap(far_second, 1)
+    exchange(7, arrived[4], far_second)
+    exchange(3, far_first_y)
+    exchange(1, far_first_y, arrived[2])
+    near = [after(own, far_second, arrived[4], arrived[6]), beside, own_y, beside_y]
+    far = [after(far_first, arrived[5], arrived[2]), far_second, far_first_y, far_second_y]
     return near, far, [arrived[apart] for apart in range(LINE_MODELS)]
 
 
@@ -184,7 +181,7 @@
             pltpu.VMEM((rows, out_width), jnp.float32),
             pltpu.SemaphoreType.DMA((len(blocks),)),
         ],
-        compiler_params=pltpu.CompilerParams(vmem_limit_bytes=ATTEND_VMEM),
+        compiler_params=pltpu.CompilerParams(vmem_limit_bytes=VMEM_LIMIT),
         cost_estimate=pl.CostEstimate(
             flops=2 * rows * width * out_width,
             bytes_accessed=2 * width * (rows + out_width) + 4 * rows * out_width,
@@ -434,20 +431,21 @@
     ).astype(jnp.bfloat16)
 
 
-def output_product(mixed, weight):
+def output_product(mixed, weight, chunk, chunks):
     rows, depth = mixed.shape
-    width = weight.shape[1]
+    width = weight.shape[1] // chunks
     tile = math.gcd(width, 1024)
+    tiles = width // tile
     return pl.pallas_call(
         output_kernel,
-        grid=(width // tile,),
+        grid=(tiles,),
         out_shape=jax.ShapeDtypeStruct((rows, width), jnp.bfloat16),
         in_specs=[
             pl.BlockSpec((rows, depth), lambda col: (0, 0)),
-            pl.BlockSpec((depth, tile), lambda col: (0, col)),
+            pl.BlockSpec((depth, tile), lambda col: (0, chunk * tiles + col)),
         ],
         out_specs=pl.BlockSpec((rows, tile), lambda col: (0, col)),
-        compiler_params=pltpu.CompilerParams(vmem_limit_bytes=ATTEND_VMEM),
+        compiler_params=pltpu.CompilerParams(vmem_limit_bytes=VMEM_LIMIT),
         cost_estimate=pl.CostEstimate(
             flops=2 * rows * depth * width,
             bytes_accessed=2 * (rows * depth + depth * width + rows * width),
@@ -575,53 +573,32 @@
         new_keys = [key_whole[part] for part in halves]
         new_values = [value_ones[part] for part in halves]
 
+    arrived, new_keys = lax.optimization_barrier((arrived, list(new_keys)))
     prefix = order_blocks(arrived, where, prefix_count.reshape(1))
 
-    row_step = min(row_count, ROW_STEP)
-    chunks = row_count // row_step
-    queries = [
-        part.reshape(q_local, n_model // 2, chunks, row_step, HD) for part in queries
-    ]
-    half_index = upper_half.reshape(1)
-    scatters = []
-    for chunk in range(chunks):
-        calls = 1 if chunk == 0 else 2
-        heads = q_local // calls
-        mixed = []
-        for call in range(calls):
-            mixed.append(
-                attend(
-                    half_index,
-                    queries,
-                    prefix,
-                    new_keys,
-                    new_values,
-                    row_step,
-                    chunk,
-                    call * heads,
-                    heads,
-                )
-            )
-            for scatter in scatters:
-                queries, mixed = scatter.step(queries, mixed)
-        mixed = jnp.concatenate(mixed, 1)
-        if chunk == 0:
-            pairs = lax.all_to_all(pairs, "mp", split_axis=0, concat_axis=0, tiled=True)
-            mixed, pairs = lax.optimization_barrier((mixed, pairs))
-        share = output_product(mixed, w_out)
-        share = share.reshape(n_model, row_step, share.shape[1])
-        scatters.append(
-            RingScatter(
-                share, n_model, my_model, upper_half * (n_model // 2), 1 if chunk % 2 == 0 else -1
-            )
-        )
-        queries = scatters[-1].step(queries)[0]
+    queries = [part.reshape(q_local, -1, 1, row_count, HD) for part in queries]
+    mixed = attend(
+        upper_half.reshape(1), queries, prefix, new_keys, new_values, row_count, 0, 0, q_local
+    )
+    pairs = lax.all_to_all(pairs, "mp", split_axis=0, concat_axis=0, tiled=True)
+    mixed, pairs = lax.optimization_barrier((mixed, pairs))
     cache_rows = (
         pairs.reshape(kv_heads, sharers, row_count, 2, kv_local)
         .transpose(2, 0, 3, 1, 4)
         .reshape(1, row_count, kv_heads * 2 * HD)
     )
-    return (jnp.concatenate([scatter.finish() for scatter in scatters], 0)[None], cache_rows)
+
+    width = w_out.shape[1]
+    first = upper_half * (n_model // 2)
+    scatters = []
+    for chunk in range(COLUMN_CHUNKS):
+        share = output_product(mixed, w_out, chunk, COLUMN_CHUNKS)
+        share = share.reshape(n_model, row_count, width // COLUMN_CHUNKS)
+        scatters.append(
+            RingScatter(share, n_model, my_model, first, 1 if chunk % 2 == 0 else -1)
+        )
+        (mixed,) = scatters[-1].step(mixed)
+    return (jnp.concatenate([scatter.finish() for scatter in scatters], 1)[None], cache_rows)
 
 
 def solution(mesh):

time: 361 us -> 350 us (0.970)
  local copies, waits for them, and re-layouts: 50 us -> 17.7 us
  starting transfers between devices: 100 us -> 111 us
  Pallas kernels: 68.6 us -> 79.1 us
  waiting for transfers between devices: 97.8 us -> 103 us
  other arithmetic: 29 us -> 24.6 us
    unnamed x89 -> x57, local copies, waits for them, and re-layouts: 44.6 us -> 9.46 us
    pallas_call x2, Pallas kernels: 19.7 us -> 31 us  [project(): pl.pallas_call(project_kernel, grid=(width // depth,), out_shape=out_shap...]
    ppermute x14, waiting for transfers between devices: 44.6 us -> 52.2 us  [send(): self.moving[way] = lax.ppermute(self.moving[way], 'mp', pairs)]
    ppermute x14, starting transfers between devices: 77 us -> 84.3 us  [swap(): lax.ppermute(block, 'mp', [(index, index ^ mask) for index in range(LINE_...]
    pallas_call x2, Pallas kernels: 14.1 us -> 17.7 us  [output_product(): pl.pallas_call(output_kernel, grid=(tiles,), out_shape=jax.ShapeDtypeStru...]
    convert_element_type x7 -> x8, other arithmetic: 10.4 us -> 7.82 us  [advance(): block = (block.astype(jnp.float32) + arrived).astype(jnp.bfloat16)]
    pallas_call x3 -> x1, Pallas kernels: 26.3 us -> 24.2 us  [attend(): pl.pallas_call(functools.partial(attend_kernel, span, row_step, chunk), g...]
  transfers between devices with their start and end apart: 32 -> 32, of which waited for: 10 -> 13; matrix products, arithmetic and copies ran while one was open for 6% -> 7% of each run, Pallas kernels for 15% -> 17%
where the time goes in v6:
time: 350 us; the launch traced here: 348 us
  starting transfers between devices  111 us (32%)
  waiting for transfers between devices  103 us (29%)
  Pallas kernels  79.1 us (23%)
  other arithmetic  24.6 us (7%)
  local copies, waits for them, and re-layouts  17.7 us (5%)
  between operations  13.1 us (4%)
    ppermute x14, starting transfers between devices, swap(): lax.ppermute(block, 'mp', [(index, index ^ mask) for index in range(LINE_...  84.3 us
    ppermute x14, waiting for transfers between devices, send(): self.moving[way] = lax.ppermute(self.moving[way], 'mp', pairs)  52.2 us
    ppermute x14, waiting for transfers between devices, swap(): lax.ppermute(block, 'mp', [(index, index ^ mask) for index in range(LINE_...  50.6 us
    pallas_call x2, Pallas kernels, project(): pl.pallas_call(project_kernel, grid=(width // depth,), out_shape=out_shap...  31 us
    pallas_call x1, Pallas kernels, attend(): pl.pallas_call(functools.partial(attend_kernel, span, row_step, chunk), g...  24.2 us
    ppermute x14, starting transfers between devices, send(): self.moving[way] = lax.ppermute(self.moving[way], 'mp', pairs)  21 us
    pallas_call x2, Pallas kernels, output_product(): pl.pallas_call(output_kernel, grid=(tiles,), out_shape=jax.ShapeDtypeStru...  17.7 us
    unnamed x57, local copies, waits for them, and re-layouts  9.46 us
  transfers between devices with their start and end apart: 32, of which 13 were waited for; matrix products, arithmetic and copies ran while one was open for 7% of the time, Pallas kernels for 17%

profile of v6, /device:TPU:0, one launch (start us, length us, event | category | flops | bytes accessed | tf_op | source)
XLA Modules:
  0.0 348.2 jit_solution(12444618008563805872)
XLA Ops:
  3.3 2.2 copy-done
  8.7 4.1 %collective-permute-start = (bf16[64,8192]{1,0:T(8,128)(2,1)}, bf16[64,8192]{1,0:T(8,128)(2,1)}, u32[]{:S(2)}, u32[]{:S(2)}) collective-permute-start(bf16[64,8192]{1,0:T(8,128)(2,1)} %fusion.2.refs_0_), channel_id=1, source_target_pairs={{0,4},{2,6},{4,0},{6,2},{8,12},{10,14},{12,8},{14,10},{1,5},{3,7},... | collective-permute-start | bytes 3145736 | tf_op jit(solution)/shard_map/ppermute | solution.py:53
  12.9 24.0 %collective-permute-start.9 = (bf16[64,8192]{1,0:T(8,128)(2,1)}, bf16[64,8192]{1,0:T(8,128)(2,1)}, u32[]{:S(2)}, u32[]{:S(2)}) collective-permute-start(bf16[64,8192]{1,0:T(8,128)(2,1)} %collective-permute-done.4), channel_id=1, source_target_pairs={{0,4},{2,6},{4,0},{6,2},{8,12},{10,14},{12,8},{14,10},{1,5},{3,7},... | collective-permute-start | bytes 3145736 | tf_op jit(solution)/shard_map/ppermute | solution.py:53
  36.9 2.8 pack_blocks.1
  47.7 2.5 collective-permute-start.6
  50.6 10.2 %collective-permute-done.9 = bf16[64,8192]{1,0:T(8,128)(2,1)} collective-permute-done((bf16[64,8192]{1,0:T(8,128)(2,1)}, bf16[64,8192]{1,0:T(8,128)(2,1)}, u32[]{:S(2)}, u32[]{:S(2)}) %collective-permute-start.9) | collective-permute-done | bytes 1048608 | tf_op jit(solution)/shard_map/ppermute | solution.py:53
  60.8 3.5 %collective-permute-start.5 = (bf16[2,32,16,256]{3,2,1,0:T(8,128)(2,1)}, bf16[2,32,16,256]{3,2,1,0:T(8,128)(2,1)S(1)}, u32[]{:S(2)}, u32[]{:S(2)}) collective-permute-start(bf16[2,32,16,256]{3,2,1,0:T(8,128)(2,1)} %get-tuple-element.49), channel_id=1, source_target_pairs={{0,8},{2,10},{4,12},{6,14},{8,0},{10,2},{12,4},{14,6},{1,9},{3,11}... | collective-permute-start | bytes 1572872 | tf_op jit(solution)/shard_map/ppermute | solution.py:53
  64.3 26.8 %collective-permute-start.3 = (bf16[64,8192]{1,0:T(8,128)(2,1)}, bf16[64,8192]{1,0:T(8,128)(2,1)S(1)}, u32[]{:S(2)}, u32[]{:S(2)}) collective-permute-start(bf16[64,8192]{1,0:T(8,128)(2,1)} %collective-permute-done.2), channel_id=1, source_target_pairs={{0,4},{2,6},{4,0},{6,2},{8,12},{10,14},{12,8},{14,10},{1,5},{3,7},... | collective-permute-start | bytes 3145736 | tf_op jit(solution)/shard_map/ppermute | solution.py:53
  94.1 10.7 %collective-permute-start.10 = (bf16[2,32,16,256]{3,2,1,0:T(8,128)(2,1)S(1)}, bf16[2,32,16,256]{3,2,1,0:T(8,128)(2,1)S(1)}, u32[]{:S(2)}, u32[]{:S(2)}) collective-permute-start(bf16[2,32,16,256]{3,2,1,0:T(8,128)(2,1)S(1)} %get-tuple-element.53), channel_id=1, source_target_pairs={{0,10},{2,8},{4,14},{6,12},{8,2},{10,0},{12,6},{14,4},{1,11},{3,9}... | collective-permute-start | bytes 1572872 | tf_op jit(solution)/shard_map/ppermute | solution.py:53
  104.8 30.3 %collective-permute-done.3 = bf16[64,8192]{1,0:T(8,128)(2,1)S(1)} collective-permute-done((bf16[64,8192]{1,0:T(8,128)(2,1)}, bf16[64,8192]{1,0:T(8,128)(2,1)S(1)}, u32[]{:S(2)}, u32[]{:S(2)}) %collective-permute-start.3) | collective-permute-done | bytes 1048608 | tf_op jit(solution)/shard_map/ppermute | solution.py:53
  149.3 2.2 pad_maximum_fusion
  151.5 3.7 %collective-permute-start.15 = (bf16[2,32,16,256]{3,2,1,0:T(8,128)(2,1)}, bf16[2,32,16,256]{3,2,1,0:T(8,128)(2,1)S(1)}, u32[]{:S(2)}, u32[]{:S(2)}) collective-permute-start(bf16[2,32,16,256]{3,2,1,0:T(8,128)(2,1)} %copy-done.9), channel_id=1, source_target_pairs={{0,6},{2,4},{4,2},{6,0},{8,14},{10,12},{12,10},{14,8},{1,7},{3,5},... | collective-permute-start | bytes 1572872 | tf_op jit(solution)/shard_map/ppermute | solution.py:53
  156.2 2.7 collective-permute-start.16
  159.0 15.5 %project.2 = (bf16[8,256,128]{2,1,0:T(8,128)(2,1)}, bf16[256,128]{1,0:T(8,128)(2,1)}, bf16[256,256]{1,0:T(8,128)(2,1)}, bf16[256,256]{1,0:T(8,128)(2,1)}) custom-call(s32[4]{0:T(128)} %add_multiply_fusion.starts_ref, bf16[64,8192]{1,0:T(8,128)(2,1)} %fusion.2.refs_0_, bf16[64,8192]{1,0:T(8,128)(2,1)} %collective-permute-done.refs_1_, ...), custom_call_target="tpu_custom_call" | custom-call | flops 5368709120 | bytes 26476544 | tf_op jit(solution)/shard_map/project/pallas_call | solution.py:173
  174.5 10.1 %collective-permute-done.13.refs_3_ = bf16[64,8192]{1,0:T(8,128)(2,1)} collective-permute-done((bf16[64,8192]{1,0:T(8,128)(2,1)}, bf16[64,8192]{1,0:T(8,128)(2,1)}, u32[]{:S(2)}, u32[]{:S(2)}) %collective-permute-start.13) | collective-permute-done | bytes 1048608 | tf_op jit(solution)/shard_map/ppermute | solution.py:53
  184.6 15.5 %project.3 = (bf16[8,256,128]{2,1,0:T(8,128)(2,1)}, bf16[256,128]{1,0:T(8,128)(2,1)}, bf16[256,256]{1,0:T(8,128)(2,1)}, bf16[256,256]{1,0:T(8,128)(2,1)}) custom-call(s32[4]{0:T(128)} %add_multiply_fusion.1.starts_ref, bf16[64,8192]{1,0:T(8,128)(2,1)} %copy-done.17, bf16[64,8192]{1,0:T(8,128)(2,1)} %broadcast_select_fusion.1.refs_1_, ...), custom_call_target="tpu_custom_call" | custom-call | flops 5368709120 | bytes 26476544 | tf_op jit(solution)/shard_map/project/pallas_call | solution.py:173
  203.6 4.7 %all-to-all-start = ((bf16[8,64,256]{2,1,0:T(8,128)(2,1)}), bf16[8,64,256]{2,1,0:T(8,128)(2,1)}, u32[]{:S(2)}, u32[]{:S(2)}) async-start(bf16[8,64,256]{2,1,0:T(8,128)(2,1)} %bitcast.132), calls=%async_computation | async-start | bytes 524288 | tf_op jit(solution)/shard_map/all_to_all | solution.py:583
  210.4 2.5 order_blocks.1
  213.0 24.2 %attend.1.mixed_ref = bf16[512,1024]{1,0:T(8,128)(2,1)S(1)} custom-call(s32[1]{0:T(128)} %bitcast.half_ref, bf16[8,4,1,64,128]{4,3,2,1,0:T(8,128)(2,1)S(1)} %bitcast.118, bf16[8,4,1,64,128]{4,3,2,1,0:T(8,128)(2,1)S(1)} %bitcast.119, bf16[4096,128]{1,0:T(8,128)(2,1)S(1)} %get-tuple-element.75.refs_2_, bf16[4096,256]{1,0:T(8,128)(2,1)S(1)} %get-tuple-element.76.refs_3_, ...), custom_call_target="tpu_custom_call" | custom-call | flops 19327352832 | bytes 5636096 | tf_op jit(solution)/shard_map/attend/pallas_call | solution.py:411
  238.2 8.9 %output_product.2 = bf16[512,4096]{1,0:T(8,128)(2,1)} custom-call(bf16[512,1024]{1,0:T(8,128)(2,1)} %copy-done.2, bf16[1024,8192]{1,0:T(8,128)(2,1)} %weight_ref.3), custom_call_target="tpu_custom_call" | custom-call | flops 4294967296 | bytes 13631488 | tf_op jit(solution)/shard_map/output_product/pallas_call | solution.py:439
  248.4 8.8 %output_product.3 = bf16[512,4096]{1,0:T(8,128)(2,1)} custom-call(bf16[512,1024]{1,0:T(8,128)(2,1)} %copy-done.2, bf16[1024,8192]{1,0:T(8,128)(2,1)} %weight_ref.3), custom_call_target="tpu_custom_call" | custom-call | flops 4294967296 | bytes 13631488 | tf_op jit(solution)/shard_map/output_product/pallas_call | solution.py:439
  268.8 5.5 %collective-permute-done.24 = bf16[64,4096]{1,0:T(8,128)(2,1)S(1)} collective-permute-done((bf16[64,4096]{1,0:T(8,128)(2,1)}, bf16[64,4096]{1,0:T(8,128)(2,1)S(1)}, u32[]{:S(2)}, u32[]{:S(2)}) %collective-permute-start.24) | collective-permute-done | bytes 524320 | tf_op jit(solution)/shard_map/ppermute | solution.py:230
  277.6 8.0 %collective-permute-done.17 = bf16[64,4096]{1,0:T(8,128)(2,1)S(1)} collective-permute-done((bf16[64,4096]{1,0:T(8,128)(2,1)S(1)}, bf16[64,4096]{1,0:T(8,128)(2,1)S(1)}, u32[]{:S(2)}, u32[]{:S(2)}) %collective-permute-start.17) | collective-permute-done | bytes 524320 | tf_op jit(solution)/shard_map/ppermute | solution.py:230
  288.8 8.0 %collective-permute-done.25 = bf16[64,4096]{1,0:T(8,128)(2,1)S(1)} collective-permute-done((bf16[64,4096]{1,0:T(8,128)(2,1)S(1)}, bf16[64,4096]{1,0:T(8,128)(2,1)S(1)}, u32[]{:S(2)}, u32[]{:S(2)}) %collective-permute-start.25) | collective-permute-done | bytes 524320 | tf_op jit(solution)/shard_map/ppermute | solution.py:230
  300.6 3.5 %collective-permute-done.18 = bf16[64,4096]{1,0:T(8,128)(2,1)S(1)} collective-permute-done((bf16[64,4096]{1,0:T(8,128)(2,1)S(1)}, bf16[64,4096]{1,0:T(8,128)(2,1)S(1)}, u32[]{:S(2)}, u32[]{:S(2)}) %collective-permute-start.18) | collective-permute-done | bytes 524320 | tf_op jit(solution)/shard_map/ppermute | solution.py:230
  306.0 5.2 %collective-permute-done.28 = bf16[64,4096]{1,0:T(8,128)(2,1)S(1)} collective-permute-done((bf16[64,4096]{1,0:T(8,128)(2,1)S(1)}, bf16[64,4096]{1,0:T(8,128)(2,1)S(1)}, u32[]{:S(2)}, u32[]{:S(2)}) %collective-permute-start.28) | collective-permute-done | bytes 524320 | tf_op jit(solution)/shard_map/ppermute | solution.py:230
  312.4 2.5 collective-permute-start.29
  314.9 6.0 %collective-permute-done.19 = bf16[64,4096]{1,0:T(8,128)(2,1)S(1)} collective-permute-done((bf16[64,4096]{1,0:T(8,128)(2,1)S(1)}, bf16[64,4096]{1,0:T(8,128)(2,1)S(1)}, u32[]{:S(2)}, u32[]{:S(2)}) %collective-permute-start.19) | collective-permute-done | bytes 524320 | tf_op jit(solution)/shard_map/ppermute | solution.py:230
  324.3 3.5 collective-permute-done.29
  331.0 4.7 %collective-permute-done.22 = bf16[64,4096]{1,0:T(8,128)(2,1)S(1)} collective-permute-done((bf16[64,4096]{1,0:T(8,128)(2,1)S(1)}, bf16[64,4096]{1,0:T(8,128)(2,1)S(1)}, u32[]{:S(2)}, u32[]{:S(2)}) %collective-permute-start.22) | collective-permute-done | bytes 524320 | tf_op jit(solution)/shard_map/ppermute | solution.py:230
  337.9 3.4 collective-permute-done.30
  342.6 4.4 %collective-permute-done.23 = bf16[64,4096]{1,0:T(8,128)(2,1)S(1)} collective-permute-done((bf16[64,4096]{1,0:T(8,128)(2,1)S(1)}, bf16[64,4096]{1,0:T(8,128)(2,1)S(1)}, u32[]{:S(2)}, u32[]{:S(2)}) %collective-permute-start.23) | collective-permute-done | bytes 524320 | tf_op jit(solution)/shard_map/ppermute | solution.py:230
  (144 shorter events, 64.6 us)
Async XLA Ops:
  6.3 30.6 %collective-permute-start.1 = (bf16[32,16,2048]{2,1,0:T(8,128)(2,1)S(1)}, bf16[32,16,2048]{2,1,0:T(8,128)(2,1)S(1)}, u32[]{:S(2)}, u32[]{:S(2)}) collective-permute-start(bf16[32,16,2048]{2,1,0:T(8,128)(2,1)S(1)} %pick_blocks.1), channel_id=1, source_target_pairs={{0,1},{1,0},{2,3},{3,2},{4,5},{5,4},{6,7},{7,6},{8,9},{9,8},{10,11... | collective-permute-start | bytes 6291464 | tf_op jit(solution)/shard_map/ppermute | solution.py:508
  8.4 4.5 %collective-permute-start.4 = (bf16[64,8192]{1,0:T(8,128)(2,1)}, bf16[64,8192]{1,0:T(8,128)(2,1)}, u32[]{:S(2)}, u32[]{:S(2)}) collective-permute-start(bf16[64,8192]{1,0:T(8,128)(2,1)} %fusion.2.refs_0_), channel_id=1, source_target_pairs={{0,1},{1,0},{2,3},{3,2},{4,8},{5,9},{6,10},{7,11},{8,4},{9,5},{10,... | collective-permute-start | bytes 3145736 | tf_op jit(solution)/shard_map/ppermute | solution.py:64
  8.7 33.4 %collective-permute-start = (bf16[64,8192]{1,0:T(8,128)(2,1)}, bf16[64,8192]{1,0:T(8,128)(2,1)}, u32[]{:S(2)}, u32[]{:S(2)}) collective-permute-start(bf16[64,8192]{1,0:T(8,128)(2,1)} %fusion.2.refs_0_), channel_id=1, source_target_pairs={{0,4},{2,6},{4,0},{6,2},{8,12},{10,14},{12,8},{14,10},{1,5},{3,7},... | collective-permute-start | bytes 3145736 | tf_op jit(solution)/shard_map/ppermute | solution.py:53
  12.9 47.9 %collective-permute-start.9 = (bf16[64,8192]{1,0:T(8,128)(2,1)}, bf16[64,8192]{1,0:T(8,128)(2,1)}, u32[]{:S(2)}, u32[]{:S(2)}) collective-permute-start(bf16[64,8192]{1,0:T(8,128)(2,1)} %collective-permute-done.4), channel_id=1, source_target_pairs={{0,4},{2,6},{4,0},{6,2},{8,12},{10,14},{12,8},{14,10},{1,5},{3,7},... | collective-permute-start | bytes 3145736 | tf_op jit(solution)/shard_map/ppermute | solution.py:53
  42.2 22.1 %collective-permute-start.2 = (bf16[64,8192]{1,0:T(8,128)(2,1)}, bf16[64,8192]{1,0:T(8,128)(2,1)}, u32[]{:S(2)}, u32[]{:S(2)}) collective-permute-start(bf16[64,8192]{1,0:T(8,128)(2,1)} %collective-permute-done.refs_1_), channel_id=1, source_target_pairs={{0,1},{1,0},{2,3},{3,2},{4,8},{5,9},{6,10},{7,11},{8,4},{9,5},{10,... | collective-permute-start | bytes 3145736 | tf_op jit(solution)/shard_map/ppermute | solution.py:64
  42.3 116.7 %collective-permute-start.7 = (bf16[64,8192]{1,0:T(8,128)(2,1)}, bf16[64,8192]{1,0:T(8,128)(2,1)}, u32[]{:S(2)}, u32[]{:S(2)}) collective-permute-start(bf16[64,8192]{1,0:T(8,128)(2,1)} %fusion.2.refs_0_), channel_id=1, source_target_pairs={{0,2},{2,0},{4,6},{6,4},{8,10},{10,8},{12,14},{14,12},{1,3},{3,1},... | collective-permute-start | bytes 3145736 | tf_op jit(solution)/shard_map/ppermute | solution.py:53
  47.7 44.9 %collective-permute-start.6 = (bf16[2,32,16,256]{3,2,1,0:T(8,128)(2,1)S(1)}, bf16[2,32,16,256]{3,2,1,0:T(8,128)(2,1)S(1)}, u32[]{:S(2)}, u32[]{:S(2)}) collective-permute-start(bf16[2,32,16,256]{3,2,1,0:T(8,128)(2,1)S(1)} %get-tuple-element.46), channel_id=1, source_target_pairs={{0,12},{2,14},{4,8},{6,10},{8,4},{10,6},{12,0},{14,2},{1,13},{3,15... | collective-permute-start | bytes 1572872 | tf_op jit(solution)/shard_map/ppermute | solution.py:53
  50.1 44.0 %collective-permute-start.8 = (bf16[64,8192]{1,0:T(8,128)(2,1)}, bf16[64,8192]{1,0:T(8,128)(2,1)S(1)}, u32[]{:S(2)}, u32[]{:S(2)}) collective-permute-start(bf16[64,8192]{1,0:T(8,128)(2,1)} %collective-permute-done.refs_1_), channel_id=1, source_target_pairs={{0,2},{2,0},{4,6},{6,4},{8,10},{10,8},{12,14},{14,12},{1,3},{3,1},... | collective-permute-start | bytes 3145736 | tf_op jit(solution)/shard_map/ppermute | solution.py:53
  60.8 95.4 %collective-permute-start.5 = (bf16[2,32,16,256]{3,2,1,0:T(8,128)(2,1)}, bf16[2,32,16,256]{3,2,1,0:T(8,128)(2,1)S(1)}, u32[]{:S(2)}, u32[]{:S(2)}) collective-permute-start(bf16[2,32,16,256]{3,2,1,0:T(8,128)(2,1)} %get-tuple-element.49), channel_id=1, source_target_pairs={{0,8},{2,10},{4,12},{6,14},{8,0},{10,2},{12,4},{14,6},{1,9},{3,11}... | collective-permute-start | bytes 1572872 | tf_op jit(solution)/shard_map/ppermute | solution.py:53
  64.3 70.7 %collective-permute-start.3 = (bf16[64,8192]{1,0:T(8,128)(2,1)}, bf16[64,8192]{1,0:T(8,128)(2,1)S(1)}, u32[]{:S(2)}, u32[]{:S(2)}) collective-permute-start(bf16[64,8192]{1,0:T(8,128)(2,1)} %collective-permute-done.2), channel_id=1, source_target_pairs={{0,4},{2,6},{4,0},{6,2},{8,12},{10,14},{12,8},{14,10},{1,5},{3,7},... | collective-permute-start | bytes 3145736 | tf_op jit(solution)/shard_map/ppermute | solution.py:53
  92.5 43.6 %collective-permute-start.12 = (bf16[64,8192]{1,0:T(8,128)(2,1)S(1)}, bf16[64,8192]{1,0:T(8,128)(2,1)S(1)}, u32[]{:S(2)}, u32[]{:S(2)}) collective-permute-start(bf16[64,8192]{1,0:T(8,128)(2,1)S(1)} %broadcast_select_fusion.refs_0_), channel_id=1, source_target_pairs={{0,2},{2,0},{4,6},{6,4},{8,10},{10,8},{12,14},{14,12},{1,3},{3,1},... | collective-permute-start | bytes 3145736 | tf_op jit(solution)/shard_map/ppermute | solution.py:53
  94.1 57.3 %collective-permute-start.10 = (bf16[2,32,16,256]{3,2,1,0:T(8,128)(2,1)S(1)}, bf16[2,32,16,256]{3,2,1,0:T(8,128)(2,1)S(1)}, u32[]{:S(2)}, u32[]{:S(2)}) collective-permute-start(bf16[2,32,16,256]{3,2,1,0:T(8,128)(2,1)S(1)} %get-tuple-element.53), channel_id=1, source_target_pairs={{0,10},{2,8},{4,14},{6,12},{8,2},{10,0},{12,6},{14,4},{1,11},{3,9}... | collective-permute-start | bytes 1572872 | tf_op jit(solution)/shard_map/ppermute | solution.py:53
  135.0 20.1 %collective-permute-start.11 = (bf16[2,32,16,256]{3,2,1,0:T(8,128)(2,1)}, bf16[2,32,16,256]{3,2,1,0:T(8,128)(2,1)S(1)}, u32[]{:S(2)}, u32[]{:S(2)}) collective-permute-start(bf16[2,32,16,256]{3,2,1,0:T(8,128)(2,1)} %get-tuple-element.55), channel_id=1, source_target_pairs={{0,4},{2,6},{4,0},{6,2},{8,12},{10,14},{12,8},{14,10},{1,5},{3,7},... | collective-permute-start | bytes 1572872 | tf_op jit(solution)/shard_map/ppermute | solution.py:53
  136.1 48.4 %collective-permute-start.13 = (bf16[64,8192]{1,0:T(8,128)(2,1)}, bf16[64,8192]{1,0:T(8,128)(2,1)}, u32[]{:S(2)}, u32[]{:S(2)}) collective-permute-start(bf16[64,8192]{1,0:T(8,128)(2,1)} %broadcast_select_fusion.1.refs_1_), channel_id=1, source_target_pairs={{0,2},{2,0},{4,6},{6,4},{8,10},{10,8},{12,14},{14,12},{1,3},{3,1},... | collective-permute-start | bytes 3145736 | tf_op jit(solution)/shard_map/ppermute | solution.py:53
  151.5 48.7 %collective-permute-start.15 = (bf16[2,32,16,256]{3,2,1,0:T(8,128)(2,1)}, bf16[2,32,16,256]{3,2,1,0:T(8,128)(2,1)S(1)}, u32[]{:S(2)}, u32[]{:S(2)}) collective-permute-start(bf16[2,32,16,256]{3,2,1,0:T(8,128)(2,1)} %copy-done.9), channel_id=1, source_target_pairs={{0,6},{2,4},{4,2},{6,0},{8,14},{10,12},{12,10},{14,8},{1,7},{3,5},... | collective-permute-start | bytes 1572872 | tf_op jit(solution)/shard_map/ppermute | solution.py:53
  155.1 45.0 %collective-permute-start.14 = (bf16[2,32,16,256]{3,2,1,0:T(8,128)(2,1)}, bf16[2,32,16,256]{3,2,1,0:T(8,128)(2,1)S(1)}, u32[]{:S(2)}, u32[]{:S(2)}) collective-permute-start(bf16[2,32,16,256]{3,2,1,0:T(8,128)(2,1)} %copy-done.8), channel_id=1, source_target_pairs={{0,2},{2,0},{4,6},{6,4},{8,10},{10,8},{12,14},{14,12},{1,3},{3,1},... | collective-permute-start | bytes 1572872 | tf_op jit(solution)/shard_map/ppermute | solution.py:53
  156.2 44.8 %collective-permute-start.16 = (bf16[2,32,16,256]{3,2,1,0:T(8,128)(2,1)}, bf16[2,32,16,256]{3,2,1,0:T(8,128)(2,1)S(1)}, u32[]{:S(2)}, u32[]{:S(2)}) collective-permute-start(bf16[2,32,16,256]{3,2,1,0:T(8,128)(2,1)} %copy-done.7), channel_id=1, source_target_pairs={{0,14},{2,12},{4,10},{6,8},{8,6},{10,4},{12,2},{14,0},{1,15},{3,13... | collective-permute-start | bytes 1572872 | tf_op jit(solution)/shard_map/ppermute | solution.py:53
  203.6 34.6 %all-to-all-start = ((bf16[8,64,256]{2,1,0:T(8,128)(2,1)}), bf16[8,64,256]{2,1,0:T(8,128)(2,1)}, u32[]{:S(2)}, u32[]{:S(2)}) async-start(bf16[8,64,256]{2,1,0:T(8,128)(2,1)} %bitcast.132), calls=%async_computation | async-start | bytes 524288 | tf_op jit(solution)/shard_map/all_to_all | solution.py:583
  259.3 15.1 %collective-permute-start.24 = (bf16[64,4096]{1,0:T(8,128)(2,1)}, bf16[64,4096]{1,0:T(8,128)(2,1)S(1)}, u32[]{:S(2)}, u32[]{:S(2)}) collective-permute-start(bf16[64,4096]{1,0:T(8,128)(2,1)} %get-tuple-element.87), channel_id=1, source_target_pairs={{0,4},{4,8},{8,12},{12,14},{14,10},{10,6},{6,2},{2,0},{1,5},{5,9},... | collective-permute-start | bytes 1572872 | tf_op jit(solution)/shard_map/ppermute | solution.py:230
  264.6 24.2 %collective-permute-start.27 = (bf16[64,4096]{1,0:T(8,128)(2,1)S(1)}, bf16[64,4096]{1,0:T(8,128)(2,1)}, u32[]{:S(2)}, u32[]{:S(2)}) collective-permute-start(bf16[64,4096]{1,0:T(8,128)(2,1)S(1)} %get-tuple-element.88), channel_id=1, source_target_pairs={{0,2},{4,0},{8,4},{12,8},{14,12},{10,14},{6,10},{2,6},{1,3},{5,1},... | collective-permute-start | bytes 1572872 | tf_op jit(solution)/shard_map/ppermute | solution.py:230
  264.6 20.9 %collective-permute-start.17 = (bf16[64,4096]{1,0:T(8,128)(2,1)S(1)}, bf16[64,4096]{1,0:T(8,128)(2,1)S(1)}, u32[]{:S(2)}, u32[]{:S(2)}) collective-permute-start(bf16[64,4096]{1,0:T(8,128)(2,1)S(1)} %get-tuple-element.84), channel_id=1, source_target_pairs={{0,4},{4,8},{8,12},{12,14},{14,10},{10,6},{6,2},{2,0},{1,5},{5,9},... | collective-permute-start | bytes 1572872 | tf_op jit(solution)/shard_map/ppermute | solution.py:230
  266.7 48.3 %collective-permute-start.21 = (bf16[64,4096]{1,0:T(8,128)(2,1)S(1)}, bf16[64,4096]{1,0:T(8,128)(2,1)}, u32[]{:S(2)}, u32[]{:S(2)}) collective-permute-start(bf16[64,4096]{1,0:T(8,128)(2,1)S(1)} %get-tuple-element.85), channel_id=1, source_target_pairs={{0,2},{4,0},{8,4},{12,8},{14,12},{10,14},{6,10},{2,6},{1,3},{5,1},... | collective-permute-start | bytes 1572872 | tf_op jit(solution)/shard_map/ppermute | solution.py:230
  275.5 21.3 %collective-permute-start.25 = (bf16[64,4096]{1,0:T(8,128)(2,1)S(1)}, bf16[64,4096]{1,0:T(8,128)(2,1)S(1)}, u32[]{:S(2)}, u32[]{:S(2)}) collective-permute-start(bf16[64,4096]{1,0:T(8,128)(2,1)S(1)} %fusion.6), channel_id=1, source_target_pairs={{0,4},{4,8},{8,12},{12,14},{14,10},{10,6},{6,2},{2,0},{1,5},{5,9},... | collective-permute-start | bytes 1572872 | tf_op jit(solution)/shard_map/ppermute | solution.py:230
  286.7 17.3 %collective-permute-start.18 = (bf16[64,4096]{1,0:T(8,128)(2,1)S(1)}, bf16[64,4096]{1,0:T(8,128)(2,1)S(1)}, u32[]{:S(2)}, u32[]{:S(2)}) collective-permute-start(bf16[64,4096]{1,0:T(8,128)(2,1)S(1)} %fusion.12), channel_id=1, source_target_pairs={{0,4},{4,8},{8,12},{12,14},{14,10},{10,6},{6,2},{2,0},{1,5},{5,9},... | collective-permute-start | bytes 1572872 | tf_op jit(solution)/shard_map/ppermute | solution.py:230
  298.4 12.8 %collective-permute-start.28 = (bf16[64,4096]{1,0:T(8,128)(2,1)S(1)}, bf16[64,4096]{1,0:T(8,128)(2,1)S(1)}, u32[]{:S(2)}, u32[]{:S(2)}) collective-permute-start(bf16[64,4096]{1,0:T(8,128)(2,1)S(1)} %get-tuple-element.95), channel_id=1, source_target_pairs={{0,2},{4,0},{8,4},{12,8},{14,12},{10,14},{6,10},{2,6},{1,3},{5,1},... | collective-permute-start | bytes 1572872 | tf_op jit(solution)/shard_map/ppermute | solution.py:230
  300.5 37.5 %collective-permute-start.26 = (bf16[64,4096]{1,0:T(8,128)(2,1)S(1)}, bf16[64,4096]{1,0:T(8,128)(2,1)S(1)}, u32[]{:S(2)}, u32[]{:S(2)}) collective-permute-start(bf16[64,4096]{1,0:T(8,128)(2,1)S(1)} %get-tuple-element.94), channel_id=1, source_target_pairs={{0,4},{4,8},{8,12},{12,14},{14,10},{10,6},{6,2},{2,0},{1,5},{5,9},... | collective-permute-start | bytes 1572872 | tf_op jit(solution)/shard_map/ppermute | solution.py:230
  304.2 16.7 %collective-permute-start.19 = (bf16[64,4096]{1,0:T(8,128)(2,1)S(1)}, bf16[64,4096]{1,0:T(8,128)(2,1)S(1)}, u32[]{:S(2)}, u32[]{:S(2)}) collective-permute-start(bf16[64,4096]{1,0:T(8,128)(2,1)S(1)} %fusion.13), channel_id=1, source_target_pairs={{0,4},{4,8},{8,12},{12,14},{14,10},{10,6},{6,2},{2,0},{1,5},{5,9},... | collective-permute-start | bytes 1572872 | tf_op jit(solution)/shard_map/ppermute | solution.py:230
  312.4 15.4 %collective-permute-start.29 = (bf16[64,4096]{1,0:T(8,128)(2,1)S(1)}, bf16[64,4096]{1,0:T(8,128)(2,1)S(1)}, u32[]{:S(2)}, u32[]{:S(2)}) collective-permute-start(bf16[64,4096]{1,0:T(8,128)(2,1)S(1)} %fusion.4), channel_id=1, source_target_pairs={{0,2},{4,0},{8,4},{12,8},{14,12},{10,14},{6,10},{2,6},{1,3},{5,1},... | collective-permute-start | bytes 1572872 | tf_op jit(solution)/shard_map/ppermute | solution.py:230
  322.2 13.5 %collective-permute-start.22 = (bf16[64,4096]{1,0:T(8,128)(2,1)S(1)}, bf16[64,4096]{1,0:T(8,128)(2,1)S(1)}, u32[]{:S(2)}, u32[]{:S(2)}) collective-permute-start(bf16[64,4096]{1,0:T(8,128)(2,1)S(1)} %get-tuple-element.93), channel_id=1, source_target_pairs={{0,2},{4,0},{8,4},{12,8},{14,12},{10,14},{6,10},{2,6},{1,3},{5,1},... | collective-permute-start | bytes 1572872 | tf_op jit(solution)/shard_map/ppermute | solution.py:230
  324.0 18.6 %collective-permute-start.20 = (bf16[64,4096]{1,0:T(8,128)(2,1)S(1)}, bf16[64,4096]{1,0:T(8,128)(2,1)S(1)}, u32[]{:S(2)}, u32[]{:S(2)}) collective-permute-start(bf16[64,4096]{1,0:T(8,128)(2,1)S(1)} %get-tuple-element.92), channel_id=1, source_target_pairs={{0,4},{4,8},{8,12},{12,14},{14,10},{10,6},{6,2},{2,0},{1,5},{5,9},... | collective-permute-start | bytes 1572872 | tf_op jit(solution)/shard_map/ppermute | solution.py:230
  328.9 12.4 %collective-permute-start.30 = (bf16[64,4096]{1,0:T(8,128)(2,1)S(1)}, bf16[64,4096]{1,0:T(8,128)(2,1)S(1)}, u32[]{:S(2)}, u32[]{:S(2)}) collective-permute-start(bf16[64,4096]{1,0:T(8,128)(2,1)S(1)} %fusion.5), channel_id=1, source_target_pairs={{0,2},{4,0},{8,4},{12,8},{14,12},{10,14},{6,10},{2,6},{1,3},{5,1},... | collective-permute-start | bytes 1572872 | tf_op jit(solution)/shard_map/ppermute | solution.py:230
  335.9 11.1 %collective-permute-start.23 = (bf16[64,4096]{1,0:T(8,128)(2,1)S(1)}, bf16[64,4096]{1,0:T(8,128)(2,1)S(1)}, u32[]{:S(2)}, u32[]{:S(2)}) collective-permute-start(bf16[64,4096]{1,0:T(8,128)(2,1)S(1)} %fusion.11), channel_id=1, source_target_pairs={{0,2},{4,0},{8,4},{12,8},{14,12},{10,14},{6,10},{2,6},{1,3},{5,1},... | collective-permute-start | bytes 1572872 | tf_op jit(solution)/shard_map/ppermute | solution.py:230
  (28 other events, 593.7 us)

commit v7 on v6

--- a/solution.py
+++ b/solution.py
@@ -16,6 +16,7 @@
 VMEM_LIMIT = 56 * 1024 * 1024
 ATTEND_VMEM = 28 * 1024 * 1024
 COLUMN_CHUNKS = 2
+STREAMS = 4
 LINE_MODELS = 8
 
 
@@ -77,35 +78,35 @@
     beside = swap(own, 2)
     over = cross(own)
     own_y = swap(own, 1)
-    exchange(6)
-    beside = after(beside, outgoing[6])
     over_beside = cross(beside)
     over_passed = swap(over, 2)
     beside_y = swap(beside, 1)
-    exchange(4, over)
-    over_beside_passed = swap(over_beside, 2)
     far_first = jnp.where(middle, over, over_passed)
     far_first_y = swap(far_first, 1)
-    exchange(5, arrived[6], over_beside)
-    exchange(2, over_passed, beside_y)
+    over_beside_passed = swap(over_beside, 2)
+    exchange(4, over_beside)
+    exchange(6, over_beside, far_first)
     far_second = jnp.where(middle, over_beside, over_beside_passed)
     far_second_y = swap(far_second, 1)
-    exchange(7, arrived[4], far_second)
-    exchange(3, far_first_y)
-    exchange(1, far_first_y, arrived[2])
-    near = [after(own, far_second, arrived[4], arrived[6]), beside, own_y, beside_y]
-    far = [after(far_first, arrived[5], arrived[2]), far_second, far_first_y, far_second_y]
+    exchange(5, arrived[4], far_second)
+    exchange(2, arrived[4], far_second)
+    exchange(7, arrived[6], far_first_y)
+    exchange(3, arrived[6], far_first_y)
+    exchange(1, arrived[6], far_first_y)
+    near = [after(own, far_second, arrived[4]), beside, own_y, beside_y]
+    far = [after(far_first, arrived[6]), far_second, far_first_y, far_second_y]
     return near, far, [arrived[apart] for apart in range(LINE_MODELS)]
 
 
 def project_kernel(starts_ref, *refs):
     n_blocks = starts_ref.shape[0]
-    blocks = refs[:n_blocks]
-    weights = refs[n_blocks : n_blocks + 3]
-    q_bias_ref, k_bias_ref, v_bias_ref, cos_ref, sin_ref = refs[n_blocks + 3 : n_blocks + 8]
-    query_ref, key_ref, value_ref, pair_ref, tokens_ref, total_ref, sems = refs[n_blocks + 8 :]
+    blocks, refs = refs[:n_blocks], refs[n_blocks:]
+    q_weights, (k_weight_ref, v_weight_ref), refs = refs[:STREAMS], refs[STREAMS:][:2], refs[STREAMS + 2 :]
+    q_bias_ref, k_bias_ref, v_bias_ref, cos_ref, sin_ref = refs[:5]
+    query_ref, key_ref, value_ref, pair_ref, tokens_ref, total_ref, sems = refs[5:]
     step = pl.program_id(0)
-    depth, q_width = weights[0].shape
+    depth = k_weight_ref.shape[0]
+    q_width = q_weights[0].shape[1]
     rows = blocks[0].shape[0]
 
     @pl.when(step == 0)
@@ -125,10 +126,9 @@
             copy.wait()
 
     tokens = tokens_ref[:, pl.ds(pl.multiple_of(step * depth, depth), depth)]
-    total_ref[:, :q_width] += jnp.dot(
-        tokens, weights[0][...], preferred_element_type=jnp.float32
-    )
-    both = jnp.concatenate([weights[1][...], weights[2][...]], axis=1)
+    q_weight = jnp.concatenate([ref[...] for ref in q_weights], axis=0)
+    total_ref[:, :q_width] += jnp.dot(tokens, q_weight, preferred_element_type=jnp.float32)
+    both = jnp.concatenate([k_weight_ref[...], v_weight_ref[...]], axis=1)
     total_ref[:, q_width:] += jnp.dot(tokens, both, preferred_element_type=jnp.float32)
 
     @pl.when(step == pl.num_programs(0) - 1)
@@ -162,7 +162,11 @@
     fixed = lambda array: pl.BlockSpec(array.shape, lambda step: (0,) * len(array.shape))
     in_specs = [pl.BlockSpec(memory_space=pltpu.SMEM)]
     in_specs += [pl.BlockSpec(memory_space=pl.ANY)] * len(blocks)
-    in_specs += [pl.BlockSpec((depth, weight.shape[1]), lambda step: (step, 0)) for weight in weights]
+    in_specs += [
+        pl.BlockSpec((depth // STREAMS, q_width), lambda step, part=part: (step * STREAMS + part, 0))
+        for part in range(STREAMS)
+    ]
+    in_specs += [pl.BlockSpec((depth, HD), lambda step: (step, 0))] * 2
     in_specs += [fixed(array) for array in (*biases, *tables)]
     out_shape = (
         jax.ShapeDtypeStruct((q_width // HD, rows, HD), jnp.bfloat16),
@@ -188,7 +192,7 @@
             transcendentals=0,
         ),
         name="project",
-    )(starts, *blocks, *weights, *biases, *tables)
+    )(starts, *blocks, *weights[:1] * STREAMS, *weights[1:], *biases, *tables)
 
 
 class RingScatter:
@@ -425,9 +429,11 @@
     )(half, *queries, *fixed)
 
 
-def output_kernel(mixed_ref, weight_ref, out_ref):
+def output_kernel(mixed_ref, *refs):
+    *weight_refs, out_ref = refs
+    weight = jnp.concatenate([ref[...] for ref in weight_refs], axis=0)
     out_ref[...] = jnp.dot(
-        mixed_ref[...], weight_ref[...], preferred_element_type=jnp.float32
+        mixed_ref[...], weight, preferred_element_type=jnp.float32
     ).astype(jnp.bfloat16)
 
 
@@ -440,9 +446,10 @@
         output_kernel,
         grid=(tiles,),
         out_shape=jax.ShapeDtypeStruct((rows, width), jnp.bfloat16),
-        in_specs=[
-            pl.BlockSpec((rows, depth), lambda col: (0, 0)),
-            pl.BlockSpec((depth, tile), lambda col: (0, chunk * tiles + col)),
+        in_specs=[pl.BlockSpec((rows, depth), lambda col: (0, 0))]
+        + [
+            pl.BlockSpec((depth // STREAMS, tile), lambda col, part=part: (part, chunk * tiles + col))
+            for part in range(STREAMS)
         ],
         out_specs=pl.BlockSpec((rows, tile), lambda col: (0, col)),
         compiler_params=pltpu.CompilerParams(vmem_limit_bytes=VMEM_LIMIT),
@@ -452,7 +459,7 @@
             transcendentals=0,
         ),
         name="output_product",
-    )(mixed, weight)
+    )(mixed, *[weight] * STREAMS)
 
 
 def on_device(

time: 350 us -> 331 us (0.946)
  starting transfers between devices: 111 us -> 75.3 us
  waiting for transfers between devices: 103 us -> 115 us
    ppermute x14, starting transfers between devices: 84.3 us -> 44.5 us  [swap(): lax.ppermute(block, 'mp', [(index, index ^ mask) for index in range(LINE_...]
    ppermute x14, waiting for transfers between devices: 52.2 us -> 63.7 us  [send(): self.moving[way] = lax.ppermute(self.moving[way], 'mp', pairs)]
    all_to_all x1, starting transfers between devices: 4.75 us -> 9.62 us  [on_device(): pairs = lax.all_to_all(pairs, 'mp', split_axis=0, concat_axis=0, tiled=True)]
    unnamed x57 -> x51, local copies, waits for them, and re-layouts: 9.46 us -> 9.14 us
  transfers between devices with their start and end apart: 32 -> 32, of which waited for: 13 -> 14; matrix products, arithmetic and copies ran while one was open for 7% -> 8% of each run, Pallas kernels for 17% -> 19%
where the time goes in v7:
time: 331 us; the launch traced here: 329 us
  waiting for transfers between devices  115 us (35%)
  Pallas kernels  80.7 us (24%)
  starting transfers between devices  75.3 us (23%)
  other arithmetic  27.8 us (8%)
  local copies, waits for them, and re-layouts  17.3 us (5%)
  between operations  12.8 us (4%)
    ppermute x14, waiting for transfers between devices, send(): self.moving[way] = lax.ppermute(self.moving[way], 'mp', pairs)  63.7 us
    ppermute x14, waiting for transfers between devices, swap(): lax.ppermute(block, 'mp', [(index, index ^ mask) for index in range(LINE_...  51.7 us
    ppermute x14, starting transfers between devices, swap(): lax.ppermute(block, 'mp', [(index, index ^ mask) for index in range(LINE_...  44.5 us
    pallas_call x2, Pallas kernels, project(): pl.pallas_call(project_kernel, grid=(width // depth,), out_shape=out_shap...  31.3 us
    pallas_call x1, Pallas kernels, attend(): pl.pallas_call(functools.partial(attend_kernel, span, row_step, chunk), g...  24.2 us
    ppermute x14, starting transfers between devices, send(): self.moving[way] = lax.ppermute(self.moving[way], 'mp', pairs)  21.1 us
    pallas_call x2, Pallas kernels, output_product(): pl.pallas_call(output_kernel, grid=(tiles,), out_shape=jax.ShapeDtypeStru...  18.1 us
    all_to_all x1, starting transfers between devices, on_device(): pairs = lax.all_to_all(pairs, 'mp', split_axis=0, concat_axis=0, tiled=True)  9.62 us
  transfers between devices with their start and end apart: 32, of which 14 were waited for; matrix products, arithmetic and copies ran while one was open for 8% of the time, Pallas kernels for 19%

profile of v7, /device:TPU:0, one launch (start us, length us, event | category | flops | bytes accessed | tf_op | source)
XLA Modules:
  0.0 329.3 jit_solution(4988472158641232620)
XLA Ops:
  2.9 2.5 fusion.2.refs_0_
  5.4 3.0 collective-permute-start
  10.0 21.9 %collective-permute-done.refs_1_ = bf16[64,8192]{1,0:T(8,128)(2,1)} collective-permute-done((bf16[64,8192]{1,0:T(8,128)(2,1)}, bf16[64,8192]{1,0:T(8,128)(2,1)}, u32[]{:S(2)}, u32[]{:S(2)}) %collective-permute-start) | collective-permute-done | bytes 1048608 | tf_op jit(solution)/shard_map/ppermute | solution.py:54
  31.9 3.3 %collective-permute-start.8 = (bf16[64,8192]{1,0:T(8,128)(2,1)S(1)}, bf16[64,8192]{1,0:T(8,128)(2,1)}, u32[]{:S(2)}, u32[]{:S(2)}) collective-permute-start(bf16[64,8192]{1,0:T(8,128)(2,1)S(1)} %collective-permute-done.7), channel_id=1, source_target_pairs={{0,4},{2,6},{4,0},{6,2},{8,12},{10,14},{12,8},{14,10},{1,5},{3,7},... | collective-permute-start | bytes 3145736 | tf_op jit(solution)/shard_map/ppermute | solution.py:54
  37.9 2.2 copy-done
  43.3 14.7 %collective-permute-start.2 = (bf16[64,8192]{1,0:T(8,128)(2,1)}, bf16[64,8192]{1,0:T(8,128)(2,1)S(1)}, u32[]{:S(2)}, u32[]{:S(2)}) collective-permute-start(bf16[64,8192]{1,0:T(8,128)(2,1)} %collective-permute-done.1), channel_id=1, source_target_pairs={{0,4},{2,6},{4,0},{6,2},{8,12},{10,14},{12,8},{14,10},{1,5},{3,7},... | collective-permute-start | bytes 3145736 | tf_op jit(solution)/shard_map/ppermute | solution.py:54
  61.3 2.2 copy-done.1
  63.4 3.8 %pack_blocks.1 = (bf16[2,32,16,256]{3,2,1,0:T(8,128)(2,1)S(1)}, bf16[2,32,16,256]{3,2,1,0:T(8,128)(2,1)}, bf16[2,32,16,256]{3,2,1,0:T(8,128)(2,1)}, bf16[2,32,16...) custom-call(s32[2,32]{1,0:T(2,128)S(1)} %pad_add_fusion.slots_ref, ...), custom_call_target="tpu_custom_call" | custom-call | tf_op jit(solution)/shard_map/pack_blocks/pallas_call | solution.py:293
  67.3 3.6 %collective-permute-start.9 = (bf16[2,32,16,256]{3,2,1,0:T(8,128)(2,1)S(1)}, bf16[2,32,16,256]{3,2,1,0:T(8,128)(2,1)S(1)}, u32[]{:S(2)}, u32[]{:S(2)}) collective-permute-start(bf16[2,32,16,256]{3,2,1,0:T(8,128)(2,1)S(1)} %get-tuple-element.51), channel_id=1, source_target_pairs={{0,12},{2,14},{4,8},{6,10},{8,4},{10,6},{12,0},{14,2},{1,13},{3,15... | collective-permute-start | bytes 1572872 | tf_op jit(solution)/shard_map/ppermute | solution.py:54
  70.9 11.1 %collective-permute-done.2 = bf16[64,8192]{1,0:T(8,128)(2,1)S(1)} collective-permute-done((bf16[64,8192]{1,0:T(8,128)(2,1)}, bf16[64,8192]{1,0:T(8,128)(2,1)S(1)}, u32[]{:S(2)}, u32[]{:S(2)}) %collective-permute-start.2) | collective-permute-done | bytes 1048608 | tf_op jit(solution)/shard_map/ppermute | solution.py:54
  87.7 6.1 %collective-permute-done.9 = bf16[2,32,16,256]{3,2,1,0:T(8,128)(2,1)S(1)} collective-permute-done((bf16[2,32,16,256]{3,2,1,0:T(8,128)(2,1)S(1)}, bf16[2,32,16,256]{3,2,1,0:T(8,128)(2,1)S(1)}, u32[]{:S(2)}, u32[]{:S(2)}) %collective-permute-start.9) | collective-permute-done | bytes 524320 | tf_op jit(solution)/shard_map/ppermute | solution.py:54
  93.8 6.4 %collective-permute-start.4 = (bf16[2,32,16,256]{3,2,1,0:T(8,128)(2,1)S(1)}, bf16[2,32,16,256]{3,2,1,0:T(8,128)(2,1)S(1)}, u32[]{:S(2)}, u32[]{:S(2)}) collective-permute-start(bf16[2,32,16,256]{3,2,1,0:T(8,128)(2,1)S(1)} %get-tuple-element.47), channel_id=1, source_target_pairs={{0,8},{2,10},{4,12},{6,14},{8,0},{10,2},{12,4},{14,6},{1,9},{3,11}... | collective-permute-start | bytes 1572872 | tf_op jit(solution)/shard_map/ppermute | solution.py:54
  111.4 2.2 pad_maximum_fusion
  122.6 15.6 %project.2 = (bf16[8,256,128]{2,1,0:T(8,128)(2,1)}, bf16[256,128]{1,0:T(8,128)(2,1)}, bf16[256,256]{1,0:T(8,128)(2,1)}, bf16[256,256]{1,0:T(8,128)(2,1)}) custom-call(s32[4]{0:T(128)} %add_multiply_fusion.starts_ref, bf16[64,8192]{1,0:T(8,128)(2,1)} %fusion.2.refs_0_, bf16[64,8192]{1,0:T(8,128)(2,1)} %collective-permute-done.refs_1_, ...), custom_call_target="tpu_custom_call" | custom-call | flops 5368709120 | bytes 26476544 | tf_op jit(solution)/shard_map/project/pallas_call | solution.py:177
  138.2 15.7 %project.3 = (bf16[8,256,128]{2,1,0:T(8,128)(2,1)}, bf16[256,128]{1,0:T(8,128)(2,1)}, bf16[256,256]{1,0:T(8,128)(2,1)}, bf16[256,256]{1,0:T(8,128)(2,1)}) custom-call(s32[4]{0:T(128)} %add_multiply_fusion.1.starts_ref, bf16[64,8192]{1,0:T(8,128)(2,1)} %copy-done.17, bf16[64,8192]{1,0:T(8,128)(2,1)} %broadcast_select_fusion.1.refs_1_, ...), custom_call_target="tpu_custom_call" | custom-call | flops 5368709120 | bytes 26476544 | tf_op jit(solution)/shard_map/project/pallas_call | solution.py:177
  154.0 10.5 %collective-permute-done.15 = bf16[2,32,16,256]{3,2,1,0:T(8,128)(2,1)S(1)} collective-permute-done((bf16[2,32,16,256]{3,2,1,0:T(8,128)(2,1)}, bf16[2,32,16,256]{3,2,1,0:T(8,128)(2,1)S(1)}, u32[]{:S(2)}, u32[]{:S(2)}) %collective-permute-start.15) | collective-permute-done | bytes 524320 | tf_op jit(solution)/shard_map/ppermute | solution.py:54
  167.9 9.6 %all-to-all-start = ((bf16[8,64,256]{2,1,0:T(8,128)(2,1)}), bf16[8,64,256]{2,1,0:T(8,128)(2,1)}, u32[]{:S(2)}, u32[]{:S(2)}) async-start(bf16[8,64,256]{2,1,0:T(8,128)(2,1)} %bitcast.132), calls=%async_computation | async-start | bytes 524288 | tf_op jit(solution)/shard_map/all_to_all | solution.py:590
  179.6 2.5 order_blocks.1
  182.2 24.2 %attend.1.mixed_ref = bf16[512,1024]{1,0:T(8,128)(2,1)S(1)} custom-call(s32[1]{0:T(128)} %bitcast.half_ref, bf16[8,4,1,64,128]{4,3,2,1,0:T(8,128)(2,1)S(1)} %bitcast.118, bf16[8,4,1,64,128]{4,3,2,1,0:T(8,128)(2,1)S(1)} %bitcast.119, bf16[4096,128]{1,0:T(8,128)(2,1)S(1)} %get-tuple-element.75.refs_2_, bf16[4096,256]{1,0:T(8,128)(2,1)S(1)} %get-tuple-element.76.refs_3_, ...), custom_call_target="tpu_custom_call" | custom-call | flops 19327352832 | bytes 5636096 | tf_op jit(solution)/shard_map/attend/pallas_call | solution.py:415
  207.4 9.1 %output_product.2 = bf16[512,4096]{1,0:T(8,128)(2,1)} custom-call(bf16[512,1024]{1,0:T(8,128)(2,1)} %copy-done.2, bf16[1024,8192]{1,0:T(8,128)(2,1)} %refs_3_.3, bf16[1024,8192]{1,0:T(8,128)(2,1)} %refs_3_.3, bf16[1024,8192]{1,0:T(8,128)(2,1)} %refs_3_.3, bf16[1024,8192]{1,0:T(8,128)(2,1)} %refs_3_.3), custom_call_target="tpu_custom_call" | custom-call | flops 4294967296 | bytes 13631488 | tf_op jit(solution)/shard_map/output_product/pallas_call | solution.py:445
  217.7 9.0 %output_product.3 = bf16[512,4096]{1,0:T(8,128)(2,1)} custom-call(bf16[512,1024]{1,0:T(8,128)(2,1)} %copy-done.2, bf16[1024,8192]{1,0:T(8,128)(2,1)} %refs_3_.3, bf16[1024,8192]{1,0:T(8,128)(2,1)} %refs_3_.3, bf16[1024,8192]{1,0:T(8,128)(2,1)} %refs_3_.3, bf16[1024,8192]{1,0:T(8,128)(2,1)} %refs_3_.3), custom_call_target="tpu_custom_call" | custom-call | flops 4294967296 | bytes 13631488 | tf_op jit(solution)/shard_map/output_product/pallas_call | solution.py:445
  226.7 2.1 dynamic-slice_bitcast_fusion
  238.3 5.6 %collective-permute-done.24 = bf16[64,4096]{1,0:T(8,128)(2,1)S(1)} collective-permute-done((bf16[64,4096]{1,0:T(8,128)(2,1)}, bf16[64,4096]{1,0:T(8,128)(2,1)S(1)}, u32[]{:S(2)}, u32[]{:S(2)}) %collective-permute-start.24) | collective-permute-done | bytes 524320 | tf_op jit(solution)/shard_map/ppermute | solution.py:234
  247.1 8.0 %collective-permute-done.17 = bf16[64,4096]{1,0:T(8,128)(2,1)S(1)} collective-permute-done((bf16[64,4096]{1,0:T(8,128)(2,1)S(1)}, bf16[64,4096]{1,0:T(8,128)(2,1)S(1)}, u32[]{:S(2)}, u32[]{:S(2)}) %collective-permute-start.17) | collective-permute-done | bytes 524320 | tf_op jit(solution)/shard_map/ppermute | solution.py:234
  258.4 8.0 %collective-permute-done.25 = bf16[64,4096]{1,0:T(8,128)(2,1)S(1)} collective-permute-done((bf16[64,4096]{1,0:T(8,128)(2,1)S(1)}, bf16[64,4096]{1,0:T(8,128)(2,1)S(1)}, u32[]{:S(2)}, u32[]{:S(2)}) %collective-permute-start.25) | collective-permute-done | bytes 524320 | tf_op jit(solution)/shard_map/ppermute | solution.py:234
  270.1 7.5 %collective-permute-done.18 = bf16[64,4096]{1,0:T(8,128)(2,1)S(1)} collective-permute-done((bf16[64,4096]{1,0:T(8,128)(2,1)S(1)}, bf16[64,4096]{1,0:T(8,128)(2,1)S(1)}, u32[]{:S(2)}, u32[]{:S(2)}) %collective-permute-start.18) | collective-permute-done | bytes 524320 | tf_op jit(solution)/shard_map/ppermute | solution.py:234
  279.8 2.3 collective-permute-done.28
  283.2 2.5 collective-permute-start.29
  285.8 9.4 %collective-permute-done.19 = bf16[64,4096]{1,0:T(8,128)(2,1)S(1)} collective-permute-done((bf16[64,4096]{1,0:T(8,128)(2,1)S(1)}, bf16[64,4096]{1,0:T(8,128)(2,1)S(1)}, u32[]{:S(2)}, u32[]{:S(2)}) %collective-permute-start.19) | collective-permute-done | bytes 524320 | tf_op jit(solution)/shard_map/ppermute | solution.py:234
  301.9 9.7 %collective-permute-done.22 = bf16[64,4096]{1,0:T(8,128)(2,1)S(1)} collective-permute-done((bf16[64,4096]{1,0:T(8,128)(2,1)S(1)}, bf16[64,4096]{1,0:T(8,128)(2,1)S(1)}, u32[]{:S(2)}, u32[]{:S(2)}) %collective-permute-start.22) | collective-permute-done | bytes 524320 | tf_op jit(solution)/shard_map/ppermute | solution.py:234
  313.6 8.9 %collective-permute-done.30 = bf16[64,4096]{1,0:T(8,128)(2,1)S(1)} collective-permute-done((bf16[64,4096]{1,0:T(8,128)(2,1)S(1)}, bf16[64,4096]{1,0:T(8,128)(2,1)S(1)}, u32[]{:S(2)}, u32[]{:S(2)}) %collective-permute-start.30) | collective-permute-done | bytes 524320 | tf_op jit(solution)/shard_map/ppermute | solution.py:234
  323.7 4.4 %collective-permute-done.23 = bf16[64,4096]{1,0:T(8,128)(2,1)S(1)} collective-permute-done((bf16[64,4096]{1,0:T(8,128)(2,1)S(1)}, bf16[64,4096]{1,0:T(8,128)(2,1)S(1)}, u32[]{:S(2)}, u32[]{:S(2)}) %collective-permute-start.23) | collective-permute-done | bytes 524320 | tf_op jit(solution)/shard_map/ppermute | solution.py:234
  (138 shorter events, 68.9 us)
Async XLA Ops:
  5.4 26.5 %collective-permute-start = (bf16[64,8192]{1,0:T(8,128)(2,1)}, bf16[64,8192]{1,0:T(8,128)(2,1)}, u32[]{:S(2)}, u32[]{:S(2)}) collective-permute-start(bf16[64,8192]{1,0:T(8,128)(2,1)} %fusion.2.refs_0_), channel_id=1, source_target_pairs={{0,4},{2,6},{4,0},{6,2},{8,12},{10,14},{12,8},{14,10},{1,5},{3,7},... | collective-permute-start | bytes 3145736 | tf_op jit(solution)/shard_map/ppermute | solution.py:54
  8.5 23.5 %collective-permute-start.7 = (bf16[64,8192]{1,0:T(8,128)(2,1)}, bf16[64,8192]{1,0:T(8,128)(2,1)S(1)}, u32[]{:S(2)}, u32[]{:S(2)}) collective-permute-start(bf16[64,8192]{1,0:T(8,128)(2,1)} %fusion.2.refs_0_), channel_id=1, source_target_pairs={{0,1},{1,0},{2,3},{3,2},{4,8},{5,9},{6,10},{7,11},{8,4},{9,5},{10,... | collective-permute-start | bytes 3145736 | tf_op jit(solution)/shard_map/ppermute | solution.py:65
  8.5 108.8 %collective-permute-start.5 = (bf16[64,8192]{1,0:T(8,128)(2,1)}, bf16[64,8192]{1,0:T(8,128)(2,1)}, u32[]{:S(2)}, u32[]{:S(2)}) collective-permute-start(bf16[64,8192]{1,0:T(8,128)(2,1)} %fusion.2.refs_0_), channel_id=1, source_target_pairs={{0,2},{2,0},{4,6},{6,4},{8,10},{10,8},{12,14},{14,12},{1,3},{3,1},... | collective-permute-start | bytes 3145736 | tf_op jit(solution)/shard_map/ppermute | solution.py:54
  31.9 11.4 %collective-permute-start.1 = (bf16[64,8192]{1,0:T(8,128)(2,1)}, bf16[64,8192]{1,0:T(8,128)(2,1)}, u32[]{:S(2)}, u32[]{:S(2)}) collective-permute-start(bf16[64,8192]{1,0:T(8,128)(2,1)} %collective-permute-done.refs_1_), channel_id=1, source_target_pairs={{0,1},{1,0},{2,3},{3,2},{4,8},{5,9},{6,10},{7,11},{8,4},{9,5},{10,... | collective-permute-start | bytes 3145736 | tf_op jit(solution)/shard_map/ppermute | solution.py:65
  31.9 26.1 %collective-permute-start.8 = (bf16[64,8192]{1,0:T(8,128)(2,1)S(1)}, bf16[64,8192]{1,0:T(8,128)(2,1)}, u32[]{:S(2)}, u32[]{:S(2)}) collective-permute-start(bf16[64,8192]{1,0:T(8,128)(2,1)S(1)} %collective-permute-done.7), channel_id=1, source_target_pairs={{0,4},{2,6},{4,0},{6,2},{8,12},{10,14},{12,8},{14,10},{1,5},{3,7},... | collective-permute-start | bytes 3145736 | tf_op jit(solution)/shard_map/ppermute | solution.py:54
  40.9 20.4 %collective-permute-start.3 = (bf16[32,16,2048]{2,1,0:T(8,128)(2,1)S(1)}, bf16[32,16,2048]{2,1,0:T(8,128)(2,1)}, u32[]{:S(2)}, u32[]{:S(2)}) collective-permute-start(bf16[32,16,2048]{2,1,0:T(8,128)(2,1)S(1)} %pick_blocks.1), channel_id=1, source_target_pairs={{0,1},{1,0},{2,3},{3,2},{4,5},{5,4},{6,7},{7,6},{8,9},{9,8},{10,11... | collective-permute-start | bytes 6291464 | tf_op jit(solution)/shard_map/ppermute | solution.py:515
  41.7 77.5 %collective-permute-start.6 = (bf16[64,8192]{1,0:T(8,128)(2,1)}, bf16[64,8192]{1,0:T(8,128)(2,1)}, u32[]{:S(2)}, u32[]{:S(2)}) collective-permute-start(bf16[64,8192]{1,0:T(8,128)(2,1)} %collective-permute-done.refs_1_), channel_id=1, source_target_pairs={{0,2},{2,0},{4,6},{6,4},{8,10},{10,8},{12,14},{14,12},{1,3},{3,1},... | collective-permute-start | bytes 3145736 | tf_op jit(solution)/shard_map/ppermute | solution.py:54
  43.3 38.7 %collective-permute-start.2 = (bf16[64,8192]{1,0:T(8,128)(2,1)}, bf16[64,8192]{1,0:T(8,128)(2,1)S(1)}, u32[]{:S(2)}, u32[]{:S(2)}) collective-permute-start(bf16[64,8192]{1,0:T(8,128)(2,1)} %collective-permute-done.1), channel_id=1, source_target_pairs={{0,4},{2,6},{4,0},{6,2},{8,12},{10,14},{12,8},{14,10},{1,5},{3,7},... | collective-permute-start | bytes 3145736 | tf_op jit(solution)/shard_map/ppermute | solution.py:54
  59.4 56.3 %collective-permute-start.10 = (bf16[64,8192]{1,0:T(8,128)(2,1)S(1)}, bf16[64,8192]{1,0:T(8,128)(2,1)}, u32[]{:S(2)}, u32[]{:S(2)}) collective-permute-start(bf16[64,8192]{1,0:T(8,128)(2,1)S(1)} %broadcast_select_fusion.refs_0_), channel_id=1, source_target_pairs={{0,2},{2,0},{4,6},{6,4},{8,10},{10,8},{12,14},{14,12},{1,3},{3,1},... | collective-permute-start | bytes 3145736 | tf_op jit(solution)/shard_map/ppermute | solution.py:54
  67.3 26.5 %collective-permute-start.9 = (bf16[2,32,16,256]{3,2,1,0:T(8,128)(2,1)S(1)}, bf16[2,32,16,256]{3,2,1,0:T(8,128)(2,1)S(1)}, u32[]{:S(2)}, u32[]{:S(2)}) collective-permute-start(bf16[2,32,16,256]{3,2,1,0:T(8,128)(2,1)S(1)} %get-tuple-element.51), channel_id=1, source_target_pairs={{0,12},{2,14},{4,8},{6,10},{8,4},{10,6},{12,0},{14,2},{1,13},{3,15... | collective-permute-start | bytes 1572872 | tf_op jit(solution)/shard_map/ppermute | solution.py:54
  83.1 37.7 %collective-permute-start.11 = (bf16[64,8192]{1,0:T(8,128)(2,1)}, bf16[64,8192]{1,0:T(8,128)(2,1)}, u32[]{:S(2)}, u32[]{:S(2)}) collective-permute-start(bf16[64,8192]{1,0:T(8,128)(2,1)} %broadcast_select_fusion.1.refs_1_), channel_id=1, source_target_pairs={{0,2},{2,0},{4,6},{6,4},{8,10},{10,8},{12,14},{14,12},{1,3},{3,1},... | collective-permute-start | bytes 3145736 | tf_op jit(solution)/shard_map/ppermute | solution.py:54
  93.8 21.9 %collective-permute-start.4 = (bf16[2,32,16,256]{3,2,1,0:T(8,128)(2,1)S(1)}, bf16[2,32,16,256]{3,2,1,0:T(8,128)(2,1)S(1)}, u32[]{:S(2)}, u32[]{:S(2)}) collective-permute-start(bf16[2,32,16,256]{3,2,1,0:T(8,128)(2,1)S(1)} %get-tuple-element.47), channel_id=1, source_target_pairs={{0,8},{2,10},{4,12},{6,14},{8,0},{10,2},{12,4},{14,6},{1,9},{3,11}... | collective-permute-start | bytes 1572872 | tf_op jit(solution)/shard_map/ppermute | solution.py:54
  115.7 38.2 %collective-permute-start.12 = (bf16[2,32,16,256]{3,2,1,0:T(8,128)(2,1)}, bf16[2,32,16,256]{3,2,1,0:T(8,128)(2,1)S(1)}, u32[]{:S(2)}, u32[]{:S(2)}) collective-permute-start(bf16[2,32,16,256]{3,2,1,0:T(8,128)(2,1)} %get-tuple-element.56), channel_id=1, source_target_pairs={{0,2},{2,0},{4,6},{6,4},{8,10},{10,8},{12,14},{14,12},{1,3},{3,1},... | collective-permute-start | bytes 1572872 | tf_op jit(solution)/shard_map/ppermute | solution.py:54
  117.2 36.7 %collective-permute-start.13 = (bf16[2,32,16,256]{3,2,1,0:T(8,128)(2,1)}, bf16[2,32,16,256]{3,2,1,0:T(8,128)(2,1)S(1)}, u32[]{:S(2)}, u32[]{:S(2)}) collective-permute-start(bf16[2,32,16,256]{3,2,1,0:T(8,128)(2,1)} %get-tuple-element.58), channel_id=1, source_target_pairs={{0,4},{2,6},{4,0},{6,2},{8,12},{10,14},{12,8},{14,10},{1,5},{3,7},... | collective-permute-start | bytes 1572872 | tf_op jit(solution)/shard_map/ppermute | solution.py:54
  117.2 36.7 %collective-permute-start.14 = (bf16[2,32,16,256]{3,2,1,0:T(8,128)(2,1)}, bf16[2,32,16,256]{3,2,1,0:T(8,128)(2,1)S(1)}, u32[]{:S(2)}, u32[]{:S(2)}) collective-permute-start(bf16[2,32,16,256]{3,2,1,0:T(8,128)(2,1)} %copy-done.9), channel_id=1, source_target_pairs={{0,6},{2,4},{4,2},{6,0},{8,14},{10,12},{12,10},{14,8},{1,7},{3,5},... | collective-permute-start | bytes 1572872 | tf_op jit(solution)/shard_map/ppermute | solution.py:54
  119.2 45.3 %collective-permute-start.15 = (bf16[2,32,16,256]{3,2,1,0:T(8,128)(2,1)}, bf16[2,32,16,256]{3,2,1,0:T(8,128)(2,1)S(1)}, u32[]{:S(2)}, u32[]{:S(2)}) collective-permute-start(bf16[2,32,16,256]{3,2,1,0:T(8,128)(2,1)} %copy-done.8), channel_id=1, source_target_pairs={{0,10},{2,8},{4,14},{6,12},{8,2},{10,0},{12,6},{14,4},{1,11},{3,9}... | collective-permute-start | bytes 1572872 | tf_op jit(solution)/shard_map/ppermute | solution.py:54
  120.8 44.6 %collective-permute-start.16 = (bf16[2,32,16,256]{3,2,1,0:T(8,128)(2,1)}, bf16[2,32,16,256]{3,2,1,0:T(8,128)(2,1)S(1)}, u32[]{:S(2)}, u32[]{:S(2)}) collective-permute-start(bf16[2,32,16,256]{3,2,1,0:T(8,128)(2,1)} %copy-done.7), channel_id=1, source_target_pairs={{0,14},{2,12},{4,10},{6,8},{8,6},{10,4},{12,2},{14,0},{1,15},{3,13... | collective-permute-start | bytes 1572872 | tf_op jit(solution)/shard_map/ppermute | solution.py:54
  167.9 39.4 %all-to-all-start = ((bf16[8,64,256]{2,1,0:T(8,128)(2,1)}), bf16[8,64,256]{2,1,0:T(8,128)(2,1)}, u32[]{:S(2)}, u32[]{:S(2)}) async-start(bf16[8,64,256]{2,1,0:T(8,128)(2,1)} %bitcast.132), calls=%async_computation | async-start | bytes 524288 | tf_op jit(solution)/shard_map/all_to_all | solution.py:590
  228.8 15.1 %collective-permute-start.24 = (bf16[64,4096]{1,0:T(8,128)(2,1)}, bf16[64,4096]{1,0:T(8,128)(2,1)S(1)}, u32[]{:S(2)}, u32[]{:S(2)}) collective-permute-start(bf16[64,4096]{1,0:T(8,128)(2,1)} %get-tuple-element.87), channel_id=1, source_target_pairs={{0,4},{4,8},{8,12},{12,14},{14,10},{10,6},{6,2},{2,0},{1,5},{5,9},... | collective-permute-start | bytes 1572872 | tf_op jit(solution)/shard_map/ppermute | solution.py:234
  234.1 24.3 %collective-permute-start.27 = (bf16[64,4096]{1,0:T(8,128)(2,1)S(1)}, bf16[64,4096]{1,0:T(8,128)(2,1)}, u32[]{:S(2)}, u32[]{:S(2)}) collective-permute-start(bf16[64,4096]{1,0:T(8,128)(2,1)S(1)} %get-tuple-element.88), channel_id=1, source_target_pairs={{0,2},{4,0},{8,4},{12,8},{14,12},{10,14},{6,10},{2,6},{1,3},{5,1},... | collective-permute-start | bytes 1572872 | tf_op jit(solution)/shard_map/ppermute | solution.py:234
  234.1 21.0 %collective-permute-start.17 = (bf16[64,4096]{1,0:T(8,128)(2,1)S(1)}, bf16[64,4096]{1,0:T(8,128)(2,1)S(1)}, u32[]{:S(2)}, u32[]{:S(2)}) collective-permute-start(bf16[64,4096]{1,0:T(8,128)(2,1)S(1)} %get-tuple-element.84), channel_id=1, source_target_pairs={{0,4},{4,8},{8,12},{12,14},{14,10},{10,6},{6,2},{2,0},{1,5},{5,9},... | collective-permute-start | bytes 1572872 | tf_op jit(solution)/shard_map/ppermute | solution.py:234
  236.2 49.6 %collective-permute-start.21 = (bf16[64,4096]{1,0:T(8,128)(2,1)S(1)}, bf16[64,4096]{1,0:T(8,128)(2,1)}, u32[]{:S(2)}, u32[]{:S(2)}) collective-permute-start(bf16[64,4096]{1,0:T(8,128)(2,1)S(1)} %get-tuple-element.85), channel_id=1, source_target_pairs={{0,2},{4,0},{8,4},{12,8},{14,12},{10,14},{6,10},{2,6},{1,3},{5,1},... | collective-permute-start | bytes 1572872 | tf_op jit(solution)/shard_map/ppermute | solution.py:234
  245.1 21.3 %collective-permute-start.25 = (bf16[64,4096]{1,0:T(8,128)(2,1)S(1)}, bf16[64,4096]{1,0:T(8,128)(2,1)S(1)}, u32[]{:S(2)}, u32[]{:S(2)}) collective-permute-start(bf16[64,4096]{1,0:T(8,128)(2,1)S(1)} %fusion.6), channel_id=1, source_target_pairs={{0,4},{4,8},{8,12},{12,14},{14,10},{10,6},{6,2},{2,0},{1,5},{5,9},... | collective-permute-start | bytes 1572872 | tf_op jit(solution)/shard_map/ppermute | solution.py:234
  256.3 21.3 %collective-permute-start.18 = (bf16[64,4096]{1,0:T(8,128)(2,1)S(1)}, bf16[64,4096]{1,0:T(8,128)(2,1)S(1)}, u32[]{:S(2)}, u32[]{:S(2)}) collective-permute-start(bf16[64,4096]{1,0:T(8,128)(2,1)S(1)} %fusion.12), channel_id=1, source_target_pairs={{0,4},{4,8},{8,12},{12,14},{14,10},{10,6},{6,2},{2,0},{1,5},{5,9},... | collective-permute-start | bytes 1572872 | tf_op jit(solution)/shard_map/ppermute | solution.py:234
  268.0 14.1 %collective-permute-start.28 = (bf16[64,4096]{1,0:T(8,128)(2,1)S(1)}, bf16[64,4096]{1,0:T(8,128)(2,1)S(1)}, u32[]{:S(2)}, u32[]{:S(2)}) collective-permute-start(bf16[64,4096]{1,0:T(8,128)(2,1)S(1)} %get-tuple-element.95), channel_id=1, source_target_pairs={{0,2},{4,0},{8,4},{12,8},{14,12},{10,14},{6,10},{2,6},{1,3},{5,1},... | collective-permute-start | bytes 1572872 | tf_op jit(solution)/shard_map/ppermute | solution.py:234
  270.1 43.5 %collective-permute-start.26 = (bf16[64,4096]{1,0:T(8,128)(2,1)S(1)}, bf16[64,4096]{1,0:T(8,128)(2,1)S(1)}, u32[]{:S(2)}, u32[]{:S(2)}) collective-permute-start(bf16[64,4096]{1,0:T(8,128)(2,1)S(1)} %get-tuple-element.94), channel_id=1, source_target_pairs={{0,4},{4,8},{8,12},{12,14},{14,10},{10,6},{6,2},{2,0},{1,5},{5,9},... | collective-permute-start | bytes 1572872 | tf_op jit(solution)/shard_map/ppermute | solution.py:234
  277.7 17.5 %collective-permute-start.19 = (bf16[64,4096]{1,0:T(8,128)(2,1)S(1)}, bf16[64,4096]{1,0:T(8,128)(2,1)S(1)}, u32[]{:S(2)}, u32[]{:S(2)}) collective-permute-start(bf16[64,4096]{1,0:T(8,128)(2,1)S(1)} %fusion.13), channel_id=1, source_target_pairs={{0,4},{4,8},{8,12},{12,14},{14,10},{10,6},{6,2},{2,0},{1,5},{5,9},... | collective-permute-start | bytes 1572872 | tf_op jit(solution)/shard_map/ppermute | solution.py:234
  283.2 15.6 %collective-permute-start.29 = (bf16[64,4096]{1,0:T(8,128)(2,1)S(1)}, bf16[64,4096]{1,0:T(8,128)(2,1)S(1)}, u32[]{:S(2)}, u32[]{:S(2)}) collective-permute-start(bf16[64,4096]{1,0:T(8,128)(2,1)S(1)} %fusion.4), channel_id=1, source_target_pairs={{0,2},{4,0},{8,4},{12,8},{14,12},{10,14},{6,10},{2,6},{1,3},{5,1},... | collective-permute-start | bytes 1572872 | tf_op jit(solution)/shard_map/ppermute | solution.py:234
  296.5 15.1 %collective-permute-start.22 = (bf16[64,4096]{1,0:T(8,128)(2,1)S(1)}, bf16[64,4096]{1,0:T(8,128)(2,1)S(1)}, u32[]{:S(2)}, u32[]{:S(2)}) collective-permute-start(bf16[64,4096]{1,0:T(8,128)(2,1)S(1)} %get-tuple-element.93), channel_id=1, source_target_pairs={{0,2},{4,0},{8,4},{12,8},{14,12},{10,14},{6,10},{2,6},{1,3},{5,1},... | collective-permute-start | bytes 1572872 | tf_op jit(solution)/shard_map/ppermute | solution.py:234
  298.5 25.1 %collective-permute-start.20 = (bf16[64,4096]{1,0:T(8,128)(2,1)S(1)}, bf16[64,4096]{1,0:T(8,128)(2,1)S(1)}, u32[]{:S(2)}, u32[]{:S(2)}) collective-permute-start(bf16[64,4096]{1,0:T(8,128)(2,1)S(1)} %get-tuple-element.92), channel_id=1, source_target_pairs={{0,4},{4,8},{8,12},{12,14},{14,10},{10,6},{6,2},{2,0},{1,5},{5,9},... | collective-permute-start | bytes 1572872 | tf_op jit(solution)/shard_map/ppermute | solution.py:234
  300.0 22.4 %collective-permute-start.30 = (bf16[64,4096]{1,0:T(8,128)(2,1)S(1)}, bf16[64,4096]{1,0:T(8,128)(2,1)S(1)}, u32[]{:S(2)}, u32[]{:S(2)}) collective-permute-start(bf16[64,4096]{1,0:T(8,128)(2,1)S(1)} %fusion.5), channel_id=1, source_target_pairs={{0,2},{4,0},{8,4},{12,8},{14,12},{10,14},{6,10},{2,6},{1,3},{5,1},... | collective-permute-start | bytes 1572872 | tf_op jit(solution)/shard_map/ppermute | solution.py:234
  311.8 16.3 %collective-permute-start.23 = (bf16[64,4096]{1,0:T(8,128)(2,1)S(1)}, bf16[64,4096]{1,0:T(8,128)(2,1)S(1)}, u32[]{:S(2)}, u32[]{:S(2)}) collective-permute-start(bf16[64,4096]{1,0:T(8,128)(2,1)S(1)} %fusion.11), channel_id=1, source_target_pairs={{0,2},{4,0},{8,4},{12,8},{14,12},{10,14},{6,10},{2,6},{1,3},{5,1},... | collective-permute-start | bytes 1572872 | tf_op jit(solution)/shard_map/ppermute | solution.py:234
  (25 other events, 558.0 us)

commit v8 on v7

--- a/solution.py
+++ b/solution.py
@@ -83,18 +83,18 @@
     beside_y = swap(beside, 1)
     far_first = jnp.where(middle, over, over_passed)
     far_first_y = swap(far_first, 1)
-    over_beside_passed = swap(over_beside, 2)
+    over_beside_passed = swap(after(over_beside, outgoing[4]), 2)
     exchange(4, over_beside)
-    exchange(6, over_beside, far_first)
+    exchange(6, over_beside)
     far_second = jnp.where(middle, over_beside, over_beside_passed)
     far_second_y = swap(far_second, 1)
-    exchange(5, arrived[4], far_second)
-    exchange(2, arrived[4], far_second)
-    exchange(7, arrived[6], far_first_y)
-    exchange(3, arrived[6], far_first_y)
-    exchange(1, arrived[6], far_first_y)
-    near = [after(own, far_second, arrived[4]), beside, own_y, beside_y]
-    far = [after(far_first, arrived[6]), far_second, far_first_y, far_second_y]
+    exchange(5, far_first_y, far_second)
+    exchange(2, far_first_y, far_second)
+    exchange(7, arrived[4], far_first_y)
+    exchange(3, arrived[4], far_first_y)
+    exchange(1, arrived[4], far_first_y)
+    near = [after(own, far_second, arrived[4], arrived[6]), beside, own_y, beside_y]
+    far = [far_first, far_second, far_first_y, far_second_y]
     return near, far, [arrived[apart] for apart in range(LINE_MODELS)]
 
 
@@ -232,14 +232,6 @@
                 (self.order[i], self.order[(i + way) % self.n_model]) for i in range(self.n_model)
             ]
             self.moving[way] = lax.ppermute(self.moving[way], "mp", pairs)
-
-    def step(self, *held):
-        started = self.advance()
-        blocks, held = lax.optimization_barrier(([self.moving[way] for way in started], held))
-        for way, block in zip(started, blocks):
-            self.moving[way] = block
-        self.send(started)
-        return held
 
     def finish(self):
         while any(self.distance.values()):
@@ -362,104 +354,121 @@
     )
 
 
-def attend_kernel(span, row_step, chunk, half_ref, *refs):
-    query_refs, (key_ref, value_ref), new_key_refs, new_value_refs, out_ref = (
+def attend_kernel(span, heads, half_ref, *refs):
+    query_refs, (key_ref, value_ref), new_key_refs, new_value_refs = (
         refs[:2],
         refs[2:4],
         refs[4:6],
         refs[6:8],
-        refs[8],
-    )
-    rows = out_ref.shape[0]
-    half = new_key_refs[0].shape[0]
-    queries = jnp.concatenate([ref[0].reshape(rows // 2, HD) for ref in query_refs], 0)
-    spans = key_ref.shape[0] // span
-    stride = 2 * half * row_step // rows
-    turn = half_ref[0] * half
-    local = lax.broadcasted_iota(jnp.int32, (rows, half), 0)
-    token = (local // row_step) * stride + chunk * row_step + local % row_step
-    token = lax.rem(token + turn, 2 * half)
-    column = lax.broadcasted_iota(jnp.int32, (rows, half), 1)
-    parts = []
-    for side, ref in enumerate(new_key_refs):
-        causal = column + lax.rem(turn + side * half, 2 * half) <= token
-        parts.append(jnp.where(causal, dot_keys(queries, ref[...]), -jnp.inf))
-    scores = jnp.concatenate(parts, 1)
-    peak = jnp.max(scores, axis=1, keepdims=True)
-    total = None
-    values = jnp.concatenate([ref[...] for ref in new_value_refs], 0)
-    for step in range(spans + 1):
-        if step < spans:
-            next_scores = dot_keys(queries, key_ref[step * span : (step + 1) * span, :])
-            next_peak = jnp.maximum(peak, jnp.max(next_scores, axis=1, keepdims=True))
-        weights = jnp.exp2((scores - peak) * SCORE_SCALE).astype(jnp.bfloat16)
-        product = jnp.dot(weights, values, preferred_element_type=jnp.float32)
-        total = product if total is None else total + product
-        if step < spans:
-            total = total * jnp.exp2((peak - next_peak) * SCORE_SCALE)
-            scores, peak = next_scores, next_peak
-            values = value_ref[step * span : (step + 1) * span, :]
-    out_ref[...] = (total[:, :HD] / total[:, HD:]).astype(jnp.bfloat16)
-
-
-def attend(half, queries, prefix, new_keys, new_values, row_step, chunk, first_head, heads):
-    owners = queries[0].shape[1]
-    rows = 2 * owners * row_step
+    )
+    weight_ref, *out_refs = refs[8 : 9 + COLUMN_CHUNKS]
+    mixed_ref, held_ref, sems = refs[9 + COLUMN_CHUNKS :]
+    step = pl.program_id(0)
+    rows = mixed_ref.shape[0]
+    half = rows // 2
+    depth = held_ref.shape[0] // STREAMS
+    copies = [
+        pltpu.make_async_copy(
+            weight_ref.at[part * depth : (part + 1) * depth, :],
+            held_ref.at[part * depth : (part + 1) * depth, :],
+            sems.at[part],
+        )
+        for part in range(STREAMS)
+    ]
+
+    @pl.when(step == 0)
+    def _():
+        for copy in copies:
+            copy.start()
+
+    @pl.when(step < heads)
+    def _():
+        queries = jnp.concatenate([ref[0] for ref in query_refs], 0)
+        spans = key_ref.shape[0] // span
+        turn = half_ref[0] * half
+        token = lax.rem(lax.broadcasted_iota(jnp.int32, (rows, half), 0) + turn, rows)
+        column = lax.broadcasted_iota(jnp.int32, (rows, half), 1)
+        parts = []
+        for side, ref in enumerate(new_key_refs):
+            causal = column + lax.rem(turn + side * half, rows) <= token
+            parts.append(jnp.where(causal, dot_keys(queries, ref[...]), -jnp.inf))
+        scores = jnp.concatenate(parts, 1)
+        peak = jnp.max(scores, axis=1, keepdims=True)
+        total = None
+        values = jnp.concatenate([ref[...] for ref in new_value_refs], 0)
+        for index in range(spans + 1):
+            if index < spans:
+                next_scores = dot_keys(queries, key_ref[index * span : (index + 1) * span, :])
+                next_peak = jnp.maximum(peak, jnp.max(next_scores, axis=1, keepdims=True))
+            weights = jnp.exp2((scores - peak) * SCORE_SCALE).astype(jnp.bfloat16)
+            product = jnp.dot(weights, values, preferred_element_type=jnp.float32)
+            total = product if total is None else total + product
+            if index < spans:
+                total = total * jnp.exp2((peak - next_peak) * SCORE_SCALE)
+                scores, peak = next_scores, next_peak
+                values = value_ref[index * span : (index + 1) * span, :]
+        mixed_ref[:, pl.ds(pl.multiple_of(step * HD, HD), HD)] = (
+            total[:, :HD] / total[:, HD:]
+        ).astype(jnp.bfloat16)
+
+    @pl.when(step == heads)
+    def _():
+        for copy in copies:
+            copy.wait()
+
+    tile = out_refs[0].shape[1]
+    tiles = held_ref.shape[1] // tile // len(out_refs)
+    for chunk, out_ref in enumerate(out_refs):
+        begin = heads + chunk * tiles
+
+        @pl.when((step >= begin) & (step < begin + tiles))
+        def _(out_ref=out_ref):
+            columns = pl.ds(pl.multiple_of((step - heads) * tile, tile), tile)
+            out_ref[...] = jnp.dot(
+                mixed_ref[...], held_ref[:, columns], preferred_element_type=jnp.float32
+            ).astype(jnp.bfloat16)
+
+
+def attend(half, queries, prefix, new_keys, new_values, weight):
+    heads = queries[0].shape[0]
+    rows = 2 * new_keys[0].shape[0]
+    depth, width = weight.shape
+    tile = math.gcd(width // COLUMN_CHUNKS, 1024)
+    tiles = width // COLUMN_CHUNKS // tile
     span = math.gcd(prefix[0].shape[0], 1024)
-    whole = lambda array: pl.BlockSpec(array.shape, lambda head: (0, 0))
-    count = prefix[0].shape[0] + 2 * new_keys[0].shape[0]
+    whole = lambda array: pl.BlockSpec(array.shape, lambda step: (0, 0))
+    count = prefix[0].shape[0] + rows
     query_spec = pl.BlockSpec(
-        (1, owners, None, row_step, HD), lambda head: (first_head + head, 0, chunk, 0, 0)
+        (1, rows // 2, HD), lambda step: (jnp.minimum(step, heads - 1), 0, 0)
     )
     fixed = (*prefix, *new_keys, *new_values)
     return pl.pallas_call(
-        functools.partial(attend_kernel, span, row_step, chunk),
-        grid=(heads,),
-        out_shape=jax.ShapeDtypeStruct((rows, heads * HD), jnp.bfloat16),
+        functools.partial(attend_kernel, span, heads),
+        grid=(heads + width // tile,),
+        out_shape=[jax.ShapeDtypeStruct((rows, tiles * tile), jnp.bfloat16)] * COLUMN_CHUNKS,
         in_specs=[pl.BlockSpec(memory_space=pltpu.SMEM), query_spec, query_spec]
-        + [whole(array) for array in fixed],
-        out_specs=pl.BlockSpec((rows, HD), lambda head: (0, head)),
-        compiler_params=pltpu.CompilerParams(vmem_limit_bytes=ATTEND_VMEM),
+        + [whole(array) for array in fixed]
+        + [pl.BlockSpec(memory_space=pl.ANY)],
+        out_specs=[
+            pl.BlockSpec(
+                (rows, tile),
+                lambda step, begin=heads + chunk * tiles: (0, jnp.clip(step - begin, 0, tiles - 1)),
+            )
+            for chunk in range(COLUMN_CHUNKS)
+        ],
+        scratch_shapes=[
+            pltpu.VMEM((rows, depth), jnp.bfloat16),
+            pltpu.VMEM((depth, width), jnp.bfloat16),
+            pltpu.SemaphoreType.DMA((STREAMS,)),
+        ],
+        compiler_params=pltpu.CompilerParams(vmem_limit_bytes=VMEM_LIMIT),
         cost_estimate=pl.CostEstimate(
-            flops=heads * rows * count * HD * 8,
-            bytes_accessed=2 * (count * 3 * HD + 2 * heads * rows * HD),
+            flops=heads * rows * count * HD * 8 + 2 * rows * depth * width,
+            bytes_accessed=2 * (count * 3 * HD + 2 * heads * rows * HD + depth * width),
             transcendentals=heads * rows * count,
         ),
         name="attend",
-    )(half, *queries, *fixed)
-
-
-def output_kernel(mixed_ref, *refs):
-    *weight_refs, out_ref = refs
-    weight = jnp.concatenate([ref[...] for ref in weight_refs], axis=0)
-    out_ref[...] = jnp.dot(
-        mixed_ref[...], weight, preferred_element_type=jnp.float32
-    ).astype(jnp.bfloat16)
-
-
-def output_product(mixed, weight, chunk, chunks):
-    rows, depth = mixed.shape
-    width = weight.shape[1] // chunks
-    tile = math.gcd(width, 1024)
-    tiles = width // tile
-    return pl.pallas_call(
-        output_kernel,
-        grid=(tiles,),
-        out_shape=jax.ShapeDtypeStruct((rows, width), jnp.bfloat16),
-        in_specs=[pl.BlockSpec((rows, depth), lambda col: (0, 0))]
-        + [
-            pl.BlockSpec((depth // STREAMS, tile), lambda col, part=part: (part, chunk * tiles + col))
-            for part in range(STREAMS)
-        ],
-        out_specs=pl.BlockSpec((rows, tile), lambda col: (0, col)),
-        compiler_params=pltpu.CompilerParams(vmem_limit_bytes=VMEM_LIMIT),
-        cost_estimate=pl.CostEstimate(
-            flops=2 * rows * depth * width,
-            bytes_accessed=2 * (rows * depth + depth * width + rows * width),
-            transcendentals=0,
-        ),
-        name="output_product",
-    )(mixed, *[weight] * STREAMS)
+    )(half, *queries, *fixed, weight)
 
 
 def on_device(
@@ -580,31 +589,27 @@
         new_keys = [key_whole[part] for part in halves]
         new_values = [value_ones[part] for part in halves]
 
-    arrived, new_keys = lax.optimization_barrier((arrived, list(new_keys)))
-    prefix = order_blocks(arrived, where, prefix_count.reshape(1))
-
-    queries = [part.reshape(q_local, -1, 1, row_count, HD) for part in queries]
-    mixed = attend(
-        upper_half.reshape(1), queries, prefix, new_keys, new_values, row_count, 0, 0, q_local
-    )
     pairs = lax.all_to_all(pairs, "mp", split_axis=0, concat_axis=0, tiled=True)
-    mixed, pairs = lax.optimization_barrier((mixed, pairs))
+    arrived, new_keys, pairs = lax.optimization_barrier((arrived, list(new_keys), pairs))
     cache_rows = (
         pairs.reshape(kv_heads, sharers, row_count, 2, kv_local)
         .transpose(2, 0, 3, 1, 4)
         .reshape(1, row_count, kv_heads * 2 * HD)
     )
-
-    width = w_out.shape[1]
+    prefix = order_blocks(arrived, where, prefix_count.reshape(1))
+    shares = attend(upper_half.reshape(1), queries, prefix, new_keys, new_values, w_out)
+
     first = upper_half * (n_model // 2)
-    scatters = []
-    for chunk in range(COLUMN_CHUNKS):
-        share = output_product(mixed, w_out, chunk, COLUMN_CHUNKS)
-        share = share.reshape(n_model, row_count, width // COLUMN_CHUNKS)
-        scatters.append(
-            RingScatter(share, n_model, my_model, first, 1 if chunk % 2 == 0 else -1)
+    scatters = [
+        RingScatter(
+            share.reshape(n_model, row_count, -1),
+            n_model,
+            my_model,
+            first,
+            1 if chunk % 2 == 0 else -1,
         )
-        (mixed,) = scatters[-1].step(mixed)
+        for chunk, share in enumerate(shares)
+    ]
     return (jnp.concatenate([scatter.finish() for scatter in scatters], 1)[None], cache_rows)
 
 

time: 331 us -> 344 us (1.039)
  waiting for transfers between devices: 115 us -> 158 us
  starting transfers between devices: 75.3 us -> 58.4 us
  other arithmetic: 27.8 us -> 21.4 us
    ppermute x14, waiting for transfers between devices: 51.7 us -> 91.9 us  [swap(): lax.ppermute(block, 'mp', [(index, index ^ mask) for index in range(LINE_...]
    ppermute x14, starting transfers between devices: 21.1 us -> 11 us  [send(): self.moving[way] = lax.ppermute(self.moving[way], 'mp', pairs)]
    all_to_all x1, starting transfers between devices: 9.62 us -> 3.59 us  [on_device(): pairs = lax.all_to_all(pairs, 'mp', split_axis=0, concat_axis=0, tiled=True)]
    all_to_all x1, waiting for transfers between devices: 0.01 us -> 5.05 us  [on_device(): pairs = lax.all_to_all(pairs, 'mp', split_axis=0, concat_axis=0, tiled=True)]
    pallas_call x3 -> x1, Pallas kernels: 42.3 us -> 38.8 us  [attend(): pl.pallas_call(functools.partial(attend_kernel, span, heads), grid=(heads...]
    unnamed x51 -> x35, local copies, waits for them, and re-layouts: 9.14 us -> 6.72 us
  transfers between devices with their start and end apart: 32 -> 32, of which waited for: 14 -> 15; matrix products, arithmetic and copies ran while one was open for 8% -> 7% of each run, Pallas kernels for 19% -> 10%
where the time goes in v8:
time: 344 us; the launch traced here: 342 us
  waiting for transfers between devices  158 us (46%)
  Pallas kernels  78.4 us (23%)
  starting transfers between devices  58.4 us (17%)
  other arithmetic  21.4 us (6%)
  local copies, waits for them, and re-layouts  14.1 us (4%)
  between operations  11.9 us (3%)
    ppermute x14, waiting for transfers between devices, swap(): lax.ppermute(block, 'mp', [(index, index ^ mask) for index in range(LINE_...  91.9 us
    ppermute x14, waiting for transfers between devices, send(): self.moving[way] = lax.ppermute(self.moving[way], 'mp', pairs)  61.1 us
    ppermute x14, starting transfers between devices, swap(): lax.ppermute(block, 'mp', [(index, index ^ mask) for index in range(LINE_...  43.3 us
    pallas_call x1, Pallas kernels, attend(): pl.pallas_call(functools.partial(attend_kernel, span, heads), grid=(heads...  38.8 us
    pallas_call x2, Pallas kernels, project(): pl.pallas_call(project_kernel, grid=(width // depth,), out_shape=out_shap...  31.4 us
    ppermute x14, starting transfers between devices, send(): self.moving[way] = lax.ppermute(self.moving[way], 'mp', pairs)  11 us
  transfers between devices with their start and end apart: 32, of which 15 were waited for; matrix products, arithmetic and copies ran while one was open for 7% of the time, Pallas kernels for 10%

profile of v8, /device:TPU:0, one launch (start us, length us, event | category | flops | bytes accessed | tf_op | source)
XLA Modules:
  0.0 342.3 jit_solution(159513636877190758)
XLA Ops:
  3.3 2.2 copy-done
  8.4 2.9 collective-permute-start
  11.3 23.8 %collective-permute-done.refs_1_ = bf16[64,8192]{1,0:T(8,128)(2,1)} collective-permute-done((bf16[64,8192]{1,0:T(8,128)(2,1)}, bf16[64,8192]{1,0:T(8,128)(2,1)}, u32[]{:S(2)}, u32[]{:S(2)}) %collective-permute-start) | collective-permute-done | bytes 1048608 | tf_op jit(solution)/shard_map/ppermute | solution.py:54
  35.2 3.3 collective-permute-start.9
  41.3 2.2 copy-done.1
  43.4 4.0 %pack_blocks.1 = (bf16[2,32,16,256]{3,2,1,0:T(8,128)(2,1)S(1)}, bf16[2,32,16,256]{3,2,1,0:T(8,128)(2,1)}, bf16[2,32,16,256]{3,2,1,0:T(8,128)(2,1)}, bf16[2,32,16...) custom-call(s32[2,32]{1,0:T(2,128)S(1)} %pad_add_fusion.slots_ref, ...), custom_call_target="tpu_custom_call" | custom-call | tf_op jit(solution)/shard_map/pack_blocks/pallas_call | solution.py:285
  47.5 14.2 %collective-permute-start.3 = (bf16[64,8192]{1,0:T(8,128)(2,1)}, bf16[64,8192]{1,0:T(8,128)(2,1)S(1)}, u32[]{:S(2)}, u32[]{:S(2)}) collective-permute-start(bf16[64,8192]{1,0:T(8,128)(2,1)} %collective-permute-done.1), channel_id=1, source_target_pairs={{0,4},{2,6},{4,0},{6,2},{8,12},{10,14},{12,8},{14,10},{1,5},{3,7},... | collective-permute-start | bytes 3145736 | tf_op jit(solution)/shard_map/ppermute | solution.py:54
  62.7 2.4 collective-permute-start.5
  66.4 28.8 %collective-permute-done.3 = bf16[64,8192]{1,0:T(8,128)(2,1)S(1)} collective-permute-done((bf16[64,8192]{1,0:T(8,128)(2,1)}, bf16[64,8192]{1,0:T(8,128)(2,1)S(1)}, u32[]{:S(2)}, u32[]{:S(2)}) %collective-permute-start.3) | collective-permute-done | bytes 1048608 | tf_op jit(solution)/shard_map/ppermute | solution.py:54
  108.3 13.1 %collective-permute-done.10.refs_2_ = bf16[64,8192]{1,0:T(8,128)(2,1)} collective-permute-done((bf16[64,8192]{1,0:T(8,128)(2,1)S(1)}, bf16[64,8192]{1,0:T(8,128)(2,1)}, u32[]{:S(2)}, u32[]{:S(2)}) %collective-permute-start.10) | collective-permute-done | bytes 1048608 | tf_op jit(solution)/shard_map/ppermute | solution.py:54
  123.0 2.0 collective-permute-start.14
  124.9 4.8 %collective-permute-start.15 = (bf16[2,32,16,256]{3,2,1,0:T(8,128)(2,1)}, bf16[2,32,16,256]{3,2,1,0:T(8,128)(2,1)}, u32[]{:S(2)}, u32[]{:S(2)}) collective-permute-start(bf16[2,32,16,256]{3,2,1,0:T(8,128)(2,1)} %copy-done.4), channel_id=1, source_target_pairs={{0,10},{2,8},{4,14},{6,12},{8,2},{10,0},{12,6},{14,4},{1,11},{3,9}... | collective-permute-start | bytes 1572872 | tf_op jit(solution)/shard_map/ppermute | solution.py:54
  129.8 15.7 %project.2 = (bf16[8,256,128]{2,1,0:T(8,128)(2,1)}, bf16[256,128]{1,0:T(8,128)(2,1)}, bf16[256,256]{1,0:T(8,128)(2,1)}, bf16[256,256]{1,0:T(8,128)(2,1)}) custom-call(s32[4]{0:T(128)} %add_multiply_fusion.starts_ref, bf16[64,8192]{1,0:T(8,128)(2,1)} %fusion.2.refs_0_, bf16[64,8192]{1,0:T(8,128)(2,1)} %collective-permute-done.refs_1_, ...), custom_call_target="tpu_custom_call" | custom-call | flops 5368709120 | bytes 26476544 | tf_op jit(solution)/shard_map/project/pallas_call | solution.py:177
  145.4 25.6 %collective-permute-done.11.refs_3_ = bf16[64,8192]{1,0:T(8,128)(2,1)} collective-permute-done((bf16[64,8192]{1,0:T(8,128)(2,1)}, bf16[64,8192]{1,0:T(8,128)(2,1)}, u32[]{:S(2)}, u32[]{:S(2)}) %collective-permute-start.11) | collective-permute-done | bytes 1048608 | tf_op jit(solution)/shard_map/ppermute | solution.py:54
  171.0 7.1 %collective-permute-start.16 = (bf16[2,32,16,256]{3,2,1,0:T(8,128)(2,1)}, bf16[2,32,16,256]{3,2,1,0:T(8,128)(2,1)}, u32[]{:S(2)}, u32[]{:S(2)}) collective-permute-start(bf16[2,32,16,256]{3,2,1,0:T(8,128)(2,1)} %get-tuple-element.60), channel_id=1, source_target_pairs={{0,14},{2,12},{4,10},{6,8},{8,6},{10,4},{12,2},{14,0},{1,15},{3,13... | collective-permute-start | bytes 1572872 | tf_op jit(solution)/shard_map/ppermute | solution.py:54
  178.2 15.7 %project.3 = (bf16[8,256,128]{2,1,0:T(8,128)(2,1)}, bf16[256,128]{1,0:T(8,128)(2,1)}, bf16[256,256]{1,0:T(8,128)(2,1)}, bf16[256,256]{1,0:T(8,128)(2,1)}) custom-call(s32[4]{0:T(128)} %add_multiply_fusion.1.starts_ref, bf16[64,8192]{1,0:T(8,128)(2,1)} %copy-done.6, bf16[64,8192]{1,0:T(8,128)(2,1)} %broadcast_select_fusion.1.refs_1_, ...), custom_call_target="tpu_custom_call" | custom-call | flops 5368709120 | bytes 26476544 | tf_op jit(solution)/shard_map/project/pallas_call | solution.py:177
  195.6 3.6 %all-to-all-start = ((bf16[8,64,256]{2,1,0:T(8,128)(2,1)}), bf16[8,64,256]{2,1,0:T(8,128)(2,1)S(1)}, u32[]{:S(2)}, u32[]{:S(2)}) async-start(bf16[8,64,256]{2,1,0:T(8,128)(2,1)} %bitcast.25), calls=%async_computation | async-start | bytes 524288 | tf_op jit(solution)/shard_map/all_to_all | solution.py:592
  202.2 5.1 %all-to-all-done = bf16[8,64,256]{2,1,0:T(8,128)(2,1)S(1)} async-done(((bf16[8,64,256]{2,1,0:T(8,128)(2,1)}), bf16[8,64,256]{2,1,0:T(8,128)(2,1)S(1)}, u32[]{:S(2)}, u32[]{:S(2)}) %all-to-all-start) | async-done | bytes 262176 | tf_op jit(solution)/shard_map/all_to_all | solution.py:592
  207.2 3.5 %order_blocks.1 = (bf16[4096,128]{1,0:T(8,128)(2,1)S(1)}, bf16[4096,256]{1,0:T(8,128)(2,1)S(1)}) custom-call(s32[1]{0:T(128)} %dynamic_slice.118.length_ref, s32[256]{0:T(256)S(1)} %multiply_add_fusion.where_ref, bf16[64,16,256]{2,1,0:T(8,128)(2,1)S(1)} %bitcast.108, bf16[64,16,256]{2,1,0:T(8,128)(2,1)S(1)} %bitcast.111, bf16[64,16,256]{2,1,0:T(8,128)(2,1)S(1)} %bitcast.112, ...), custom_call_target="tpu_custom_call" | custom-call | tf_op jit(solution)/shard_map/order_blocks/pallas_call | solution.py:330
  213.0 38.8 %attend.1 = (bf16[512,4096]{1,0:T(8,128)(2,1)}, bf16[512,4096]{1,0:T(8,128)(2,1)}) custom-call(s32[1]{0:T(128)} %bitcast.half_ref, bf16[8,256,128]{2,1,0:T(8,128)(2,1)} %get-tuple-element.48.refs_0_, bf16[8,256,128]{2,1,0:T(8,128)(2,1)} %get-tuple-element.49.refs_1_, bf16[4096,128]{1,0:T(8,128)(2,1)} %copy-done.3, bf16[4096,256]{1,0:T(8,128)(2,1)} %copy-done.2, ...), custom_call_target="tpu_custom_call" | custom-call | flops 27917287424 | bytes 22413312 | tf_op jit(solution)/shard_map/attend/pallas_call | solution.py:445
  257.5 2.1 collective-permute-start.27
  259.6 2.3 dynamic-slice_bitcast_fusion.3
  261.9 2.0 collective-permute-start.21
  265.1 2.9 collective-permute-done.24
  269.2 10.0 %collective-permute-done.17 = bf16[64,4096]{1,0:T(8,128)(2,1)S(1)} collective-permute-done((bf16[64,4096]{1,0:T(8,128)(2,1)}, bf16[64,4096]{1,0:T(8,128)(2,1)S(1)}, u32[]{:S(2)}, u32[]{:S(2)}) %collective-permute-start.17) | collective-permute-done | bytes 524320 | tf_op jit(solution)/shard_map/ppermute | solution.py:234
  280.4 10.0 %collective-permute-done.25 = bf16[64,4096]{1,0:T(8,128)(2,1)S(1)} collective-permute-done((bf16[64,4096]{1,0:T(8,128)(2,1)S(1)}, bf16[64,4096]{1,0:T(8,128)(2,1)S(1)}, u32[]{:S(2)}, u32[]{:S(2)}) %collective-permute-start.25) | collective-permute-done | bytes 524320 | tf_op jit(solution)/shard_map/ppermute | solution.py:234
  292.1 2.0 collective-permute-start.26
  294.1 6.1 %collective-permute-done.18 = bf16[64,4096]{1,0:T(8,128)(2,1)S(1)} collective-permute-done((bf16[64,4096]{1,0:T(8,128)(2,1)S(1)}, bf16[64,4096]{1,0:T(8,128)(2,1)S(1)}, u32[]{:S(2)}, u32[]{:S(2)}) %collective-permute-start.18) | collective-permute-done | bytes 524320 | tf_op jit(solution)/shard_map/ppermute | solution.py:234
  303.6 13.4 %collective-permute-done.19 = bf16[64,4096]{1,0:T(8,128)(2,1)S(1)} collective-permute-done((bf16[64,4096]{1,0:T(8,128)(2,1)S(1)}, bf16[64,4096]{1,0:T(8,128)(2,1)S(1)}, u32[]{:S(2)}, u32[]{:S(2)}) %collective-permute-start.19) | collective-permute-done | bytes 524320 | tf_op jit(solution)/shard_map/ppermute | solution.py:234
  320.9 8.9 %collective-permute-done.22 = bf16[64,4096]{1,0:T(8,128)(2,1)S(1)} collective-permute-done((bf16[64,4096]{1,0:T(8,128)(2,1)S(1)}, bf16[64,4096]{1,0:T(8,128)(2,1)S(1)}, u32[]{:S(2)}, u32[]{:S(2)}) %collective-permute-start.22) | collective-permute-done | bytes 524320 | tf_op jit(solution)/shard_map/ppermute | solution.py:234
  330.6 4.8 %collective-permute-done.30 = bf16[64,4096]{1,0:T(8,128)(2,1)S(1)} collective-permute-done((bf16[64,4096]{1,0:T(8,128)(2,1)S(1)}, bf16[64,4096]{1,0:T(8,128)(2,1)S(1)}, u32[]{:S(2)}, u32[]{:S(2)}) %collective-permute-start.30) | collective-permute-done | bytes 524320 | tf_op jit(solution)/shard_map/ppermute | solution.py:234
  336.7 4.4 %collective-permute-done.23 = bf16[64,4096]{1,0:T(8,128)(2,1)S(1)} collective-permute-done((bf16[64,4096]{1,0:T(8,128)(2,1)S(1)}, bf16[64,4096]{1,0:T(8,128)(2,1)S(1)}, u32[]{:S(2)}, u32[]{:S(2)}) %collective-permute-start.23) | collective-permute-done | bytes 524320 | tf_op jit(solution)/shard_map/ppermute | solution.py:234
  (120 shorter events, 42.9 us)
Async XLA Ops:
  6.3 35.0 %collective-permute-start.2 = (bf16[32,16,2048]{2,1,0:T(8,128)(2,1)S(1)}, bf16[32,16,2048]{2,1,0:T(8,128)(2,1)}, u32[]{:S(2)}, u32[]{:S(2)}) collective-permute-start(bf16[32,16,2048]{2,1,0:T(8,128)(2,1)S(1)} %pick_blocks.1), channel_id=1, source_target_pairs={{0,1},{1,0},{2,3},{3,2},{4,5},{5,4},{6,7},{7,6},{8,9},{9,8},{10,11... | collective-permute-start | bytes 6291464 | tf_op jit(solution)/shard_map/ppermute | solution.py:524
  8.4 26.7 %collective-permute-start = (bf16[64,8192]{1,0:T(8,128)(2,1)}, bf16[64,8192]{1,0:T(8,128)(2,1)}, u32[]{:S(2)}, u32[]{:S(2)}) collective-permute-start(bf16[64,8192]{1,0:T(8,128)(2,1)} %fusion.2.refs_0_), channel_id=1, source_target_pairs={{0,4},{2,6},{4,0},{6,2},{8,12},{10,14},{12,8},{14,10},{1,5},{3,7},... | collective-permute-start | bytes 3145736 | tf_op jit(solution)/shard_map/ppermute | solution.py:54
  11.3 23.8 %collective-permute-start.8 = (bf16[64,8192]{1,0:T(8,128)(2,1)}, bf16[64,8192]{1,0:T(8,128)(2,1)S(1)}, u32[]{:S(2)}, u32[]{:S(2)}) collective-permute-start(bf16[64,8192]{1,0:T(8,128)(2,1)} %fusion.2.refs_0_), channel_id=1, source_target_pairs={{0,1},{1,0},{2,3},{3,2},{4,8},{5,9},{6,10},{7,11},{8,4},{9,5},{10,... | collective-permute-start | bytes 3145736 | tf_op jit(solution)/shard_map/ppermute | solution.py:65
  35.1 12.3 %collective-permute-start.1 = (bf16[64,8192]{1,0:T(8,128)(2,1)}, bf16[64,8192]{1,0:T(8,128)(2,1)}, u32[]{:S(2)}, u32[]{:S(2)}) collective-permute-start(bf16[64,8192]{1,0:T(8,128)(2,1)} %collective-permute-done.refs_1_), channel_id=1, source_target_pairs={{0,1},{1,0},{2,3},{3,2},{4,8},{5,9},{6,10},{7,11},{8,4},{9,5},{10,... | collective-permute-start | bytes 3145736 | tf_op jit(solution)/shard_map/ppermute | solution.py:65
  35.2 27.5 %collective-permute-start.9 = (bf16[64,8192]{1,0:T(8,128)(2,1)S(1)}, bf16[64,8192]{1,0:T(8,128)(2,1)}, u32[]{:S(2)}, u32[]{:S(2)}) collective-permute-start(bf16[64,8192]{1,0:T(8,128)(2,1)S(1)} %collective-permute-done.8), channel_id=1, source_target_pairs={{0,4},{2,6},{4,0},{6,2},{8,12},{10,14},{12,8},{14,10},{1,5},{3,7},... | collective-permute-start | bytes 3145736 | tf_op jit(solution)/shard_map/ppermute | solution.py:54
  38.5 84.5 %collective-permute-start.6 = (bf16[64,8192]{1,0:T(8,128)(2,1)}, bf16[64,8192]{1,0:T(8,128)(2,1)}, u32[]{:S(2)}, u32[]{:S(2)}) collective-permute-start(bf16[64,8192]{1,0:T(8,128)(2,1)} %fusion.2.refs_0_), channel_id=1, source_target_pairs={{0,2},{2,0},{4,6},{6,4},{8,10},{10,8},{12,14},{14,12},{1,3},{3,1},... | collective-permute-start | bytes 3145736 | tf_op jit(solution)/shard_map/ppermute | solution.py:54
  40.7 84.3 %collective-permute-start.7 = (bf16[64,8192]{1,0:T(8,128)(2,1)}, bf16[64,8192]{1,0:T(8,128)(2,1)}, u32[]{:S(2)}, u32[]{:S(2)}) collective-permute-start(bf16[64,8192]{1,0:T(8,128)(2,1)} %collective-permute-done.refs_1_), channel_id=1, source_target_pairs={{0,2},{2,0},{4,6},{6,4},{8,10},{10,8},{12,14},{14,12},{1,3},{3,1},... | collective-permute-start | bytes 3145736 | tf_op jit(solution)/shard_map/ppermute | solution.py:54
  47.5 47.8 %collective-permute-start.3 = (bf16[64,8192]{1,0:T(8,128)(2,1)}, bf16[64,8192]{1,0:T(8,128)(2,1)S(1)}, u32[]{:S(2)}, u32[]{:S(2)}) collective-permute-start(bf16[64,8192]{1,0:T(8,128)(2,1)} %collective-permute-done.1), channel_id=1, source_target_pairs={{0,4},{2,6},{4,0},{6,2},{8,12},{10,14},{12,8},{14,10},{1,5},{3,7},... | collective-permute-start | bytes 3145736 | tf_op jit(solution)/shard_map/ppermute | solution.py:54
  61.6 36.2 %collective-permute-start.4 = (bf16[2,32,16,256]{3,2,1,0:T(8,128)(2,1)S(1)}, bf16[2,32,16,256]{3,2,1,0:T(8,128)(2,1)S(1)}, u32[]{:S(2)}, u32[]{:S(2)}) collective-permute-start(bf16[2,32,16,256]{3,2,1,0:T(8,128)(2,1)S(1)} %get-tuple-element.44), channel_id=1, source_target_pairs={{0,8},{2,10},{4,12},{6,14},{8,0},{10,2},{12,4},{14,6},{1,9},{3,11}... | collective-permute-start | bytes 1572872 | tf_op jit(solution)/shard_map/ppermute | solution.py:54
  62.7 45.6 %collective-permute-start.5 = (bf16[2,32,16,256]{3,2,1,0:T(8,128)(2,1)S(1)}, bf16[2,32,16,256]{3,2,1,0:T(8,128)(2,1)S(1)}, u32[]{:S(2)}, u32[]{:S(2)}) collective-permute-start(bf16[2,32,16,256]{3,2,1,0:T(8,128)(2,1)S(1)} %get-tuple-element.46), channel_id=1, source_target_pairs={{0,12},{2,14},{4,8},{6,10},{8,4},{10,6},{12,0},{14,2},{1,13},{3,15... | collective-permute-start | bytes 1572872 | tf_op jit(solution)/shard_map/ppermute | solution.py:54
  95.2 26.2 %collective-permute-start.10 = (bf16[64,8192]{1,0:T(8,128)(2,1)S(1)}, bf16[64,8192]{1,0:T(8,128)(2,1)}, u32[]{:S(2)}, u32[]{:S(2)}) collective-permute-start(bf16[64,8192]{1,0:T(8,128)(2,1)S(1)} %broadcast_select_fusion.refs_0_), channel_id=1, source_target_pairs={{0,2},{2,0},{4,6},{6,4},{8,10},{10,8},{12,14},{14,12},{1,3},{3,1},... | collective-permute-start | bytes 3145736 | tf_op jit(solution)/shard_map/ppermute | solution.py:54
  97.9 73.2 %collective-permute-start.11 = (bf16[64,8192]{1,0:T(8,128)(2,1)}, bf16[64,8192]{1,0:T(8,128)(2,1)}, u32[]{:S(2)}, u32[]{:S(2)}) collective-permute-start(bf16[64,8192]{1,0:T(8,128)(2,1)} %broadcast_select_fusion.1.refs_1_), channel_id=1, source_target_pairs={{0,2},{2,0},{4,6},{6,4},{8,10},{10,8},{12,14},{14,12},{1,3},{3,1},... | collective-permute-start | bytes 3145736 | tf_op jit(solution)/shard_map/ppermute | solution.py:54
  121.4 80.7 %collective-permute-start.12 = (bf16[2,32,16,256]{3,2,1,0:T(8,128)(2,1)}, bf16[2,32,16,256]{3,2,1,0:T(8,128)(2,1)S(1)}, u32[]{:S(2)}, u32[]{:S(2)}) collective-permute-start(bf16[2,32,16,256]{3,2,1,0:T(8,128)(2,1)} %get-tuple-element.52), channel_id=1, source_target_pairs={{0,2},{2,0},{4,6},{6,4},{8,10},{10,8},{12,14},{14,12},{1,3},{3,1},... | collective-permute-start | bytes 1572872 | tf_op jit(solution)/shard_map/ppermute | solution.py:54
  123.0 79.2 %collective-permute-start.13 = (bf16[2,32,16,256]{3,2,1,0:T(8,128)(2,1)}, bf16[2,32,16,256]{3,2,1,0:T(8,128)(2,1)S(1)}, u32[]{:S(2)}, u32[]{:S(2)}) collective-permute-start(bf16[2,32,16,256]{3,2,1,0:T(8,128)(2,1)} %get-tuple-element.54), channel_id=1, source_target_pairs={{0,4},{2,6},{4,0},{6,2},{8,12},{10,14},{12,8},{14,10},{1,5},{3,7},... | collective-permute-start | bytes 1572872 | tf_op jit(solution)/shard_map/ppermute | solution.py:54
  123.0 79.2 %collective-permute-start.14 = (bf16[2,32,16,256]{3,2,1,0:T(8,128)(2,1)}, bf16[2,32,16,256]{3,2,1,0:T(8,128)(2,1)S(1)}, u32[]{:S(2)}, u32[]{:S(2)}) collective-permute-start(bf16[2,32,16,256]{3,2,1,0:T(8,128)(2,1)} %copy-done.5), channel_id=1, source_target_pairs={{0,6},{2,4},{4,2},{6,0},{8,14},{10,12},{12,10},{14,8},{1,7},{3,5},... | collective-permute-start | bytes 1572872 | tf_op jit(solution)/shard_map/ppermute | solution.py:54
  124.9 77.2 %collective-permute-start.15 = (bf16[2,32,16,256]{3,2,1,0:T(8,128)(2,1)}, bf16[2,32,16,256]{3,2,1,0:T(8,128)(2,1)}, u32[]{:S(2)}, u32[]{:S(2)}) collective-permute-start(bf16[2,32,16,256]{3,2,1,0:T(8,128)(2,1)} %copy-done.4), channel_id=1, source_target_pairs={{0,10},{2,8},{4,14},{6,12},{8,2},{10,0},{12,6},{14,4},{1,11},{3,9}... | collective-permute-start | bytes 1572872 | tf_op jit(solution)/shard_map/ppermute | solution.py:54
  171.0 31.1 %collective-permute-start.16 = (bf16[2,32,16,256]{3,2,1,0:T(8,128)(2,1)}, bf16[2,32,16,256]{3,2,1,0:T(8,128)(2,1)}, u32[]{:S(2)}, u32[]{:S(2)}) collective-permute-start(bf16[2,32,16,256]{3,2,1,0:T(8,128)(2,1)} %get-tuple-element.60), channel_id=1, source_target_pairs={{0,14},{2,12},{4,10},{6,8},{8,6},{10,4},{12,2},{14,0},{1,15},{3,13... | collective-permute-start | bytes 1572872 | tf_op jit(solution)/shard_map/ppermute | solution.py:54
  195.6 11.6 %all-to-all-start = ((bf16[8,64,256]{2,1,0:T(8,128)(2,1)}), bf16[8,64,256]{2,1,0:T(8,128)(2,1)S(1)}, u32[]{:S(2)}, u32[]{:S(2)}) async-start(bf16[8,64,256]{2,1,0:T(8,128)(2,1)} %bitcast.25), calls=%async_computation | async-start | bytes 524288 | tf_op jit(solution)/shard_map/all_to_all | solution.py:592
  253.1 14.9 %collective-permute-start.24 = (bf16[64,4096]{1,0:T(8,128)(2,1)S(1)}, bf16[64,4096]{1,0:T(8,128)(2,1)S(1)}, u32[]{:S(2)}, u32[]{:S(2)}) collective-permute-start(bf16[64,4096]{1,0:T(8,128)(2,1)S(1)} %get-tuple-element.90), channel_id=1, source_target_pairs={{0,4},{4,8},{8,12},{12,14},{14,10},{10,6},{6,2},{2,0},{1,5},{5,9},... | collective-permute-start | bytes 1572872 | tf_op jit(solution)/shard_map/ppermute | solution.py:234
  257.5 22.9 %collective-permute-start.27 = (bf16[64,4096]{1,0:T(8,128)(2,1)S(1)}, bf16[64,4096]{1,0:T(8,128)(2,1)}, u32[]{:S(2)}, u32[]{:S(2)}) collective-permute-start(bf16[64,4096]{1,0:T(8,128)(2,1)S(1)} %get-tuple-element.91), channel_id=1, source_target_pairs={{0,2},{4,0},{8,4},{12,8},{14,12},{10,14},{6,10},{2,6},{1,3},{5,1},... | collective-permute-start | bytes 1572872 | tf_op jit(solution)/shard_map/ppermute | solution.py:234
  261.9 17.3 %collective-permute-start.17 = (bf16[64,4096]{1,0:T(8,128)(2,1)}, bf16[64,4096]{1,0:T(8,128)(2,1)S(1)}, u32[]{:S(2)}, u32[]{:S(2)}) collective-permute-start(bf16[64,4096]{1,0:T(8,128)(2,1)} %get-tuple-element.86), channel_id=1, source_target_pairs={{0,4},{4,8},{8,12},{12,14},{14,10},{10,6},{6,2},{2,0},{1,5},{5,9},... | collective-permute-start | bytes 1572872 | tf_op jit(solution)/shard_map/ppermute | solution.py:234
  261.9 41.7 %collective-permute-start.21 = (bf16[64,4096]{1,0:T(8,128)(2,1)}, bf16[64,4096]{1,0:T(8,128)(2,1)S(1)}, u32[]{:S(2)}, u32[]{:S(2)}) collective-permute-start(bf16[64,4096]{1,0:T(8,128)(2,1)} %get-tuple-element.87), channel_id=1, source_target_pairs={{0,2},{4,0},{8,4},{12,8},{14,12},{10,14},{6,10},{2,6},{1,3},{5,1},... | collective-permute-start | bytes 1572872 | tf_op jit(solution)/shard_map/ppermute | solution.py:234
  269.1 21.3 %collective-permute-start.25 = (bf16[64,4096]{1,0:T(8,128)(2,1)S(1)}, bf16[64,4096]{1,0:T(8,128)(2,1)S(1)}, u32[]{:S(2)}, u32[]{:S(2)}) collective-permute-start(bf16[64,4096]{1,0:T(8,128)(2,1)S(1)} %fusion.6), channel_id=1, source_target_pairs={{0,4},{4,8},{8,12},{12,14},{14,10},{10,6},{6,2},{2,0},{1,5},{5,9},... | collective-permute-start | bytes 1572872 | tf_op jit(solution)/shard_map/ppermute | solution.py:234
  280.4 19.8 %collective-permute-start.18 = (bf16[64,4096]{1,0:T(8,128)(2,1)S(1)}, bf16[64,4096]{1,0:T(8,128)(2,1)S(1)}, u32[]{:S(2)}, u32[]{:S(2)}) collective-permute-start(bf16[64,4096]{1,0:T(8,128)(2,1)S(1)} %fusion.12), channel_id=1, source_target_pairs={{0,4},{4,8},{8,12},{12,14},{14,10},{10,6},{6,2},{2,0},{1,5},{5,9},... | collective-permute-start | bytes 1572872 | tf_op jit(solution)/shard_map/ppermute | solution.py:234
  292.0 9.2 %collective-permute-start.28 = (bf16[64,4096]{1,0:T(8,128)(2,1)S(1)}, bf16[64,4096]{1,0:T(8,128)(2,1)S(1)}, u32[]{:S(2)}, u32[]{:S(2)}) collective-permute-start(bf16[64,4096]{1,0:T(8,128)(2,1)S(1)} %get-tuple-element.89), channel_id=1, source_target_pairs={{0,2},{4,0},{8,4},{12,8},{14,12},{10,14},{6,10},{2,6},{1,3},{5,1},... | collective-permute-start | bytes 1572872 | tf_op jit(solution)/shard_map/ppermute | solution.py:234
  292.1 38.5 %collective-permute-start.26 = (bf16[64,4096]{1,0:T(8,128)(2,1)S(1)}, bf16[64,4096]{1,0:T(8,128)(2,1)S(1)}, u32[]{:S(2)}, u32[]{:S(2)}) collective-permute-start(bf16[64,4096]{1,0:T(8,128)(2,1)S(1)} %get-tuple-element.88), channel_id=1, source_target_pairs={{0,4},{4,8},{8,12},{12,14},{14,10},{10,6},{6,2},{2,0},{1,5},{5,9},... | collective-permute-start | bytes 1572872 | tf_op jit(solution)/shard_map/ppermute | solution.py:234
  300.3 16.7 %collective-permute-start.19 = (bf16[64,4096]{1,0:T(8,128)(2,1)S(1)}, bf16[64,4096]{1,0:T(8,128)(2,1)S(1)}, u32[]{:S(2)}, u32[]{:S(2)}) collective-permute-start(bf16[64,4096]{1,0:T(8,128)(2,1)S(1)} %fusion.13), channel_id=1, source_target_pairs={{0,4},{4,8},{8,12},{12,14},{14,10},{10,6},{6,2},{2,0},{1,5},{5,9},... | collective-permute-start | bytes 1572872 | tf_op jit(solution)/shard_map/ppermute | solution.py:234
  302.4 17.0 %collective-permute-start.29 = (bf16[64,4096]{1,0:T(8,128)(2,1)S(1)}, bf16[64,4096]{1,0:T(8,128)(2,1)S(1)}, u32[]{:S(2)}, u32[]{:S(2)}) collective-permute-start(bf16[64,4096]{1,0:T(8,128)(2,1)S(1)} %fusion.4), channel_id=1, source_target_pairs={{0,2},{4,0},{8,4},{12,8},{14,12},{10,14},{6,10},{2,6},{1,3},{5,1},... | collective-permute-start | bytes 1572872 | tf_op jit(solution)/shard_map/ppermute | solution.py:234
  317.3 12.5 %collective-permute-start.22 = (bf16[64,4096]{1,0:T(8,128)(2,1)S(1)}, bf16[64,4096]{1,0:T(8,128)(2,1)S(1)}, u32[]{:S(2)}, u32[]{:S(2)}) collective-permute-start(bf16[64,4096]{1,0:T(8,128)(2,1)S(1)} %get-tuple-element.85), channel_id=1, source_target_pairs={{0,2},{4,0},{8,4},{12,8},{14,12},{10,14},{6,10},{2,6},{1,3},{5,1},... | collective-permute-start | bytes 1572872 | tf_op jit(solution)/shard_map/ppermute | solution.py:234
  317.7 19.0 %collective-permute-start.20 = (bf16[64,4096]{1,0:T(8,128)(2,1)S(1)}, bf16[64,4096]{1,0:T(8,128)(2,1)S(1)}, u32[]{:S(2)}, u32[]{:S(2)}) collective-permute-start(bf16[64,4096]{1,0:T(8,128)(2,1)S(1)} %get-tuple-element.84), channel_id=1, source_target_pairs={{0,4},{4,8},{8,12},{12,14},{14,10},{10,6},{6,2},{2,0},{1,5},{5,9},... | collective-permute-start | bytes 1572872 | tf_op jit(solution)/shard_map/ppermute | solution.py:234
  320.6 14.9 %collective-permute-start.30 = (bf16[64,4096]{1,0:T(8,128)(2,1)S(1)}, bf16[64,4096]{1,0:T(8,128)(2,1)S(1)}, u32[]{:S(2)}, u32[]{:S(2)}) collective-permute-start(bf16[64,4096]{1,0:T(8,128)(2,1)S(1)} %fusion.5), channel_id=1, source_target_pairs={{0,2},{4,0},{8,4},{12,8},{14,12},{10,14},{6,10},{2,6},{1,3},{5,1},... | collective-permute-start | bytes 1572872 | tf_op jit(solution)/shard_map/ppermute | solution.py:234
  330.0 11.1 %collective-permute-start.23 = (bf16[64,4096]{1,0:T(8,128)(2,1)S(1)}, bf16[64,4096]{1,0:T(8,128)(2,1)S(1)}, u32[]{:S(2)}, u32[]{:S(2)}) collective-permute-start(bf16[64,4096]{1,0:T(8,128)(2,1)S(1)} %fusion.11), channel_id=1, source_target_pairs={{0,2},{4,0},{8,4},{12,8},{14,12},{10,14},{6,10},{2,6},{1,3},{5,1},... | collective-permute-start | bytes 1572872 | tf_op jit(solution)/shard_map/ppermute | solution.py:234
  (17 other events, 461.1 us)

commit v9 on v7

--- a/solution.py
+++ b/solution.py
@@ -80,21 +80,21 @@
     own_y = swap(own, 1)
     over_beside = cross(beside)
     over_passed = swap(over, 2)
-    beside_y = swap(beside, 1)
+    beside_y = swap(after(beside, own_y), 1)
     far_first = jnp.where(middle, over, over_passed)
-    far_first_y = swap(far_first, 1)
-    over_beside_passed = swap(over_beside, 2)
+    far_first_y = swap(after(far_first, beside_y), 1)
+    over_beside_passed = swap(after(over_beside, outgoing[4]), 2)
     exchange(4, over_beside)
-    exchange(6, over_beside, far_first)
+    exchange(6, over_beside)
     far_second = jnp.where(middle, over_beside, over_beside_passed)
-    far_second_y = swap(far_second, 1)
-    exchange(5, arrived[4], far_second)
-    exchange(2, arrived[4], far_second)
-    exchange(7, arrived[6], far_first_y)
-    exchange(3, arrived[6], far_first_y)
-    exchange(1, arrived[6], far_first_y)
-    near = [after(own, far_second, arrived[4]), beside, own_y, beside_y]
-    far = [after(far_first, arrived[6]), far_second, far_first_y, far_second_y]
+    far_second_y = swap(after(far_second, far_first_y), 1)
+    exchange(5, far_first_y, far_second)
+    exchange(2, far_first_y, far_second)
+    exchange(7, arrived[4], far_first_y)
+    exchange(3, arrived[4], far_first_y)
+    exchange(1, arrived[4], far_first_y)
+    near = [after(own, far_second, arrived[4], arrived[6]), beside, own_y, beside_y]
+    far = [far_first, far_second, far_first_y, far_second_y]
     return near, far, [arrived[apart] for apart in range(LINE_MODELS)]
 
 
@@ -232,14 +232,6 @@
                 (self.order[i], self.order[(i + way) % self.n_model]) for i in range(self.n_model)
             ]
             self.moving[way] = lax.ppermute(self.moving[way], "mp", pairs)
-
-    def step(self, *held):
-        started = self.advance()
-        blocks, held = lax.optimization_barrier(([self.moving[way] for way in started], held))
-        for way, block in zip(started, blocks):
-            self.moving[way] = block
-        self.send(started)
-        return held
 
     def finish(self):
         while any(self.distance.values()):
@@ -362,7 +354,7 @@
     )
 
 
-def attend_kernel(span, row_step, chunk, half_ref, *refs):
+def attend_kernel(span, half_ref, *refs):
     query_refs, (key_ref, value_ref), new_key_refs, new_value_refs, out_ref = (
         refs[:2],
         refs[2:4],
@@ -371,54 +363,49 @@
         refs[8],
     )
     rows = out_ref.shape[0]
-    half = new_key_refs[0].shape[0]
-    queries = jnp.concatenate([ref[0].reshape(rows // 2, HD) for ref in query_refs], 0)
+    half = rows // 2
+    queries = jnp.concatenate([ref[0] for ref in query_refs], 0)
     spans = key_ref.shape[0] // span
-    stride = 2 * half * row_step // rows
     turn = half_ref[0] * half
-    local = lax.broadcasted_iota(jnp.int32, (rows, half), 0)
-    token = (local // row_step) * stride + chunk * row_step + local % row_step
-    token = lax.rem(token + turn, 2 * half)
+    token = lax.rem(lax.broadcasted_iota(jnp.int32, (rows, half), 0) + turn, rows)
     column = lax.broadcasted_iota(jnp.int32, (rows, half), 1)
     parts = []
     for side, ref in enumerate(new_key_refs):
-        causal = column + lax.rem(turn + side * half, 2 * half) <= token
+        causal = column + lax.rem(turn + side * half, rows) <= token
         parts.append(jnp.where(causal, dot_keys(queries, ref[...]), -jnp.inf))
     scores = jnp.concatenate(parts, 1)
     peak = jnp.max(scores, axis=1, keepdims=True)
     total = None
     values = jnp.concatenate([ref[...] for ref in new_value_refs], 0)
-    for step in range(spans + 1):
-        if step < spans:
-            next_scores = dot_keys(queries, key_ref[step * span : (step + 1) * span, :])
+    for index in range(spans + 1):
+        if index < spans:
+            next_scores = dot_keys(queries, key_ref[index * span : (index + 1) * span, :])
             next_peak = jnp.maximum(peak, jnp.max(next_scores, axis=1, keepdims=True))
         weights = jnp.exp2((scores - peak) * SCORE_SCALE).astype(jnp.bfloat16)
         product = jnp.dot(weights, values, preferred_element_type=jnp.float32)
         total = product if total is None else total + product
-        if step < spans:
+        if index < spans:
             total = total * jnp.exp2((peak - next_peak) * SCORE_SCALE)
             scores, peak = next_scores, next_peak
-            values = value_ref[step * span : (step + 1) * span, :]
+            values = value_ref[index * span : (index + 1) * span, :]
     out_ref[...] = (total[:, :HD] / total[:, HD:]).astype(jnp.bfloat16)
 
 
-def attend(half, queries, prefix, new_keys, new_values, row_step, chunk, first_head, heads):
-    owners = queries[0].shape[1]
-    rows = 2 * owners * row_step
+def attend(half, queries, prefix, new_keys, new_values):
+    heads = queries[0].shape[0]
+    rows = 2 * new_keys[0].shape[0]
     span = math.gcd(prefix[0].shape[0], 1024)
-    whole = lambda array: pl.BlockSpec(array.shape, lambda head: (0, 0))
-    count = prefix[0].shape[0] + 2 * new_keys[0].shape[0]
-    query_spec = pl.BlockSpec(
-        (1, owners, None, row_step, HD), lambda head: (first_head + head, 0, chunk, 0, 0)
-    )
+    whole = lambda array: pl.BlockSpec(array.shape, lambda step: (0, 0))
+    count = prefix[0].shape[0] + rows
+    query_spec = pl.BlockSpec((1, rows // 2, HD), lambda step: (step, 0, 0))
     fixed = (*prefix, *new_keys, *new_values)
     return pl.pallas_call(
-        functools.partial(attend_kernel, span, row_step, chunk),
+        functools.partial(attend_kernel, span),
         grid=(heads,),
         out_shape=jax.ShapeDtypeStruct((rows, heads * HD), jnp.bfloat16),
         in_specs=[pl.BlockSpec(memory_space=pltpu.SMEM), query_spec, query_spec]
         + [whole(array) for array in fixed],
-        out_specs=pl.BlockSpec((rows, HD), lambda head: (0, head)),
+        out_specs=pl.BlockSpec((rows, HD), lambda step: (0, step)),
         compiler_params=pltpu.CompilerParams(vmem_limit_bytes=ATTEND_VMEM),
         cost_estimate=pl.CostEstimate(
             flops=heads * rows * count * HD * 8,
@@ -427,39 +414,6 @@
         ),
         name="attend",
     )(half, *queries, *fixed)
-
-
-def output_kernel(mixed_ref, *refs):
-    *weight_refs, out_ref = refs
-    weight = jnp.concatenate([ref[...] for ref in weight_refs], axis=0)
-    out_ref[...] = jnp.dot(
-        mixed_ref[...], weight, preferred_element_type=jnp.float32
-    ).astype(jnp.bfloat16)
-
-
-def output_product(mixed, weight, chunk, chunks):
-    rows, depth = mixed.shape
-    width = weight.shape[1] // chunks
-    tile = math.gcd(width, 1024)
-    tiles = width // tile
-    return pl.pallas_call(
-        output_kernel,
-        grid=(tiles,),
-        out_shape=jax.ShapeDtypeStruct((rows, width), jnp.bfloat16),
-        in_specs=[pl.BlockSpec((rows, depth), lambda col: (0, 0))]
-        + [
-            pl.BlockSpec((depth // STREAMS, tile), lambda col, part=part: (part, chunk * tiles + col))
-            for part in range(STREAMS)
-        ],
-        out_specs=pl.BlockSpec((rows, tile), lambda col: (0, col)),
-        compiler_params=pltpu.CompilerParams(vmem_limit_bytes=VMEM_LIMIT),
-        cost_estimate=pl.CostEstimate(
-            flops=2 * rows * depth * width,
-            bytes_accessed=2 * (rows * depth + depth * width + rows * width),
-            transcendentals=0,
-        ),
-        name="output_product",
-    )(mixed, *[weight] * STREAMS)
 
 
 def on_device(
@@ -580,31 +534,36 @@
         new_keys = [key_whole[part] for part in halves]
         new_values = [value_ones[part] for part in halves]
 
-    arrived, new_keys = lax.optimization_barrier((arrived, list(new_keys)))
-    prefix = order_blocks(arrived, where, prefix_count.reshape(1))
-
-    queries = [part.reshape(q_local, -1, 1, row_count, HD) for part in queries]
-    mixed = attend(
-        upper_half.reshape(1), queries, prefix, new_keys, new_values, row_count, 0, 0, q_local
-    )
     pairs = lax.all_to_all(pairs, "mp", split_axis=0, concat_axis=0, tiled=True)
-    mixed, pairs = lax.optimization_barrier((mixed, pairs))
+    arrived, new_keys, pairs = lax.optimization_barrier((arrived, list(new_keys), pairs))
     cache_rows = (
         pairs.reshape(kv_heads, sharers, row_count, 2, kv_local)
         .transpose(2, 0, 3, 1, 4)
         .reshape(1, row_count, kv_heads * 2 * HD)
     )
-
-    width = w_out.shape[1]
+    prefix = order_blocks(arrived, where, prefix_count.reshape(1))
+    mixed = attend(upper_half.reshape(1), queries, prefix, new_keys, new_values)
+    width = w_out.shape[1] // COLUMN_CHUNKS
+    shares = [
+        jnp.dot(
+            mixed,
+            w_out[:, chunk * width : (chunk + 1) * width],
+            preferred_element_type=jnp.float32,
+        ).astype(jnp.bfloat16)
+        for chunk in range(COLUMN_CHUNKS)
+    ]
+
     first = upper_half * (n_model // 2)
-    scatters = []
-    for chunk in range(COLUMN_CHUNKS):
-        share = output_product(mixed, w_out, chunk, COLUMN_CHUNKS)
-        share = share.reshape(n_model, row_count, width // COLUMN_CHUNKS)
-        scatters.append(
-            RingScatter(share, n_model, my_model, first, 1 if chunk % 2 == 0 else -1)
+    scatters = [
+        RingScatter(
+            share.reshape(n_model, row_count, -1),
+            n_model,
+            my_model,
+            first,
+            1 if chunk % 2 == 0 else -1,
         )
-        (mixed,) = scatters[-1].step(mixed)
+        for chunk, share in enumerate(shares)
+    ]
     return (jnp.concatenate([scatter.finish() for scatter in scatters], 1)[None], cache_rows)
 
 

time: 331 us -> 321 us (0.970)
  waiting for transfers between devices: 115 us -> 132 us
  Pallas kernels: 80.7 us -> 64.6 us
  starting transfers between devices: 75.3 us -> 61.1 us
  matrix products: 0 us -> 10.8 us
  local copies, waits for them, and re-layouts: 17.3 us -> 13.4 us
    pallas_call x3 -> x1, Pallas kernels: 42.3 us -> 24.7 us  [attend(): pl.pallas_call(functools.partial(attend_kernel, span), grid=(heads,), out...]
    all_to_all x1, waiting for transfers between devices: 0.01 us -> 11.3 us  [on_device(): pairs = lax.all_to_all(pairs, 'mp', split_axis=0, concat_axis=0, tiled=True)]
    dot_general x0 -> x2, matrix products: none -> 10.8 us  [on_device(): jnp.dot(mixed, w_out[:, chunk * width:(chunk + 1) * width], preferred_ele...]
    ppermute x14, starting transfers between devices: 21.1 us -> 14.4 us  [send(): self.moving[way] = lax.ppermute(self.moving[way], 'mp', pairs)]
    ppermute x14, waiting for transfers between devices: 63.7 us -> 69.5 us  [send(): self.moving[way] = lax.ppermute(self.moving[way], 'mp', pairs)]
    all_to_all x1, starting transfers between devices: 9.62 us -> 4.22 us  [on_device(): pairs = lax.all_to_all(pairs, 'mp', split_axis=0, concat_axis=0, tiled=True)]
    unnamed x51 -> x55, local copies, waits for them, and re-layouts: 9.14 us -> 5.49 us
  transfers between devices with their start and end apart: 32 -> 32, of which waited for: 14 -> 12; matrix products, arithmetic and copies ran while one was open for 8% -> 10% of each run, Pallas kernels for 19% -> 11%
where the time goes in v9:
time: 321 us; the launch traced here: 320 us
  waiting for transfers between devices  132 us (41%)
  Pallas kernels  64.6 us (20%)
  starting transfers between devices  61.1 us (19%)
  other arithmetic  24.8 us (8%)
  local copies, waits for them, and re-layouts  13.4 us (4%)
  between operations  12.8 us (4%)
  matrix products  10.8 us (3%)
    ppermute x14, waiting for transfers between devices, send(): self.moving[way] = lax.ppermute(self.moving[way], 'mp', pairs)  69.5 us
    ppermute x14, waiting for transfers between devices, swap(): lax.ppermute(block, 'mp', [(index, index ^ mask) for index in range(LINE_...  51.4 us
    ppermute x14, starting transfers between devices, swap(): lax.ppermute(block, 'mp', [(index, index ^ mask) for index in range(LINE_...  42 us
    pallas_call x2, Pallas kernels, project(): pl.pallas_call(project_kernel, grid=(width // depth,), out_shape=out_shap...  31.3 us
    pallas_call x1, Pallas kernels, attend(): pl.pallas_call(functools.partial(attend_kernel, span), grid=(heads,), out...  24.7 us
    ppermute x14, starting transfers between devices, send(): self.moving[way] = lax.ppermute(self.moving[way], 'mp', pairs)  14.4 us
    all_to_all x1, waiting for transfers between devices, on_device(): pairs = lax.all_to_all(pairs, 'mp', split_axis=0, concat_axis=0, tiled=True)  11.3 us
    dot_general x2, matrix products, on_device(): jnp.dot(mixed, w_out[:, chunk * width:(chunk + 1) * width], preferred_ele...  10.8 us
  transfers between devices with their start and end apart: 32, of which 12 were waited for; matrix products, arithmetic and copies ran while one was open for 10% of the time, Pallas kernels for 11%

profile of v9, /device:TPU:0, one launch (start us, length us, event | category | flops | bytes accessed | tf_op | source)
XLA Modules:
  0.0 319.8 jit_solution(5487358260309957112)
XLA Ops:
  3.3 2.2 copy-done
  7.5 2.9 collective-permute-start
  11.9 22.1 %collective-permute-done.refs_1_ = bf16[64,8192]{1,0:T(8,128)(2,1)} collective-permute-done((bf16[64,8192]{1,0:T(8,128)(2,1)S(1)}, bf16[64,8192]{1,0:T(8,128)(2,1)}, u32[]{:S(2)}, u32[]{:S(2)}) %collective-permute-start) | collective-permute-done | bytes 1048608 | tf_op jit(solution)/shard_map/ppermute | solution.py:54
  34.1 3.3 %collective-permute-start.9 = (bf16[64,8192]{1,0:T(8,128)(2,1)}, bf16[64,8192]{1,0:T(8,128)(2,1)}, u32[]{:S(2)}, u32[]{:S(2)}) collective-permute-start(bf16[64,8192]{1,0:T(8,128)(2,1)} %collective-permute-done.8), channel_id=1, source_target_pairs={{0,4},{2,6},{4,0},{6,2},{8,12},{10,14},{12,8},{14,10},{1,5},{3,7},... | collective-permute-start | bytes 3145736 | tf_op jit(solution)/shard_map/ppermute | solution.py:54
  38.0 1.6 collective-permute-start.7
  39.6 2.2 copy-done.1
  41.8 4.1 %pack_blocks.1 = (bf16[2,32,16,256]{3,2,1,0:T(8,128)(2,1)S(1)}, bf16[2,32,16,256]{3,2,1,0:T(8,128)(2,1)}, bf16[2,32,16,256]{3,2,1,0:T(8,128)(2,1)}, bf16[2,32,16...) custom-call(s32[2,32]{1,0:T(2,128)S(1)} %pad_add_fusion.slots_ref, ...), custom_call_target="tpu_custom_call" | custom-call | tf_op jit(solution)/shard_map/pack_blocks/pallas_call | solution.py:285
  45.9 14.6 %collective-permute-start.3 = (bf16[64,8192]{1,0:T(8,128)(2,1)}, bf16[64,8192]{1,0:T(8,128)(2,1)S(1)}, u32[]{:S(2)}, u32[]{:S(2)}) collective-permute-start(bf16[64,8192]{1,0:T(8,128)(2,1)} %collective-permute-done.1), channel_id=1, source_target_pairs={{0,4},{2,6},{4,0},{6,2},{8,12},{10,14},{12,8},{14,10},{1,5},{3,7},... | collective-permute-start | bytes 3145736 | tf_op jit(solution)/shard_map/ppermute | solution.py:54
  67.0 27.2 %collective-permute-done.3 = bf16[64,8192]{1,0:T(8,128)(2,1)S(1)} collective-permute-done((bf16[64,8192]{1,0:T(8,128)(2,1)}, bf16[64,8192]{1,0:T(8,128)(2,1)S(1)}, u32[]{:S(2)}, u32[]{:S(2)}) %collective-permute-start.3) | collective-permute-done | bytes 1048608 | tf_op jit(solution)/shard_map/ppermute | solution.py:54
  95.3 1.6 collective-permute-start.11
  113.8 1.8 collective-permute-start.14
  115.7 5.3 %collective-permute-start.15 = (bf16[2,32,16,256]{3,2,1,0:T(8,128)(2,1)}, bf16[2,32,16,256]{3,2,1,0:T(8,128)(2,1)}, u32[]{:S(2)}, u32[]{:S(2)}) collective-permute-start(bf16[2,32,16,256]{3,2,1,0:T(8,128)(2,1)} %copy-done.2), channel_id=1, source_target_pairs={{0,10},{2,8},{4,14},{6,12},{8,2},{10,0},{12,6},{14,4},{1,11},{3,9}... | collective-permute-start | bytes 1572872 | tf_op jit(solution)/shard_map/ppermute | solution.py:54
  121.0 15.6 %project.2 = (bf16[8,256,128]{2,1,0:T(8,128)(2,1)}, bf16[256,128]{1,0:T(8,128)(2,1)}, bf16[256,256]{1,0:T(8,128)(2,1)}, bf16[256,256]{1,0:T(8,128)(2,1)}) custom-call(s32[4]{0:T(128)} %add_multiply_fusion.starts_ref, bf16[64,8192]{1,0:T(8,128)(2,1)} %copy-done.10, bf16[64,8192]{1,0:T(8,128)(2,1)} %collective-permute-done.refs_1_, ...), custom_call_target="tpu_custom_call" | custom-call | flops 5368709120 | bytes 26476544 | tf_op jit(solution)/shard_map/project/pallas_call | solution.py:177
  136.6 3.6 %collective-permute-start.16 = (bf16[2,32,16,256]{3,2,1,0:T(8,128)(2,1)}, bf16[2,32,16,256]{3,2,1,0:T(8,128)(2,1)}, u32[]{:S(2)}, u32[]{:S(2)}) collective-permute-start(bf16[2,32,16,256]{3,2,1,0:T(8,128)(2,1)} %get-tuple-element.64), channel_id=1, source_target_pairs={{0,14},{2,12},{4,10},{6,8},{8,6},{10,4},{12,2},{14,0},{1,15},{3,13... | collective-permute-start | bytes 1572872 | tf_op jit(solution)/shard_map/ppermute | solution.py:54
  140.2 15.7 %project.3 = (bf16[8,256,128]{2,1,0:T(8,128)(2,1)}, bf16[256,128]{1,0:T(8,128)(2,1)}, bf16[256,256]{1,0:T(8,128)(2,1)}, bf16[256,256]{1,0:T(8,128)(2,1)}) custom-call(s32[4]{0:T(128)} %add_multiply_fusion.1.starts_ref, bf16[64,8192]{1,0:T(8,128)(2,1)} %copy-done.11, bf16[64,8192]{1,0:T(8,128)(2,1)} %broadcast_select_fusion.1.refs_1_, ...), custom_call_target="tpu_custom_call" | custom-call | flops 5368709120 | bytes 26476544 | tf_op jit(solution)/shard_map/project/pallas_call | solution.py:177
  155.9 1.8 maximum_select_fusion
  157.7 4.2 %all-to-all-start = ((bf16[8,64,256]{2,1,0:T(8,128)(2,1)}), bf16[8,64,256]{2,1,0:T(8,128)(2,1)}, u32[]{:S(2)}, u32[]{:S(2)}) async-start(bf16[8,64,256]{2,1,0:T(8,128)(2,1)} %bitcast.122), calls=%async_computation | async-start | bytes 524288 | tf_op jit(solution)/shard_map/all_to_all | solution.py:537
  164.2 2.1 collective-permute-done.16
  166.3 11.3 %all-to-all-done = bf16[8,64,256]{2,1,0:T(8,128)(2,1)} async-done(((bf16[8,64,256]{2,1,0:T(8,128)(2,1)}), bf16[8,64,256]{2,1,0:T(8,128)(2,1)}, u32[]{:S(2)}, u32[]{:S(2)}) %all-to-all-start) | async-done | bytes 262176 | tf_op jit(solution)/shard_map/all_to_all | solution.py:537
  177.7 3.7 %order_blocks.1 = (bf16[4096,128]{1,0:T(8,128)(2,1)S(1)}, bf16[4096,256]{1,0:T(8,128)(2,1)S(1)}) custom-call(s32[1]{0:T(128)} %dynamic_slice.118.length_ref, s32[256]{0:T(256)S(1)} %multiply_add_fusion.where_ref, bf16[64,16,256]{2,1,0:T(8,128)(2,1)S(1)} %bitcast.110, bf16[64,16,256]{2,1,0:T(8,128)(2,1)S(1)} %bitcast.113, bf16[64,16,256]{2,1,0:T(8,128)(2,1)S(1)} %bitcast.114, ...), custom_call_target="tpu_custom_call" | custom-call | tf_op jit(solution)/shard_map/order_blocks/pallas_call | solution.py:330
  181.5 24.7 %attend.1 = bf16[512,1024]{1,0:T(8,128)(2,1)S(1)} custom-call(s32[1]{0:T(128)} %bitcast.half_ref, bf16[8,256,128]{2,1,0:T(8,128)(2,1)S(1)} %copy-done.4, bf16[8,256,128]{2,1,0:T(8,128)(2,1)S(1)} %copy-done.5, bf16[4096,128]{1,0:T(8,128)(2,1)S(1)} %get-tuple-element.77.refs_2_, bf16[4096,256]{1,0:T(8,128)(2,1)S(1)} %get-tuple-element.78.refs_3_, ...), custom_call_target="tpu_custom_call" | custom-call | flops 19327352832 | bytes 5636096 | tf_op jit(solution)/shard_map/attend/pallas_call | solution.py:402
  206.3 4.7 %fusion.7 = bf16[512,4096]{1,0:T(8,128)(2,1)S(1)} fusion(bf16[512,1024]{1,0:T(8,128)(2,1)S(1)} %attend.1, bf16[1024,8192]{1,0:T(8,128)(2,1)S(1)} %bitcast.133), kind=kOutput, calls=%fused_computation.5 | convolution fusion | flops 4297064448 | bytes 13631488 | tf_op jit(solution)/shard_map/dot_general | solution.py:548
  212.6 6.0 %fusion.4 = bf16[512,4096]{1,0:T(8,128)(2,1)} fusion(bf16[512,1024]{1,0:T(8,128)(2,1)S(1)} %attend.1, bf16[1024,8192]{1,0:T(8,128)(2,1)S(1)} %bitcast.133), kind=kOutput, calls=%fused_computation.4 | convolution fusion | flops 4297064448 | bytes 13631488 | tf_op jit(solution)/shard_map/dot_general | solution.py:548
  220.1 2.1 dynamic-slice_bitcast_fusion.3
  228.9 8.9 %collective-permute-done.17 = bf16[64,4096]{1,0:T(8,128)(2,1)S(1)} collective-permute-done((bf16[64,4096]{1,0:T(8,128)(2,1)}, bf16[64,4096]{1,0:T(8,128)(2,1)S(1)}, u32[]{:S(2)}, u32[]{:S(2)}) %collective-permute-start.17) | collective-permute-done | bytes 524320 | tf_op jit(solution)/shard_map/ppermute | solution.py:234
  240.2 8.9 %collective-permute-done.25 = bf16[64,4096]{1,0:T(8,128)(2,1)S(1)} collective-permute-done((bf16[64,4096]{1,0:T(8,128)(2,1)S(1)}, bf16[64,4096]{1,0:T(8,128)(2,1)S(1)}, u32[]{:S(2)}, u32[]{:S(2)}) %collective-permute-start.25) | collective-permute-done | bytes 524320 | tf_op jit(solution)/shard_map/ppermute | solution.py:234
  249.1 1.6 fusion.17
  252.8 7.5 %collective-permute-done.18 = bf16[64,4096]{1,0:T(8,128)(2,1)S(1)} collective-permute-done((bf16[64,4096]{1,0:T(8,128)(2,1)S(1)}, bf16[64,4096]{1,0:T(8,128)(2,1)S(1)}, u32[]{:S(2)}, u32[]{:S(2)}) %collective-permute-start.18) | collective-permute-done | bytes 524320 | tf_op jit(solution)/shard_map/ppermute | solution.py:234
  264.8 16.4 %collective-permute-done.19 = bf16[64,4096]{1,0:T(8,128)(2,1)S(1)} collective-permute-done((bf16[64,4096]{1,0:T(8,128)(2,1)S(1)}, bf16[64,4096]{1,0:T(8,128)(2,1)S(1)}, u32[]{:S(2)}, u32[]{:S(2)}) %collective-permute-start.19) | collective-permute-done | bytes 524320 | tf_op jit(solution)/shard_map/ppermute | solution.py:234
  286.7 10.8 %collective-permute-done.22 = bf16[64,4096]{1,0:T(8,128)(2,1)S(1)} collective-permute-done((bf16[64,4096]{1,0:T(8,128)(2,1)S(1)}, bf16[64,4096]{1,0:T(8,128)(2,1)S(1)}, u32[]{:S(2)}, u32[]{:S(2)}) %collective-permute-start.22) | collective-permute-done | bytes 524320 | tf_op jit(solution)/shard_map/ppermute | solution.py:234
  299.6 9.2 %collective-permute-done.30 = bf16[64,4096]{1,0:T(8,128)(2,1)S(1)} collective-permute-done((bf16[64,4096]{1,0:T(8,128)(2,1)S(1)}, bf16[64,4096]{1,0:T(8,128)(2,1)S(1)}, u32[]{:S(2)}, u32[]{:S(2)}) %collective-permute-start.30) | collective-permute-done | bytes 524320 | tf_op jit(solution)/shard_map/ppermute | solution.py:234
  310.0 7.5 %collective-permute-done.23 = bf16[64,4096]{1,0:T(8,128)(2,1)S(1)} collective-permute-done((bf16[64,4096]{1,0:T(8,128)(2,1)S(1)}, bf16[64,4096]{1,0:T(8,128)(2,1)S(1)}, u32[]{:S(2)}, u32[]{:S(2)}) %collective-permute-start.23) | collective-permute-done | bytes 524320 | tf_op jit(solution)/shard_map/ppermute | solution.py:234
  (143 shorter events, 51.7 us)
Async XLA Ops:
  6.3 33.3 %collective-permute-start.2 = (bf16[32,16,2048]{2,1,0:T(8,128)(2,1)S(1)}, bf16[32,16,2048]{2,1,0:T(8,128)(2,1)}, u32[]{:S(2)}, u32[]{:S(2)}) collective-permute-start(bf16[32,16,2048]{2,1,0:T(8,128)(2,1)S(1)} %pick_blocks.1), channel_id=1, source_target_pairs={{0,1},{1,0},{2,3},{3,2},{4,5},{5,4},{6,7},{7,6},{8,9},{9,8},{10,11... | collective-permute-start | bytes 6291464 | tf_op jit(solution)/shard_map/ppermute | solution.py:469
  7.5 26.6 %collective-permute-start = (bf16[64,8192]{1,0:T(8,128)(2,1)S(1)}, bf16[64,8192]{1,0:T(8,128)(2,1)}, u32[]{:S(2)}, u32[]{:S(2)}) collective-permute-start(bf16[64,8192]{1,0:T(8,128)(2,1)S(1)} %fusion.12.refs_0_), channel_id=1, source_target_pairs={{0,4},{2,6},{4,0},{6,2},{8,12},{10,14},{12,8},{14,10},{1,5},{3,7},... | collective-permute-start | bytes 3145736 | tf_op jit(solution)/shard_map/ppermute | solution.py:54
  10.4 23.6 %collective-permute-start.8 = (bf16[64,8192]{1,0:T(8,128)(2,1)S(1)}, bf16[64,8192]{1,0:T(8,128)(2,1)}, u32[]{:S(2)}, u32[]{:S(2)}) collective-permute-start(bf16[64,8192]{1,0:T(8,128)(2,1)S(1)} %fusion.12.refs_0_), channel_id=1, source_target_pairs={{0,1},{1,0},{2,3},{3,2},{4,8},{5,9},{6,10},{7,11},{8,4},{9,5},{10,... | collective-permute-start | bytes 3145736 | tf_op jit(solution)/shard_map/ppermute | solution.py:65
  10.4 27.6 %collective-permute-start.6 = (bf16[64,8192]{1,0:T(8,128)(2,1)S(1)}, bf16[64,8192]{1,0:T(8,128)(2,1)}, u32[]{:S(2)}, u32[]{:S(2)}) collective-permute-start(bf16[64,8192]{1,0:T(8,128)(2,1)S(1)} %fusion.12.refs_0_), channel_id=1, source_target_pairs={{0,2},{2,0},{4,6},{6,4},{8,10},{10,8},{12,14},{14,12},{1,3},{3,1},... | collective-permute-start | bytes 3145736 | tf_op jit(solution)/shard_map/ppermute | solution.py:54
  34.1 11.9 %collective-permute-start.1 = (bf16[64,8192]{1,0:T(8,128)(2,1)}, bf16[64,8192]{1,0:T(8,128)(2,1)}, u32[]{:S(2)}, u32[]{:S(2)}) collective-permute-start(bf16[64,8192]{1,0:T(8,128)(2,1)} %collective-permute-done.refs_1_), channel_id=1, source_target_pairs={{0,1},{1,0},{2,3},{3,2},{4,8},{5,9},{6,10},{7,11},{8,4},{9,5},{10,... | collective-permute-start | bytes 3145736 | tf_op jit(solution)/shard_map/ppermute | solution.py:65
  34.1 29.0 %collective-permute-start.9 = (bf16[64,8192]{1,0:T(8,128)(2,1)}, bf16[64,8192]{1,0:T(8,128)(2,1)}, u32[]{:S(2)}, u32[]{:S(2)}) collective-permute-start(bf16[64,8192]{1,0:T(8,128)(2,1)} %collective-permute-done.8), channel_id=1, source_target_pairs={{0,4},{2,6},{4,0},{6,2},{8,12},{10,14},{12,8},{14,10},{1,5},{3,7},... | collective-permute-start | bytes 3145736 | tf_op jit(solution)/shard_map/ppermute | solution.py:54
  38.0 26.4 %collective-permute-start.7 = (bf16[64,8192]{1,0:T(8,128)(2,1)}, bf16[64,8192]{1,0:T(8,128)(2,1)S(1)}, u32[]{:S(2)}, u32[]{:S(2)}) collective-permute-start(bf16[64,8192]{1,0:T(8,128)(2,1)} %collective-permute-done.refs_1_), channel_id=1, source_target_pairs={{0,2},{2,0},{4,6},{6,4},{8,10},{10,8},{12,14},{14,12},{1,3},{3,1},... | collective-permute-start | bytes 3145736 | tf_op jit(solution)/shard_map/ppermute | solution.py:54
  45.9 48.2 %collective-permute-start.3 = (bf16[64,8192]{1,0:T(8,128)(2,1)}, bf16[64,8192]{1,0:T(8,128)(2,1)S(1)}, u32[]{:S(2)}, u32[]{:S(2)}) collective-permute-start(bf16[64,8192]{1,0:T(8,128)(2,1)} %collective-permute-done.1), channel_id=1, source_target_pairs={{0,4},{2,6},{4,0},{6,2},{8,12},{10,14},{12,8},{14,10},{1,5},{3,7},... | collective-permute-start | bytes 3145736 | tf_op jit(solution)/shard_map/ppermute | solution.py:54
  60.5 51.6 %collective-permute-start.4 = (bf16[2,32,16,256]{3,2,1,0:T(8,128)(2,1)S(1)}, bf16[2,32,16,256]{3,2,1,0:T(8,128)(2,1)S(1)}, u32[]{:S(2)}, u32[]{:S(2)}) collective-permute-start(bf16[2,32,16,256]{3,2,1,0:T(8,128)(2,1)S(1)} %get-tuple-element.45), channel_id=1, source_target_pairs={{0,8},{2,10},{4,12},{6,14},{8,0},{10,2},{12,4},{14,6},{1,9},{3,11}... | collective-permute-start | bytes 1572872 | tf_op jit(solution)/shard_map/ppermute | solution.py:54
  61.6 50.6 %collective-permute-start.5 = (bf16[2,32,16,256]{3,2,1,0:T(8,128)(2,1)S(1)}, bf16[2,32,16,256]{3,2,1,0:T(8,128)(2,1)S(1)}, u32[]{:S(2)}, u32[]{:S(2)}) collective-permute-start(bf16[2,32,16,256]{3,2,1,0:T(8,128)(2,1)S(1)} %get-tuple-element.47), channel_id=1, source_target_pairs={{0,12},{2,14},{4,8},{6,10},{8,4},{10,6},{12,0},{14,2},{1,13},{3,15... | collective-permute-start | bytes 1572872 | tf_op jit(solution)/shard_map/ppermute | solution.py:54
  65.5 29.8 %collective-permute-start.10 = (bf16[64,8192]{1,0:T(8,128)(2,1)S(1)}, bf16[64,8192]{1,0:T(8,128)(2,1)S(1)}, u32[]{:S(2)}, u32[]{:S(2)}) collective-permute-start(bf16[64,8192]{1,0:T(8,128)(2,1)S(1)} %broadcast_select_fusion.refs_0_), channel_id=1, source_target_pairs={{0,2},{2,0},{4,6},{6,4},{8,10},{10,8},{12,14},{14,12},{1,3},{3,1},... | collective-permute-start | bytes 3145736 | tf_op jit(solution)/shard_map/ppermute | solution.py:54
  95.3 41.3 %collective-permute-start.11 = (bf16[64,8192]{1,0:T(8,128)(2,1)}, bf16[64,8192]{1,0:T(8,128)(2,1)}, u32[]{:S(2)}, u32[]{:S(2)}) collective-permute-start(bf16[64,8192]{1,0:T(8,128)(2,1)} %broadcast_select_fusion.1.refs_1_), channel_id=1, source_target_pairs={{0,2},{2,0},{4,6},{6,4},{8,10},{10,8},{12,14},{14,12},{1,3},{3,1},... | collective-permute-start | bytes 3145736 | tf_op jit(solution)/shard_map/ppermute | solution.py:54
  112.1 52.0 %collective-permute-start.12 = (bf16[2,32,16,256]{3,2,1,0:T(8,128)(2,1)}, bf16[2,32,16,256]{3,2,1,0:T(8,128)(2,1)S(1)}, u32[]{:S(2)}, u32[]{:S(2)}) collective-permute-start(bf16[2,32,16,256]{3,2,1,0:T(8,128)(2,1)} %get-tuple-element.56), channel_id=1, source_target_pairs={{0,2},{2,0},{4,6},{6,4},{8,10},{10,8},{12,14},{14,12},{1,3},{3,1},... | collective-permute-start | bytes 1572872 | tf_op jit(solution)/shard_map/ppermute | solution.py:54
  113.1 51.1 %collective-permute-start.13 = (bf16[2,32,16,256]{3,2,1,0:T(8,128)(2,1)}, bf16[2,32,16,256]{3,2,1,0:T(8,128)(2,1)S(1)}, u32[]{:S(2)}, u32[]{:S(2)}) collective-permute-start(bf16[2,32,16,256]{3,2,1,0:T(8,128)(2,1)} %get-tuple-element.58), channel_id=1, source_target_pairs={{0,4},{2,6},{4,0},{6,2},{8,12},{10,14},{12,8},{14,10},{1,5},{3,7},... | collective-permute-start | bytes 1572872 | tf_op jit(solution)/shard_map/ppermute | solution.py:54
  113.8 50.3 %collective-permute-start.14 = (bf16[2,32,16,256]{3,2,1,0:T(8,128)(2,1)}, bf16[2,32,16,256]{3,2,1,0:T(8,128)(2,1)S(1)}, u32[]{:S(2)}, u32[]{:S(2)}) collective-permute-start(bf16[2,32,16,256]{3,2,1,0:T(8,128)(2,1)} %copy-done.3), channel_id=1, source_target_pairs={{0,6},{2,4},{4,2},{6,0},{8,14},{10,12},{12,10},{14,8},{1,7},{3,5},... | collective-permute-start | bytes 1572872 | tf_op jit(solution)/shard_map/ppermute | solution.py:54
  115.7 48.5 %collective-permute-start.15 = (bf16[2,32,16,256]{3,2,1,0:T(8,128)(2,1)}, bf16[2,32,16,256]{3,2,1,0:T(8,128)(2,1)}, u32[]{:S(2)}, u32[]{:S(2)}) collective-permute-start(bf16[2,32,16,256]{3,2,1,0:T(8,128)(2,1)} %copy-done.2), channel_id=1, source_target_pairs={{0,10},{2,8},{4,14},{6,12},{8,2},{10,0},{12,6},{14,4},{1,11},{3,9}... | collective-permute-start | bytes 1572872 | tf_op jit(solution)/shard_map/ppermute | solution.py:54
  136.6 29.7 %collective-permute-start.16 = (bf16[2,32,16,256]{3,2,1,0:T(8,128)(2,1)}, bf16[2,32,16,256]{3,2,1,0:T(8,128)(2,1)}, u32[]{:S(2)}, u32[]{:S(2)}) collective-permute-start(bf16[2,32,16,256]{3,2,1,0:T(8,128)(2,1)} %get-tuple-element.64), channel_id=1, source_target_pairs={{0,14},{2,12},{4,10},{6,8},{8,6},{10,4},{12,2},{14,0},{1,15},{3,13... | collective-permute-start | bytes 1572872 | tf_op jit(solution)/shard_map/ppermute | solution.py:54
  157.7 19.9 %all-to-all-start = ((bf16[8,64,256]{2,1,0:T(8,128)(2,1)}), bf16[8,64,256]{2,1,0:T(8,128)(2,1)}, u32[]{:S(2)}, u32[]{:S(2)}) async-start(bf16[8,64,256]{2,1,0:T(8,128)(2,1)} %bitcast.122), calls=%async_computation | async-start | bytes 524288 | tf_op jit(solution)/shard_map/all_to_all | solution.py:537
  212.0 14.5 %collective-permute-start.24 = (bf16[64,4096]{1,0:T(8,128)(2,1)}, bf16[64,4096]{1,0:T(8,128)(2,1)S(1)}, u32[]{:S(2)}, u32[]{:S(2)}) collective-permute-start(bf16[64,4096]{1,0:T(8,128)(2,1)} %get-tuple-element.92), channel_id=1, source_target_pairs={{0,4},{4,8},{8,12},{12,14},{14,10},{10,6},{6,2},{2,0},{1,5},{5,9},... | collective-permute-start | bytes 1572872 | tf_op jit(solution)/shard_map/ppermute | solution.py:234
  218.7 21.5 %collective-permute-start.27 = (bf16[64,4096]{1,0:T(8,128)(2,1)S(1)}, bf16[64,4096]{1,0:T(8,128)(2,1)}, u32[]{:S(2)}, u32[]{:S(2)}) collective-permute-start(bf16[64,4096]{1,0:T(8,128)(2,1)S(1)} %get-tuple-element.93), channel_id=1, source_target_pairs={{0,2},{4,0},{8,4},{12,8},{14,12},{10,14},{6,10},{2,6},{1,3},{5,1},... | collective-permute-start | bytes 1572872 | tf_op jit(solution)/shard_map/ppermute | solution.py:234
  222.2 15.6 %collective-permute-start.17 = (bf16[64,4096]{1,0:T(8,128)(2,1)}, bf16[64,4096]{1,0:T(8,128)(2,1)S(1)}, u32[]{:S(2)}, u32[]{:S(2)}) collective-permute-start(bf16[64,4096]{1,0:T(8,128)(2,1)} %get-tuple-element.88), channel_id=1, source_target_pairs={{0,4},{4,8},{8,12},{12,14},{14,10},{10,6},{6,2},{2,0},{1,5},{5,9},... | collective-permute-start | bytes 1572872 | tf_op jit(solution)/shard_map/ppermute | solution.py:234
  222.8 42.0 %collective-permute-start.21 = (bf16[64,4096]{1,0:T(8,128)(2,1)S(1)}, bf16[64,4096]{1,0:T(8,128)(2,1)S(1)}, u32[]{:S(2)}, u32[]{:S(2)}) collective-permute-start(bf16[64,4096]{1,0:T(8,128)(2,1)S(1)} %get-tuple-element.89), channel_id=1, source_target_pairs={{0,2},{4,0},{8,4},{12,8},{14,12},{10,14},{6,10},{2,6},{1,3},{5,1},... | collective-permute-start | bytes 1572872 | tf_op jit(solution)/shard_map/ppermute | solution.py:234
  227.7 21.3 %collective-permute-start.25 = (bf16[64,4096]{1,0:T(8,128)(2,1)S(1)}, bf16[64,4096]{1,0:T(8,128)(2,1)S(1)}, u32[]{:S(2)}, u32[]{:S(2)}) collective-permute-start(bf16[64,4096]{1,0:T(8,128)(2,1)S(1)} %fusion.16), channel_id=1, source_target_pairs={{0,4},{4,8},{8,12},{12,14},{14,10},{10,6},{6,2},{2,0},{1,5},{5,9},... | collective-permute-start | bytes 1572872 | tf_op jit(solution)/shard_map/ppermute | solution.py:234
  239.0 21.3 %collective-permute-start.18 = (bf16[64,4096]{1,0:T(8,128)(2,1)S(1)}, bf16[64,4096]{1,0:T(8,128)(2,1)S(1)}, u32[]{:S(2)}, u32[]{:S(2)}) collective-permute-start(bf16[64,4096]{1,0:T(8,128)(2,1)S(1)} %fusion.22), channel_id=1, source_target_pairs={{0,4},{4,8},{8,12},{12,14},{14,10},{10,6},{6,2},{2,0},{1,5},{5,9},... | collective-permute-start | bytes 1572872 | tf_op jit(solution)/shard_map/ppermute | solution.py:234
  250.7 12.0 %collective-permute-start.28 = (bf16[64,4096]{1,0:T(8,128)(2,1)S(1)}, bf16[64,4096]{1,0:T(8,128)(2,1)S(1)}, u32[]{:S(2)}, u32[]{:S(2)}) collective-permute-start(bf16[64,4096]{1,0:T(8,128)(2,1)S(1)} %get-tuple-element.91), channel_id=1, source_target_pairs={{0,2},{4,0},{8,4},{12,8},{14,12},{10,14},{6,10},{2,6},{1,3},{5,1},... | collective-permute-start | bytes 1572872 | tf_op jit(solution)/shard_map/ppermute | solution.py:234
  251.5 48.1 %collective-permute-start.26 = (bf16[64,4096]{1,0:T(8,128)(2,1)S(1)}, bf16[64,4096]{1,0:T(8,128)(2,1)S(1)}, u32[]{:S(2)}, u32[]{:S(2)}) collective-permute-start(bf16[64,4096]{1,0:T(8,128)(2,1)S(1)} %get-tuple-element.90), channel_id=1, source_target_pairs={{0,4},{4,8},{8,12},{12,14},{14,10},{10,6},{6,2},{2,0},{1,5},{5,9},... | collective-permute-start | bytes 1572872 | tf_op jit(solution)/shard_map/ppermute | solution.py:234
  261.5 19.7 %collective-permute-start.19 = (bf16[64,4096]{1,0:T(8,128)(2,1)S(1)}, bf16[64,4096]{1,0:T(8,128)(2,1)S(1)}, u32[]{:S(2)}, u32[]{:S(2)}) collective-permute-start(bf16[64,4096]{1,0:T(8,128)(2,1)S(1)} %fusion.23), channel_id=1, source_target_pairs={{0,4},{4,8},{8,12},{12,14},{14,10},{10,6},{6,2},{2,0},{1,5},{5,9},... | collective-permute-start | bytes 1572872 | tf_op jit(solution)/shard_map/ppermute | solution.py:234
  263.8 20.9 %collective-permute-start.29 = (bf16[64,4096]{1,0:T(8,128)(2,1)S(1)}, bf16[64,4096]{1,0:T(8,128)(2,1)S(1)}, u32[]{:S(2)}, u32[]{:S(2)}) collective-permute-start(bf16[64,4096]{1,0:T(8,128)(2,1)S(1)} %fusion.14), channel_id=1, source_target_pairs={{0,2},{4,0},{8,4},{12,8},{14,12},{10,14},{6,10},{2,6},{1,3},{5,1},... | collective-permute-start | bytes 1572872 | tf_op jit(solution)/shard_map/ppermute | solution.py:234
  282.6 14.9 %collective-permute-start.22 = (bf16[64,4096]{1,0:T(8,128)(2,1)S(1)}, bf16[64,4096]{1,0:T(8,128)(2,1)S(1)}, u32[]{:S(2)}, u32[]{:S(2)}) collective-permute-start(bf16[64,4096]{1,0:T(8,128)(2,1)S(1)} %get-tuple-element.87), channel_id=1, source_target_pairs={{0,2},{4,0},{8,4},{12,8},{14,12},{10,14},{6,10},{2,6},{1,3},{5,1},... | collective-permute-start | bytes 1572872 | tf_op jit(solution)/shard_map/ppermute | solution.py:234
  283.5 26.5 %collective-permute-start.20 = (bf16[64,4096]{1,0:T(8,128)(2,1)S(1)}, bf16[64,4096]{1,0:T(8,128)(2,1)S(1)}, u32[]{:S(2)}, u32[]{:S(2)}) collective-permute-start(bf16[64,4096]{1,0:T(8,128)(2,1)S(1)} %get-tuple-element.86), channel_id=1, source_target_pairs={{0,4},{4,8},{8,12},{12,14},{14,10},{10,6},{6,2},{2,0},{1,5},{5,9},... | collective-permute-start | bytes 1572872 | tf_op jit(solution)/shard_map/ppermute | solution.py:234
  285.9 22.9 %collective-permute-start.30 = (bf16[64,4096]{1,0:T(8,128)(2,1)S(1)}, bf16[64,4096]{1,0:T(8,128)(2,1)S(1)}, u32[]{:S(2)}, u32[]{:S(2)}) collective-permute-start(bf16[64,4096]{1,0:T(8,128)(2,1)S(1)} %fusion.15), channel_id=1, source_target_pairs={{0,2},{4,0},{8,4},{12,8},{14,12},{10,14},{6,10},{2,6},{1,3},{5,1},... | collective-permute-start | bytes 1572872 | tf_op jit(solution)/shard_map/ppermute | solution.py:234
  298.7 18.8 %collective-permute-start.23 = (bf16[64,4096]{1,0:T(8,128)(2,1)S(1)}, bf16[64,4096]{1,0:T(8,128)(2,1)S(1)}, u32[]{:S(2)}, u32[]{:S(2)}) collective-permute-start(bf16[64,4096]{1,0:T(8,128)(2,1)S(1)} %fusion.21), channel_id=1, source_target_pairs={{0,2},{4,0},{8,4},{12,8},{14,12},{10,14},{6,10},{2,6},{1,3},{5,1},... | collective-permute-start | bytes 1572872 | tf_op jit(solution)/shard_map/ppermute | solution.py:234
  (27 other events, 601.5 us)

commit v10 on v9

--- a/solution.py
+++ b/solution.py
@@ -212,30 +212,25 @@
         owner = (owner - self.first + self.n_model) % self.n_model
         return lax.dynamic_index_in_dim(self.shares, owner, 0, keepdims=False)
 
-    def advance(self):
-        started = []
-        for way in (self.way, -self.way):
-            if not self.distance[way]:
-                continue
+    def step(self, *before):
+        ways = [way for way in (self.way, -self.way) if self.distance[way]]
+        blocks = []
+        for way in ways:
             block = self.share_of(way * self.distance[way])
             if way in self.moving:
                 arrived = self.moving[way].astype(jnp.float32)
                 block = (block.astype(jnp.float32) + arrived).astype(jnp.bfloat16)
-            started.append(way)
-            self.moving[way] = block
+            blocks.append(block)
             self.distance[way] -= 1
-        return started
-
-    def send(self, started):
-        for way in started:
+        blocks, _ = lax.optimization_barrier((blocks, (before, list(self.moving.values()))))
+        for way, block in zip(ways, blocks):
             pairs = [
                 (self.order[i], self.order[(i + way) % self.n_model]) for i in range(self.n_model)
             ]
-            self.moving[way] = lax.ppermute(self.moving[way], "mp", pairs)
+            self.moving[way] = lax.ppermute(block, "mp", pairs)
+        return blocks
 
     def finish(self):
-        while any(self.distance.values()):
-            self.send(self.advance())
         total = self.share_of(0).astype(jnp.float32)
         for way in (1, -1):
             total = total + self.moving[way].astype(jnp.float32)
@@ -564,6 +559,10 @@
         )
         for chunk, share in enumerate(shares)
     ]
+    sent = []
+    for _ in range(n_model // 2):
+        for scatter in scatters:
+            sent = scatter.step(*sent)
     return (jnp.concatenate([scatter.finish() for scatter in scatters], 1)[None], cache_rows)
 
 

time: 321 us -> 300 us (0.935)
  waiting for transfers between devices: 132 us -> 119 us
  other arithmetic: 24.8 us -> 16.1 us
    ppermute x14, waiting for transfers between devices: 69.5 us -> 56.9 us  [step(): self.moving[way] = lax.ppermute(block, 'mp', pairs)]
    convert_element_type x8 -> x6, other arithmetic: 10.1 us -> 1.26 us  [step(): block = (block.astype(jnp.float32) + arrived).astype(jnp.bfloat16)]
  transfers between devices with their start and end apart: 32 -> 32, of which waited for: 12 -> 15; matrix products, arithmetic and copies ran while one was open for 10% -> 8% of each run, Pallas kernels for 11% -> 12%
where the time goes in v10:
time: 300 us; the launch traced here: 299 us
  waiting for transfers between devices  119 us (40%)
  Pallas kernels  64.7 us (22%)
  starting transfers between devices  62.7 us (21%)
  other arithmetic  16.1 us (5%)
  between operations  13 us (4%)
  matrix products  12.8 us (4%)
  local copies, waits for them, and re-layouts  10.6 us (4%)
    ppermute x14, waiting for transfers between devices, step(): self.moving[way] = lax.ppermute(block, 'mp', pairs)  56.9 us
    ppermute x14, waiting for transfers between devices, swap(): lax.ppermute(block, 'mp', [(index, index ^ mask) for index in range(LINE_...  50.7 us
    ppermute x14, starting transfers between devices, swap(): lax.ppermute(block, 'mp', [(index, index ^ mask) for index in range(LINE_...  42.6 us
    pallas_call x2, Pallas kernels, project(): pl.pallas_call(project_kernel, grid=(width // depth,), out_shape=out_shap...  31.3 us
    pallas_call x1, Pallas kernels, attend(): pl.pallas_call(functools.partial(attend_kernel, span), grid=(heads,), out...  24.7 us
    ppermute x14, starting transfers between devices, step(): self.moving[way] = lax.ppermute(block, 'mp', pairs)  15.3 us
    dot_general x2, matrix products, on_device(): jnp.dot(mixed, w_out[:, chunk * width:(chunk + 1) * width], preferred_ele...  12.8 us
    all_to_all x1, waiting for transfers between devices, on_device(): pairs = lax.all_to_all(pairs, 'mp', split_axis=0, concat_axis=0, tiled=True)  11.8 us
  transfers between devices with their start and end apart: 32, of which 15 were waited for; matrix products, arithmetic and copies ran while one was open for 8% of the time, Pallas kernels for 12%

profile of v10, /device:TPU:0, one launch (start us, length us, event | category | flops | bytes accessed | tf_op | source)
XLA Modules:
  0.0 299.3 jit_solution(5320681923088290664)
XLA Ops:
  3.3 2.2 copy-done
  7.5 2.9 collective-permute-start
  11.9 22.1 %collective-permute-done.refs_1_ = bf16[64,8192]{1,0:T(8,128)(2,1)} collective-permute-done((bf16[64,8192]{1,0:T(8,128)(2,1)S(1)}, bf16[64,8192]{1,0:T(8,128)(2,1)}, u32[]{:S(2)}, u32[]{:S(2)}) %collective-permute-start) | collective-permute-done | bytes 1048608 | tf_op jit(solution)/shard_map/ppermute | solution.py:54
  34.1 3.3 %collective-permute-start.9 = (bf16[64,8192]{1,0:T(8,128)(2,1)}, bf16[64,8192]{1,0:T(8,128)(2,1)}, u32[]{:S(2)}, u32[]{:S(2)}) collective-permute-start(bf16[64,8192]{1,0:T(8,128)(2,1)} %collective-permute-done.8), channel_id=1, source_target_pairs={{0,4},{2,6},{4,0},{6,2},{8,12},{10,14},{12,8},{14,10},{1,5},{3,7},... | collective-permute-start | bytes 3145736 | tf_op jit(solution)/shard_map/ppermute | solution.py:54
  38.0 1.6 collective-permute-start.7
  39.6 2.2 copy-done.1
  41.8 4.1 %pack_blocks.1 = (bf16[2,32,16,256]{3,2,1,0:T(8,128)(2,1)S(1)}, bf16[2,32,16,256]{3,2,1,0:T(8,128)(2,1)}, bf16[2,32,16,256]{3,2,1,0:T(8,128)(2,1)}, bf16[2,32,16...) custom-call(s32[2,32]{1,0:T(2,128)S(1)} %pad_add_fusion.slots_ref, ...), custom_call_target="tpu_custom_call" | custom-call | tf_op jit(solution)/shard_map/pack_blocks/pallas_call | solution.py:280
  45.9 14.6 %collective-permute-start.3 = (bf16[64,8192]{1,0:T(8,128)(2,1)}, bf16[64,8192]{1,0:T(8,128)(2,1)S(1)}, u32[]{:S(2)}, u32[]{:S(2)}) collective-permute-start(bf16[64,8192]{1,0:T(8,128)(2,1)} %collective-permute-done.1), channel_id=1, source_target_pairs={{0,4},{2,6},{4,0},{6,2},{8,12},{10,14},{12,8},{14,10},{1,5},{3,7},... | collective-permute-start | bytes 3145736 | tf_op jit(solution)/shard_map/ppermute | solution.py:54
  67.0 27.1 %collective-permute-done.3 = bf16[64,8192]{1,0:T(8,128)(2,1)S(1)} collective-permute-done((bf16[64,8192]{1,0:T(8,128)(2,1)}, bf16[64,8192]{1,0:T(8,128)(2,1)S(1)}, u32[]{:S(2)}, u32[]{:S(2)}) %collective-permute-start.3) | collective-permute-done | bytes 1048608 | tf_op jit(solution)/shard_map/ppermute | solution.py:54
  95.3 1.6 collective-permute-start.11
  113.6 1.8 collective-permute-start.14
  115.4 5.3 %collective-permute-start.15 = (bf16[2,32,16,256]{3,2,1,0:T(8,128)(2,1)}, bf16[2,32,16,256]{3,2,1,0:T(8,128)(2,1)}, u32[]{:S(2)}, u32[]{:S(2)}) collective-permute-start(bf16[2,32,16,256]{3,2,1,0:T(8,128)(2,1)} %copy-done.2), channel_id=1, source_target_pairs={{0,10},{2,8},{4,14},{6,12},{8,2},{10,0},{12,6},{14,4},{1,11},{3,9}... | collective-permute-start | bytes 1572872 | tf_op jit(solution)/shard_map/ppermute | solution.py:54
  120.7 15.6 %project.2 = (bf16[8,256,128]{2,1,0:T(8,128)(2,1)}, bf16[256,128]{1,0:T(8,128)(2,1)}, bf16[256,256]{1,0:T(8,128)(2,1)}, bf16[256,256]{1,0:T(8,128)(2,1)}) custom-call(s32[4]{0:T(128)} %add_multiply_fusion.starts_ref, bf16[64,8192]{1,0:T(8,128)(2,1)} %copy-done.10, bf16[64,8192]{1,0:T(8,128)(2,1)} %collective-permute-done.refs_1_, ...), custom_call_target="tpu_custom_call" | custom-call | flops 5368709120 | bytes 26476544 | tf_op jit(solution)/shard_map/project/pallas_call | solution.py:177
  136.3 4.1 %collective-permute-start.16 = (bf16[2,32,16,256]{3,2,1,0:T(8,128)(2,1)}, bf16[2,32,16,256]{3,2,1,0:T(8,128)(2,1)}, u32[]{:S(2)}, u32[]{:S(2)}) collective-permute-start(bf16[2,32,16,256]{3,2,1,0:T(8,128)(2,1)} %get-tuple-element.78), channel_id=1, source_target_pairs={{0,14},{2,12},{4,10},{6,8},{8,6},{10,4},{12,2},{14,0},{1,15},{3,13... | collective-permute-start | bytes 1572872 | tf_op jit(solution)/shard_map/ppermute | solution.py:54
  140.5 15.7 %project.3 = (bf16[8,256,128]{2,1,0:T(8,128)(2,1)}, bf16[256,128]{1,0:T(8,128)(2,1)}, bf16[256,256]{1,0:T(8,128)(2,1)}, bf16[256,256]{1,0:T(8,128)(2,1)}) custom-call(s32[4]{0:T(128)} %add_multiply_fusion.1.starts_ref, bf16[64,8192]{1,0:T(8,128)(2,1)} %copy-done.11, bf16[64,8192]{1,0:T(8,128)(2,1)} %broadcast_select_fusion.1.refs_1_, ...), custom_call_target="tpu_custom_call" | custom-call | flops 5368709120 | bytes 26476544 | tf_op jit(solution)/shard_map/project/pallas_call | solution.py:177
  156.2 1.8 maximum_select_fusion
  158.0 4.2 %all-to-all-start = ((bf16[8,64,256]{2,1,0:T(8,128)(2,1)}), bf16[8,64,256]{2,1,0:T(8,128)(2,1)}, u32[]{:S(2)}, u32[]{:S(2)}) async-start(bf16[8,64,256]{2,1,0:T(8,128)(2,1)} %bitcast.126), calls=%async_computation | async-start | bytes 524288 | tf_op jit(solution)/shard_map/all_to_all | solution.py:532
  166.0 11.8 %all-to-all-done = bf16[8,64,256]{2,1,0:T(8,128)(2,1)} async-done(((bf16[8,64,256]{2,1,0:T(8,128)(2,1)}), bf16[8,64,256]{2,1,0:T(8,128)(2,1)}, u32[]{:S(2)}, u32[]{:S(2)}) %all-to-all-start) | async-done | bytes 262176 | tf_op jit(solution)/shard_map/all_to_all | solution.py:532
  177.8 3.7 %order_blocks.1 = (bf16[4096,128]{1,0:T(8,128)(2,1)S(1)}, bf16[4096,256]{1,0:T(8,128)(2,1)S(1)}) custom-call(s32[1]{0:T(128)} %dynamic_slice.118.length_ref, s32[256]{0:T(256)S(1)} %multiply_add_fusion.where_ref, bf16[64,16,256]{2,1,0:T(8,128)(2,1)S(1)} %bitcast.110, bf16[64,16,256]{2,1,0:T(8,128)(2,1)S(1)} %bitcast.113, bf16[64,16,256]{2,1,0:T(8,128)(2,1)S(1)} %bitcast.114, ...), custom_call_target="tpu_custom_call" | custom-call | tf_op jit(solution)/shard_map/order_blocks/pallas_call | solution.py:325
  181.6 24.7 %attend.1 = bf16[512,1024]{1,0:T(8,128)(2,1)S(1)} custom-call(s32[1]{0:T(128)} %bitcast.half_ref, bf16[8,256,128]{2,1,0:T(8,128)(2,1)S(1)} %copy-done.4, bf16[8,256,128]{2,1,0:T(8,128)(2,1)S(1)} %copy-done.5, bf16[4096,128]{1,0:T(8,128)(2,1)S(1)} %get-tuple-element.91.refs_2_, bf16[4096,256]{1,0:T(8,128)(2,1)S(1)} %get-tuple-element.92.refs_3_, ...), custom_call_target="tpu_custom_call" | custom-call | flops 19327352832 | bytes 5636096 | tf_op jit(solution)/shard_map/attend/pallas_call | solution.py:397
  206.4 4.7 %fusion.4 = bf16[512,4096]{1,0:T(8,128)(2,1)S(1)} fusion(bf16[512,1024]{1,0:T(8,128)(2,1)S(1)} %attend.1, bf16[1024,8192]{1,0:T(8,128)(2,1)S(1)} %bitcast.137), kind=kOutput, calls=%fused_computation.4 | convolution fusion | flops 4297064448 | bytes 13631488 | tf_op jit(solution)/shard_map/dot_general | solution.py:543
  213.3 8.1 %fusion.7 = bf16[512,4096]{1,0:T(8,128)(2,1)S(1)} fusion(bf16[512,1024]{1,0:T(8,128)(2,1)S(1)} %attend.1, bf16[1024,8192]{1,0:T(8,128)(2,1)} %param.39), kind=kOutput, calls=%fused_computation.5 | convolution fusion | flops 4297064448 | bytes 13631488 | tf_op jit(solution)/shard_map/dot_general | solution.py:543
  221.8 1.8 collective-permute-start.21
  228.5 8.7 %collective-permute-done.22 = bf16[64,4096]{1,0:T(8,128)(2,1)S(1)} collective-permute-done((bf16[64,4096]{1,0:T(8,128)(2,1)S(1)}, bf16[64,4096]{1,0:T(8,128)(2,1)S(1)}, u32[]{:S(2)}, u32[]{:S(2)}) %collective-permute-start.22) | collective-permute-done | bytes 524320 | tf_op jit(solution)/shard_map/ppermute | solution.py:230
  237.4 2.3 collective-permute-start.25
  239.7 8.2 %collective-permute-done.20 = bf16[64,4096]{1,0:T(8,128)(2,1)S(1)} collective-permute-done((bf16[64,4096]{1,0:T(8,128)(2,1)S(1)}, bf16[64,4096]{1,0:T(8,128)(2,1)S(1)}, u32[]{:S(2)}, u32[]{:S(2)}) %collective-permute-start.20) | collective-permute-done | bytes 524320 | tf_op jit(solution)/shard_map/ppermute | solution.py:230
  248.6 2.3 collective-permute-start.23
  250.9 8.7 %collective-permute-done.25 = bf16[64,4096]{1,0:T(8,128)(2,1)S(1)} collective-permute-done((bf16[64,4096]{1,0:T(8,128)(2,1)S(1)}, bf16[64,4096]{1,0:T(8,128)(2,1)S(1)}, u32[]{:S(2)}, u32[]{:S(2)}) %collective-permute-start.25) | collective-permute-done | bytes 524320 | tf_op jit(solution)/shard_map/ppermute | solution.py:230
  262.2 8.6 %collective-permute-done.23 = bf16[64,4096]{1,0:T(8,128)(2,1)S(1)} collective-permute-done((bf16[64,4096]{1,0:T(8,128)(2,1)S(1)}, bf16[64,4096]{1,0:T(8,128)(2,1)S(1)}, u32[]{:S(2)}, u32[]{:S(2)}) %collective-permute-start.23) | collective-permute-done | bytes 524320 | tf_op jit(solution)/shard_map/ppermute | solution.py:230
  271.0 9.3 %collective-permute-done.29 = bf16[64,4096]{1,0:T(8,128)(2,1)S(1)} collective-permute-done((bf16[64,4096]{1,0:T(8,128)(2,1)S(1)}, bf16[64,4096]{1,0:T(8,128)(2,1)S(1)}, u32[]{:S(2)}, u32[]{:S(2)}) %collective-permute-start.29) | collective-permute-done | bytes 524320 | tf_op jit(solution)/shard_map/ppermute | solution.py:230
  285.2 7.9 %collective-permute-done.30 = bf16[64,4096]{1,0:T(8,128)(2,1)S(1)} collective-permute-done((bf16[64,4096]{1,0:T(8,128)(2,1)S(1)}, bf16[64,4096]{1,0:T(8,128)(2,1)S(1)}, u32[]{:S(2)}, u32[]{:S(2)}) %collective-permute-start.30) | collective-permute-done | bytes 524320 | tf_op jit(solution)/shard_map/ppermute | solution.py:230
  294.3 2.7 collective-permute-done.27
  (143 shorter events, 42.6 us)
Async XLA Ops:
  6.3 33.3 %collective-permute-start.2 = (bf16[32,16,2048]{2,1,0:T(8,128)(2,1)S(1)}, bf16[32,16,2048]{2,1,0:T(8,128)(2,1)}, u32[]{:S(2)}, u32[]{:S(2)}) collective-permute-start(bf16[32,16,2048]{2,1,0:T(8,128)(2,1)S(1)} %pick_blocks.1), channel_id=1, source_target_pairs={{0,1},{1,0},{2,3},{3,2},{4,5},{5,4},{6,7},{7,6},{8,9},{9,8},{10,11... | collective-permute-start | bytes 6291464 | tf_op jit(solution)/shard_map/ppermute | solution.py:464
  7.5 26.6 %collective-permute-start = (bf16[64,8192]{1,0:T(8,128)(2,1)S(1)}, bf16[64,8192]{1,0:T(8,128)(2,1)}, u32[]{:S(2)}, u32[]{:S(2)}) collective-permute-start(bf16[64,8192]{1,0:T(8,128)(2,1)S(1)} %fusion.12.refs_0_), channel_id=1, source_target_pairs={{0,4},{2,6},{4,0},{6,2},{8,12},{10,14},{12,8},{14,10},{1,5},{3,7},... | collective-permute-start | bytes 3145736 | tf_op jit(solution)/shard_map/ppermute | solution.py:54
  10.4 23.6 %collective-permute-start.8 = (bf16[64,8192]{1,0:T(8,128)(2,1)S(1)}, bf16[64,8192]{1,0:T(8,128)(2,1)}, u32[]{:S(2)}, u32[]{:S(2)}) collective-permute-start(bf16[64,8192]{1,0:T(8,128)(2,1)S(1)} %fusion.12.refs_0_), channel_id=1, source_target_pairs={{0,1},{1,0},{2,3},{3,2},{4,8},{5,9},{6,10},{7,11},{8,4},{9,5},{10,... | collective-permute-start | bytes 3145736 | tf_op jit(solution)/shard_map/ppermute | solution.py:65
  10.4 27.6 %collective-permute-start.6 = (bf16[64,8192]{1,0:T(8,128)(2,1)S(1)}, bf16[64,8192]{1,0:T(8,128)(2,1)}, u32[]{:S(2)}, u32[]{:S(2)}) collective-permute-start(bf16[64,8192]{1,0:T(8,128)(2,1)S(1)} %fusion.12.refs_0_), channel_id=1, source_target_pairs={{0,2},{2,0},{4,6},{6,4},{8,10},{10,8},{12,14},{14,12},{1,3},{3,1},... | collective-permute-start | bytes 3145736 | tf_op jit(solution)/shard_map/ppermute | solution.py:54
  34.1 11.9 %collective-permute-start.1 = (bf16[64,8192]{1,0:T(8,128)(2,1)}, bf16[64,8192]{1,0:T(8,128)(2,1)}, u32[]{:S(2)}, u32[]{:S(2)}) collective-permute-start(bf16[64,8192]{1,0:T(8,128)(2,1)} %collective-permute-done.refs_1_), channel_id=1, source_target_pairs={{0,1},{1,0},{2,3},{3,2},{4,8},{5,9},{6,10},{7,11},{8,4},{9,5},{10,... | collective-permute-start | bytes 3145736 | tf_op jit(solution)/shard_map/ppermute | solution.py:65
  34.1 29.0 %collective-permute-start.9 = (bf16[64,8192]{1,0:T(8,128)(2,1)}, bf16[64,8192]{1,0:T(8,128)(2,1)}, u32[]{:S(2)}, u32[]{:S(2)}) collective-permute-start(bf16[64,8192]{1,0:T(8,128)(2,1)} %collective-permute-done.8), channel_id=1, source_target_pairs={{0,4},{2,6},{4,0},{6,2},{8,12},{10,14},{12,8},{14,10},{1,5},{3,7},... | collective-permute-start | bytes 3145736 | tf_op jit(solution)/shard_map/ppermute | solution.py:54
  38.0 26.4 %collective-permute-start.7 = (bf16[64,8192]{1,0:T(8,128)(2,1)}, bf16[64,8192]{1,0:T(8,128)(2,1)S(1)}, u32[]{:S(2)}, u32[]{:S(2)}) collective-permute-start(bf16[64,8192]{1,0:T(8,128)(2,1)} %collective-permute-done.refs_1_), channel_id=1, source_target_pairs={{0,2},{2,0},{4,6},{6,4},{8,10},{10,8},{12,14},{14,12},{1,3},{3,1},... | collective-permute-start | bytes 3145736 | tf_op jit(solution)/shard_map/ppermute | solution.py:54
  45.9 48.2 %collective-permute-start.3 = (bf16[64,8192]{1,0:T(8,128)(2,1)}, bf16[64,8192]{1,0:T(8,128)(2,1)S(1)}, u32[]{:S(2)}, u32[]{:S(2)}) collective-permute-start(bf16[64,8192]{1,0:T(8,128)(2,1)} %collective-permute-done.1), channel_id=1, source_target_pairs={{0,4},{2,6},{4,0},{6,2},{8,12},{10,14},{12,8},{14,10},{1,5},{3,7},... | collective-permute-start | bytes 3145736 | tf_op jit(solution)/shard_map/ppermute | solution.py:54
  60.5 51.3 %collective-permute-start.4 = (bf16[2,32,16,256]{3,2,1,0:T(8,128)(2,1)S(1)}, bf16[2,32,16,256]{3,2,1,0:T(8,128)(2,1)S(1)}, u32[]{:S(2)}, u32[]{:S(2)}) collective-permute-start(bf16[2,32,16,256]{3,2,1,0:T(8,128)(2,1)S(1)} %get-tuple-element.59), channel_id=1, source_target_pairs={{0,8},{2,10},{4,12},{6,14},{8,0},{10,2},{12,4},{14,6},{1,9},{3,11}... | collective-permute-start | bytes 1572872 | tf_op jit(solution)/shard_map/ppermute | solution.py:54
  61.6 50.3 %collective-permute-start.5 = (bf16[2,32,16,256]{3,2,1,0:T(8,128)(2,1)S(1)}, bf16[2,32,16,256]{3,2,1,0:T(8,128)(2,1)S(1)}, u32[]{:S(2)}, u32[]{:S(2)}) collective-permute-start(bf16[2,32,16,256]{3,2,1,0:T(8,128)(2,1)S(1)} %get-tuple-element.61), channel_id=1, source_target_pairs={{0,12},{2,14},{4,8},{6,10},{8,4},{10,6},{12,0},{14,2},{1,13},{3,15... | collective-permute-start | bytes 1572872 | tf_op jit(solution)/shard_map/ppermute | solution.py:54
  65.5 29.8 %collective-permute-start.10 = (bf16[64,8192]{1,0:T(8,128)(2,1)S(1)}, bf16[64,8192]{1,0:T(8,128)(2,1)S(1)}, u32[]{:S(2)}, u32[]{:S(2)}) collective-permute-start(bf16[64,8192]{1,0:T(8,128)(2,1)S(1)} %broadcast_select_fusion.refs_0_), channel_id=1, source_target_pairs={{0,2},{2,0},{4,6},{6,4},{8,10},{10,8},{12,14},{14,12},{1,3},{3,1},... | collective-permute-start | bytes 3145736 | tf_op jit(solution)/shard_map/ppermute | solution.py:54
  95.3 41.0 %collective-permute-start.11 = (bf16[64,8192]{1,0:T(8,128)(2,1)}, bf16[64,8192]{1,0:T(8,128)(2,1)}, u32[]{:S(2)}, u32[]{:S(2)}) collective-permute-start(bf16[64,8192]{1,0:T(8,128)(2,1)} %broadcast_select_fusion.1.refs_1_), channel_id=1, source_target_pairs={{0,2},{2,0},{4,6},{6,4},{8,10},{10,8},{12,14},{14,12},{1,3},{3,1},... | collective-permute-start | bytes 3145736 | tf_op jit(solution)/shard_map/ppermute | solution.py:54
  111.9 52.7 %collective-permute-start.12 = (bf16[2,32,16,256]{3,2,1,0:T(8,128)(2,1)}, bf16[2,32,16,256]{3,2,1,0:T(8,128)(2,1)S(1)}, u32[]{:S(2)}, u32[]{:S(2)}) collective-permute-start(bf16[2,32,16,256]{3,2,1,0:T(8,128)(2,1)} %get-tuple-element.70), channel_id=1, source_target_pairs={{0,2},{2,0},{4,6},{6,4},{8,10},{10,8},{12,14},{14,12},{1,3},{3,1},... | collective-permute-start | bytes 1572872 | tf_op jit(solution)/shard_map/ppermute | solution.py:54
  112.8 51.7 %collective-permute-start.13 = (bf16[2,32,16,256]{3,2,1,0:T(8,128)(2,1)}, bf16[2,32,16,256]{3,2,1,0:T(8,128)(2,1)S(1)}, u32[]{:S(2)}, u32[]{:S(2)}) collective-permute-start(bf16[2,32,16,256]{3,2,1,0:T(8,128)(2,1)} %get-tuple-element.72), channel_id=1, source_target_pairs={{0,4},{2,6},{4,0},{6,2},{8,12},{10,14},{12,8},{14,10},{1,5},{3,7},... | collective-permute-start | bytes 1572872 | tf_op jit(solution)/shard_map/ppermute | solution.py:54
  113.6 51.0 %collective-permute-start.14 = (bf16[2,32,16,256]{3,2,1,0:T(8,128)(2,1)}, bf16[2,32,16,256]{3,2,1,0:T(8,128)(2,1)S(1)}, u32[]{:S(2)}, u32[]{:S(2)}) collective-permute-start(bf16[2,32,16,256]{3,2,1,0:T(8,128)(2,1)} %copy-done.3), channel_id=1, source_target_pairs={{0,6},{2,4},{4,2},{6,0},{8,14},{10,12},{12,10},{14,8},{1,7},{3,5},... | collective-permute-start | bytes 1572872 | tf_op jit(solution)/shard_map/ppermute | solution.py:54
  115.4 49.2 %collective-permute-start.15 = (bf16[2,32,16,256]{3,2,1,0:T(8,128)(2,1)}, bf16[2,32,16,256]{3,2,1,0:T(8,128)(2,1)}, u32[]{:S(2)}, u32[]{:S(2)}) collective-permute-start(bf16[2,32,16,256]{3,2,1,0:T(8,128)(2,1)} %copy-done.2), channel_id=1, source_target_pairs={{0,10},{2,8},{4,14},{6,12},{8,2},{10,0},{12,6},{14,4},{1,11},{3,9}... | collective-permute-start | bytes 1572872 | tf_op jit(solution)/shard_map/ppermute | solution.py:54
  136.3 29.7 %collective-permute-start.16 = (bf16[2,32,16,256]{3,2,1,0:T(8,128)(2,1)}, bf16[2,32,16,256]{3,2,1,0:T(8,128)(2,1)}, u32[]{:S(2)}, u32[]{:S(2)}) collective-permute-start(bf16[2,32,16,256]{3,2,1,0:T(8,128)(2,1)} %get-tuple-element.78), channel_id=1, source_target_pairs={{0,14},{2,12},{4,10},{6,8},{8,6},{10,4},{12,2},{14,0},{1,15},{3,13... | collective-permute-start | bytes 1572872 | tf_op jit(solution)/shard_map/ppermute | solution.py:54
  158.0 19.8 %all-to-all-start = ((bf16[8,64,256]{2,1,0:T(8,128)(2,1)}), bf16[8,64,256]{2,1,0:T(8,128)(2,1)}, u32[]{:S(2)}, u32[]{:S(2)}) async-start(bf16[8,64,256]{2,1,0:T(8,128)(2,1)} %bitcast.126), calls=%async_computation | async-start | bytes 524288 | tf_op jit(solution)/shard_map/all_to_all | solution.py:532
  211.3 13.3 %collective-permute-start.18 = (bf16[64,4096]{1,0:T(8,128)(2,1)S(1)}, bf16[64,4096]{1,0:T(8,128)(2,1)S(1)}, u32[]{:S(2)}, u32[]{:S(2)}) collective-permute-start(bf16[64,4096]{1,0:T(8,128)(2,1)S(1)} %get-tuple-element.98), channel_id=1, source_target_pairs={{0,2},{4,0},{8,4},{12,8},{14,12},{10,14},{6,10},{2,6},{1,3},{5,1},... | collective-permute-start | bytes 1572872 | tf_op jit(solution)/shard_map/ppermute | solution.py:230
  212.4 13.5 %collective-permute-start.17 = (bf16[64,4096]{1,0:T(8,128)(2,1)S(1)}, bf16[64,4096]{1,0:T(8,128)(2,1)S(1)}, u32[]{:S(2)}, u32[]{:S(2)}) collective-permute-start(bf16[64,4096]{1,0:T(8,128)(2,1)S(1)} %get-tuple-element.97), channel_id=1, source_target_pairs={{0,4},{4,8},{8,12},{12,14},{14,10},{10,6},{6,2},{2,0},{1,5},{5,9},... | collective-permute-start | bytes 1572872 | tf_op jit(solution)/shard_map/ppermute | solution.py:230
  221.5 15.6 %collective-permute-start.22 = (bf16[64,4096]{1,0:T(8,128)(2,1)S(1)}, bf16[64,4096]{1,0:T(8,128)(2,1)S(1)}, u32[]{:S(2)}, u32[]{:S(2)}) collective-permute-start(bf16[64,4096]{1,0:T(8,128)(2,1)S(1)} %get-tuple-element.100), channel_id=1, source_target_pairs={{0,4},{4,8},{8,12},{12,14},{14,10},{10,6},{6,2},{2,0},{1,5},{5,9},... | collective-permute-start | bytes 1572872 | tf_op jit(solution)/shard_map/ppermute | solution.py:230
  221.8 15.4 %collective-permute-start.21 = (bf16[64,4096]{1,0:T(8,128)(2,1)S(1)}, bf16[64,4096]{1,0:T(8,128)(2,1)S(1)}, u32[]{:S(2)}, u32[]{:S(2)}) collective-permute-start(bf16[64,4096]{1,0:T(8,128)(2,1)S(1)} %get-tuple-element.99), channel_id=1, source_target_pairs={{0,2},{4,0},{8,4},{12,8},{14,12},{10,14},{6,10},{2,6},{1,3},{5,1},... | collective-permute-start | bytes 1572872 | tf_op jit(solution)/shard_map/ppermute | solution.py:230
  226.2 21.7 %collective-permute-start.20 = (bf16[64,4096]{1,0:T(8,128)(2,1)S(1)}, bf16[64,4096]{1,0:T(8,128)(2,1)S(1)}, u32[]{:S(2)}, u32[]{:S(2)}) collective-permute-start(bf16[64,4096]{1,0:T(8,128)(2,1)S(1)} %get-tuple-element.102), channel_id=1, source_target_pairs={{0,2},{4,0},{8,4},{12,8},{14,12},{10,14},{6,10},{2,6},{1,3},{5,1},... | collective-permute-start | bytes 1572872 | tf_op jit(solution)/shard_map/ppermute | solution.py:230
  227.6 20.8 %collective-permute-start.19 = (bf16[64,4096]{1,0:T(8,128)(2,1)S(1)}, bf16[64,4096]{1,0:T(8,128)(2,1)S(1)}, u32[]{:S(2)}, u32[]{:S(2)}) collective-permute-start(bf16[64,4096]{1,0:T(8,128)(2,1)S(1)} %get-tuple-element.101), channel_id=1, source_target_pairs={{0,4},{4,8},{8,12},{12,14},{14,10},{10,6},{6,2},{2,0},{1,5},{5,9},... | collective-permute-start | bytes 1572872 | tf_op jit(solution)/shard_map/ppermute | solution.py:230
  237.4 22.2 %collective-permute-start.25 = (bf16[64,4096]{1,0:T(8,128)(2,1)S(1)}, bf16[64,4096]{1,0:T(8,128)(2,1)S(1)}, u32[]{:S(2)}, u32[]{:S(2)}) collective-permute-start(bf16[64,4096]{1,0:T(8,128)(2,1)S(1)} %get-tuple-element.104), channel_id=1, source_target_pairs={{0,4},{4,8},{8,12},{12,14},{14,10},{10,6},{6,2},{2,0},{1,5},{5,9},... | collective-permute-start | bytes 1572872 | tf_op jit(solution)/shard_map/ppermute | solution.py:230
  239.7 19.9 %collective-permute-start.24 = (bf16[64,4096]{1,0:T(8,128)(2,1)S(1)}, bf16[64,4096]{1,0:T(8,128)(2,1)S(1)}, u32[]{:S(2)}, u32[]{:S(2)}) collective-permute-start(bf16[64,4096]{1,0:T(8,128)(2,1)S(1)} %get-tuple-element.103), channel_id=1, source_target_pairs={{0,2},{4,0},{8,4},{12,8},{14,12},{10,14},{6,10},{2,6},{1,3},{5,1},... | collective-permute-start | bytes 1572872 | tf_op jit(solution)/shard_map/ppermute | solution.py:230
  248.6 22.2 %collective-permute-start.23 = (bf16[64,4096]{1,0:T(8,128)(2,1)S(1)}, bf16[64,4096]{1,0:T(8,128)(2,1)S(1)}, u32[]{:S(2)}, u32[]{:S(2)}) collective-permute-start(bf16[64,4096]{1,0:T(8,128)(2,1)S(1)} %get-tuple-element.105), channel_id=1, source_target_pairs={{0,4},{4,8},{8,12},{12,14},{14,10},{10,6},{6,2},{2,0},{1,5},{5,9},... | collective-permute-start | bytes 1572872 | tf_op jit(solution)/shard_map/ppermute | solution.py:230
  250.9 20.1 %collective-permute-start.26 = (bf16[64,4096]{1,0:T(8,128)(2,1)S(1)}, bf16[64,4096]{1,0:T(8,128)(2,1)S(1)}, u32[]{:S(2)}, u32[]{:S(2)}) collective-permute-start(bf16[64,4096]{1,0:T(8,128)(2,1)S(1)} %get-tuple-element.106), channel_id=1, source_target_pairs={{0,2},{4,0},{8,4},{12,8},{14,12},{10,14},{6,10},{2,6},{1,3},{5,1},... | collective-permute-start | bytes 1572872 | tf_op jit(solution)/shard_map/ppermute | solution.py:230
  259.9 20.4 %collective-permute-start.29 = (bf16[64,4096]{1,0:T(8,128)(2,1)S(1)}, bf16[64,4096]{1,0:T(8,128)(2,1)S(1)}, u32[]{:S(2)}, u32[]{:S(2)}) collective-permute-start(bf16[64,4096]{1,0:T(8,128)(2,1)S(1)} %get-tuple-element.107), channel_id=1, source_target_pairs={{0,2},{4,0},{8,4},{12,8},{14,12},{10,14},{6,10},{2,6},{1,3},{5,1},... | collective-permute-start | bytes 1572872 | tf_op jit(solution)/shard_map/ppermute | solution.py:230
  261.3 19.1 %collective-permute-start.28 = (bf16[64,4096]{1,0:T(8,128)(2,1)S(1)}, bf16[64,4096]{1,0:T(8,128)(2,1)S(1)}, u32[]{:S(2)}, u32[]{:S(2)}) collective-permute-start(bf16[64,4096]{1,0:T(8,128)(2,1)S(1)} %get-tuple-element.108), channel_id=1, source_target_pairs={{0,4},{4,8},{8,12},{12,14},{14,10},{10,6},{6,2},{2,0},{1,5},{5,9},... | collective-permute-start | bytes 1572872 | tf_op jit(solution)/shard_map/ppermute | solution.py:230
  280.4 12.6 %collective-permute-start.30 = (bf16[64,4096]{1,0:T(8,128)(2,1)S(1)}, bf16[64,4096]{1,0:T(8,128)(2,1)S(1)}, u32[]{:S(2)}, u32[]{:S(2)}) collective-permute-start(bf16[64,4096]{1,0:T(8,128)(2,1)S(1)} %fusion.13), channel_id=1, source_target_pairs={{0,2},{4,0},{8,4},{12,8},{14,12},{10,14},{6,10},{2,6},{1,3},{5,1},... | collective-permute-start | bytes 1572872 | tf_op jit(solution)/shard_map/ppermute | solution.py:230
  284.1 12.9 %collective-permute-start.27 = (bf16[64,4096]{1,0:T(8,128)(2,1)S(1)}, bf16[64,4096]{1,0:T(8,128)(2,1)S(1)}, u32[]{:S(2)}, u32[]{:S(2)}) collective-permute-start(bf16[64,4096]{1,0:T(8,128)(2,1)S(1)} %fusion.24), channel_id=1, source_target_pairs={{0,4},{4,8},{8,12},{12,14},{14,10},{10,6},{6,2},{2,0},{1,5},{5,9},... | collective-permute-start | bytes 1572872 | tf_op jit(solution)/shard_map/ppermute | solution.py:230
  (28 other events, 711.3 us)

commit v11 on v10

--- a/solution.py
+++ b/solution.py
@@ -15,7 +15,7 @@
 SCORE_SCALE = HD ** (-0.5) * math.log2(math.e)
 VMEM_LIMIT = 56 * 1024 * 1024
 ATTEND_VMEM = 28 * 1024 * 1024
-COLUMN_CHUNKS = 2
+ROW_CHUNKS = 2
 STREAMS = 4
 LINE_MODELS = 8
 
@@ -349,7 +349,7 @@
     )
 
 
-def attend_kernel(span, half_ref, *refs):
+def attend_kernel(span, row_step, chunk, half_ref, *refs):
     query_refs, (key_ref, value_ref), new_key_refs, new_value_refs, out_ref = (
         refs[:2],
         refs[2:4],
@@ -358,15 +358,18 @@
         refs[8],
     )
     rows = out_ref.shape[0]
-    half = rows // 2
-    queries = jnp.concatenate([ref[0] for ref in query_refs], 0)
+    half = new_key_refs[0].shape[0]
+    queries = jnp.concatenate([ref[0].reshape(rows // 2, HD) for ref in query_refs], 0)
     spans = key_ref.shape[0] // span
+    stride = 2 * half * row_step // rows
     turn = half_ref[0] * half
-    token = lax.rem(lax.broadcasted_iota(jnp.int32, (rows, half), 0) + turn, rows)
+    local = lax.broadcasted_iota(jnp.int32, (rows, half), 0)
+    token = (local // row_step) * stride + chunk * row_step + local % row_step
+    token = lax.rem(token + turn, 2 * half)
     column = lax.broadcasted_iota(jnp.int32, (rows, half), 1)
     parts = []
     for side, ref in enumerate(new_key_refs):
-        causal = column + lax.rem(turn + side * half, rows) <= token
+        causal = column + lax.rem(turn + side * half, 2 * half) <= token
         parts.append(jnp.where(causal, dot_keys(queries, ref[...]), -jnp.inf))
     scores = jnp.concatenate(parts, 1)
     peak = jnp.max(scores, axis=1, keepdims=True)
@@ -386,16 +389,18 @@
     out_ref[...] = (total[:, :HD] / total[:, HD:]).astype(jnp.bfloat16)
 
 
-def attend(half, queries, prefix, new_keys, new_values):
-    heads = queries[0].shape[0]
-    rows = 2 * new_keys[0].shape[0]
+def attend(half, queries, prefix, new_keys, new_values, chunk):
+    heads, owners, _, row_step, _ = queries[0].shape
+    rows = 2 * owners * row_step
     span = math.gcd(prefix[0].shape[0], 1024)
     whole = lambda array: pl.BlockSpec(array.shape, lambda step: (0, 0))
-    count = prefix[0].shape[0] + rows
-    query_spec = pl.BlockSpec((1, rows // 2, HD), lambda step: (step, 0, 0))
+    count = prefix[0].shape[0] + 2 * new_keys[0].shape[0]
+    query_spec = pl.BlockSpec(
+        (1, owners, None, row_step, HD), lambda step: (step, 0, chunk, 0, 0)
+    )
     fixed = (*prefix, *new_keys, *new_values)
     return pl.pallas_call(
-        functools.partial(attend_kernel, span),
+        functools.partial(attend_kernel, span, row_step, chunk),
         grid=(heads,),
         out_shape=jax.ShapeDtypeStruct((rows, heads * HD), jnp.bfloat16),
         in_specs=[pl.BlockSpec(memory_space=pltpu.SMEM), query_spec, query_spec]
@@ -537,33 +542,33 @@
         .reshape(1, row_count, kv_heads * 2 * HD)
     )
     prefix = order_blocks(arrived, where, prefix_count.reshape(1))
-    mixed = attend(upper_half.reshape(1), queries, prefix, new_keys, new_values)
-    width = w_out.shape[1] // COLUMN_CHUNKS
-    shares = [
-        jnp.dot(
-            mixed,
-            w_out[:, chunk * width : (chunk + 1) * width],
-            preferred_element_type=jnp.float32,
-        ).astype(jnp.bfloat16)
-        for chunk in range(COLUMN_CHUNKS)
-    ]
-
+
+    row_step = max(row_count // ROW_CHUNKS, 16)
+    chunks = row_count // row_step
+    queries = [part.reshape(q_local, -1, chunks, row_step, HD) for part in queries]
     first = upper_half * (n_model // 2)
-    scatters = [
-        RingScatter(
-            share.reshape(n_model, row_count, -1),
-            n_model,
-            my_model,
-            first,
-            1 if chunk % 2 == 0 else -1,
-        )
-        for chunk, share in enumerate(shares)
-    ]
-    sent = []
-    for _ in range(n_model // 2):
-        for scatter in scatters:
-            sent = scatter.step(*sent)
-    return (jnp.concatenate([scatter.finish() for scatter in scatters], 1)[None], cache_rows)
+    steps = n_model // 2
+    scatters, taken, sums, sent = [], [], [], []
+    for chunk in range(chunks):
+        queries, _ = lax.optimization_barrier((queries, sent))
+        mixed = attend(upper_half.reshape(1), queries, prefix, new_keys, new_values, chunk)
+        if scatters:
+            mixed, _ = lax.optimization_barrier((mixed, scatters[-1].step()))
+            taken[-1] += 1
+        share = jnp.dot(mixed, w_out, preferred_element_type=jnp.float32).astype(jnp.bfloat16)
+        share = share.reshape(n_model, row_step, -1)
+        way = 1 if chunk % 2 == 0 else -1
+        scatters.append(RingScatter(share, n_model, my_model, first, way))
+        sent = scatters[-1].step()
+        taken.append(1)
+    while len(sums) < chunks:
+        for chunk, scatter in enumerate(scatters):
+            if taken[chunk] < steps:
+                sent = scatter.step(sent, sums)
+                taken[chunk] += 1
+            elif len(sums) == chunk:
+                sums.append(scatter.finish())
+    return (jnp.concatenate(sums, 0)[None], cache_rows)
 
 
 def solution(mesh):

time: 300 us -> 307 us (1.023)
  matrix products: 12.8 us -> 21 us
    dot_general x2, matrix products: 12.8 us -> 21 us  [on_device(): jnp.dot(mixed, w_out, preferred_element_type=jnp.float32)]
    pallas_call x1 -> x2, Pallas kernels: 24.7 us -> 27.8 us  [attend(): pl.pallas_call(functools.partial(attend_kernel, span, row_step, chunk), g...]
  transfers between devices with their start and end apart: 32 -> 32, of which waited for: 15 -> 12; matrix products, arithmetic and copies ran while one was open for 8% -> 8% of each run, Pallas kernels for 12% -> 16%
where the time goes in v11:
time: 307 us; the launch traced here: 306 us
  waiting for transfers between devices  118 us (38%)
  Pallas kernels  67.5 us (22%)
  starting transfers between devices  61.6 us (20%)
  matrix products  21 us (7%)
  other arithmetic  14.9 us (5%)
  between operations  13 us (4%)
  local copies, waits for them, and re-layouts  10.4 us (3%)
    ppermute x14, waiting for transfers between devices, step(): self.moving[way] = lax.ppermute(block, 'mp', pairs)  54.2 us
    ppermute x14, waiting for transfers between devices, swap(): lax.ppermute(block, 'mp', [(index, index ^ mask) for index in range(LINE_...  52.1 us
    ppermute x14, starting transfers between devices, swap(): lax.ppermute(block, 'mp', [(index, index ^ mask) for index in range(LINE_...  41.5 us
    pallas_call x2, Pallas kernels, project(): pl.pallas_call(project_kernel, grid=(width // depth,), out_shape=out_shap...  31.3 us
    pallas_call x2, Pallas kernels, attend(): pl.pallas_call(functools.partial(attend_kernel, span, row_step, chunk), g...  27.8 us
    dot_general x2, matrix products, on_device(): jnp.dot(mixed, w_out, preferred_element_type=jnp.float32)  21 us
    ppermute x14, starting transfers between devices, step(): self.moving[way] = lax.ppermute(block, 'mp', pairs)  15.5 us
    all_to_all x1, waiting for transfers between devices, on_device(): pairs = lax.all_to_all(pairs, 'mp', split_axis=0, concat_axis=0, tiled=True)  11.4 us
  transfers between devices with their start and end apart: 32, of which 12 were waited for; matrix products, arithmetic and copies ran while one was open for 8% of the time, Pallas kernels for 16%

profile of v11, /device:TPU:0, one launch (start us, length us, event | category | flops | bytes accessed | tf_op | source)
XLA Modules:
  0.0 306.2 jit_solution(15990623094178104318)
XLA Ops:
  3.3 2.2 copy-done
  7.5 2.9 collective-permute-start
  11.9 22.1 %collective-permute-done.refs_1_ = bf16[64,8192]{1,0:T(8,128)(2,1)} collective-permute-done((bf16[64,8192]{1,0:T(8,128)(2,1)S(1)}, bf16[64,8192]{1,0:T(8,128)(2,1)}, u32[]{:S(2)}, u32[]{:S(2)}) %collective-permute-start) | collective-permute-done | bytes 1048608 | tf_op jit(solution)/shard_map/ppermute | solution.py:54
  34.1 3.3 %collective-permute-start.9 = (bf16[64,8192]{1,0:T(8,128)(2,1)}, bf16[64,8192]{1,0:T(8,128)(2,1)}, u32[]{:S(2)}, u32[]{:S(2)}) collective-permute-start(bf16[64,8192]{1,0:T(8,128)(2,1)} %collective-permute-done.8), channel_id=1, source_target_pairs={{0,4},{2,6},{4,0},{6,2},{8,12},{10,14},{12,8},{14,10},{1,5},{3,7},... | collective-permute-start | bytes 3145736 | tf_op jit(solution)/shard_map/ppermute | solution.py:54
  38.0 1.6 collective-permute-start.7
  39.6 2.2 copy-done.1
  41.8 4.0 %pack_blocks.1 = (bf16[2,32,16,256]{3,2,1,0:T(8,128)(2,1)S(1)}, bf16[2,32,16,256]{3,2,1,0:T(8,128)(2,1)}, bf16[2,32,16,256]{3,2,1,0:T(8,128)(2,1)}, bf16[2,32,16...) custom-call(s32[2,32]{1,0:T(2,128)S(1)} %pad_add_fusion.slots_ref, ...), custom_call_target="tpu_custom_call" | custom-call | tf_op jit(solution)/shard_map/pack_blocks/pallas_call | solution.py:280
  45.9 14.6 %collective-permute-start.3 = (bf16[64,8192]{1,0:T(8,128)(2,1)}, bf16[64,8192]{1,0:T(8,128)(2,1)S(1)}, u32[]{:S(2)}, u32[]{:S(2)}) collective-permute-start(bf16[64,8192]{1,0:T(8,128)(2,1)} %collective-permute-done.1), channel_id=1, source_target_pairs={{0,4},{2,6},{4,0},{6,2},{8,12},{10,14},{12,8},{14,10},{1,5},{3,7},... | collective-permute-start | bytes 3145736 | tf_op jit(solution)/shard_map/ppermute | solution.py:54
  67.0 27.2 %collective-permute-done.3 = bf16[64,8192]{1,0:T(8,128)(2,1)S(1)} collective-permute-done((bf16[64,8192]{1,0:T(8,128)(2,1)}, bf16[64,8192]{1,0:T(8,128)(2,1)S(1)}, u32[]{:S(2)}, u32[]{:S(2)}) %collective-permute-start.3) | collective-permute-done | bytes 1048608 | tf_op jit(solution)/shard_map/ppermute | solution.py:54
  95.3 1.6 collective-permute-start.11
  114.1 1.8 collective-permute-start.14
  115.9 5.3 %collective-permute-start.15 = (bf16[2,32,16,256]{3,2,1,0:T(8,128)(2,1)}, bf16[2,32,16,256]{3,2,1,0:T(8,128)(2,1)}, u32[]{:S(2)}, u32[]{:S(2)}) collective-permute-start(bf16[2,32,16,256]{3,2,1,0:T(8,128)(2,1)} %copy-done.2), channel_id=1, source_target_pairs={{0,10},{2,8},{4,14},{6,12},{8,2},{10,0},{12,6},{14,4},{1,11},{3,9}... | collective-permute-start | bytes 1572872 | tf_op jit(solution)/shard_map/ppermute | solution.py:54
  121.2 15.6 %project.2 = (bf16[8,256,128]{2,1,0:T(8,128)(2,1)}, bf16[256,128]{1,0:T(8,128)(2,1)}, bf16[256,256]{1,0:T(8,128)(2,1)}, bf16[256,256]{1,0:T(8,128)(2,1)}) custom-call(s32[4]{0:T(128)} %add_multiply_fusion.starts_ref, bf16[64,8192]{1,0:T(8,128)(2,1)} %copy-done.10, bf16[64,8192]{1,0:T(8,128)(2,1)} %collective-permute-done.refs_1_, ...), custom_call_target="tpu_custom_call" | custom-call | flops 5368709120 | bytes 26476544 | tf_op jit(solution)/shard_map/project/pallas_call | solution.py:177
  136.9 3.1 %collective-permute-start.16 = (bf16[2,32,16,256]{3,2,1,0:T(8,128)(2,1)}, bf16[2,32,16,256]{3,2,1,0:T(8,128)(2,1)}, u32[]{:S(2)}, u32[]{:S(2)}) collective-permute-start(bf16[2,32,16,256]{3,2,1,0:T(8,128)(2,1)} %get-tuple-element.85), channel_id=1, source_target_pairs={{0,14},{2,12},{4,10},{6,8},{8,6},{10,4},{12,2},{14,0},{1,15},{3,13... | collective-permute-start | bytes 1572872 | tf_op jit(solution)/shard_map/ppermute | solution.py:54
  139.9 15.7 %project.3 = (bf16[8,256,128]{2,1,0:T(8,128)(2,1)}, bf16[256,128]{1,0:T(8,128)(2,1)}, bf16[256,256]{1,0:T(8,128)(2,1)}, bf16[256,256]{1,0:T(8,128)(2,1)}) custom-call(s32[4]{0:T(128)} %add_multiply_fusion.1.starts_ref, bf16[64,8192]{1,0:T(8,128)(2,1)} %copy-done.11, bf16[64,8192]{1,0:T(8,128)(2,1)} %broadcast_select_fusion.1.refs_1_, ...), custom_call_target="tpu_custom_call" | custom-call | flops 5368709120 | bytes 26476544 | tf_op jit(solution)/shard_map/project/pallas_call | solution.py:177
  155.7 1.8 maximum_select_fusion
  157.5 4.0 %all-to-all-start = ((bf16[8,64,256]{2,1,0:T(8,128)(2,1)}), bf16[8,64,256]{2,1,0:T(8,128)(2,1)}, u32[]{:S(2)}, u32[]{:S(2)}) async-start(bf16[8,64,256]{2,1,0:T(8,128)(2,1)} %bitcast.134), calls=%async_computation | async-start | bytes 524288 | tf_op jit(solution)/shard_map/all_to_all | solution.py:537
  163.8 2.8 collective-permute-done.16
  166.6 11.4 %all-to-all-done = bf16[8,64,256]{2,1,0:T(8,128)(2,1)} async-done(((bf16[8,64,256]{2,1,0:T(8,128)(2,1)}), bf16[8,64,256]{2,1,0:T(8,128)(2,1)}, u32[]{:S(2)}, u32[]{:S(2)}) %all-to-all-start) | async-done | bytes 262176 | tf_op jit(solution)/shard_map/all_to_all | solution.py:537
  177.9 3.5 %order_blocks.1 = (bf16[4096,128]{1,0:T(8,128)(2,1)S(1)}, bf16[4096,256]{1,0:T(8,128)(2,1)S(1)}) custom-call(s32[1]{0:T(128)} %dynamic_slice.118.length_ref, s32[256]{0:T(256)S(1)} %multiply_add_fusion.where_ref, bf16[64,16,256]{2,1,0:T(8,128)(2,1)S(1)} %bitcast.114, bf16[64,16,256]{2,1,0:T(8,128)(2,1)S(1)} %bitcast.117, bf16[64,16,256]{2,1,0:T(8,128)(2,1)S(1)} %bitcast.118, ...), custom_call_target="tpu_custom_call" | custom-call | tf_op jit(solution)/shard_map/order_blocks/pallas_call | solution.py:325
  181.5 13.9 %attend.2 = bf16[256,1024]{1,0:T(8,128)(2,1)S(1)} custom-call(s32[1]{0:T(128)} %bitcast.half_ref, bf16[8,4,2,32,128]{4,3,2,1,0:T(8,128)(2,1)S(1)} %bitcast.120, bf16[8,4,2,32,128]{4,3,2,1,0:T(8,128)(2,1)S(1)} %bitcast.122, bf16[4096,128]{1,0:T(8,128)(2,1)S(1)} %get-tuple-element.98.refs_2_, bf16[4096,256]{1,0:T(8,128)(2,1)S(1)} %get-tuple-element.99.refs_3_, ...), custom_call_target="tpu_custom_call" | custom-call | flops 9663676416 | bytes 4587520 | tf_op jit(solution)/shard_map/attend/pallas_call | solution.py:402
  195.4 10.5 %convolution_convert_fusion.1 = bf16[256,8192]{1,0:T(8,128)(2,1)S(1)} fusion(bf16[256,1024]{1,0:T(8,128)(2,1)S(1)} %attend.2, bf16[1024,8192]{1,0:T(8,128)(2,1)} %param.39), kind=kOutput, calls=%fused_computation.1 | convolution fusion | flops 4297064448 | bytes 21495808 | tf_op jit(solution)/shard_map/dot_general | solution.py:558
  208.1 13.9 %attend.3 = bf16[256,1024]{1,0:T(8,128)(2,1)S(1)} custom-call(s32[1]{0:T(128)} %bitcast.half_ref, bf16[8,4,2,32,128]{4,3,2,1,0:T(8,128)(2,1)S(1)} %bitcast.121, bf16[8,4,2,32,128]{4,3,2,1,0:T(8,128)(2,1)S(1)} %bitcast.123, bf16[4096,128]{1,0:T(8,128)(2,1)S(1)} %get-tuple-element.98.refs_2_, bf16[4096,256]{1,0:T(8,128)(2,1)S(1)} %get-tuple-element.99.refs_3_, ...), custom_call_target="tpu_custom_call" | custom-call | flops 9663676416 | bytes 4587520 | tf_op jit(solution)/shard_map/attend/pallas_call | solution.py:402
  224.4 10.5 %convolution_convert_fusion = bf16[256,8192]{1,0:T(8,128)(2,1)S(1)} fusion(bf16[256,1024]{1,0:T(8,128)(2,1)S(1)} %attend.3, bf16[1024,8192]{1,0:T(8,128)(2,1)} %param.39), kind=kOutput, calls=%fused_computation | convolution fusion | flops 4297064448 | bytes 21495808 | tf_op jit(solution)/shard_map/dot_general | solution.py:558
  239.4 10.5 %collective-permute-done.23 = bf16[32,8192]{1,0:T(8,128)(2,1)S(1)} collective-permute-done((bf16[32,8192]{1,0:T(8,128)(2,1)S(1)}, bf16[32,8192]{1,0:T(8,128)(2,1)S(1)}, u32[]{:S(2)}, u32[]{:S(2)}) %collective-permute-start.23) | collective-permute-done | bytes 524320 | tf_op jit(solution)/shard_map/ppermute | solution.py:230
  250.7 1.9 collective-permute-start.27
  252.8 8.4 %collective-permute-done.21 = bf16[32,8192]{1,0:T(8,128)(2,1)S(1)} collective-permute-done((bf16[32,8192]{1,0:T(8,128)(2,1)S(1)}, bf16[32,8192]{1,0:T(8,128)(2,1)S(1)}, u32[]{:S(2)}, u32[]{:S(2)}) %collective-permute-start.21) | collective-permute-done | bytes 524320 | tf_op jit(solution)/shard_map/ppermute | solution.py:230
  261.7 1.8 collective-permute-start.25
  263.5 8.8 %collective-permute-done.27 = bf16[32,8192]{1,0:T(8,128)(2,1)S(1)} collective-permute-done((bf16[32,8192]{1,0:T(8,128)(2,1)S(1)}, bf16[32,8192]{1,0:T(8,128)(2,1)S(1)}, u32[]{:S(2)}, u32[]{:S(2)}) %collective-permute-start.27) | collective-permute-done | bytes 524320 | tf_op jit(solution)/shard_map/ppermute | solution.py:230
  274.7 8.9 %collective-permute-done.25 = bf16[32,8192]{1,0:T(8,128)(2,1)S(1)} collective-permute-done((bf16[32,8192]{1,0:T(8,128)(2,1)S(1)}, bf16[32,8192]{1,0:T(8,128)(2,1)S(1)}, u32[]{:S(2)}, u32[]{:S(2)}) %collective-permute-start.25) | collective-permute-done | bytes 524320 | tf_op jit(solution)/shard_map/ppermute | solution.py:230
  284.0 7.7 %collective-permute-done.28 = bf16[32,8192]{1,0:T(8,128)(2,1)S(1)} collective-permute-done((bf16[32,8192]{1,0:T(8,128)(2,1)S(1)}, bf16[32,8192]{1,0:T(8,128)(2,1)S(1)}, u32[]{:S(2)}, u32[]{:S(2)}) %collective-permute-start.28) | collective-permute-done | bytes 524320 | tf_op jit(solution)/shard_map/ppermute | solution.py:230
  294.9 9.0 %collective-permute-done.30 = bf16[32,8192]{1,0:T(8,128)(2,1)S(1)} collective-permute-done((bf16[32,8192]{1,0:T(8,128)(2,1)S(1)}, bf16[32,8192]{1,0:T(8,128)(2,1)S(1)}, u32[]{:S(2)}, u32[]{:S(2)}) %collective-permute-start.30) | collective-permute-done | bytes 524320 | tf_op jit(solution)/shard_map/ppermute | solution.py:230
  (133 shorter events, 40.6 us)
Async XLA Ops:
  6.3 33.3 %collective-permute-start.2 = (bf16[32,16,2048]{2,1,0:T(8,128)(2,1)S(1)}, bf16[32,16,2048]{2,1,0:T(8,128)(2,1)}, u32[]{:S(2)}, u32[]{:S(2)}) collective-permute-start(bf16[32,16,2048]{2,1,0:T(8,128)(2,1)S(1)} %pick_blocks.1), channel_id=1, source_target_pairs={{0,1},{1,0},{2,3},{3,2},{4,5},{5,4},{6,7},{7,6},{8,9},{9,8},{10,11... | collective-permute-start | bytes 6291464 | tf_op jit(solution)/shard_map/ppermute | solution.py:469
  7.5 26.6 %collective-permute-start = (bf16[64,8192]{1,0:T(8,128)(2,1)S(1)}, bf16[64,8192]{1,0:T(8,128)(2,1)}, u32[]{:S(2)}, u32[]{:S(2)}) collective-permute-start(bf16[64,8192]{1,0:T(8,128)(2,1)S(1)} %fusion.2.refs_0_), channel_id=1, source_target_pairs={{0,4},{2,6},{4,0},{6,2},{8,12},{10,14},{12,8},{14,10},{1,5},{3,7},... | collective-permute-start | bytes 3145736 | tf_op jit(solution)/shard_map/ppermute | solution.py:54
  10.4 23.6 %collective-permute-start.8 = (bf16[64,8192]{1,0:T(8,128)(2,1)S(1)}, bf16[64,8192]{1,0:T(8,128)(2,1)}, u32[]{:S(2)}, u32[]{:S(2)}) collective-permute-start(bf16[64,8192]{1,0:T(8,128)(2,1)S(1)} %fusion.2.refs_0_), channel_id=1, source_target_pairs={{0,1},{1,0},{2,3},{3,2},{4,8},{5,9},{6,10},{7,11},{8,4},{9,5},{10,... | collective-permute-start | bytes 3145736 | tf_op jit(solution)/shard_map/ppermute | solution.py:65
  10.4 27.6 %collective-permute-start.6 = (bf16[64,8192]{1,0:T(8,128)(2,1)S(1)}, bf16[64,8192]{1,0:T(8,128)(2,1)}, u32[]{:S(2)}, u32[]{:S(2)}) collective-permute-start(bf16[64,8192]{1,0:T(8,128)(2,1)S(1)} %fusion.2.refs_0_), channel_id=1, source_target_pairs={{0,2},{2,0},{4,6},{6,4},{8,10},{10,8},{12,14},{14,12},{1,3},{3,1},... | collective-permute-start | bytes 3145736 | tf_op jit(solution)/shard_map/ppermute | solution.py:54
  34.1 11.9 %collective-permute-start.1 = (bf16[64,8192]{1,0:T(8,128)(2,1)}, bf16[64,8192]{1,0:T(8,128)(2,1)}, u32[]{:S(2)}, u32[]{:S(2)}) collective-permute-start(bf16[64,8192]{1,0:T(8,128)(2,1)} %collective-permute-done.refs_1_), channel_id=1, source_target_pairs={{0,1},{1,0},{2,3},{3,2},{4,8},{5,9},{6,10},{7,11},{8,4},{9,5},{10,... | collective-permute-start | bytes 3145736 | tf_op jit(solution)/shard_map/ppermute | solution.py:65
  34.1 29.0 %collective-permute-start.9 = (bf16[64,8192]{1,0:T(8,128)(2,1)}, bf16[64,8192]{1,0:T(8,128)(2,1)}, u32[]{:S(2)}, u32[]{:S(2)}) collective-permute-start(bf16[64,8192]{1,0:T(8,128)(2,1)} %collective-permute-done.8), channel_id=1, source_target_pairs={{0,4},{2,6},{4,0},{6,2},{8,12},{10,14},{12,8},{14,10},{1,5},{3,7},... | collective-permute-start | bytes 3145736 | tf_op jit(solution)/shard_map/ppermute | solution.py:54
  38.0 26.4 %collective-permute-start.7 = (bf16[64,8192]{1,0:T(8,128)(2,1)}, bf16[64,8192]{1,0:T(8,128)(2,1)S(1)}, u32[]{:S(2)}, u32[]{:S(2)}) collective-permute-start(bf16[64,8192]{1,0:T(8,128)(2,1)} %collective-permute-done.refs_1_), channel_id=1, source_target_pairs={{0,2},{2,0},{4,6},{6,4},{8,10},{10,8},{12,14},{14,12},{1,3},{3,1},... | collective-permute-start | bytes 3145736 | tf_op jit(solution)/shard_map/ppermute | solution.py:54
  45.9 48.2 %collective-permute-start.3 = (bf16[64,8192]{1,0:T(8,128)(2,1)}, bf16[64,8192]{1,0:T(8,128)(2,1)S(1)}, u32[]{:S(2)}, u32[]{:S(2)}) collective-permute-start(bf16[64,8192]{1,0:T(8,128)(2,1)} %collective-permute-done.1), channel_id=1, source_target_pairs={{0,4},{2,6},{4,0},{6,2},{8,12},{10,14},{12,8},{14,10},{1,5},{3,7},... | collective-permute-start | bytes 3145736 | tf_op jit(solution)/shard_map/ppermute | solution.py:54
  60.5 51.8 %collective-permute-start.4 = (bf16[2,32,16,256]{3,2,1,0:T(8,128)(2,1)S(1)}, bf16[2,32,16,256]{3,2,1,0:T(8,128)(2,1)S(1)}, u32[]{:S(2)}, u32[]{:S(2)}) collective-permute-start(bf16[2,32,16,256]{3,2,1,0:T(8,128)(2,1)S(1)} %get-tuple-element.64), channel_id=1, source_target_pairs={{0,8},{2,10},{4,12},{6,14},{8,0},{10,2},{12,4},{14,6},{1,9},{3,11}... | collective-permute-start | bytes 1572872 | tf_op jit(solution)/shard_map/ppermute | solution.py:54
  61.6 50.8 %collective-permute-start.5 = (bf16[2,32,16,256]{3,2,1,0:T(8,128)(2,1)S(1)}, bf16[2,32,16,256]{3,2,1,0:T(8,128)(2,1)S(1)}, u32[]{:S(2)}, u32[]{:S(2)}) collective-permute-start(bf16[2,32,16,256]{3,2,1,0:T(8,128)(2,1)S(1)} %get-tuple-element.66), channel_id=1, source_target_pairs={{0,12},{2,14},{4,8},{6,10},{8,4},{10,6},{12,0},{14,2},{1,13},{3,15... | collective-permute-start | bytes 1572872 | tf_op jit(solution)/shard_map/ppermute | solution.py:54
  65.4 29.8 %collective-permute-start.10 = (bf16[64,8192]{1,0:T(8,128)(2,1)S(1)}, bf16[64,8192]{1,0:T(8,128)(2,1)S(1)}, u32[]{:S(2)}, u32[]{:S(2)}) collective-permute-start(bf16[64,8192]{1,0:T(8,128)(2,1)S(1)} %broadcast_select_fusion.refs_0_), channel_id=1, source_target_pairs={{0,2},{2,0},{4,6},{6,4},{8,10},{10,8},{12,14},{14,12},{1,3},{3,1},... | collective-permute-start | bytes 3145736 | tf_op jit(solution)/shard_map/ppermute | solution.py:54
  95.3 41.6 %collective-permute-start.11 = (bf16[64,8192]{1,0:T(8,128)(2,1)}, bf16[64,8192]{1,0:T(8,128)(2,1)}, u32[]{:S(2)}, u32[]{:S(2)}) collective-permute-start(bf16[64,8192]{1,0:T(8,128)(2,1)} %broadcast_select_fusion.1.refs_1_), channel_id=1, source_target_pairs={{0,2},{2,0},{4,6},{6,4},{8,10},{10,8},{12,14},{14,12},{1,3},{3,1},... | collective-permute-start | bytes 3145736 | tf_op jit(solution)/shard_map/ppermute | solution.py:54
  112.4 51.3 %collective-permute-start.12 = (bf16[2,32,16,256]{3,2,1,0:T(8,128)(2,1)}, bf16[2,32,16,256]{3,2,1,0:T(8,128)(2,1)S(1)}, u32[]{:S(2)}, u32[]{:S(2)}) collective-permute-start(bf16[2,32,16,256]{3,2,1,0:T(8,128)(2,1)} %get-tuple-element.77), channel_id=1, source_target_pairs={{0,2},{2,0},{4,6},{6,4},{8,10},{10,8},{12,14},{14,12},{1,3},{3,1},... | collective-permute-start | bytes 1572872 | tf_op jit(solution)/shard_map/ppermute | solution.py:54
  113.4 50.4 %collective-permute-start.13 = (bf16[2,32,16,256]{3,2,1,0:T(8,128)(2,1)}, bf16[2,32,16,256]{3,2,1,0:T(8,128)(2,1)S(1)}, u32[]{:S(2)}, u32[]{:S(2)}) collective-permute-start(bf16[2,32,16,256]{3,2,1,0:T(8,128)(2,1)} %get-tuple-element.79), channel_id=1, source_target_pairs={{0,4},{2,6},{4,0},{6,2},{8,12},{10,14},{12,8},{14,10},{1,5},{3,7},... | collective-permute-start | bytes 1572872 | tf_op jit(solution)/shard_map/ppermute | solution.py:54
  114.1 49.6 %collective-permute-start.14 = (bf16[2,32,16,256]{3,2,1,0:T(8,128)(2,1)}, bf16[2,32,16,256]{3,2,1,0:T(8,128)(2,1)S(1)}, u32[]{:S(2)}, u32[]{:S(2)}) collective-permute-start(bf16[2,32,16,256]{3,2,1,0:T(8,128)(2,1)} %copy-done.3), channel_id=1, source_target_pairs={{0,6},{2,4},{4,2},{6,0},{8,14},{10,12},{12,10},{14,8},{1,7},{3,5},... | collective-permute-start | bytes 1572872 | tf_op jit(solution)/shard_map/ppermute | solution.py:54
  115.9 47.8 %collective-permute-start.15 = (bf16[2,32,16,256]{3,2,1,0:T(8,128)(2,1)}, bf16[2,32,16,256]{3,2,1,0:T(8,128)(2,1)}, u32[]{:S(2)}, u32[]{:S(2)}) collective-permute-start(bf16[2,32,16,256]{3,2,1,0:T(8,128)(2,1)} %copy-done.2), channel_id=1, source_target_pairs={{0,10},{2,8},{4,14},{6,12},{8,2},{10,0},{12,6},{14,4},{1,11},{3,9}... | collective-permute-start | bytes 1572872 | tf_op jit(solution)/shard_map/ppermute | solution.py:54
  136.9 29.7 %collective-permute-start.16 = (bf16[2,32,16,256]{3,2,1,0:T(8,128)(2,1)}, bf16[2,32,16,256]{3,2,1,0:T(8,128)(2,1)}, u32[]{:S(2)}, u32[]{:S(2)}) collective-permute-start(bf16[2,32,16,256]{3,2,1,0:T(8,128)(2,1)} %get-tuple-element.85), channel_id=1, source_target_pairs={{0,14},{2,12},{4,10},{6,8},{8,6},{10,4},{12,2},{14,0},{1,15},{3,13... | collective-permute-start | bytes 1572872 | tf_op jit(solution)/shard_map/ppermute | solution.py:54
  157.5 20.5 %all-to-all-start = ((bf16[8,64,256]{2,1,0:T(8,128)(2,1)}), bf16[8,64,256]{2,1,0:T(8,128)(2,1)}, u32[]{:S(2)}, u32[]{:S(2)}) async-start(bf16[8,64,256]{2,1,0:T(8,128)(2,1)} %bitcast.134), calls=%async_computation | async-start | bytes 524288 | tf_op jit(solution)/shard_map/all_to_all | solution.py:537
  206.1 16.0 %collective-permute-start.18 = (bf16[32,8192]{1,0:T(8,128)(2,1)S(1)}, bf16[32,8192]{1,0:T(8,128)(2,1)S(1)}, u32[]{:S(2)}, u32[]{:S(2)}) collective-permute-start(bf16[32,8192]{1,0:T(8,128)(2,1)S(1)} %get-tuple-element.105), channel_id=1, source_target_pairs={{0,2},{4,0},{8,4},{12,8},{14,12},{10,14},{6,10},{2,6},{1,3},{5,1},... | collective-permute-start | bytes 1572872 | tf_op jit(solution)/shard_map/ppermute | solution.py:230
  207.2 14.8 %collective-permute-start.17 = (bf16[32,8192]{1,0:T(8,128)(2,1)S(1)}, bf16[32,8192]{1,0:T(8,128)(2,1)S(1)}, u32[]{:S(2)}, u32[]{:S(2)}) collective-permute-start(bf16[32,8192]{1,0:T(8,128)(2,1)S(1)} %get-tuple-element.104), channel_id=1, source_target_pairs={{0,4},{4,8},{8,12},{12,14},{14,10},{10,6},{6,2},{2,0},{1,5},{5,9},... | collective-permute-start | bytes 1572872 | tf_op jit(solution)/shard_map/ppermute | solution.py:230
  222.3 14.8 %collective-permute-start.20 = (bf16[32,8192]{1,0:T(8,128)(2,1)S(1)}, bf16[32,8192]{1,0:T(8,128)(2,1)S(1)}, u32[]{:S(2)}, u32[]{:S(2)}) collective-permute-start(bf16[32,8192]{1,0:T(8,128)(2,1)S(1)} %get-tuple-element.107), channel_id=1, source_target_pairs={{0,2},{4,0},{8,4},{12,8},{14,12},{10,14},{6,10},{2,6},{1,3},{5,1},... | collective-permute-start | bytes 1572872 | tf_op jit(solution)/shard_map/ppermute | solution.py:230
  223.5 13.6 %collective-permute-start.19 = (bf16[32,8192]{1,0:T(8,128)(2,1)S(1)}, bf16[32,8192]{1,0:T(8,128)(2,1)S(1)}, u32[]{:S(2)}, u32[]{:S(2)}) collective-permute-start(bf16[32,8192]{1,0:T(8,128)(2,1)S(1)} %get-tuple-element.106), channel_id=1, source_target_pairs={{0,4},{4,8},{8,12},{12,14},{14,10},{10,6},{6,2},{2,0},{1,5},{5,9},... | collective-permute-start | bytes 1572872 | tf_op jit(solution)/shard_map/ppermute | solution.py:230
  235.0 14.9 %collective-permute-start.23 = (bf16[32,8192]{1,0:T(8,128)(2,1)S(1)}, bf16[32,8192]{1,0:T(8,128)(2,1)S(1)}, u32[]{:S(2)}, u32[]{:S(2)}) collective-permute-start(bf16[32,8192]{1,0:T(8,128)(2,1)S(1)} %get-tuple-element.112), channel_id=1, source_target_pairs={{0,4},{4,8},{8,12},{12,14},{14,10},{10,6},{6,2},{2,0},{1,5},{5,9},... | collective-permute-start | bytes 1572872 | tf_op jit(solution)/shard_map/ppermute | solution.py:230
  235.6 14.9 %collective-permute-start.22 = (bf16[32,8192]{1,0:T(8,128)(2,1)S(1)}, bf16[32,8192]{1,0:T(8,128)(2,1)S(1)}, u32[]{:S(2)}, u32[]{:S(2)}) collective-permute-start(bf16[32,8192]{1,0:T(8,128)(2,1)S(1)} %get-tuple-element.111), channel_id=1, source_target_pairs={{0,2},{4,0},{8,4},{12,8},{14,12},{10,14},{6,10},{2,6},{1,3},{5,1},... | collective-permute-start | bytes 1572872 | tf_op jit(solution)/shard_map/ppermute | solution.py:230
  237.3 23.8 %collective-permute-start.21 = (bf16[32,8192]{1,0:T(8,128)(2,1)S(1)}, bf16[32,8192]{1,0:T(8,128)(2,1)S(1)}, u32[]{:S(2)}, u32[]{:S(2)}) collective-permute-start(bf16[32,8192]{1,0:T(8,128)(2,1)S(1)} %get-tuple-element.113), channel_id=1, source_target_pairs={{0,4},{4,8},{8,12},{12,14},{14,10},{10,6},{6,2},{2,0},{1,5},{5,9},... | collective-permute-start | bytes 1572872 | tf_op jit(solution)/shard_map/ppermute | solution.py:230
  237.9 23.8 %collective-permute-start.24 = (bf16[32,8192]{1,0:T(8,128)(2,1)S(1)}, bf16[32,8192]{1,0:T(8,128)(2,1)S(1)}, u32[]{:S(2)}, u32[]{:S(2)}) collective-permute-start(bf16[32,8192]{1,0:T(8,128)(2,1)S(1)} %get-tuple-element.114), channel_id=1, source_target_pairs={{0,2},{4,0},{8,4},{12,8},{14,12},{10,14},{6,10},{2,6},{1,3},{5,1},... | collective-permute-start | bytes 1572872 | tf_op jit(solution)/shard_map/ppermute | solution.py:230
  250.7 21.7 %collective-permute-start.27 = (bf16[32,8192]{1,0:T(8,128)(2,1)S(1)}, bf16[32,8192]{1,0:T(8,128)(2,1)S(1)}, u32[]{:S(2)}, u32[]{:S(2)}) collective-permute-start(bf16[32,8192]{1,0:T(8,128)(2,1)S(1)} %get-tuple-element.116), channel_id=1, source_target_pairs={{0,4},{4,8},{8,12},{12,14},{14,10},{10,6},{6,2},{2,0},{1,5},{5,9},... | collective-permute-start | bytes 1572872 | tf_op jit(solution)/shard_map/ppermute | solution.py:230
  252.6 19.8 %collective-permute-start.26 = (bf16[32,8192]{1,0:T(8,128)(2,1)S(1)}, bf16[32,8192]{1,0:T(8,128)(2,1)S(1)}, u32[]{:S(2)}, u32[]{:S(2)}) collective-permute-start(bf16[32,8192]{1,0:T(8,128)(2,1)S(1)} %get-tuple-element.115), channel_id=1, source_target_pairs={{0,2},{4,0},{8,4},{12,8},{14,12},{10,14},{6,10},{2,6},{1,3},{5,1},... | collective-permute-start | bytes 1572872 | tf_op jit(solution)/shard_map/ppermute | solution.py:230
  261.7 21.9 %collective-permute-start.25 = (bf16[32,8192]{1,0:T(8,128)(2,1)S(1)}, bf16[32,8192]{1,0:T(8,128)(2,1)S(1)}, u32[]{:S(2)}, u32[]{:S(2)}) collective-permute-start(bf16[32,8192]{1,0:T(8,128)(2,1)S(1)} %fusion.14), channel_id=1, source_target_pairs={{0,4},{4,8},{8,12},{12,14},{14,10},{10,6},{6,2},{2,0},{1,5},{5,9},... | collective-permute-start | bytes 1572872 | tf_op jit(solution)/shard_map/ppermute | solution.py:230
  272.6 11.2 %collective-permute-start.29 = (bf16[32,8192]{1,0:T(8,128)(2,1)S(1)}, bf16[32,8192]{1,0:T(8,128)(2,1)S(1)}, u32[]{:S(2)}, u32[]{:S(2)}) collective-permute-start(bf16[32,8192]{1,0:T(8,128)(2,1)S(1)} %get-tuple-element.119), channel_id=1, source_target_pairs={{0,2},{4,0},{8,4},{12,8},{14,12},{10,14},{6,10},{2,6},{1,3},{5,1},... | collective-permute-start | bytes 1572872 | tf_op jit(solution)/shard_map/ppermute | solution.py:230
  273.8 17.9 %collective-permute-start.28 = (bf16[32,8192]{1,0:T(8,128)(2,1)S(1)}, bf16[32,8192]{1,0:T(8,128)(2,1)S(1)}, u32[]{:S(2)}, u32[]{:S(2)}) collective-permute-start(bf16[32,8192]{1,0:T(8,128)(2,1)S(1)} %get-tuple-element.118), channel_id=1, source_target_pairs={{0,4},{4,8},{8,12},{12,14},{14,10},{10,6},{6,2},{2,0},{1,5},{5,9},... | collective-permute-start | bytes 1572872 | tf_op jit(solution)/shard_map/ppermute | solution.py:230
  291.6 12.3 %collective-permute-start.30 = (bf16[32,8192]{1,0:T(8,128)(2,1)S(1)}, bf16[32,8192]{1,0:T(8,128)(2,1)S(1)}, u32[]{:S(2)}, u32[]{:S(2)}) collective-permute-start(bf16[32,8192]{1,0:T(8,128)(2,1)S(1)} %fusion.3), channel_id=1, source_target_pairs={{0,2},{4,0},{8,4},{12,8},{14,12},{10,14},{6,10},{2,6},{1,3},{5,1},... | collective-permute-start | bytes 1572872 | tf_op jit(solution)/shard_map/ppermute | solution.py:230
  (23 other events, 542.8 us)

commit v12 on v11

--- a/solution.py
+++ b/solution.py
@@ -16,6 +16,7 @@
 VMEM_LIMIT = 56 * 1024 * 1024
 ATTEND_VMEM = 28 * 1024 * 1024
 ROW_CHUNKS = 2
+DOT_ROWS = 128
 STREAMS = 4
 LINE_MODELS = 8
 
@@ -86,13 +87,13 @@
     over_beside_passed = swap(after(over_beside, outgoing[4]), 2)
     exchange(4, over_beside)
     exchange(6, over_beside)
+    exchange(1, over_beside)
     far_second = jnp.where(middle, over_beside, over_beside_passed)
     far_second_y = swap(after(far_second, far_first_y), 1)
     exchange(5, far_first_y, far_second)
     exchange(2, far_first_y, far_second)
     exchange(7, arrived[4], far_first_y)
     exchange(3, arrived[4], far_first_y)
-    exchange(1, arrived[4], far_first_y)
     near = [after(own, far_second, arrived[4], arrived[6]), beside, own_y, beside_y]
     far = [far_first, far_second, far_first_y, far_second_y]
     return near, far, [arrived[apart] for apart in range(LINE_MODELS)]
@@ -210,7 +211,13 @@
         table = jnp.array(self.order, jnp.int32)
         owner = table[(self.spot + offset + self.n_model) % self.n_model]
         owner = (owner - self.first + self.n_model) % self.n_model
-        return lax.dynamic_index_in_dim(self.shares, owner, 0, keepdims=False)
+        size = self.shares[0].shape[0]
+        block = None
+        for index, part in enumerate(self.shares):
+            place = jnp.clip(owner - index * size, 0, size - 1)
+            found = lax.dynamic_index_in_dim(part, place, 0, keepdims=False)
+            block = found if block is None else jnp.where(owner >= index * size, found, block)
+        return block
 
     def step(self, *before):
         ways = [way for way in (self.way, -self.way) if self.distance[way]]
@@ -465,6 +472,7 @@
             lax.dynamic_index_in_dim(slot_ids, pool, 0, keepdims=False)
             for pool in (my_pool, 1 - my_pool)
         )
+        others, normed = lax.optimization_barrier((others, normed))
         pool_blocks = kv_pool[0]
         got = lax.ppermute(pick_blocks(pool_blocks, others), "pool", [(0, 1), (1, 0)])
         slots = jnp.stack([mine, jnp.arange(capacity, dtype=jnp.int32)])
@@ -555,8 +563,14 @@
         if scatters:
             mixed, _ = lax.optimization_barrier((mixed, scatters[-1].step()))
             taken[-1] += 1
-        share = jnp.dot(mixed, w_out, preferred_element_type=jnp.float32).astype(jnp.bfloat16)
-        share = share.reshape(n_model, row_step, -1)
+        count = max(row_step, DOT_ROWS)
+        share = [
+            jnp.dot(
+                mixed[start : start + count], w_out, preferred_element_type=jnp.float32
+            ).astype(jnp.bfloat16)
+            for start in range(0, mixed.shape[0], count)
+        ]
+        share = [part.reshape(-1, row_step, part.shape[1]) for part in share]
         way = 1 if chunk % 2 == 0 else -1
         scatters.append(RingScatter(share, n_model, my_model, first, way))
         sent = scatters[-1].step()

time: 307 us -> 308 us (level)
  waiting for transfers between devices: 118 us -> 130 us
  matrix products: 21 us -> 9.66 us
  other arithmetic: 14.9 us -> 19.7 us
  starting transfers between devices: 61.6 us -> 57.6 us
    dot_general x2 -> x4, matrix products: 21 us -> 9.66 us  [on_device(): jnp.dot(mixed[start:start + count], w_out, preferred_element_type=jnp.flo...]
    ppermute x14, waiting for transfers between devices: 54.2 us -> 64.1 us  [step(): self.moving[way] = lax.ppermute(block, 'mp', pairs)]
  transfers between devices with their start and end apart: 32 -> 32, of which waited for: 12 -> 12; matrix products, arithmetic and copies ran while one was open for 8% -> 5% of each run, Pallas kernels for 16% -> 16%
where the time goes in v12:
time: 308 us; the launch traced here: 307 us
  waiting for transfers between devices  130 us (42%)
  Pallas kernels  68.1 us (22%)
  starting transfers between devices  57.6 us (19%)
  other arithmetic  19.7 us (6%)
  between operations  13.1 us (4%)
  matrix products  9.66 us (3%)
  local copies, waits for them, and re-layouts  9.6 us (3%)
    ppermute x14, waiting for transfers between devices, step(): self.moving[way] = lax.ppermute(block, 'mp', pairs)  64.1 us
    ppermute x14, waiting for transfers between devices, swap(): lax.ppermute(block, 'mp', [(index, index ^ mask) for index in range(LINE_...  52.6 us
    ppermute x14, starting transfers between devices, swap(): lax.ppermute(block, 'mp', [(index, index ^ mask) for index in range(LINE_...  39.3 us
    pallas_call x2, Pallas kernels, project(): pl.pallas_call(project_kernel, grid=(width // depth,), out_shape=out_shap...  31.3 us
    pallas_call x2, Pallas kernels, attend(): pl.pallas_call(functools.partial(attend_kernel, span, row_step, chunk), g...  27.9 us
    ppermute x14, starting transfers between devices, step(): self.moving[way] = lax.ppermute(block, 'mp', pairs)  14 us
    all_to_all x1, waiting for transfers between devices, on_device(): pairs = lax.all_to_all(pairs, 'mp', split_axis=0, concat_axis=0, tiled=True)  12.9 us
    dot_general x4, matrix products, on_device(): jnp.dot(mixed[start:start + count], w_out, preferred_element_type=jnp.flo...  9.66 us
  transfers between devices with their start and end apart: 32, of which 12 were waited for; matrix products, arithmetic and copies ran while one was open for 5% of the time, Pallas kernels for 16%

profile of v12, /device:TPU:0, one launch (start us, length us, event | category | flops | bytes accessed | tf_op | source)
XLA Modules:
  0.0 307.4 jit_solution(6978144866589038860)
XLA Ops:
  6.4 2.4 copy-done
  10.2 2.7 collective-permute-start
  14.5 22.2 %collective-permute-done.refs_1_ = bf16[64,8192]{1,0:T(8,128)(2,1)} collective-permute-done((bf16[64,8192]{1,0:T(8,128)(2,1)S(1)}, bf16[64,8192]{1,0:T(8,128)(2,1)}, u32[]{:S(2)}, u32[]{:S(2)}) %collective-permute-start) | collective-permute-done | bytes 1048608 | tf_op jit(solution)/shard_map/ppermute | solution.py:55
  36.7 3.3 %collective-permute-start.9 = (bf16[64,8192]{1,0:T(8,128)(2,1)}, bf16[64,8192]{1,0:T(8,128)(2,1)}, u32[]{:S(2)}, u32[]{:S(2)}) collective-permute-start(bf16[64,8192]{1,0:T(8,128)(2,1)} %collective-permute-done.8), channel_id=1, source_target_pairs={{0,4},{2,6},{4,0},{6,2},{8,12},{10,14},{12,8},{14,10},{1,5},{3,7},... | collective-permute-start | bytes 3145736 | tf_op jit(solution)/shard_map/ppermute | solution.py:55
  42.3 2.2 copy-done.1
  44.5 4.4 %pack_blocks.1 = (bf16[2,32,16,256]{3,2,1,0:T(8,128)(2,1)S(1)}, bf16[2,32,16,256]{3,2,1,0:T(8,128)(2,1)}, bf16[2,32,16,256]{3,2,1,0:T(8,128)(2,1)}, bf16[2,32,16...) custom-call(s32[2,32]{1,0:T(2,128)S(1)} %pad_add_fusion.slots_ref, ...), custom_call_target="tpu_custom_call" | custom-call | tf_op jit(solution)/shard_map/pack_blocks/pallas_call | solution.py:287
  48.8 14.6 %collective-permute-start.3 = (bf16[64,8192]{1,0:T(8,128)(2,1)}, bf16[64,8192]{1,0:T(8,128)(2,1)S(1)}, u32[]{:S(2)}, u32[]{:S(2)}) collective-permute-start(bf16[64,8192]{1,0:T(8,128)(2,1)} %collective-permute-done.1), channel_id=1, source_target_pairs={{0,4},{2,6},{4,0},{6,2},{8,12},{10,14},{12,8},{14,10},{1,5},{3,7},... | collective-permute-start | bytes 3145736 | tf_op jit(solution)/shard_map/ppermute | solution.py:55
  69.9 27.2 %collective-permute-done.3 = bf16[64,8192]{1,0:T(8,128)(2,1)S(1)} collective-permute-done((bf16[64,8192]{1,0:T(8,128)(2,1)}, bf16[64,8192]{1,0:T(8,128)(2,1)S(1)}, u32[]{:S(2)}, u32[]{:S(2)}) %collective-permute-start.3) | collective-permute-done | bytes 1048608 | tf_op jit(solution)/shard_map/ppermute | solution.py:55
  119.5 4.1 %collective-permute-start.15 = (bf16[2,32,16,256]{3,2,1,0:T(8,128)(2,1)}, bf16[2,32,16,256]{3,2,1,0:T(8,128)(2,1)}, u32[]{:S(2)}, u32[]{:S(2)}) collective-permute-start(bf16[2,32,16,256]{3,2,1,0:T(8,128)(2,1)} %get-tuple-element.87), channel_id=1, source_target_pairs={{0,10},{2,8},{4,14},{6,12},{8,2},{10,0},{12,6},{14,4},{1,11},{3,9}... | collective-permute-start | bytes 1572872 | tf_op jit(solution)/shard_map/ppermute | solution.py:55
  123.6 15.6 %project.2 = (bf16[8,256,128]{2,1,0:T(8,128)(2,1)}, bf16[256,128]{1,0:T(8,128)(2,1)}, bf16[256,256]{1,0:T(8,128)(2,1)}, bf16[256,256]{1,0:T(8,128)(2,1)}) custom-call(s32[4]{0:T(128)} %add_multiply_fusion.starts_ref, bf16[64,8192]{1,0:T(8,128)(2,1)} %copy-done.13, bf16[64,8192]{1,0:T(8,128)(2,1)} %collective-permute-done.refs_1_, ...), custom_call_target="tpu_custom_call" | custom-call | flops 5368709120 | bytes 26476544 | tf_op jit(solution)/shard_map/project/pallas_call | solution.py:178
  139.2 2.4 collective-permute-start.16
  141.6 15.7 %project.3 = (bf16[8,256,128]{2,1,0:T(8,128)(2,1)}, bf16[256,128]{1,0:T(8,128)(2,1)}, bf16[256,256]{1,0:T(8,128)(2,1)}, bf16[256,256]{1,0:T(8,128)(2,1)}) custom-call(s32[4]{0:T(128)} %add_multiply_fusion.1.starts_ref, bf16[64,8192]{1,0:T(8,128)(2,1)} %copy-done.14, bf16[64,8192]{1,0:T(8,128)(2,1)} %broadcast_select_fusion.1.refs_1_, ...), custom_call_target="tpu_custom_call" | custom-call | flops 5368709120 | bytes 26476544 | tf_op jit(solution)/shard_map/project/pallas_call | solution.py:178
  157.3 1.8 maximum_select_fusion
  159.1 3.6 %all-to-all-start = ((bf16[8,64,256]{2,1,0:T(8,128)(2,1)}), bf16[8,64,256]{2,1,0:T(8,128)(2,1)S(1)}, u32[]{:S(2)}, u32[]{:S(2)}) async-start(bf16[8,64,256]{2,1,0:T(8,128)(2,1)} %bitcast.29), calls=%async_computation | async-start | bytes 524288 | tf_op jit(solution)/shard_map/all_to_all | solution.py:545
  164.4 3.2 %collective-permute-done.12 = bf16[2,32,16,256]{3,2,1,0:T(8,128)(2,1)S(1)} collective-permute-done((bf16[2,32,16,256]{3,2,1,0:T(8,128)(2,1)}, bf16[2,32,16,256]{3,2,1,0:T(8,128)(2,1)S(1)}, u32[]{:S(2)}, u32[]{:S(2)}) %collective-permute-start.12) | collective-permute-done | bytes 524320 | tf_op jit(solution)/shard_map/ppermute | solution.py:55
  167.6 12.9 %all-to-all-done = bf16[8,64,256]{2,1,0:T(8,128)(2,1)S(1)} async-done(((bf16[8,64,256]{2,1,0:T(8,128)(2,1)}), bf16[8,64,256]{2,1,0:T(8,128)(2,1)S(1)}, u32[]{:S(2)}, u32[]{:S(2)}) %all-to-all-start) | async-done | bytes 262176 | tf_op jit(solution)/shard_map/all_to_all | solution.py:545
  180.5 3.8 %order_blocks.1 = (bf16[4096,128]{1,0:T(8,128)(2,1)S(1)}, bf16[4096,256]{1,0:T(8,128)(2,1)S(1)}) custom-call(s32[1]{0:T(128)} %dynamic_slice.168.length_ref, s32[256]{0:T(256)S(1)} %multiply_add_fusion.where_ref, bf16[64,16,256]{2,1,0:T(8,128)(2,1)S(1)} %bitcast.116, bf16[64,16,256]{2,1,0:T(8,128)(2,1)S(1)} %bitcast.119, bf16[64,16,256]{2,1,0:T(8,128)(2,1)S(1)} %bitcast.120, ...), custom_call_target="tpu_custom_call" | custom-call | tf_op jit(solution)/shard_map/order_blocks/pallas_call | solution.py:332
  184.4 14.0 %attend.2 = bf16[256,1024]{1,0:T(8,128)(2,1)S(1)} custom-call(s32[1]{0:T(128)} %bitcast.2.half_ref, bf16[8,4,2,32,128]{4,3,2,1,0:T(8,128)(2,1)S(1)} %bitcast.122, bf16[8,4,2,32,128]{4,3,2,1,0:T(8,128)(2,1)S(1)} %bitcast.124, bf16[4096,128]{1,0:T(8,128)(2,1)S(1)} %get-tuple-element.102.refs_2_, bf16[4096,256]{1,0:T(8,128)(2,1)S(1)} %get-tuple-element.103.refs_3_, ...), custom_call_target="tpu_custom_call" | custom-call | flops 9663676416 | bytes 4587520 | tf_op jit(solution)/shard_map/attend/pallas_call | solution.py:409
  198.5 2.4 convolution_convert_fusion.2
  200.9 2.4 convolution_convert_fusion.3
  205.6 13.9 %attend.3 = bf16[256,1024]{1,0:T(8,128)(2,1)S(1)} custom-call(s32[1]{0:T(128)} %bitcast.2.half_ref, bf16[8,4,2,32,128]{4,3,2,1,0:T(8,128)(2,1)S(1)} %bitcast.123, bf16[8,4,2,32,128]{4,3,2,1,0:T(8,128)(2,1)S(1)} %bitcast.125, bf16[4096,128]{1,0:T(8,128)(2,1)S(1)} %get-tuple-element.102.refs_2_, bf16[4096,256]{1,0:T(8,128)(2,1)S(1)} %get-tuple-element.103.refs_3_, ...), custom_call_target="tpu_custom_call" | custom-call | flops 9663676416 | bytes 4587520 | tf_op jit(solution)/shard_map/attend/pallas_call | solution.py:409
  219.9 2.4 convolution_convert_fusion
  222.3 2.4 convolution_convert_fusion.1
  229.1 10.6 %collective-permute-done.20 = bf16[32,8192]{1,0:T(8,128)(2,1)S(1)} collective-permute-done((bf16[32,8192]{1,0:T(8,128)(2,1)S(1)}, bf16[32,8192]{1,0:T(8,128)(2,1)S(1)}, u32[]{:S(2)}, u32[]{:S(2)}) %collective-permute-start.20) | collective-permute-done | bytes 524320 | tf_op jit(solution)/shard_map/ppermute | solution.py:237
  243.3 8.8 %collective-permute-done.23 = bf16[32,8192]{1,0:T(8,128)(2,1)S(1)} collective-permute-done((bf16[32,8192]{1,0:T(8,128)(2,1)S(1)}, bf16[32,8192]{1,0:T(8,128)(2,1)S(1)}, u32[]{:S(2)}, u32[]{:S(2)}) %collective-permute-start.23) | collective-permute-done | bytes 524320 | tf_op jit(solution)/shard_map/ppermute | solution.py:237
  254.5 8.7 %collective-permute-done.21 = bf16[32,8192]{1,0:T(8,128)(2,1)S(1)} collective-permute-done((bf16[32,8192]{1,0:T(8,128)(2,1)S(1)}, bf16[32,8192]{1,0:T(8,128)(2,1)S(1)}, u32[]{:S(2)}, u32[]{:S(2)}) %collective-permute-start.21) | collective-permute-done | bytes 524320 | tf_op jit(solution)/shard_map/ppermute | solution.py:237
  264.4 10.1 %collective-permute-done.27 = bf16[32,8192]{1,0:T(8,128)(2,1)S(1)} collective-permute-done((bf16[32,8192]{1,0:T(8,128)(2,1)S(1)}, bf16[32,8192]{1,0:T(8,128)(2,1)S(1)}, u32[]{:S(2)}, u32[]{:S(2)}) %collective-permute-start.27) | collective-permute-done | bytes 524320 | tf_op jit(solution)/shard_map/ppermute | solution.py:237
  275.3 1.7 collective-permute-start.28
  277.0 8.7 %collective-permute-done.25 = bf16[32,8192]{1,0:T(8,128)(2,1)S(1)} collective-permute-done((bf16[32,8192]{1,0:T(8,128)(2,1)S(1)}, bf16[32,8192]{1,0:T(8,128)(2,1)S(1)}, u32[]{:S(2)}, u32[]{:S(2)}) %collective-permute-start.25) | collective-permute-done | bytes 524320 | tf_op jit(solution)/shard_map/ppermute | solution.py:237
  287.0 6.7 %collective-permute-done.28 = bf16[32,8192]{1,0:T(8,128)(2,1)} collective-permute-done((bf16[32,8192]{1,0:T(8,128)(2,1)S(1)}, bf16[32,8192]{1,0:T(8,128)(2,1)}, u32[]{:S(2)}, u32[]{:S(2)}) %collective-permute-start.28) | collective-permute-done | bytes 524320 | tf_op jit(solution)/shard_map/ppermute | solution.py:237
  295.4 9.3 %collective-permute-done.30 = bf16[32,8192]{1,0:T(8,128)(2,1)} collective-permute-done((bf16[32,8192]{1,0:T(8,128)(2,1)}, bf16[32,8192]{1,0:T(8,128)(2,1)}, u32[]{:S(2)}, u32[]{:S(2)}) %collective-permute-start.30) | collective-permute-done | bytes 524320 | tf_op jit(solution)/shard_map/ppermute | solution.py:237
  304.8 1.6 fusion.7
  (146 shorter events, 48.4 us)
Async XLA Ops:
  9.7 32.6 %collective-permute-start.2 = (bf16[32,16,2048]{2,1,0:T(8,128)(2,1)S(1)}, bf16[32,16,2048]{2,1,0:T(8,128)(2,1)}, u32[]{:S(2)}, u32[]{:S(2)}) collective-permute-start(bf16[32,16,2048]{2,1,0:T(8,128)(2,1)S(1)} %pick_blocks.1), channel_id=1, source_target_pairs={{0,1},{1,0},{2,3},{3,2},{4,5},{5,4},{6,7},{7,6},{8,9},{9,8},{10,11... | collective-permute-start | bytes 6291464 | tf_op jit(solution)/shard_map/ppermute | solution.py:477
  10.2 26.5 %collective-permute-start = (bf16[64,8192]{1,0:T(8,128)(2,1)S(1)}, bf16[64,8192]{1,0:T(8,128)(2,1)}, u32[]{:S(2)}, u32[]{:S(2)}) collective-permute-start(bf16[64,8192]{1,0:T(8,128)(2,1)S(1)} %fusion.2.refs_0_), channel_id=1, source_target_pairs={{0,4},{2,6},{4,0},{6,2},{8,12},{10,14},{12,8},{14,10},{1,5},{3,7},... | collective-permute-start | bytes 3145736 | tf_op jit(solution)/shard_map/ppermute | solution.py:55
  12.8 23.9 %collective-permute-start.8 = (bf16[64,8192]{1,0:T(8,128)(2,1)S(1)}, bf16[64,8192]{1,0:T(8,128)(2,1)}, u32[]{:S(2)}, u32[]{:S(2)}) collective-permute-start(bf16[64,8192]{1,0:T(8,128)(2,1)S(1)} %fusion.2.refs_0_), channel_id=1, source_target_pairs={{0,1},{1,0},{2,3},{3,2},{4,8},{5,9},{6,10},{7,11},{8,4},{9,5},{10,... | collective-permute-start | bytes 3145736 | tf_op jit(solution)/shard_map/ppermute | solution.py:66
  13.0 27.7 %collective-permute-start.6 = (bf16[64,8192]{1,0:T(8,128)(2,1)S(1)}, bf16[64,8192]{1,0:T(8,128)(2,1)}, u32[]{:S(2)}, u32[]{:S(2)}) collective-permute-start(bf16[64,8192]{1,0:T(8,128)(2,1)S(1)} %fusion.2.refs_0_), channel_id=1, source_target_pairs={{0,2},{2,0},{4,6},{6,4},{8,10},{10,8},{12,14},{14,12},{1,3},{3,1},... | collective-permute-start | bytes 3145736 | tf_op jit(solution)/shard_map/ppermute | solution.py:55
  36.7 12.2 %collective-permute-start.1 = (bf16[64,8192]{1,0:T(8,128)(2,1)}, bf16[64,8192]{1,0:T(8,128)(2,1)}, u32[]{:S(2)}, u32[]{:S(2)}) collective-permute-start(bf16[64,8192]{1,0:T(8,128)(2,1)} %collective-permute-done.refs_1_), channel_id=1, source_target_pairs={{0,1},{1,0},{2,3},{3,2},{4,8},{5,9},{6,10},{7,11},{8,4},{9,5},{10,... | collective-permute-start | bytes 3145736 | tf_op jit(solution)/shard_map/ppermute | solution.py:66
  36.7 29.3 %collective-permute-start.9 = (bf16[64,8192]{1,0:T(8,128)(2,1)}, bf16[64,8192]{1,0:T(8,128)(2,1)}, u32[]{:S(2)}, u32[]{:S(2)}) collective-permute-start(bf16[64,8192]{1,0:T(8,128)(2,1)} %collective-permute-done.8), channel_id=1, source_target_pairs={{0,4},{2,6},{4,0},{6,2},{8,12},{10,14},{12,8},{14,10},{1,5},{3,7},... | collective-permute-start | bytes 3145736 | tf_op jit(solution)/shard_map/ppermute | solution.py:55
  40.7 26.7 %collective-permute-start.7 = (bf16[64,8192]{1,0:T(8,128)(2,1)}, bf16[64,8192]{1,0:T(8,128)(2,1)S(1)}, u32[]{:S(2)}, u32[]{:S(2)}) collective-permute-start(bf16[64,8192]{1,0:T(8,128)(2,1)} %collective-permute-done.refs_1_), channel_id=1, source_target_pairs={{0,2},{2,0},{4,6},{6,4},{8,10},{10,8},{12,14},{14,12},{1,3},{3,1},... | collective-permute-start | bytes 3145736 | tf_op jit(solution)/shard_map/ppermute | solution.py:55
  48.8 48.2 %collective-permute-start.3 = (bf16[64,8192]{1,0:T(8,128)(2,1)}, bf16[64,8192]{1,0:T(8,128)(2,1)S(1)}, u32[]{:S(2)}, u32[]{:S(2)}) collective-permute-start(bf16[64,8192]{1,0:T(8,128)(2,1)} %collective-permute-done.1), channel_id=1, source_target_pairs={{0,4},{2,6},{4,0},{6,2},{8,12},{10,14},{12,8},{14,10},{1,5},{3,7},... | collective-permute-start | bytes 3145736 | tf_op jit(solution)/shard_map/ppermute | solution.py:55
  63.5 53.4 %collective-permute-start.4 = (bf16[2,32,16,256]{3,2,1,0:T(8,128)(2,1)S(1)}, bf16[2,32,16,256]{3,2,1,0:T(8,128)(2,1)S(1)}, u32[]{:S(2)}, u32[]{:S(2)}) collective-permute-start(bf16[2,32,16,256]{3,2,1,0:T(8,128)(2,1)S(1)} %get-tuple-element.68), channel_id=1, source_target_pairs={{0,8},{2,10},{4,12},{6,14},{8,0},{10,2},{12,4},{14,6},{1,9},{3,11}... | collective-permute-start | bytes 1572872 | tf_op jit(solution)/shard_map/ppermute | solution.py:55
  64.5 52.4 %collective-permute-start.5 = (bf16[2,32,16,256]{3,2,1,0:T(8,128)(2,1)S(1)}, bf16[2,32,16,256]{3,2,1,0:T(8,128)(2,1)S(1)}, u32[]{:S(2)}, u32[]{:S(2)}) collective-permute-start(bf16[2,32,16,256]{3,2,1,0:T(8,128)(2,1)S(1)} %get-tuple-element.70), channel_id=1, source_target_pairs={{0,12},{2,14},{4,8},{6,10},{8,4},{10,6},{12,0},{14,2},{1,13},{3,15... | collective-permute-start | bytes 1572872 | tf_op jit(solution)/shard_map/ppermute | solution.py:55
  68.4 29.8 %collective-permute-start.10 = (bf16[64,8192]{1,0:T(8,128)(2,1)S(1)}, bf16[64,8192]{1,0:T(8,128)(2,1)S(1)}, u32[]{:S(2)}, u32[]{:S(2)}) collective-permute-start(bf16[64,8192]{1,0:T(8,128)(2,1)S(1)} %broadcast_select_fusion.refs_0_), channel_id=1, source_target_pairs={{0,2},{2,0},{4,6},{6,4},{8,10},{10,8},{12,14},{14,12},{1,3},{3,1},... | collective-permute-start | bytes 3145736 | tf_op jit(solution)/shard_map/ppermute | solution.py:55
  98.2 41.0 %collective-permute-start.11 = (bf16[64,8192]{1,0:T(8,128)(2,1)}, bf16[64,8192]{1,0:T(8,128)(2,1)}, u32[]{:S(2)}, u32[]{:S(2)}) collective-permute-start(bf16[64,8192]{1,0:T(8,128)(2,1)} %broadcast_select_fusion.1.refs_1_), channel_id=1, source_target_pairs={{0,2},{2,0},{4,6},{6,4},{8,10},{10,8},{12,14},{14,12},{1,3},{3,1},... | collective-permute-start | bytes 3145736 | tf_op jit(solution)/shard_map/ppermute | solution.py:55
  116.0 51.6 %collective-permute-start.12 = (bf16[2,32,16,256]{3,2,1,0:T(8,128)(2,1)}, bf16[2,32,16,256]{3,2,1,0:T(8,128)(2,1)S(1)}, u32[]{:S(2)}, u32[]{:S(2)}) collective-permute-start(bf16[2,32,16,256]{3,2,1,0:T(8,128)(2,1)} %get-tuple-element.81), channel_id=1, source_target_pairs={{0,2},{2,0},{4,6},{6,4},{8,10},{10,8},{12,14},{14,12},{1,3},{3,1},... | collective-permute-start | bytes 1572872 | tf_op jit(solution)/shard_map/ppermute | solution.py:55
  116.9 50.7 %collective-permute-start.13 = (bf16[2,32,16,256]{3,2,1,0:T(8,128)(2,1)}, bf16[2,32,16,256]{3,2,1,0:T(8,128)(2,1)S(1)}, u32[]{:S(2)}, u32[]{:S(2)}) collective-permute-start(bf16[2,32,16,256]{3,2,1,0:T(8,128)(2,1)} %get-tuple-element.83), channel_id=1, source_target_pairs={{0,4},{2,6},{4,0},{6,2},{8,12},{10,14},{12,8},{14,10},{1,5},{3,7},... | collective-permute-start | bytes 1572872 | tf_op jit(solution)/shard_map/ppermute | solution.py:55
  117.9 49.7 %collective-permute-start.14 = (bf16[2,32,16,256]{3,2,1,0:T(8,128)(2,1)}, bf16[2,32,16,256]{3,2,1,0:T(8,128)(2,1)S(1)}, u32[]{:S(2)}, u32[]{:S(2)}) collective-permute-start(bf16[2,32,16,256]{3,2,1,0:T(8,128)(2,1)} %get-tuple-element.85), channel_id=1, source_target_pairs={{0,6},{2,4},{4,2},{6,0},{8,14},{10,12},{12,10},{14,8},{1,7},{3,5},... | collective-permute-start | bytes 1572872 | tf_op jit(solution)/shard_map/ppermute | solution.py:55
  119.5 48.1 %collective-permute-start.15 = (bf16[2,32,16,256]{3,2,1,0:T(8,128)(2,1)}, bf16[2,32,16,256]{3,2,1,0:T(8,128)(2,1)}, u32[]{:S(2)}, u32[]{:S(2)}) collective-permute-start(bf16[2,32,16,256]{3,2,1,0:T(8,128)(2,1)} %get-tuple-element.87), channel_id=1, source_target_pairs={{0,10},{2,8},{4,14},{6,12},{8,2},{10,0},{12,6},{14,4},{1,11},{3,9}... | collective-permute-start | bytes 1572872 | tf_op jit(solution)/shard_map/ppermute | solution.py:55
  139.2 28.4 %collective-permute-start.16 = (bf16[2,32,16,256]{3,2,1,0:T(8,128)(2,1)}, bf16[2,32,16,256]{3,2,1,0:T(8,128)(2,1)}, u32[]{:S(2)}, u32[]{:S(2)}) collective-permute-start(bf16[2,32,16,256]{3,2,1,0:T(8,128)(2,1)} %get-tuple-element.89), channel_id=1, source_target_pairs={{0,14},{2,12},{4,10},{6,8},{8,6},{10,4},{12,2},{14,0},{1,15},{3,13... | collective-permute-start | bytes 1572872 | tf_op jit(solution)/shard_map/ppermute | solution.py:55
  159.1 21.4 %all-to-all-start = ((bf16[8,64,256]{2,1,0:T(8,128)(2,1)}), bf16[8,64,256]{2,1,0:T(8,128)(2,1)S(1)}, u32[]{:S(2)}, u32[]{:S(2)}) async-start(bf16[8,64,256]{2,1,0:T(8,128)(2,1)} %bitcast.29), calls=%async_computation | async-start | bytes 524288 | tf_op jit(solution)/shard_map/all_to_all | solution.py:545
  203.5 16.0 %collective-permute-start.18 = (bf16[32,8192]{1,0:T(8,128)(2,1)S(1)}, bf16[32,8192]{1,0:T(8,128)(2,1)S(1)}, u32[]{:S(2)}, u32[]{:S(2)}) collective-permute-start(bf16[32,8192]{1,0:T(8,128)(2,1)S(1)} %get-tuple-element.109), channel_id=1, source_target_pairs={{0,2},{4,0},{8,4},{12,8},{14,12},{10,14},{6,10},{2,6},{1,3},{5,1},... | collective-permute-start | bytes 1572872 | tf_op jit(solution)/shard_map/ppermute | solution.py:237
  204.6 14.8 %collective-permute-start.17 = (bf16[32,8192]{1,0:T(8,128)(2,1)S(1)}, bf16[32,8192]{1,0:T(8,128)(2,1)S(1)}, u32[]{:S(2)}, u32[]{:S(2)}) collective-permute-start(bf16[32,8192]{1,0:T(8,128)(2,1)S(1)} %get-tuple-element.108), channel_id=1, source_target_pairs={{0,4},{4,8},{8,12},{12,14},{14,10},{10,6},{6,2},{2,0},{1,5},{5,9},... | collective-permute-start | bytes 1572872 | tf_op jit(solution)/shard_map/ppermute | solution.py:237
  224.8 14.9 %collective-permute-start.20 = (bf16[32,8192]{1,0:T(8,128)(2,1)S(1)}, bf16[32,8192]{1,0:T(8,128)(2,1)S(1)}, u32[]{:S(2)}, u32[]{:S(2)}) collective-permute-start(bf16[32,8192]{1,0:T(8,128)(2,1)S(1)} %get-tuple-element.111), channel_id=1, source_target_pairs={{0,2},{4,0},{8,4},{12,8},{14,12},{10,14},{6,10},{2,6},{1,3},{5,1},... | collective-permute-start | bytes 1572872 | tf_op jit(solution)/shard_map/ppermute | solution.py:237
  225.9 14.9 %collective-permute-start.19 = (bf16[32,8192]{1,0:T(8,128)(2,1)S(1)}, bf16[32,8192]{1,0:T(8,128)(2,1)S(1)}, u32[]{:S(2)}, u32[]{:S(2)}) collective-permute-start(bf16[32,8192]{1,0:T(8,128)(2,1)S(1)} %get-tuple-element.110), channel_id=1, source_target_pairs={{0,4},{4,8},{8,12},{12,14},{14,10},{10,6},{6,2},{2,0},{1,5},{5,9},... | collective-permute-start | bytes 1572872 | tf_op jit(solution)/shard_map/ppermute | solution.py:237
  227.0 25.0 %collective-permute-start.23 = (bf16[32,8192]{1,0:T(8,128)(2,1)S(1)}, bf16[32,8192]{1,0:T(8,128)(2,1)S(1)}, u32[]{:S(2)}, u32[]{:S(2)}) collective-permute-start(bf16[32,8192]{1,0:T(8,128)(2,1)S(1)} %get-tuple-element.116), channel_id=1, source_target_pairs={{0,4},{4,8},{8,12},{12,14},{14,10},{10,6},{6,2},{2,0},{1,5},{5,9},... | collective-permute-start | bytes 1572872 | tf_op jit(solution)/shard_map/ppermute | solution.py:237
  227.6 24.5 %collective-permute-start.22 = (bf16[32,8192]{1,0:T(8,128)(2,1)S(1)}, bf16[32,8192]{1,0:T(8,128)(2,1)S(1)}, u32[]{:S(2)}, u32[]{:S(2)}) collective-permute-start(bf16[32,8192]{1,0:T(8,128)(2,1)S(1)} %get-tuple-element.115), channel_id=1, source_target_pairs={{0,2},{4,0},{8,4},{12,8},{14,12},{10,14},{6,10},{2,6},{1,3},{5,1},... | collective-permute-start | bytes 1572872 | tf_op jit(solution)/shard_map/ppermute | solution.py:237
  241.2 22.1 %collective-permute-start.21 = (bf16[32,8192]{1,0:T(8,128)(2,1)S(1)}, bf16[32,8192]{1,0:T(8,128)(2,1)S(1)}, u32[]{:S(2)}, u32[]{:S(2)}) collective-permute-start(bf16[32,8192]{1,0:T(8,128)(2,1)S(1)} %get-tuple-element.117), channel_id=1, source_target_pairs={{0,4},{4,8},{8,12},{12,14},{14,10},{10,6},{6,2},{2,0},{1,5},{5,9},... | collective-permute-start | bytes 1572872 | tf_op jit(solution)/shard_map/ppermute | solution.py:237
  242.1 21.3 %collective-permute-start.24 = (bf16[32,8192]{1,0:T(8,128)(2,1)S(1)}, bf16[32,8192]{1,0:T(8,128)(2,1)S(1)}, u32[]{:S(2)}, u32[]{:S(2)}) collective-permute-start(bf16[32,8192]{1,0:T(8,128)(2,1)S(1)} %get-tuple-element.118), channel_id=1, source_target_pairs={{0,2},{4,0},{8,4},{12,8},{14,12},{10,14},{6,10},{2,6},{1,3},{5,1},... | collective-permute-start | bytes 1572872 | tf_op jit(solution)/shard_map/ppermute | solution.py:237
  252.4 22.1 %collective-permute-start.27 = (bf16[32,8192]{1,0:T(8,128)(2,1)S(1)}, bf16[32,8192]{1,0:T(8,128)(2,1)S(1)}, u32[]{:S(2)}, u32[]{:S(2)}) collective-permute-start(bf16[32,8192]{1,0:T(8,128)(2,1)S(1)} %get-tuple-element.120), channel_id=1, source_target_pairs={{0,4},{4,8},{8,12},{12,14},{14,10},{10,6},{6,2},{2,0},{1,5},{5,9},... | collective-permute-start | bytes 1572872 | tf_op jit(solution)/shard_map/ppermute | solution.py:237
  253.4 21.1 %collective-permute-start.26 = (bf16[32,8192]{1,0:T(8,128)(2,1)S(1)}, bf16[32,8192]{1,0:T(8,128)(2,1)S(1)}, u32[]{:S(2)}, u32[]{:S(2)}) collective-permute-start(bf16[32,8192]{1,0:T(8,128)(2,1)S(1)} %get-tuple-element.119), channel_id=1, source_target_pairs={{0,2},{4,0},{8,4},{12,8},{14,12},{10,14},{6,10},{2,6},{1,3},{5,1},... | collective-permute-start | bytes 1572872 | tf_op jit(solution)/shard_map/ppermute | solution.py:237
  263.5 22.3 %collective-permute-start.25 = (bf16[32,8192]{1,0:T(8,128)(2,1)S(1)}, bf16[32,8192]{1,0:T(8,128)(2,1)S(1)}, u32[]{:S(2)}, u32[]{:S(2)}) collective-permute-start(bf16[32,8192]{1,0:T(8,128)(2,1)S(1)} %fusion.14), channel_id=1, source_target_pairs={{0,4},{4,8},{8,12},{12,14},{14,10},{10,6},{6,2},{2,0},{1,5},{5,9},... | collective-permute-start | bytes 1572872 | tf_op jit(solution)/shard_map/ppermute | solution.py:237
  274.9 11.1 %collective-permute-start.29 = (bf16[32,8192]{1,0:T(8,128)(2,1)S(1)}, bf16[32,8192]{1,0:T(8,128)(2,1)S(1)}, u32[]{:S(2)}, u32[]{:S(2)}) collective-permute-start(bf16[32,8192]{1,0:T(8,128)(2,1)S(1)} %get-tuple-element.123), channel_id=1, source_target_pairs={{0,2},{4,0},{8,4},{12,8},{14,12},{10,14},{6,10},{2,6},{1,3},{5,1},... | collective-permute-start | bytes 1572872 | tf_op jit(solution)/shard_map/ppermute | solution.py:237
  275.3 18.5 %collective-permute-start.28 = (bf16[32,8192]{1,0:T(8,128)(2,1)S(1)}, bf16[32,8192]{1,0:T(8,128)(2,1)}, u32[]{:S(2)}, u32[]{:S(2)}) collective-permute-start(bf16[32,8192]{1,0:T(8,128)(2,1)S(1)} %get-tuple-element.122), channel_id=1, source_target_pairs={{0,4},{4,8},{8,12},{12,14},{14,10},{10,6},{6,2},{2,0},{1,5},{5,9},... | collective-permute-start | bytes 1572872 | tf_op jit(solution)/shard_map/ppermute | solution.py:237
  293.7 11.0 %collective-permute-start.30 = (bf16[32,8192]{1,0:T(8,128)(2,1)}, bf16[32,8192]{1,0:T(8,128)(2,1)}, u32[]{:S(2)}, u32[]{:S(2)}) collective-permute-start(bf16[32,8192]{1,0:T(8,128)(2,1)} %fusion.3), channel_id=1, source_target_pairs={{0,2},{4,0},{8,4},{12,8},{14,12},{10,14},{6,10},{2,6},{1,3},{5,1},... | collective-permute-start | bytes 1572872 | tf_op jit(solution)/shard_map/ppermute | solution.py:237
  (28 other events, 464.2 us)

commit v13 on v10

--- a/solution.py
+++ b/solution.py
@@ -65,7 +65,7 @@
     return lax.ppermute(block, ("mp", "pool"), pairs)
 
 
-def gather_and_exchange(own, outgoing, middle):
+def gather_and_exchange(own, outgoing, middle, project_near):
     arrived = {0: outgoing[0]}
 
     def after(block, *events):
@@ -86,14 +86,16 @@
     over_beside_passed = swap(after(over_beside, outgoing[4]), 2)
     exchange(4, over_beside)
     exchange(6, over_beside)
+    near = project_near([after(own, far_first), beside, own_y, beside_y])
     far_second = jnp.where(middle, over_beside, over_beside_passed)
+    far_second, near, _ = lax.optimization_barrier((far_second, near, arrived[4]))
     far_second_y = swap(after(far_second, far_first_y), 1)
-    exchange(5, far_first_y, far_second)
-    exchange(2, far_first_y, far_second)
-    exchange(7, arrived[4], far_first_y)
-    exchange(3, arrived[4], far_first_y)
-    exchange(1, arrived[4], far_first_y)
-    near = [after(own, far_second, arrived[4], arrived[6]), beside, own_y, beside_y]
+    exchange(2, arrived[4], far_first_y)
+    exchange(5, arrived[6], far_first_y)
+    exchange(7, arrived[6], far_first_y)
+    exchange(3, arrived[6], far_first_y)
+    exchange(1, arrived[6], far_first_y)
+    far_first = after(far_first, arrived[2], arrived[6])
     far = [far_first, far_second, far_first_y, far_second_y]
     return near, far, [arrived[apart] for apart in range(LINE_MODELS)]
 
@@ -455,6 +457,14 @@
     earlier = (my_holder[:, None] == my_holder[None, :]) & (block_ids[None, :] < block_ids[:, None])
     rank = jnp.sum(earlier.astype(jnp.int32), -1)
     normed = normalize(states[0], norm_gain)
+    upper_half = (my_model // (n_model // 2)).astype(jnp.int32) if lined else jnp.int32(0)
+    half_rows = suffix // 2
+    order = (jnp.arange(suffix, dtype=jnp.int32) + upper_half * half_rows) % suffix
+    cosine, sine = angle_tables(prefix_count + order)
+    cosine, sine = jnp.concatenate([cosine, cosine], 1), jnp.concatenate([-sine, sine], 1)
+    halves = [slice(0, half_rows), slice(half_rows, suffix)]
+    biases = [bias.reshape(1, -1) for bias in (q_bias, k_bias, v_bias)]
+    weights = (w_query, w_key, w_value)
     if lined:
         mine, others = (
             lax.dynamic_index_in_dim(slot_ids, pool, 0, keepdims=False)
@@ -465,7 +475,21 @@
         slots = jnp.stack([mine, jnp.arange(capacity, dtype=jnp.int32)])
         outgoing = pack_blocks((pool_blocks, got), slots, (models ^ my_model) * q_local // group_size)
         my_z, my_y = my_model // 2, my_model % 2
-        near, far, arrived = gather_and_exchange(normed, outgoing, (my_z == 1) | (my_z == 2))
+
+        def project_half(blocks, inner, part):
+            starts = jnp.stack(
+                [2 * (inner ^ other) + (my_y ^ side) for side in range(2) for other in range(2)]
+            )
+            table = [values[halves[part]] for values in (cosine, sine)]
+            return project(starts.astype(jnp.int32) * row_count, blocks, weights, biases, table)
+
+        near, far, arrived = gather_and_exchange(
+            normed,
+            outgoing,
+            (my_z == 1) | (my_z == 2),
+            lambda blocks: project_half(blocks, my_z % 2, 0),
+        )
+        results = near, project_half(far, upper_half, 1)
         arrived = [block.reshape(-1, block_len, 2 * HD) for block in arrived]
         distance = (my_holder // n_pool) ^ my_model
         where = (distance * n_pool + (my_holder % n_pool ^ my_pool)) * capacity + rank
@@ -476,28 +500,7 @@
         arrived = [arrived.reshape(holders * capacity, block_len, 2 * HD)]
         where = my_holder * capacity + rank
 
-    upper_half = (my_model // (n_model // 2)).astype(jnp.int32) if lined else jnp.int32(0)
-    half_rows = suffix // 2
-    order = (jnp.arange(suffix, dtype=jnp.int32) + upper_half * half_rows) % suffix
-    cosine, sine = angle_tables(prefix_count + order)
-    cosine, sine = jnp.concatenate([cosine, cosine], 1), jnp.concatenate([-sine, sine], 1)
-    halves = [slice(0, half_rows), slice(half_rows, suffix)]
-    biases = [bias.reshape(1, -1) for bias in (q_bias, k_bias, v_bias)]
-    weights = (w_query, w_key, w_value)
     if lined:
-        results = []
-        for blocks, inner in ((near, my_z % 2), (far, upper_half)):
-            starts = jnp.stack(
-                [
-                    2 * (inner ^ other) + (my_y ^ side)
-                    for side in range(2)
-                    for other in range(2)
-                ]
-            )
-            table = [part[halves[len(results)]] for part in (cosine, sine)]
-            results.append(
-                project(starts.astype(jnp.int32) * row_count, blocks, weights, biases, table)
-            )
         queries, new_keys, new_values, pairs = zip(*results)
         pairs = jnp.where(
             upper_half == 0, jnp.concatenate(pairs, 0), jnp.concatenate(pairs[::-1], 0)
@@ -559,11 +562,14 @@
         )
         for chunk, share in enumerate(shares)
     ]
-    sent = []
-    for _ in range(n_model // 2):
+    sent, sums = [], []
+    steps = n_model // 2
+    for step in range(steps):
         for scatter in scatters:
-            sent = scatter.step(*sent)
-    return (jnp.concatenate([scatter.finish() for scatter in scatters], 1)[None], cache_rows)
+            sent = scatter.step(sent, sums)
+            if step == steps - 1:
+                sums.append(scatter.finish())
+    return (jnp.concatenate(sums, 1)[None], cache_rows)
 
 
 def solution(mesh):

time: 300 us -> 306 us (1.020)
  starting transfers between devices: 62.7 us -> 79.5 us
  waiting for transfers between devices: 119 us -> 109 us
  matrix products: 12.8 us -> 16.2 us
    all_to_all x1, starting transfers between devices: 4.24 us -> 21.7 us  [on_device(): pairs = lax.all_to_all(pairs, 'mp', split_axis=0, concat_axis=0, tiled=True)]
    ppermute x14, waiting for transfers between devices: 50.7 us -> 36.2 us  [swap(): lax.ppermute(block, 'mp', [(index, index ^ mask) for index in range(LINE_...]
    ppermute x14, waiting for transfers between devices: 56.9 us -> 63 us  [step(): self.moving[way] = lax.ppermute(block, 'mp', pairs)]
    dot_general x2, matrix products: 12.8 us -> 16.2 us  [on_device(): jnp.dot(mixed, w_out[:, chunk * width:(chunk + 1) * width], preferred_ele...]
  transfers between devices with their start and end apart: 32 -> 32, of which waited for: 15 -> 16; matrix products, arithmetic and copies ran while one was open for 8% -> 8% of each run, Pallas kernels for 12% -> 12%
where the time goes in v13:
time: 306 us; the launch traced here: 305 us
  waiting for transfers between devices  109 us (36%)
  starting transfers between devices  79.5 us (26%)
  Pallas kernels  63.6 us (21%)
  matrix products  16.2 us (5%)
  other arithmetic  14.9 us (5%)
  between operations  12.4 us (4%)
  local copies, waits for them, and re-layouts  9.41 us (3%)
    ppermute x14, waiting for transfers between devices, step(): self.moving[way] = lax.ppermute(block, 'mp', pairs)  63 us
    ppermute x14, starting transfers between devices, swap(): lax.ppermute(block, 'mp', [(index, index ^ mask) for index in range(LINE_...  42.5 us
    ppermute x14, waiting for transfers between devices, swap(): lax.ppermute(block, 'mp', [(index, index ^ mask) for index in range(LINE_...  36.2 us
    pallas_call x2, Pallas kernels, project(): pl.pallas_call(project_kernel, grid=(width // depth,), out_shape=out_shap...  31.3 us
    pallas_call x1, Pallas kernels, attend(): pl.pallas_call(functools.partial(attend_kernel, span), grid=(heads,), out...  24.1 us
    all_to_all x1, starting transfers between devices, on_device(): pairs = lax.all_to_all(pairs, 'mp', split_axis=0, concat_axis=0, tiled=True)  21.7 us
    dot_general x2, matrix products, on_device(): jnp.dot(mixed, w_out[:, chunk * width:(chunk + 1) * width], preferred_ele...  16.2 us
    ppermute x14, starting transfers between devices, step(): self.moving[way] = lax.ppermute(block, 'mp', pairs)  14.8 us
  transfers between devices with their start and end apart: 32, of which 16 were waited for; matrix products, arithmetic and copies ran while one was open for 8% of the time, Pallas kernels for 12%

profile of v13, /device:TPU:0, one launch (start us, length us, event | category | flops | bytes accessed | tf_op | source)
XLA Modules:
  0.0 305.2 jit_solution(7555434754286638379)
XLA Ops:
  3.3 2.2 copy-done
  7.5 3.0 collective-permute-start
  12.0 22.1 %collective-permute-done.refs_1_ = bf16[64,8192]{1,0:T(8,128)(2,1)} collective-permute-done((bf16[64,8192]{1,0:T(8,128)(2,1)S(1)}, bf16[64,8192]{1,0:T(8,128)(2,1)}, u32[]{:S(2)}, u32[]{:S(2)}) %collective-permute-start) | collective-permute-done | bytes 1048608 | tf_op jit(solution)/shard_map/ppermute | solution.py:54
  34.1 3.3 %collective-permute-start.5 = (bf16[64,8192]{1,0:T(8,128)(2,1)}, bf16[64,8192]{1,0:T(8,128)(2,1)}, u32[]{:S(2)}, u32[]{:S(2)}) collective-permute-start(bf16[64,8192]{1,0:T(8,128)(2,1)} %collective-permute-done.4), channel_id=1, source_target_pairs={{0,4},{2,6},{4,0},{6,2},{8,12},{10,14},{12,8},{14,10},{1,5},{3,7},... | collective-permute-start | bytes 3145736 | tf_op jit(solution)/shard_map/ppermute | solution.py:54
  41.7 1.5 collective-permute-start.7
  43.2 2.2 copy-done.1
  45.4 3.8 %pack_blocks.1 = (bf16[2,32,16,256]{3,2,1,0:T(8,128)(2,1)S(1)}, bf16[2,32,16,256]{3,2,1,0:T(8,128)(2,1)}, bf16[2,32,16,256]{3,2,1,0:T(8,128)(2,1)}, bf16[2,32,16...) custom-call(s32[2,32]{1,0:T(2,128)S(1)} %pad_add_fusion.slots_ref, ...), custom_call_target="tpu_custom_call" | custom-call | tf_op jit(solution)/shard_map/pack_blocks/pallas_call | solution.py:282
  49.2 11.3 %collective-permute-start.3 = (bf16[64,8192]{1,0:T(8,128)(2,1)}, bf16[64,8192]{1,0:T(8,128)(2,1)S(1)}, u32[]{:S(2)}, u32[]{:S(2)}) collective-permute-start(bf16[64,8192]{1,0:T(8,128)(2,1)} %collective-permute-done.1), channel_id=1, source_target_pairs={{0,4},{2,6},{4,0},{6,2},{8,12},{10,14},{12,8},{14,10},{1,5},{3,7},... | collective-permute-start | bytes 3145736 | tf_op jit(solution)/shard_map/ppermute | solution.py:54
  61.9 3.8 %collective-permute-done.7.refs_3_ = bf16[64,8192]{1,0:T(8,128)(2,1)S(1)} collective-permute-done((bf16[64,8192]{1,0:T(8,128)(2,1)}, bf16[64,8192]{1,0:T(8,128)(2,1)S(1)}, u32[]{:S(2)}, u32[]{:S(2)}) %collective-permute-start.7) | collective-permute-done | bytes 1048608 | tf_op jit(solution)/shard_map/ppermute | solution.py:54
  67.3 2.4 collective-permute-start.8
  69.7 15.7 %project.2 = (bf16[8,256,128]{2,1,0:T(8,128)(2,1)}, bf16[256,128]{1,0:T(8,128)(2,1)}, bf16[256,256]{1,0:T(8,128)(2,1)}, bf16[256,256]{1,0:T(8,128)(2,1)}) custom-call(s32[4]{0:T(128)} %add_multiply_fusion.starts_ref, bf16[64,8192]{1,0:T(8,128)(2,1)} %copy-done.11, bf16[64,8192]{1,0:T(8,128)(2,1)} %collective-permute-done.refs_1_, ...), custom_call_target="tpu_custom_call" | custom-call | flops 5368709120 | bytes 26476544 | tf_op jit(solution)/shard_map/project/pallas_call | solution.py:179
  85.4 8.3 %collective-permute-done.3 = bf16[64,8192]{1,0:T(8,128)(2,1)S(1)} collective-permute-done((bf16[64,8192]{1,0:T(8,128)(2,1)}, bf16[64,8192]{1,0:T(8,128)(2,1)S(1)}, u32[]{:S(2)}, u32[]{:S(2)}) %collective-permute-start.3) | collective-permute-done | bytes 1048608 | tf_op jit(solution)/shard_map/ppermute | solution.py:54
  94.9 1.6 collective-permute-start.12
  96.5 3.6 %collective-permute-start.11 = (bf16[2,32,16,256]{3,2,1,0:T(8,128)(2,1)S(1)}, bf16[2,32,16,256]{3,2,1,0:T(8,128)(2,1)S(1)}, u32[]{:S(2)}, u32[]{:S(2)}) collective-permute-start(bf16[2,32,16,256]{3,2,1,0:T(8,128)(2,1)S(1)} %get-tuple-element.77), channel_id=1, source_target_pairs={{0,12},{2,14},{4,8},{6,10},{8,4},{10,6},{12,0},{14,2},{1,13},{3,15... | collective-permute-start | bytes 1572872 | tf_op jit(solution)/shard_map/ppermute | solution.py:54
  111.2 1.9 collective-permute-done.11
  113.7 9.7 %collective-permute-start.14 = (bf16[2,32,16,256]{3,2,1,0:T(8,128)(2,1)}, bf16[2,32,16,256]{3,2,1,0:T(8,128)(2,1)S(1)}, u32[]{:S(2)}, u32[]{:S(2)}) collective-permute-start(bf16[2,32,16,256]{3,2,1,0:T(8,128)(2,1)} %copy-done.5), channel_id=1, source_target_pairs={{0,6},{2,4},{4,2},{6,0},{8,14},{10,12},{12,10},{14,8},{1,7},{3,5},... | collective-permute-start | bytes 1572872 | tf_op jit(solution)/shard_map/ppermute | solution.py:54
  126.0 15.6 %project.3 = (bf16[8,256,128]{2,1,0:T(8,128)(2,1)}, bf16[256,128]{1,0:T(8,128)(2,1)}, bf16[256,256]{1,0:T(8,128)(2,1)}, bf16[256,256]{1,0:T(8,128)(2,1)}) custom-call(s32[4]{0:T(128)} %add_multiply_fusion.1.starts_ref, bf16[64,8192]{1,0:T(8,128)(2,1)} %copy-done.12, bf16[64,8192]{1,0:T(8,128)(2,1)} %broadcast_select_fusion.1.refs_1_, ...), custom_call_target="tpu_custom_call" | custom-call | flops 5368709120 | bytes 26476544 | tf_op jit(solution)/shard_map/project/pallas_call | solution.py:179
  141.7 1.8 maximum_select_fusion
  143.5 21.7 %all-to-all-start = ((bf16[8,64,256]{2,1,0:T(8,128)(2,1)}), bf16[8,64,256]{2,1,0:T(8,128)(2,1)}, u32[]{:S(2)}, u32[]{:S(2)}) async-start(bf16[8,64,256]{2,1,0:T(8,128)(2,1)} %bitcast.126), calls=%async_computation | async-start | bytes 524288 | tf_op jit(solution)/shard_map/all_to_all | solution.py:535
  167.4 10.0 %all-to-all-done = bf16[8,64,256]{2,1,0:T(8,128)(2,1)} async-done(((bf16[8,64,256]{2,1,0:T(8,128)(2,1)}), bf16[8,64,256]{2,1,0:T(8,128)(2,1)}, u32[]{:S(2)}, u32[]{:S(2)}) %all-to-all-start) | async-done | bytes 262176 | tf_op jit(solution)/shard_map/all_to_all | solution.py:535
  177.5 3.5 %order_blocks.1 = (bf16[4096,128]{1,0:T(8,128)(2,1)S(1)}, bf16[4096,256]{1,0:T(8,128)(2,1)S(1)}) custom-call(s32[1]{0:T(128)} %dynamic_slice.118.length_ref, s32[256]{0:T(256)S(1)} %multiply_add_fusion.where_ref, bf16[64,16,256]{2,1,0:T(8,128)(2,1)S(1)} %bitcast.110, bf16[64,16,256]{2,1,0:T(8,128)(2,1)S(1)} %bitcast.114, bf16[64,16,256]{2,1,0:T(8,128)(2,1)S(1)} %bitcast.113, ...), custom_call_target="tpu_custom_call" | custom-call | tf_op jit(solution)/shard_map/order_blocks/pallas_call | solution.py:327
  181.1 24.1 %attend.1 = bf16[512,1024]{1,0:T(8,128)(2,1)S(1)} custom-call(s32[1]{0:T(128)} %bitcast.half_ref, bf16[8,256,128]{2,1,0:T(8,128)(2,1)S(1)} %copy-done.4, bf16[8,256,128]{2,1,0:T(8,128)(2,1)S(1)} %copy-done.6, bf16[4096,128]{1,0:T(8,128)(2,1)S(1)} %get-tuple-element.103.refs_2_, bf16[4096,256]{1,0:T(8,128)(2,1)S(1)} %get-tuple-element.104.refs_3_, ...), custom_call_target="tpu_custom_call" | custom-call | flops 19327352832 | bytes 5636096 | tf_op jit(solution)/shard_map/attend/pallas_call | solution.py:399
  205.2 8.1 %fusion.4 = bf16[512,4096]{1,0:T(8,128)(2,1)S(1)} fusion(bf16[512,1024]{1,0:T(8,128)(2,1)S(1)} %attend.1, bf16[1024,8192]{1,0:T(8,128)(2,1)} %param.39), kind=kOutput, calls=%fused_computation.4 | convolution fusion | flops 4297064448 | bytes 13631488 | tf_op jit(solution)/shard_map/dot_general | solution.py:546
  213.8 1.7 collective-permute-start.18
  215.5 8.1 %fusion.7 = bf16[512,4096]{1,0:T(8,128)(2,1)S(1)} fusion(bf16[512,1024]{1,0:T(8,128)(2,1)S(1)} %attend.1, bf16[1024,8192]{1,0:T(8,128)(2,1)} %param.39), kind=kOutput, calls=%fused_computation.5 | convolution fusion | flops 4297064448 | bytes 13631488 | tf_op jit(solution)/shard_map/dot_general | solution.py:546
  229.5 9.1 %collective-permute-done.21 = bf16[64,4096]{1,0:T(8,128)(2,1)S(1)} collective-permute-done((bf16[64,4096]{1,0:T(8,128)(2,1)S(1)}, bf16[64,4096]{1,0:T(8,128)(2,1)S(1)}, u32[]{:S(2)}, u32[]{:S(2)}) %collective-permute-start.21) | collective-permute-done | bytes 524320 | tf_op jit(solution)/shard_map/ppermute | solution.py:232
  242.0 8.9 %collective-permute-done.19 = bf16[64,4096]{1,0:T(8,128)(2,1)S(1)} collective-permute-done((bf16[64,4096]{1,0:T(8,128)(2,1)S(1)}, bf16[64,4096]{1,0:T(8,128)(2,1)S(1)}, u32[]{:S(2)}, u32[]{:S(2)}) %collective-permute-start.19) | collective-permute-done | bytes 524320 | tf_op jit(solution)/shard_map/ppermute | solution.py:232
  253.2 7.8 %collective-permute-done.24 = bf16[64,4096]{1,0:T(8,128)(2,1)S(1)} collective-permute-done((bf16[64,4096]{1,0:T(8,128)(2,1)S(1)}, bf16[64,4096]{1,0:T(8,128)(2,1)S(1)}, u32[]{:S(2)}, u32[]{:S(2)}) %collective-permute-start.24) | collective-permute-done | bytes 524320 | tf_op jit(solution)/shard_map/ppermute | solution.py:232
  264.5 8.9 %collective-permute-done.23 = bf16[64,4096]{1,0:T(8,128)(2,1)S(1)} collective-permute-done((bf16[64,4096]{1,0:T(8,128)(2,1)S(1)}, bf16[64,4096]{1,0:T(8,128)(2,1)S(1)}, u32[]{:S(2)}, u32[]{:S(2)}) %collective-permute-start.23) | collective-permute-done | bytes 524320 | tf_op jit(solution)/shard_map/ppermute | solution.py:232
  274.5 6.7 %collective-permute-done.29 = bf16[64,4096]{1,0:T(8,128)(2,1)S(1)} collective-permute-done((bf16[64,4096]{1,0:T(8,128)(2,1)S(1)}, bf16[64,4096]{1,0:T(8,128)(2,1)S(1)}, u32[]{:S(2)}, u32[]{:S(2)}) %collective-permute-start.29) | collective-permute-done | bytes 524320 | tf_op jit(solution)/shard_map/ppermute | solution.py:232
  281.3 11.0 %collective-permute-done.27 = bf16[64,4096]{1,0:T(8,128)(2,1)S(1)} collective-permute-done((bf16[64,4096]{1,0:T(8,128)(2,1)S(1)}, bf16[64,4096]{1,0:T(8,128)(2,1)S(1)}, u32[]{:S(2)}, u32[]{:S(2)}) %collective-permute-start.27) | collective-permute-done | bytes 524320 | tf_op jit(solution)/shard_map/ppermute | solution.py:232
  295.4 7.6 %collective-permute-done.30 = bf16[64,4096]{1,0:T(8,128)(2,1)S(1)} collective-permute-done((bf16[64,4096]{1,0:T(8,128)(2,1)S(1)}, bf16[64,4096]{1,0:T(8,128)(2,1)S(1)}, u32[]{:S(2)}, u32[]{:S(2)}) %collective-permute-start.30) | collective-permute-done | bytes 524320 | tf_op jit(solution)/shard_map/ppermute | solution.py:232
  (134 shorter events, 41.8 us)
Async XLA Ops:
  6.3 36.9 %collective-permute-start.2 = (bf16[32,16,2048]{2,1,0:T(8,128)(2,1)S(1)}, bf16[32,16,2048]{2,1,0:T(8,128)(2,1)}, u32[]{:S(2)}, u32[]{:S(2)}) collective-permute-start(bf16[32,16,2048]{2,1,0:T(8,128)(2,1)S(1)} %pick_blocks.1), channel_id=1, source_target_pairs={{0,1},{1,0},{2,3},{3,2},{4,5},{5,4},{6,7},{7,6},{8,9},{9,8},{10,11... | collective-permute-start | bytes 6291464 | tf_op jit(solution)/shard_map/ppermute | solution.py:474
  7.5 26.6 %collective-permute-start = (bf16[64,8192]{1,0:T(8,128)(2,1)S(1)}, bf16[64,8192]{1,0:T(8,128)(2,1)}, u32[]{:S(2)}, u32[]{:S(2)}) collective-permute-start(bf16[64,8192]{1,0:T(8,128)(2,1)S(1)} %fusion.12.refs_0_), channel_id=1, source_target_pairs={{0,4},{2,6},{4,0},{6,2},{8,12},{10,14},{12,8},{14,10},{1,5},{3,7},... | collective-permute-start | bytes 3145736 | tf_op jit(solution)/shard_map/ppermute | solution.py:54
  10.4 23.6 %collective-permute-start.4 = (bf16[64,8192]{1,0:T(8,128)(2,1)S(1)}, bf16[64,8192]{1,0:T(8,128)(2,1)}, u32[]{:S(2)}, u32[]{:S(2)}) collective-permute-start(bf16[64,8192]{1,0:T(8,128)(2,1)S(1)} %fusion.12.refs_0_), channel_id=1, source_target_pairs={{0,1},{1,0},{2,3},{3,2},{4,8},{5,9},{6,10},{7,11},{8,4},{9,5},{10,... | collective-permute-start | bytes 3145736 | tf_op jit(solution)/shard_map/ppermute | solution.py:65
  10.4 31.2 %collective-permute-start.6 = (bf16[64,8192]{1,0:T(8,128)(2,1)S(1)}, bf16[64,8192]{1,0:T(8,128)(2,1)}, u32[]{:S(2)}, u32[]{:S(2)}) collective-permute-start(bf16[64,8192]{1,0:T(8,128)(2,1)S(1)} %fusion.12.refs_0_), channel_id=1, source_target_pairs={{0,2},{2,0},{4,6},{6,4},{8,10},{10,8},{12,14},{14,12},{1,3},{3,1},... | collective-permute-start | bytes 3145736 | tf_op jit(solution)/shard_map/ppermute | solution.py:54
  34.1 15.2 %collective-permute-start.1 = (bf16[64,8192]{1,0:T(8,128)(2,1)}, bf16[64,8192]{1,0:T(8,128)(2,1)}, u32[]{:S(2)}, u32[]{:S(2)}) collective-permute-start(bf16[64,8192]{1,0:T(8,128)(2,1)} %collective-permute-done.refs_1_), channel_id=1, source_target_pairs={{0,1},{1,0},{2,3},{3,2},{4,8},{5,9},{6,10},{7,11},{8,4},{9,5},{10,... | collective-permute-start | bytes 3145736 | tf_op jit(solution)/shard_map/ppermute | solution.py:65
  34.1 26.5 %collective-permute-start.5 = (bf16[64,8192]{1,0:T(8,128)(2,1)}, bf16[64,8192]{1,0:T(8,128)(2,1)}, u32[]{:S(2)}, u32[]{:S(2)}) collective-permute-start(bf16[64,8192]{1,0:T(8,128)(2,1)} %collective-permute-done.4), channel_id=1, source_target_pairs={{0,4},{2,6},{4,0},{6,2},{8,12},{10,14},{12,8},{14,10},{1,5},{3,7},... | collective-permute-start | bytes 3145736 | tf_op jit(solution)/shard_map/ppermute | solution.py:54
  41.7 24.1 %collective-permute-start.7 = (bf16[64,8192]{1,0:T(8,128)(2,1)}, bf16[64,8192]{1,0:T(8,128)(2,1)S(1)}, u32[]{:S(2)}, u32[]{:S(2)}) collective-permute-start(bf16[64,8192]{1,0:T(8,128)(2,1)} %collective-permute-done.refs_1_), channel_id=1, source_target_pairs={{0,2},{2,0},{4,6},{6,4},{8,10},{10,8},{12,14},{14,12},{1,3},{3,1},... | collective-permute-start | bytes 3145736 | tf_op jit(solution)/shard_map/ppermute | solution.py:54
  49.2 44.5 %collective-permute-start.3 = (bf16[64,8192]{1,0:T(8,128)(2,1)}, bf16[64,8192]{1,0:T(8,128)(2,1)S(1)}, u32[]{:S(2)}, u32[]{:S(2)}) collective-permute-start(bf16[64,8192]{1,0:T(8,128)(2,1)} %collective-permute-done.1), channel_id=1, source_target_pairs={{0,4},{2,6},{4,0},{6,2},{8,12},{10,14},{12,8},{14,10},{1,5},{3,7},... | collective-permute-start | bytes 3145736 | tf_op jit(solution)/shard_map/ppermute | solution.py:54
  65.7 29.1 %collective-permute-start.9 = (bf16[64,8192]{1,0:T(8,128)(2,1)S(1)}, bf16[64,8192]{1,0:T(8,128)(2,1)S(1)}, u32[]{:S(2)}, u32[]{:S(2)}) collective-permute-start(bf16[64,8192]{1,0:T(8,128)(2,1)S(1)} %broadcast_select_fusion.refs_0_), channel_id=1, source_target_pairs={{0,2},{2,0},{4,6},{6,4},{8,10},{10,8},{12,14},{14,12},{1,3},{3,1},... | collective-permute-start | bytes 3145736 | tf_op jit(solution)/shard_map/ppermute | solution.py:54
  67.3 27.6 %collective-permute-start.8 = (bf16[2,32,16,256]{3,2,1,0:T(8,128)(2,1)S(1)}, bf16[2,32,16,256]{3,2,1,0:T(8,128)(2,1)S(1)}, u32[]{:S(2)}, u32[]{:S(2)}) collective-permute-start(bf16[2,32,16,256]{3,2,1,0:T(8,128)(2,1)S(1)} %get-tuple-element.71), channel_id=1, source_target_pairs={{0,8},{2,10},{4,12},{6,14},{8,0},{10,2},{12,4},{14,6},{1,9},{3,11}... | collective-permute-start | bytes 1572872 | tf_op jit(solution)/shard_map/ppermute | solution.py:54
  94.9 31.1 %collective-permute-start.12 = (bf16[64,8192]{1,0:T(8,128)(2,1)}, bf16[64,8192]{1,0:T(8,128)(2,1)}, u32[]{:S(2)}, u32[]{:S(2)}) collective-permute-start(bf16[64,8192]{1,0:T(8,128)(2,1)} %broadcast_select_fusion.1.refs_1_), channel_id=1, source_target_pairs={{0,2},{2,0},{4,6},{6,4},{8,10},{10,8},{12,14},{14,12},{1,3},{3,1},... | collective-permute-start | bytes 3145736 | tf_op jit(solution)/shard_map/ppermute | solution.py:54
  96.5 16.7 %collective-permute-start.11 = (bf16[2,32,16,256]{3,2,1,0:T(8,128)(2,1)S(1)}, bf16[2,32,16,256]{3,2,1,0:T(8,128)(2,1)S(1)}, u32[]{:S(2)}, u32[]{:S(2)}) collective-permute-start(bf16[2,32,16,256]{3,2,1,0:T(8,128)(2,1)S(1)} %get-tuple-element.77), channel_id=1, source_target_pairs={{0,12},{2,14},{4,8},{6,10},{8,4},{10,6},{12,0},{14,2},{1,13},{3,15... | collective-permute-start | bytes 1572872 | tf_op jit(solution)/shard_map/ppermute | solution.py:54
  100.0 24.5 %collective-permute-start.10 = (bf16[2,32,16,256]{3,2,1,0:T(8,128)(2,1)}, bf16[2,32,16,256]{3,2,1,0:T(8,128)(2,1)S(1)}, u32[]{:S(2)}, u32[]{:S(2)}) collective-permute-start(bf16[2,32,16,256]{3,2,1,0:T(8,128)(2,1)} %get-tuple-element.75), channel_id=1, source_target_pairs={{0,4},{2,6},{4,0},{6,2},{8,12},{10,14},{12,8},{14,10},{1,5},{3,7},... | collective-permute-start | bytes 1572872 | tf_op jit(solution)/shard_map/ppermute | solution.py:54
  113.2 54.2 %collective-permute-start.13 = (bf16[2,32,16,256]{3,2,1,0:T(8,128)(2,1)}, bf16[2,32,16,256]{3,2,1,0:T(8,128)(2,1)S(1)}, u32[]{:S(2)}, u32[]{:S(2)}) collective-permute-start(bf16[2,32,16,256]{3,2,1,0:T(8,128)(2,1)} %get-tuple-element.84), channel_id=1, source_target_pairs={{0,2},{2,0},{4,6},{6,4},{8,10},{10,8},{12,14},{14,12},{1,3},{3,1},... | collective-permute-start | bytes 1572872 | tf_op jit(solution)/shard_map/ppermute | solution.py:54
  113.7 53.7 %collective-permute-start.14 = (bf16[2,32,16,256]{3,2,1,0:T(8,128)(2,1)}, bf16[2,32,16,256]{3,2,1,0:T(8,128)(2,1)S(1)}, u32[]{:S(2)}, u32[]{:S(2)}) collective-permute-start(bf16[2,32,16,256]{3,2,1,0:T(8,128)(2,1)} %copy-done.5), channel_id=1, source_target_pairs={{0,6},{2,4},{4,2},{6,0},{8,14},{10,12},{12,10},{14,8},{1,7},{3,5},... | collective-permute-start | bytes 1572872 | tf_op jit(solution)/shard_map/ppermute | solution.py:54
  123.4 44.0 %collective-permute-start.15 = (bf16[2,32,16,256]{3,2,1,0:T(8,128)(2,1)}, bf16[2,32,16,256]{3,2,1,0:T(8,128)(2,1)}, u32[]{:S(2)}, u32[]{:S(2)}) collective-permute-start(bf16[2,32,16,256]{3,2,1,0:T(8,128)(2,1)} %copy-done.3), channel_id=1, source_target_pairs={{0,10},{2,8},{4,14},{6,12},{8,2},{10,0},{12,6},{14,4},{1,11},{3,9}... | collective-permute-start | bytes 1572872 | tf_op jit(solution)/shard_map/ppermute | solution.py:54
  124.6 42.8 %collective-permute-start.16 = (bf16[2,32,16,256]{3,2,1,0:T(8,128)(2,1)}, bf16[2,32,16,256]{3,2,1,0:T(8,128)(2,1)}, u32[]{:S(2)}, u32[]{:S(2)}) collective-permute-start(bf16[2,32,16,256]{3,2,1,0:T(8,128)(2,1)} %copy-done.2), channel_id=1, source_target_pairs={{0,14},{2,12},{4,10},{6,8},{8,6},{10,4},{12,2},{14,0},{1,15},{3,13... | collective-permute-start | bytes 1572872 | tf_op jit(solution)/shard_map/ppermute | solution.py:54
  143.5 33.9 %all-to-all-start = ((bf16[8,64,256]{2,1,0:T(8,128)(2,1)}), bf16[8,64,256]{2,1,0:T(8,128)(2,1)}, u32[]{:S(2)}, u32[]{:S(2)}) async-start(bf16[8,64,256]{2,1,0:T(8,128)(2,1)} %bitcast.126), calls=%async_computation | async-start | bytes 524288 | tf_op jit(solution)/shard_map/all_to_all | solution.py:535
  213.4 12.5 %collective-permute-start.17 = (bf16[64,4096]{1,0:T(8,128)(2,1)S(1)}, bf16[64,4096]{1,0:T(8,128)(2,1)S(1)}, u32[]{:S(2)}, u32[]{:S(2)}) collective-permute-start(bf16[64,4096]{1,0:T(8,128)(2,1)S(1)} %get-tuple-element.109), channel_id=1, source_target_pairs={{0,4},{4,8},{8,12},{12,14},{14,10},{10,6},{6,2},{2,0},{1,5},{5,9},... | collective-permute-start | bytes 1572872 | tf_op jit(solution)/shard_map/ppermute | solution.py:232
  213.8 12.8 %collective-permute-start.18 = (bf16[64,4096]{1,0:T(8,128)(2,1)S(1)}, bf16[64,4096]{1,0:T(8,128)(2,1)S(1)}, u32[]{:S(2)}, u32[]{:S(2)}) collective-permute-start(bf16[64,4096]{1,0:T(8,128)(2,1)S(1)} %get-tuple-element.110), channel_id=1, source_target_pairs={{0,2},{4,0},{8,4},{12,8},{14,12},{10,14},{6,10},{2,6},{1,3},{5,1},... | collective-permute-start | bytes 1572872 | tf_op jit(solution)/shard_map/ppermute | solution.py:232
  223.6 14.9 %collective-permute-start.21 = (bf16[64,4096]{1,0:T(8,128)(2,1)S(1)}, bf16[64,4096]{1,0:T(8,128)(2,1)S(1)}, u32[]{:S(2)}, u32[]{:S(2)}) collective-permute-start(bf16[64,4096]{1,0:T(8,128)(2,1)S(1)} %get-tuple-element.111), channel_id=1, source_target_pairs={{0,2},{4,0},{8,4},{12,8},{14,12},{10,14},{6,10},{2,6},{1,3},{5,1},... | collective-permute-start | bytes 1572872 | tf_op jit(solution)/shard_map/ppermute | solution.py:232
  224.8 14.9 %collective-permute-start.22 = (bf16[64,4096]{1,0:T(8,128)(2,1)S(1)}, bf16[64,4096]{1,0:T(8,128)(2,1)S(1)}, u32[]{:S(2)}, u32[]{:S(2)}) collective-permute-start(bf16[64,4096]{1,0:T(8,128)(2,1)S(1)} %get-tuple-element.112), channel_id=1, source_target_pairs={{0,4},{4,8},{8,12},{12,14},{14,10},{10,6},{6,2},{2,0},{1,5},{5,9},... | collective-permute-start | bytes 1572872 | tf_op jit(solution)/shard_map/ppermute | solution.py:232
  226.9 24.0 %collective-permute-start.19 = (bf16[64,4096]{1,0:T(8,128)(2,1)S(1)}, bf16[64,4096]{1,0:T(8,128)(2,1)S(1)}, u32[]{:S(2)}, u32[]{:S(2)}) collective-permute-start(bf16[64,4096]{1,0:T(8,128)(2,1)S(1)} %get-tuple-element.113), channel_id=1, source_target_pairs={{0,4},{4,8},{8,12},{12,14},{14,10},{10,6},{6,2},{2,0},{1,5},{5,9},... | collective-permute-start | bytes 1572872 | tf_op jit(solution)/shard_map/ppermute | solution.py:232
  228.2 22.7 %collective-permute-start.20 = (bf16[64,4096]{1,0:T(8,128)(2,1)S(1)}, bf16[64,4096]{1,0:T(8,128)(2,1)S(1)}, u32[]{:S(2)}, u32[]{:S(2)}) collective-permute-start(bf16[64,4096]{1,0:T(8,128)(2,1)S(1)} %get-tuple-element.114), channel_id=1, source_target_pairs={{0,2},{4,0},{8,4},{12,8},{14,12},{10,14},{6,10},{2,6},{1,3},{5,1},... | collective-permute-start | bytes 1572872 | tf_op jit(solution)/shard_map/ppermute | solution.py:232
  239.9 21.1 %collective-permute-start.24 = (bf16[64,4096]{1,0:T(8,128)(2,1)S(1)}, bf16[64,4096]{1,0:T(8,128)(2,1)S(1)}, u32[]{:S(2)}, u32[]{:S(2)}) collective-permute-start(bf16[64,4096]{1,0:T(8,128)(2,1)S(1)} %get-tuple-element.115), channel_id=1, source_target_pairs={{0,2},{4,0},{8,4},{12,8},{14,12},{10,14},{6,10},{2,6},{1,3},{5,1},... | collective-permute-start | bytes 1572872 | tf_op jit(solution)/shard_map/ppermute | solution.py:232
  240.6 21.5 %collective-permute-start.25 = (bf16[64,4096]{1,0:T(8,128)(2,1)S(1)}, bf16[64,4096]{1,0:T(8,128)(2,1)S(1)}, u32[]{:S(2)}, u32[]{:S(2)}) collective-permute-start(bf16[64,4096]{1,0:T(8,128)(2,1)S(1)} %get-tuple-element.116), channel_id=1, source_target_pairs={{0,4},{4,8},{8,12},{12,14},{14,10},{10,6},{6,2},{2,0},{1,5},{5,9},... | collective-permute-start | bytes 1572872 | tf_op jit(solution)/shard_map/ppermute | solution.py:232
  251.2 22.2 %collective-permute-start.23 = (bf16[64,4096]{1,0:T(8,128)(2,1)S(1)}, bf16[64,4096]{1,0:T(8,128)(2,1)S(1)}, u32[]{:S(2)}, u32[]{:S(2)}) collective-permute-start(bf16[64,4096]{1,0:T(8,128)(2,1)S(1)} %get-tuple-element.117), channel_id=1, source_target_pairs={{0,4},{4,8},{8,12},{12,14},{14,10},{10,6},{6,2},{2,0},{1,5},{5,9},... | collective-permute-start | bytes 1572872 | tf_op jit(solution)/shard_map/ppermute | solution.py:232
  252.1 21.4 %collective-permute-start.26 = (bf16[64,4096]{1,0:T(8,128)(2,1)S(1)}, bf16[64,4096]{1,0:T(8,128)(2,1)S(1)}, u32[]{:S(2)}, u32[]{:S(2)}) collective-permute-start(bf16[64,4096]{1,0:T(8,128)(2,1)S(1)} %get-tuple-element.118), channel_id=1, source_target_pairs={{0,2},{4,0},{8,4},{12,8},{14,12},{10,14},{6,10},{2,6},{1,3},{5,1},... | collective-permute-start | bytes 1572872 | tf_op jit(solution)/shard_map/ppermute | solution.py:232
  262.4 18.7 %collective-permute-start.29 = (bf16[64,4096]{1,0:T(8,128)(2,1)S(1)}, bf16[64,4096]{1,0:T(8,128)(2,1)S(1)}, u32[]{:S(2)}, u32[]{:S(2)}) collective-permute-start(bf16[64,4096]{1,0:T(8,128)(2,1)S(1)} %get-tuple-element.119), channel_id=1, source_target_pairs={{0,2},{4,0},{8,4},{12,8},{14,12},{10,14},{6,10},{2,6},{1,3},{5,1},... | collective-permute-start | bytes 1572872 | tf_op jit(solution)/shard_map/ppermute | solution.py:232
  263.1 29.4 %collective-permute-start.28 = (bf16[64,4096]{1,0:T(8,128)(2,1)S(1)}, bf16[64,4096]{1,0:T(8,128)(2,1)S(1)}, u32[]{:S(2)}, u32[]{:S(2)}) collective-permute-start(bf16[64,4096]{1,0:T(8,128)(2,1)S(1)} %get-tuple-element.120), channel_id=1, source_target_pairs={{0,4},{4,8},{8,12},{12,14},{14,10},{10,6},{6,2},{2,0},{1,5},{5,9},... | collective-permute-start | bytes 1572872 | tf_op jit(solution)/shard_map/ppermute | solution.py:232
  273.5 18.8 %collective-permute-start.27 = (bf16[64,4096]{1,0:T(8,128)(2,1)S(1)}, bf16[64,4096]{1,0:T(8,128)(2,1)S(1)}, u32[]{:S(2)}, u32[]{:S(2)}) collective-permute-start(bf16[64,4096]{1,0:T(8,128)(2,1)S(1)} %fusion.24), channel_id=1, source_target_pairs={{0,4},{4,8},{8,12},{12,14},{14,10},{10,6},{6,2},{2,0},{1,5},{5,9},... | collective-permute-start | bytes 1572872 | tf_op jit(solution)/shard_map/ppermute | solution.py:232
  292.5 10.5 %collective-permute-start.30 = (bf16[64,4096]{1,0:T(8,128)(2,1)S(1)}, bf16[64,4096]{1,0:T(8,128)(2,1)S(1)}, u32[]{:S(2)}, u32[]{:S(2)}) collective-permute-start(bf16[64,4096]{1,0:T(8,128)(2,1)S(1)} %fusion.13), channel_id=1, source_target_pairs={{0,2},{4,0},{8,4},{12,8},{14,12},{10,14},{6,10},{2,6},{1,3},{5,1},... | collective-permute-start | bytes 1572872 | tf_op jit(solution)/shard_map/ppermute | solution.py:232
  (24 other events, 545.6 us)

commit v14 on v13

--- a/solution.py
+++ b/solution.py
@@ -14,7 +14,7 @@
 EPSILON = 1e-06
 SCORE_SCALE = HD ** (-0.5) * math.log2(math.e)
 VMEM_LIMIT = 56 * 1024 * 1024
-ATTEND_VMEM = 28 * 1024 * 1024
+ATTEND_VMEM = 20 * 1024 * 1024
 COLUMN_CHUNKS = 2
 STREAMS = 4
 LINE_MODELS = 8
@@ -86,16 +86,15 @@
     over_beside_passed = swap(after(over_beside, outgoing[4]), 2)
     exchange(4, over_beside)
     exchange(6, over_beside)
+    exchange(1, far_first_y)
+    exchange(3, far_first_y)
     near = project_near([after(own, far_first), beside, own_y, beside_y])
     far_second = jnp.where(middle, over_beside, over_beside_passed)
-    far_second, near, _ = lax.optimization_barrier((far_second, near, arrived[4]))
+    first_sent = [arrived[apart] for apart in (4, 6, 1, 3)]
+    far_second, near, _ = lax.optimization_barrier((far_second, near, first_sent))
     far_second_y = swap(after(far_second, far_first_y), 1)
-    exchange(2, arrived[4], far_first_y)
-    exchange(5, arrived[6], far_first_y)
-    exchange(7, arrived[6], far_first_y)
-    exchange(3, arrived[6], far_first_y)
-    exchange(1, arrived[6], far_first_y)
-    far_first = after(far_first, arrived[2], arrived[6])
+    for apart in (5, 7, 2):
+        exchange(apart, arrived[4], arrived[6])
     far = [far_first, far_second, far_first_y, far_second_y]
     return near, far, [arrived[apart] for apart in range(LINE_MODELS)]
 

time: 306 us -> 327 us (1.069)
  waiting for transfers between devices: 109 us -> 141 us
  starting transfers between devices: 79.5 us -> 62.6 us
  other arithmetic: 14.9 us -> 20.5 us
    ppermute x14, waiting for transfers between devices: 36.2 us -> 69.3 us  [swap(): lax.ppermute(block, 'mp', [(index, index ^ mask) for index in range(LINE_...]
    all_to_all x1, starting transfers between devices: 21.7 us -> 4.23 us  [on_device(): pairs = lax.all_to_all(pairs, 'mp', split_axis=0, concat_axis=0, tiled=True)]
  transfers between devices with their start and end apart: 32 -> 32, of which waited for: 16 -> 16; matrix products, arithmetic and copies ran while one was open for 8% -> 8% of each run, Pallas kernels for 12% -> 11%
where the time goes in v14:
time: 327 us; the launch traced here: 326 us
  waiting for transfers between devices  141 us (43%)
  Pallas kernels  62.7 us (19%)
  starting transfers between devices  62.6 us (19%)
  other arithmetic  20.5 us (6%)
  matrix products  16.2 us (5%)
  between operations  13.5 us (4%)
  local copies, waits for them, and re-layouts  9.56 us (3%)
    ppermute x14, waiting for transfers between devices, swap(): lax.ppermute(block, 'mp', [(index, index ^ mask) for index in range(LINE_...  69.3 us
    ppermute x14, waiting for transfers between devices, step(): self.moving[way] = lax.ppermute(block, 'mp', pairs)  61.9 us
    ppermute x14, starting transfers between devices, swap(): lax.ppermute(block, 'mp', [(index, index ^ mask) for index in range(LINE_...  42.7 us
    pallas_call x2, Pallas kernels, project(): pl.pallas_call(project_kernel, grid=(width // depth,), out_shape=out_shap...  31.4 us
    pallas_call x1, Pallas kernels, attend(): pl.pallas_call(functools.partial(attend_kernel, span), grid=(heads,), out...  24.1 us
    dot_general x2, matrix products, on_device(): jnp.dot(mixed, w_out[:, chunk * width:(chunk + 1) * width], preferred_ele...  16.2 us
    ppermute x14, starting transfers between devices, step(): self.moving[way] = lax.ppermute(block, 'mp', pairs)  15 us
    all_to_all x1, waiting for transfers between devices, on_device(): pairs = lax.all_to_all(pairs, 'mp', split_axis=0, concat_axis=0, tiled=True)  9.51 us
  transfers between devices with their start and end apart: 32, of which 16 were waited for; matrix products, arithmetic and copies ran while one was open for 8% of the time, Pallas kernels for 11%

profile of v14, /device:TPU:0, one launch (start us, length us, event | category | flops | bytes accessed | tf_op | source)
XLA Modules:
  0.0 325.7 jit_solution(3380630724210634511)
XLA Ops:
  2.9 2.5 fusion.12.refs_0_
  5.9 2.5 collective-permute-start.6
  8.4 3.1 collective-permute-start
  11.6 22.1 %collective-permute-start.5 = (bf16[64,8192]{1,0:T(8,128)(2,1)}, bf16[64,8192]{1,0:T(8,128)(2,1)}, u32[]{:S(2)}, u32[]{:S(2)}) collective-permute-start(bf16[64,8192]{1,0:T(8,128)(2,1)} %collective-permute-done.4), channel_id=1, source_target_pairs={{0,4},{2,6},{4,0},{6,2},{8,12},{10,14},{12,8},{14,10},{1,5},{3,7},... | collective-permute-start | bytes 3145736 | tf_op jit(solution)/shard_map/ppermute | solution.py:54
  36.3 2.2 copy-done
  42.5 14.5 %collective-permute-done.5 = bf16[64,8192]{1,0:T(8,128)(2,1)} collective-permute-done((bf16[64,8192]{1,0:T(8,128)(2,1)}, bf16[64,8192]{1,0:T(8,128)(2,1)}, u32[]{:S(2)}, u32[]{:S(2)}) %collective-permute-start.5) | collective-permute-done | bytes 1048608 | tf_op jit(solution)/shard_map/ppermute | solution.py:54
  58.3 8.2 %collective-permute-done.7.refs_3_ = bf16[64,8192]{1,0:T(8,128)(2,1)S(1)} collective-permute-done((bf16[64,8192]{1,0:T(8,128)(2,1)}, bf16[64,8192]{1,0:T(8,128)(2,1)S(1)}, u32[]{:S(2)}, u32[]{:S(2)}) %collective-permute-start.7) | collective-permute-done | bytes 1048608 | tf_op jit(solution)/shard_map/ppermute | solution.py:54
  68.1 2.2 copy-done.1
  70.3 2.8 pack_blocks.1
  76.6 2.9 collective-permute-start.8
  80.8 15.7 %project.2 = (bf16[8,256,128]{2,1,0:T(8,128)(2,1)}, bf16[256,128]{1,0:T(8,128)(2,1)}, bf16[256,256]{1,0:T(8,128)(2,1)}, bf16[256,256]{1,0:T(8,128)(2,1)}) custom-call(s32[4]{0:T(128)} %add_multiply_fusion.starts_ref, bf16[64,8192]{1,0:T(8,128)(2,1)} %fusion.12.refs_0_, bf16[64,8192]{1,0:T(8,128)(2,1)} %collective-permute-done.refs_1_, ...), custom_call_target="tpu_custom_call" | custom-call | flops 5368709120 | bytes 26476544 | tf_op jit(solution)/shard_map/project/pallas_call | solution.py:178
  97.4 24.2 %collective-permute-done.3 = bf16[64,8192]{1,0:T(8,128)(2,1)} collective-permute-done((bf16[64,8192]{1,0:T(8,128)(2,1)}, bf16[64,8192]{1,0:T(8,128)(2,1)}, u32[]{:S(2)}, u32[]{:S(2)}) %collective-permute-start.3) | collective-permute-done | bytes 1048608 | tf_op jit(solution)/shard_map/ppermute | solution.py:54
  121.5 2.3 broadcast_select_fusion.1.refs_1_
  123.8 7.8 %collective-permute-done.12 = bf16[2,32,16,256]{3,2,1,0:T(8,128)(2,1)S(1)} collective-permute-done((bf16[2,32,16,256]{3,2,1,0:T(8,128)(2,1)S(1)}, bf16[2,32,16,256]{3,2,1,0:T(8,128)(2,1)S(1)}, u32[]{:S(2)}, u32[]{:S(2)}) %collective-permute-start.12) | collective-permute-done | bytes 524320 | tf_op jit(solution)/shard_map/ppermute | solution.py:54
  145.5 2.7 collective-permute-start.15
  148.3 2.2 collective-permute-start.16
  150.4 14.6 %collective-permute-done.13.refs_3_ = bf16[64,8192]{1,0:T(8,128)(2,1)} collective-permute-done((bf16[64,8192]{1,0:T(8,128)(2,1)}, bf16[64,8192]{1,0:T(8,128)(2,1)}, u32[]{:S(2)}, u32[]{:S(2)}) %collective-permute-start.13) | collective-permute-done | bytes 1048608 | tf_op jit(solution)/shard_map/ppermute | solution.py:54
  165.1 15.7 %project.3 = (bf16[8,256,128]{2,1,0:T(8,128)(2,1)}, bf16[256,128]{1,0:T(8,128)(2,1)}, bf16[256,256]{1,0:T(8,128)(2,1)}, bf16[256,256]{1,0:T(8,128)(2,1)}) custom-call(s32[4]{0:T(128)} %add_multiply_fusion.1.starts_ref, bf16[64,8192]{1,0:T(8,128)(2,1)} %copy-done.11, bf16[64,8192]{1,0:T(8,128)(2,1)} %broadcast_select_fusion.1.refs_1_, ...), custom_call_target="tpu_custom_call" | custom-call | flops 5368709120 | bytes 26476544 | tf_op jit(solution)/shard_map/project/pallas_call | solution.py:178
  182.7 4.2 %all-to-all-start = ((bf16[8,64,256]{2,1,0:T(8,128)(2,1)}), bf16[8,64,256]{2,1,0:T(8,128)(2,1)}, u32[]{:S(2)}, u32[]{:S(2)}) async-start(bf16[8,64,256]{2,1,0:T(8,128)(2,1)} %bitcast.126), calls=%async_computation | async-start | bytes 524288 | tf_op jit(solution)/shard_map/all_to_all | solution.py:534
  189.3 9.5 %all-to-all-done = bf16[8,64,256]{2,1,0:T(8,128)(2,1)} async-done(((bf16[8,64,256]{2,1,0:T(8,128)(2,1)}), bf16[8,64,256]{2,1,0:T(8,128)(2,1)}, u32[]{:S(2)}, u32[]{:S(2)}) %all-to-all-start) | async-done | bytes 262176 | tf_op jit(solution)/shard_map/all_to_all | solution.py:534
  198.8 3.6 %order_blocks.1 = (bf16[4096,128]{1,0:T(8,128)(2,1)S(1)}, bf16[4096,256]{1,0:T(8,128)(2,1)S(1)}) custom-call(s32[1]{0:T(128)} %dynamic_slice.118.length_ref, s32[256]{0:T(256)S(1)} %multiply_add_fusion.where_ref, bf16[64,16,256]{2,1,0:T(8,128)(2,1)S(1)} %bitcast.110, bf16[64,16,256]{2,1,0:T(8,128)(2,1)S(1)} %bitcast.114, bf16[64,16,256]{2,1,0:T(8,128)(2,1)S(1)} %bitcast.115, ...), custom_call_target="tpu_custom_call" | custom-call | tf_op jit(solution)/shard_map/order_blocks/pallas_call | solution.py:326
  202.5 24.1 %attend.1 = bf16[512,1024]{1,0:T(8,128)(2,1)S(1)} custom-call(s32[1]{0:T(128)} %bitcast.half_ref, bf16[8,256,128]{2,1,0:T(8,128)(2,1)S(1)} %copy-done.5, bf16[8,256,128]{2,1,0:T(8,128)(2,1)S(1)} %copy-done.6, bf16[4096,128]{1,0:T(8,128)(2,1)S(1)} %get-tuple-element.101.refs_2_, bf16[4096,256]{1,0:T(8,128)(2,1)S(1)} %get-tuple-element.102.refs_3_, ...), custom_call_target="tpu_custom_call" | custom-call | flops 19327352832 | bytes 5636096 | tf_op jit(solution)/shard_map/attend/pallas_call | solution.py:398
  226.6 8.1 %fusion.4 = bf16[512,4096]{1,0:T(8,128)(2,1)S(1)} fusion(bf16[512,1024]{1,0:T(8,128)(2,1)S(1)} %attend.1, bf16[1024,8192]{1,0:T(8,128)(2,1)} %param.39), kind=kOutput, calls=%fused_computation.4 | convolution fusion | flops 4297064448 | bytes 13631488 | tf_op jit(solution)/shard_map/dot_general | solution.py:545
  236.9 8.1 %fusion.7 = bf16[512,4096]{1,0:T(8,128)(2,1)S(1)} fusion(bf16[512,1024]{1,0:T(8,128)(2,1)S(1)} %attend.1, bf16[1024,8192]{1,0:T(8,128)(2,1)} %param.39), kind=kOutput, calls=%fused_computation.5 | convolution fusion | flops 4297064448 | bytes 13631488 | tf_op jit(solution)/shard_map/dot_general | solution.py:545
  247.8 2.9 collective-permute-start.19
  250.7 9.3 %collective-permute-done.21 = bf16[64,4096]{1,0:T(8,128)(2,1)S(1)} collective-permute-done((bf16[64,4096]{1,0:T(8,128)(2,1)S(1)}, bf16[64,4096]{1,0:T(8,128)(2,1)S(1)}, u32[]{:S(2)}, u32[]{:S(2)}) %collective-permute-start.21) | collective-permute-done | bytes 524320 | tf_op jit(solution)/shard_map/ppermute | solution.py:231
  263.4 8.9 %collective-permute-done.19 = bf16[64,4096]{1,0:T(8,128)(2,1)S(1)} collective-permute-done((bf16[64,4096]{1,0:T(8,128)(2,1)S(1)}, bf16[64,4096]{1,0:T(8,128)(2,1)S(1)}, u32[]{:S(2)}, u32[]{:S(2)}) %collective-permute-start.19) | collective-permute-done | bytes 524320 | tf_op jit(solution)/shard_map/ppermute | solution.py:231
  274.6 7.8 %collective-permute-done.24 = bf16[64,4096]{1,0:T(8,128)(2,1)S(1)} collective-permute-done((bf16[64,4096]{1,0:T(8,128)(2,1)S(1)}, bf16[64,4096]{1,0:T(8,128)(2,1)S(1)}, u32[]{:S(2)}, u32[]{:S(2)}) %collective-permute-start.24) | collective-permute-done | bytes 524320 | tf_op jit(solution)/shard_map/ppermute | solution.py:231
  285.9 8.9 %collective-permute-done.23 = bf16[64,4096]{1,0:T(8,128)(2,1)S(1)} collective-permute-done((bf16[64,4096]{1,0:T(8,128)(2,1)S(1)}, bf16[64,4096]{1,0:T(8,128)(2,1)S(1)}, u32[]{:S(2)}, u32[]{:S(2)}) %collective-permute-start.23) | collective-permute-done | bytes 524320 | tf_op jit(solution)/shard_map/ppermute | solution.py:231
  295.9 6.2 %collective-permute-done.29 = bf16[64,4096]{1,0:T(8,128)(2,1)S(1)} collective-permute-done((bf16[64,4096]{1,0:T(8,128)(2,1)S(1)}, bf16[64,4096]{1,0:T(8,128)(2,1)S(1)}, u32[]{:S(2)}, u32[]{:S(2)}) %collective-permute-start.29) | collective-permute-done | bytes 524320 | tf_op jit(solution)/shard_map/ppermute | solution.py:231
  302.2 11.0 %collective-permute-done.27 = bf16[64,4096]{1,0:T(8,128)(2,1)S(1)} collective-permute-done((bf16[64,4096]{1,0:T(8,128)(2,1)S(1)}, bf16[64,4096]{1,0:T(8,128)(2,1)S(1)}, u32[]{:S(2)}, u32[]{:S(2)}) %collective-permute-start.27) | collective-permute-done | bytes 524320 | tf_op jit(solution)/shard_map/ppermute | solution.py:231
  316.4 7.1 %collective-permute-done.30 = bf16[64,4096]{1,0:T(8,128)(2,1)S(1)} collective-permute-done((bf16[64,4096]{1,0:T(8,128)(2,1)S(1)}, bf16[64,4096]{1,0:T(8,128)(2,1)S(1)}, u32[]{:S(2)}, u32[]{:S(2)}) %collective-permute-start.30) | collective-permute-done | bytes 524320 | tf_op jit(solution)/shard_map/ppermute | solution.py:231
  (128 shorter events, 44.3 us)
Async XLA Ops:
  5.4 6.1 %collective-permute-start.4 = (bf16[64,8192]{1,0:T(8,128)(2,1)}, bf16[64,8192]{1,0:T(8,128)(2,1)}, u32[]{:S(2)}, u32[]{:S(2)}) collective-permute-start(bf16[64,8192]{1,0:T(8,128)(2,1)} %fusion.12.refs_0_), channel_id=1, source_target_pairs={{0,1},{1,0},{2,3},{3,2},{4,8},{5,9},{6,10},{7,11},{8,4},{9,5},{10,... | collective-permute-start | bytes 3145736 | tf_op jit(solution)/shard_map/ppermute | solution.py:65
  5.9 34.9 %collective-permute-start.6 = (bf16[64,8192]{1,0:T(8,128)(2,1)}, bf16[64,8192]{1,0:T(8,128)(2,1)}, u32[]{:S(2)}, u32[]{:S(2)}) collective-permute-start(bf16[64,8192]{1,0:T(8,128)(2,1)} %fusion.12.refs_0_), channel_id=1, source_target_pairs={{0,2},{2,0},{4,6},{6,4},{8,10},{10,8},{12,14},{14,12},{1,3},{3,1},... | collective-permute-start | bytes 3145736 | tf_op jit(solution)/shard_map/ppermute | solution.py:54
  8.4 32.4 %collective-permute-start = (bf16[64,8192]{1,0:T(8,128)(2,1)}, bf16[64,8192]{1,0:T(8,128)(2,1)}, u32[]{:S(2)}, u32[]{:S(2)}) collective-permute-start(bf16[64,8192]{1,0:T(8,128)(2,1)} %fusion.12.refs_0_), channel_id=1, source_target_pairs={{0,4},{2,6},{4,0},{6,2},{8,12},{10,14},{12,8},{14,10},{1,5},{3,7},... | collective-permute-start | bytes 3145736 | tf_op jit(solution)/shard_map/ppermute | solution.py:54
  11.6 45.4 %collective-permute-start.5 = (bf16[64,8192]{1,0:T(8,128)(2,1)}, bf16[64,8192]{1,0:T(8,128)(2,1)}, u32[]{:S(2)}, u32[]{:S(2)}) collective-permute-start(bf16[64,8192]{1,0:T(8,128)(2,1)} %collective-permute-done.4), channel_id=1, source_target_pairs={{0,4},{2,6},{4,0},{6,2},{8,12},{10,14},{12,8},{14,10},{1,5},{3,7},... | collective-permute-start | bytes 3145736 | tf_op jit(solution)/shard_map/ppermute | solution.py:54
  39.3 28.8 %collective-permute-start.2 = (bf16[32,16,2048]{2,1,0:T(8,128)(2,1)S(1)}, bf16[32,16,2048]{2,1,0:T(8,128)(2,1)}, u32[]{:S(2)}, u32[]{:S(2)}) collective-permute-start(bf16[32,16,2048]{2,1,0:T(8,128)(2,1)S(1)} %pick_blocks.1), channel_id=1, source_target_pairs={{0,1},{1,0},{2,3},{3,2},{4,5},{5,4},{6,7},{7,6},{8,9},{9,8},{10,11... | collective-permute-start | bytes 6291464 | tf_op jit(solution)/shard_map/ppermute | solution.py:473
  40.8 25.8 %collective-permute-start.7 = (bf16[64,8192]{1,0:T(8,128)(2,1)}, bf16[64,8192]{1,0:T(8,128)(2,1)S(1)}, u32[]{:S(2)}, u32[]{:S(2)}) collective-permute-start(bf16[64,8192]{1,0:T(8,128)(2,1)} %collective-permute-done.refs_1_), channel_id=1, source_target_pairs={{0,2},{2,0},{4,6},{6,4},{8,10},{10,8},{12,14},{14,12},{1,3},{3,1},... | collective-permute-start | bytes 3145736 | tf_op jit(solution)/shard_map/ppermute | solution.py:54
  42.4 30.8 %collective-permute-start.1 = (bf16[64,8192]{1,0:T(8,128)(2,1)}, bf16[64,8192]{1,0:T(8,128)(2,1)}, u32[]{:S(2)}, u32[]{:S(2)}) collective-permute-start(bf16[64,8192]{1,0:T(8,128)(2,1)} %collective-permute-done.refs_1_), channel_id=1, source_target_pairs={{0,1},{1,0},{2,3},{3,2},{4,8},{5,9},{6,10},{7,11},{8,4},{9,5},{10,... | collective-permute-start | bytes 3145736 | tf_op jit(solution)/shard_map/ppermute | solution.py:65
  66.5 30.0 %collective-permute-start.10 = (bf16[64,8192]{1,0:T(8,128)(2,1)S(1)}, bf16[64,8192]{1,0:T(8,128)(2,1)S(1)}, u32[]{:S(2)}, u32[]{:S(2)}) collective-permute-start(bf16[64,8192]{1,0:T(8,128)(2,1)S(1)} %broadcast_select_fusion.refs_0_), channel_id=1, source_target_pairs={{0,2},{2,0},{4,6},{6,4},{8,10},{10,8},{12,14},{14,12},{1,3},{3,1},... | collective-permute-start | bytes 3145736 | tf_op jit(solution)/shard_map/ppermute | solution.py:54
  73.1 48.4 %collective-permute-start.3 = (bf16[64,8192]{1,0:T(8,128)(2,1)}, bf16[64,8192]{1,0:T(8,128)(2,1)}, u32[]{:S(2)}, u32[]{:S(2)}) collective-permute-start(bf16[64,8192]{1,0:T(8,128)(2,1)} %collective-permute-done.1), channel_id=1, source_target_pairs={{0,4},{2,6},{4,0},{6,2},{8,12},{10,14},{12,8},{14,10},{1,5},{3,7},... | collective-permute-start | bytes 3145736 | tf_op jit(solution)/shard_map/ppermute | solution.py:54
  76.6 47.3 %collective-permute-start.8 = (bf16[2,32,16,256]{3,2,1,0:T(8,128)(2,1)S(1)}, bf16[2,32,16,256]{3,2,1,0:T(8,128)(2,1)S(1)}, u32[]{:S(2)}, u32[]{:S(2)}) collective-permute-start(bf16[2,32,16,256]{3,2,1,0:T(8,128)(2,1)S(1)} %get-tuple-element.70), channel_id=1, source_target_pairs={{0,8},{2,10},{4,12},{6,14},{8,0},{10,2},{12,4},{14,6},{1,9},{3,11}... | collective-permute-start | bytes 1572872 | tf_op jit(solution)/shard_map/ppermute | solution.py:54
  79.5 44.4 %collective-permute-start.9 = (bf16[2,32,16,256]{3,2,1,0:T(8,128)(2,1)S(1)}, bf16[2,32,16,256]{3,2,1,0:T(8,128)(2,1)S(1)}, u32[]{:S(2)}, u32[]{:S(2)}) collective-permute-start(bf16[2,32,16,256]{3,2,1,0:T(8,128)(2,1)S(1)} %get-tuple-element.72), channel_id=1, source_target_pairs={{0,12},{2,14},{4,8},{6,10},{8,4},{10,6},{12,0},{14,2},{1,13},{3,15... | collective-permute-start | bytes 1572872 | tf_op jit(solution)/shard_map/ppermute | solution.py:54
  96.5 35.1 %collective-permute-start.12 = (bf16[2,32,16,256]{3,2,1,0:T(8,128)(2,1)S(1)}, bf16[2,32,16,256]{3,2,1,0:T(8,128)(2,1)S(1)}, u32[]{:S(2)}, u32[]{:S(2)}) collective-permute-start(bf16[2,32,16,256]{3,2,1,0:T(8,128)(2,1)S(1)} %get-tuple-element.77), channel_id=1, source_target_pairs={{0,6},{2,4},{4,2},{6,0},{8,14},{10,12},{12,10},{14,8},{1,7},{3,5},... | collective-permute-start | bytes 1572872 | tf_op jit(solution)/shard_map/ppermute | solution.py:54
  96.6 35.0 %collective-permute-start.11 = (bf16[2,32,16,256]{3,2,1,0:T(8,128)(2,1)S(1)}, bf16[2,32,16,256]{3,2,1,0:T(8,128)(2,1)S(1)}, u32[]{:S(2)}, u32[]{:S(2)}) collective-permute-start(bf16[2,32,16,256]{3,2,1,0:T(8,128)(2,1)S(1)} %get-tuple-element.75), channel_id=1, source_target_pairs={{0,2},{2,0},{4,6},{6,4},{8,10},{10,8},{12,14},{14,12},{1,3},{3,1},... | collective-permute-start | bytes 1572872 | tf_op jit(solution)/shard_map/ppermute | solution.py:54
  131.6 33.4 %collective-permute-start.13 = (bf16[64,8192]{1,0:T(8,128)(2,1)}, bf16[64,8192]{1,0:T(8,128)(2,1)}, u32[]{:S(2)}, u32[]{:S(2)}) collective-permute-start(bf16[64,8192]{1,0:T(8,128)(2,1)} %broadcast_select_fusion.1.refs_1_), channel_id=1, source_target_pairs={{0,2},{2,0},{4,6},{6,4},{8,10},{10,8},{12,14},{14,12},{1,3},{3,1},... | collective-permute-start | bytes 3145736 | tf_op jit(solution)/shard_map/ppermute | solution.py:54
  145.1 44.1 %collective-permute-start.14 = (bf16[2,32,16,256]{3,2,1,0:T(8,128)(2,1)}, bf16[2,32,16,256]{3,2,1,0:T(8,128)(2,1)S(1)}, u32[]{:S(2)}, u32[]{:S(2)}) collective-permute-start(bf16[2,32,16,256]{3,2,1,0:T(8,128)(2,1)} %copy-done.4), channel_id=1, source_target_pairs={{0,4},{2,6},{4,0},{6,2},{8,12},{10,14},{12,8},{14,10},{1,5},{3,7},... | collective-permute-start | bytes 1572872 | tf_op jit(solution)/shard_map/ppermute | solution.py:54
  145.5 43.7 %collective-permute-start.15 = (bf16[2,32,16,256]{3,2,1,0:T(8,128)(2,1)}, bf16[2,32,16,256]{3,2,1,0:T(8,128)(2,1)}, u32[]{:S(2)}, u32[]{:S(2)}) collective-permute-start(bf16[2,32,16,256]{3,2,1,0:T(8,128)(2,1)} %copy-done.3), channel_id=1, source_target_pairs={{0,10},{2,8},{4,14},{6,12},{8,2},{10,0},{12,6},{14,4},{1,11},{3,9}... | collective-permute-start | bytes 1572872 | tf_op jit(solution)/shard_map/ppermute | solution.py:54
  148.3 41.0 %collective-permute-start.16 = (bf16[2,32,16,256]{3,2,1,0:T(8,128)(2,1)}, bf16[2,32,16,256]{3,2,1,0:T(8,128)(2,1)}, u32[]{:S(2)}, u32[]{:S(2)}) collective-permute-start(bf16[2,32,16,256]{3,2,1,0:T(8,128)(2,1)} %copy-done.2), channel_id=1, source_target_pairs={{0,14},{2,12},{4,10},{6,8},{8,6},{10,4},{12,2},{14,0},{1,15},{3,13... | collective-permute-start | bytes 1572872 | tf_op jit(solution)/shard_map/ppermute | solution.py:54
  182.7 16.1 %all-to-all-start = ((bf16[8,64,256]{2,1,0:T(8,128)(2,1)}), bf16[8,64,256]{2,1,0:T(8,128)(2,1)}, u32[]{:S(2)}, u32[]{:S(2)}) async-start(bf16[8,64,256]{2,1,0:T(8,128)(2,1)} %bitcast.126), calls=%async_computation | async-start | bytes 524288 | tf_op jit(solution)/shard_map/all_to_all | solution.py:534
  234.8 12.3 %collective-permute-start.17 = (bf16[64,4096]{1,0:T(8,128)(2,1)S(1)}, bf16[64,4096]{1,0:T(8,128)(2,1)S(1)}, u32[]{:S(2)}, u32[]{:S(2)}) collective-permute-start(bf16[64,4096]{1,0:T(8,128)(2,1)S(1)} %get-tuple-element.107), channel_id=1, source_target_pairs={{0,4},{4,8},{8,12},{12,14},{14,10},{10,6},{6,2},{2,0},{1,5},{5,9},... | collective-permute-start | bytes 1572872 | tf_op jit(solution)/shard_map/ppermute | solution.py:231
  235.4 12.2 %collective-permute-start.18 = (bf16[64,4096]{1,0:T(8,128)(2,1)S(1)}, bf16[64,4096]{1,0:T(8,128)(2,1)S(1)}, u32[]{:S(2)}, u32[]{:S(2)}) collective-permute-start(bf16[64,4096]{1,0:T(8,128)(2,1)S(1)} %get-tuple-element.108), channel_id=1, source_target_pairs={{0,2},{4,0},{8,4},{12,8},{14,12},{10,14},{6,10},{2,6},{1,3},{5,1},... | collective-permute-start | bytes 1572872 | tf_op jit(solution)/shard_map/ppermute | solution.py:231
  245.0 14.9 %collective-permute-start.21 = (bf16[64,4096]{1,0:T(8,128)(2,1)S(1)}, bf16[64,4096]{1,0:T(8,128)(2,1)S(1)}, u32[]{:S(2)}, u32[]{:S(2)}) collective-permute-start(bf16[64,4096]{1,0:T(8,128)(2,1)S(1)} %get-tuple-element.109), channel_id=1, source_target_pairs={{0,2},{4,0},{8,4},{12,8},{14,12},{10,14},{6,10},{2,6},{1,3},{5,1},... | collective-permute-start | bytes 1572872 | tf_op jit(solution)/shard_map/ppermute | solution.py:231
  246.2 14.9 %collective-permute-start.22 = (bf16[64,4096]{1,0:T(8,128)(2,1)S(1)}, bf16[64,4096]{1,0:T(8,128)(2,1)S(1)}, u32[]{:S(2)}, u32[]{:S(2)}) collective-permute-start(bf16[64,4096]{1,0:T(8,128)(2,1)S(1)} %get-tuple-element.110), channel_id=1, source_target_pairs={{0,4},{4,8},{8,12},{12,14},{14,10},{10,6},{6,2},{2,0},{1,5},{5,9},... | collective-permute-start | bytes 1572872 | tf_op jit(solution)/shard_map/ppermute | solution.py:231
  247.8 24.5 %collective-permute-start.19 = (bf16[64,4096]{1,0:T(8,128)(2,1)S(1)}, bf16[64,4096]{1,0:T(8,128)(2,1)S(1)}, u32[]{:S(2)}, u32[]{:S(2)}) collective-permute-start(bf16[64,4096]{1,0:T(8,128)(2,1)S(1)} %get-tuple-element.111), channel_id=1, source_target_pairs={{0,4},{4,8},{8,12},{12,14},{14,10},{10,6},{6,2},{2,0},{1,5},{5,9},... | collective-permute-start | bytes 1572872 | tf_op jit(solution)/shard_map/ppermute | solution.py:231
  250.7 21.6 %collective-permute-start.20 = (bf16[64,4096]{1,0:T(8,128)(2,1)S(1)}, bf16[64,4096]{1,0:T(8,128)(2,1)S(1)}, u32[]{:S(2)}, u32[]{:S(2)}) collective-permute-start(bf16[64,4096]{1,0:T(8,128)(2,1)S(1)} %get-tuple-element.112), channel_id=1, source_target_pairs={{0,2},{4,0},{8,4},{12,8},{14,12},{10,14},{6,10},{2,6},{1,3},{5,1},... | collective-permute-start | bytes 1572872 | tf_op jit(solution)/shard_map/ppermute | solution.py:231
  261.3 21.1 %collective-permute-start.24 = (bf16[64,4096]{1,0:T(8,128)(2,1)S(1)}, bf16[64,4096]{1,0:T(8,128)(2,1)S(1)}, u32[]{:S(2)}, u32[]{:S(2)}) collective-permute-start(bf16[64,4096]{1,0:T(8,128)(2,1)S(1)} %get-tuple-element.113), channel_id=1, source_target_pairs={{0,2},{4,0},{8,4},{12,8},{14,12},{10,14},{6,10},{2,6},{1,3},{5,1},... | collective-permute-start | bytes 1572872 | tf_op jit(solution)/shard_map/ppermute | solution.py:231
  261.6 21.9 %collective-permute-start.25 = (bf16[64,4096]{1,0:T(8,128)(2,1)S(1)}, bf16[64,4096]{1,0:T(8,128)(2,1)S(1)}, u32[]{:S(2)}, u32[]{:S(2)}) collective-permute-start(bf16[64,4096]{1,0:T(8,128)(2,1)S(1)} %get-tuple-element.114), channel_id=1, source_target_pairs={{0,4},{4,8},{8,12},{12,14},{14,10},{10,6},{6,2},{2,0},{1,5},{5,9},... | collective-permute-start | bytes 1572872 | tf_op jit(solution)/shard_map/ppermute | solution.py:231
  272.6 22.2 %collective-permute-start.23 = (bf16[64,4096]{1,0:T(8,128)(2,1)S(1)}, bf16[64,4096]{1,0:T(8,128)(2,1)S(1)}, u32[]{:S(2)}, u32[]{:S(2)}) collective-permute-start(bf16[64,4096]{1,0:T(8,128)(2,1)S(1)} %get-tuple-element.115), channel_id=1, source_target_pairs={{0,4},{4,8},{8,12},{12,14},{14,10},{10,6},{6,2},{2,0},{1,5},{5,9},... | collective-permute-start | bytes 1572872 | tf_op jit(solution)/shard_map/ppermute | solution.py:231
  273.5 21.4 %collective-permute-start.26 = (bf16[64,4096]{1,0:T(8,128)(2,1)S(1)}, bf16[64,4096]{1,0:T(8,128)(2,1)S(1)}, u32[]{:S(2)}, u32[]{:S(2)}) collective-permute-start(bf16[64,4096]{1,0:T(8,128)(2,1)S(1)} %get-tuple-element.116), channel_id=1, source_target_pairs={{0,2},{4,0},{8,4},{12,8},{14,12},{10,14},{6,10},{2,6},{1,3},{5,1},... | collective-permute-start | bytes 1572872 | tf_op jit(solution)/shard_map/ppermute | solution.py:231
  283.8 18.3 %collective-permute-start.29 = (bf16[64,4096]{1,0:T(8,128)(2,1)S(1)}, bf16[64,4096]{1,0:T(8,128)(2,1)S(1)}, u32[]{:S(2)}, u32[]{:S(2)}) collective-permute-start(bf16[64,4096]{1,0:T(8,128)(2,1)S(1)} %get-tuple-element.117), channel_id=1, source_target_pairs={{0,2},{4,0},{8,4},{12,8},{14,12},{10,14},{6,10},{2,6},{1,3},{5,1},... | collective-permute-start | bytes 1572872 | tf_op jit(solution)/shard_map/ppermute | solution.py:231
  284.1 29.4 %collective-permute-start.28 = (bf16[64,4096]{1,0:T(8,128)(2,1)S(1)}, bf16[64,4096]{1,0:T(8,128)(2,1)S(1)}, u32[]{:S(2)}, u32[]{:S(2)}) collective-permute-start(bf16[64,4096]{1,0:T(8,128)(2,1)S(1)} %get-tuple-element.118), channel_id=1, source_target_pairs={{0,4},{4,8},{8,12},{12,14},{14,10},{10,6},{6,2},{2,0},{1,5},{5,9},... | collective-permute-start | bytes 1572872 | tf_op jit(solution)/shard_map/ppermute | solution.py:231
  294.9 18.3 %collective-permute-start.27 = (bf16[64,4096]{1,0:T(8,128)(2,1)S(1)}, bf16[64,4096]{1,0:T(8,128)(2,1)S(1)}, u32[]{:S(2)}, u32[]{:S(2)}) collective-permute-start(bf16[64,4096]{1,0:T(8,128)(2,1)S(1)} %fusion.24), channel_id=1, source_target_pairs={{0,4},{4,8},{8,12},{12,14},{14,10},{10,6},{6,2},{2,0},{1,5},{5,9},... | collective-permute-start | bytes 1572872 | tf_op jit(solution)/shard_map/ppermute | solution.py:231
  313.5 10.0 %collective-permute-start.30 = (bf16[64,4096]{1,0:T(8,128)(2,1)S(1)}, bf16[64,4096]{1,0:T(8,128)(2,1)S(1)}, u32[]{:S(2)}, u32[]{:S(2)}) collective-permute-start(bf16[64,4096]{1,0:T(8,128)(2,1)S(1)} %fusion.13), channel_id=1, source_target_pairs={{0,2},{4,0},{8,4},{12,8},{14,12},{10,14},{6,10},{2,6},{1,3},{5,1},... | collective-permute-start | bytes 1572872 | tf_op jit(solution)/shard_map/ppermute | solution.py:231
  (21 other events, 461.1 us)

commit v15 on v10

--- a/solution.py
+++ b/solution.py
@@ -92,8 +92,8 @@
     exchange(2, far_first_y, far_second)
     exchange(7, arrived[4], far_first_y)
     exchange(3, arrived[4], far_first_y)
-    exchange(1, arrived[4], far_first_y)
-    near = [after(own, far_second, arrived[4], arrived[6]), beside, own_y, beside_y]
+    exchange(1, far_first_y)
+    near = [after(own, far_second, arrived[4], arrived[6], arrived[1]), beside, own_y, beside_y]
     far = [far_first, far_second, far_first_y, far_second_y]
     return near, far, [arrived[apart] for apart in range(LINE_MODELS)]
 
@@ -196,21 +196,15 @@
 
 
 class RingScatter:
-    def __init__(self, shares, n_model, my_model, first, way):
-        order = [m for m in range(0, n_model, 2)] + [m for m in range(n_model - 1, 0, -2)]
-        self.order = order
-        self.n_model = n_model
-        self.way = way
-        spot = jnp.array([order.index(m) for m in range(n_model)], jnp.int32)[my_model]
-        self.shares, self.spot, self.first = shares, spot, first
-        self.distance = {way: n_model // 2, -way: n_model // 2 - 1}
+    def __init__(self, shares, places, order, way):
+        self.shares, self.places, self.order, self.way = shares, places, order, way
+        self.n_model = len(order)
+        self.distance = {way: self.n_model // 2, -way: self.n_model // 2 - 1}
         self.moving = {}
 
     def share_of(self, offset):
-        table = jnp.array(self.order, jnp.int32)
-        owner = table[(self.spot + offset + self.n_model) % self.n_model]
-        owner = (owner - self.first + self.n_model) % self.n_model
-        return lax.dynamic_index_in_dim(self.shares, owner, 0, keepdims=False)
+        place = self.places[offset % self.n_model]
+        return lax.dynamic_index_in_dim(self.shares, place, 0, keepdims=False)
 
     def step(self, *before):
         ways = [way for way in (self.way, -self.way) if self.distance[way]]
@@ -389,7 +383,7 @@
 def attend(half, queries, prefix, new_keys, new_values):
     heads = queries[0].shape[0]
     rows = 2 * new_keys[0].shape[0]
-    span = math.gcd(prefix[0].shape[0], 1024)
+    span = math.gcd(prefix[0].shape[0], 2048)
     whole = lambda array: pl.BlockSpec(array.shape, lambda step: (0, 0))
     count = prefix[0].shape[0] + rows
     query_spec = pl.BlockSpec((1, rows // 2, HD), lambda step: (step, 0, 0))
@@ -548,22 +542,24 @@
         for chunk in range(COLUMN_CHUNKS)
     ]
 
-    first = upper_half * (n_model // 2)
+    order = [m for m in range(0, n_model, 2)] + [m for m in range(n_model - 1, 0, -2)]
+    spot = jnp.array([order.index(m) for m in range(n_model)], jnp.int32)[my_model]
+    places = jnp.array(order, jnp.int32)[(spot + models) % n_model]
+    places = (places + n_model - upper_half * (n_model // 2)) % n_model
     scatters = [
         RingScatter(
-            share.reshape(n_model, row_count, -1),
-            n_model,
-            my_model,
-            first,
-            1 if chunk % 2 == 0 else -1,
+            share.reshape(n_model, row_count, -1), places, order, 1 if chunk % 2 == 0 else -1
         )
         for chunk, share in enumerate(shares)
     ]
-    sent = []
-    for _ in range(n_model // 2):
+    sent, sums = [], []
+    steps = n_model // 2
+    for step in range(steps):
         for scatter in scatters:
-            sent = scatter.step(*sent)
-    return (jnp.concatenate([scatter.finish() for scatter in scatters], 1)[None], cache_rows)
+            sent = scatter.step(sent, sums)
+            if step == steps - 1:
+                sums.append(scatter.finish())
+    return (jnp.concatenate(sums, 1)[None], cache_rows)
 
 
 def solution(mesh):

time: 300 us -> 316 us (1.053)
  starting transfers between devices: 62.7 us -> 68.5 us
  other arithmetic: 16.1 us -> 19.8 us
  between operations: 13 us -> 16.5 us
  matrix products: 12.8 us -> 16.2 us
    ppermute x14, waiting for transfers between devices: 50.7 us -> 73.8 us  [swap(): lax.ppermute(block, 'mp', [(index, index ^ mask) for index in range(LINE_...]
    all_to_all x1, waiting for transfers between devices: 11.8 us -> 0.01 us  [on_device(): pairs = lax.all_to_all(pairs, 'mp', split_axis=0, concat_axis=0, tiled=True)]
    ppermute x14, waiting for transfers between devices: 56.9 us -> 46.3 us  [step(): self.moving[way] = lax.ppermute(block, 'mp', pairs)]
    ppermute x14, starting transfers between devices: 42.6 us -> 48 us  [swap(): lax.ppermute(block, 'mp', [(index, index ^ mask) for index in range(LINE_...]
    dot_general x2, matrix products: 12.8 us -> 16.2 us  [on_device(): jnp.dot(mixed, w_out[:, chunk * width:(chunk + 1) * width], preferred_ele...]
  transfers between devices with their start and end apart: 32 -> 32, of which waited for: 15 -> 17; matrix products, arithmetic and copies ran while one was open for 8% -> 9% of each run, Pallas kernels for 12% -> 12%
where the time goes in v15:
time: 316 us; the launch traced here: 314 us
  waiting for transfers between devices  120 us (38%)
  starting transfers between devices  68.5 us (22%)
  Pallas kernels  62.2 us (20%)
  other arithmetic  19.8 us (6%)
  between operations  16.5 us (5%)
  matrix products  16.2 us (5%)
  local copies, waits for them, and re-layouts  11 us (3%)
    ppermute x14, waiting for transfers between devices, swap(): lax.ppermute(block, 'mp', [(index, index ^ mask) for index in range(LINE_...  73.8 us
    ppermute x14, starting transfers between devices, swap(): lax.ppermute(block, 'mp', [(index, index ^ mask) for index in range(LINE_...  48 us
    ppermute x14, waiting for transfers between devices, step(): self.moving[way] = lax.ppermute(block, 'mp', pairs)  46.3 us
    pallas_call x2, Pallas kernels, project(): pl.pallas_call(project_kernel, grid=(width // depth,), out_shape=out_shap...  31.4 us
    pallas_call x1, Pallas kernels, attend(): pl.pallas_call(functools.partial(attend_kernel, span), grid=(heads,), out...  22.2 us
    dot_general x2, matrix products, on_device(): jnp.dot(mixed, w_out[:, chunk * width:(chunk + 1) * width], preferred_ele...  16.2 us
    ppermute x14, starting transfers between devices, step(): self.moving[way] = lax.ppermute(block, 'mp', pairs)  15.5 us
  transfers between devices with their start and end apart: 32, of which 17 were waited for; matrix products, arithmetic and copies ran while one was open for 9% of the time, Pallas kernels for 12%

profile of v15, /device:TPU:0, one launch (start us, length us, event | category | flops | bytes accessed | tf_op | source)
XLA Modules:
  0.0 314.3 jit_solution(16955948703412015813)
XLA Ops:
  5.0 4.1 %collective-permute-start = (bf16[64,8192]{1,0:T(8,128)(2,1)S(1)}, bf16[64,8192]{1,0:T(8,128)(2,1)}, u32[]{:S(2)}, u32[]{:S(2)}) collective-permute-start(bf16[64,8192]{1,0:T(8,128)(2,1)S(1)} %fusion.12.refs_0_), channel_id=1, source_target_pairs={{0,4},{2,6},{4,0},{6,2},{8,12},{10,14},{12,8},{14,10},{1,5},{3,7},... | collective-permute-start | bytes 3145736 | tf_op jit(solution)/shard_map/ppermute | solution.py:54
  10.6 21.9 %collective-permute-start.7 = (bf16[64,8192]{1,0:T(8,128)(2,1)}, bf16[64,8192]{1,0:T(8,128)(2,1)}, u32[]{:S(2)}, u32[]{:S(2)}) collective-permute-start(bf16[64,8192]{1,0:T(8,128)(2,1)} %collective-permute-done.6), channel_id=1, source_target_pairs={{0,4},{2,6},{4,0},{6,2},{8,12},{10,14},{12,8},{14,10},{1,5},{3,7},... | collective-permute-start | bytes 3145736 | tf_op jit(solution)/shard_map/ppermute | solution.py:54
  40.2 15.0 %collective-permute-done.7 = bf16[64,8192]{1,0:T(8,128)(2,1)} collective-permute-done((bf16[64,8192]{1,0:T(8,128)(2,1)}, bf16[64,8192]{1,0:T(8,128)(2,1)}, u32[]{:S(2)}, u32[]{:S(2)}) %collective-permute-start.7) | collective-permute-done | bytes 1048608 | tf_op jit(solution)/shard_map/ppermute | solution.py:54
  55.1 2.3 broadcast_select_fusion.refs_0_
  57.5 6.8 %collective-permute-done.9.refs_3_ = bf16[64,8192]{1,0:T(8,128)(2,1)S(1)} collective-permute-done((bf16[64,8192]{1,0:T(8,128)(2,1)}, bf16[64,8192]{1,0:T(8,128)(2,1)S(1)}, u32[]{:S(2)}, u32[]{:S(2)}) %collective-permute-start.9) | collective-permute-done | bytes 1048608 | tf_op jit(solution)/shard_map/ppermute | solution.py:54
  65.7 2.2 copy-done.1
  67.9 4.3 %pack_blocks.1 = (bf16[2,32,16,256]{3,2,1,0:T(8,128)(2,1)S(1)}, bf16[2,32,16,256]{3,2,1,0:T(8,128)(2,1)}, bf16[2,32,16,256]{3,2,1,0:T(8,128)(2,1)}, bf16[2,32,16...) custom-call(s32[2,32]{1,0:T(2,128)S(1)} %pad_add_fusion.slots_ref, ...), custom_call_target="tpu_custom_call" | custom-call | tf_op jit(solution)/shard_map/pack_blocks/pallas_call | solution.py:274
  76.9 3.0 collective-permute-start.4
  81.2 8.0 %collective-permute-done.10.refs_2_ = bf16[64,8192]{1,0:T(8,128)(2,1)} collective-permute-done((bf16[64,8192]{1,0:T(8,128)(2,1)}, bf16[64,8192]{1,0:T(8,128)(2,1)}, u32[]{:S(2)}, u32[]{:S(2)}) %collective-permute-start.10) | collective-permute-done | bytes 1048608 | tf_op jit(solution)/shard_map/ppermute | solution.py:54
  90.8 17.9 %collective-permute-done.3 = bf16[64,8192]{1,0:T(8,128)(2,1)} collective-permute-done((bf16[64,8192]{1,0:T(8,128)(2,1)}, bf16[64,8192]{1,0:T(8,128)(2,1)}, u32[]{:S(2)}, u32[]{:S(2)}) %collective-permute-start.3) | collective-permute-done | bytes 1048608 | tf_op jit(solution)/shard_map/ppermute | solution.py:54
  113.3 2.5 collective-permute-start.14
  115.8 5.7 %collective-permute-done.5 = bf16[2,32,16,256]{3,2,1,0:T(8,128)(2,1)S(1)} collective-permute-done((bf16[2,32,16,256]{3,2,1,0:T(8,128)(2,1)}, bf16[2,32,16,256]{3,2,1,0:T(8,128)(2,1)S(1)}, u32[]{:S(2)}, u32[]{:S(2)}) %collective-permute-start.5) | collective-permute-done | bytes 524320 | tf_op jit(solution)/shard_map/ppermute | solution.py:54
  121.5 6.4 %collective-permute-start.15 = (bf16[2,32,16,256]{3,2,1,0:T(8,128)(2,1)}, bf16[2,32,16,256]{3,2,1,0:T(8,128)(2,1)}, u32[]{:S(2)}, u32[]{:S(2)}) collective-permute-start(bf16[2,32,16,256]{3,2,1,0:T(8,128)(2,1)} %get-tuple-element.76), channel_id=1, source_target_pairs={{0,10},{2,8},{4,14},{6,12},{8,2},{10,0},{12,6},{14,4},{1,11},{3,9}... | collective-permute-start | bytes 1572872 | tf_op jit(solution)/shard_map/ppermute | solution.py:54
  129.4 15.7 %project.2 = (bf16[8,256,128]{2,1,0:T(8,128)(2,1)}, bf16[256,128]{1,0:T(8,128)(2,1)}, bf16[256,256]{1,0:T(8,128)(2,1)}, bf16[256,256]{1,0:T(8,128)(2,1)}) custom-call(s32[4]{0:T(128)} %add_multiply_fusion.starts_ref, bf16[64,8192]{1,0:T(8,128)(2,1)} %copy-done.9, bf16[64,8192]{1,0:T(8,128)(2,1)} %collective-permute-done.refs_1_, ...), custom_call_target="tpu_custom_call" | custom-call | flops 5368709120 | bytes 26476544 | tf_op jit(solution)/shard_map/project/pallas_call | solution.py:177
  145.1 20.4 %collective-permute-done.12.refs_3_ = bf16[64,8192]{1,0:T(8,128)(2,1)S(1)} collective-permute-done((bf16[64,8192]{1,0:T(8,128)(2,1)S(1)}, bf16[64,8192]{1,0:T(8,128)(2,1)S(1)}, u32[]{:S(2)}, u32[]{:S(2)}) %collective-permute-start.12) | collective-permute-done | bytes 1048608 | tf_op jit(solution)/shard_map/ppermute | solution.py:54
  166.5 15.7 %project.3 = (bf16[8,256,128]{2,1,0:T(8,128)(2,1)}, bf16[256,128]{1,0:T(8,128)(2,1)}, bf16[256,256]{1,0:T(8,128)(2,1)}, bf16[256,256]{1,0:T(8,128)(2,1)}) custom-call(s32[4]{0:T(128)} %add_multiply_fusion.1.starts_ref, bf16[64,8192]{1,0:T(8,128)(2,1)} %broadcast_select_fusion.refs_0_, bf16[64,8192]{1,0:T(8,128)(2,1)} %copy-done.10, ...), custom_call_target="tpu_custom_call" | custom-call | flops 5368709120 | bytes 26476544 | tf_op jit(solution)/shard_map/project/pallas_call | solution.py:177
  184.0 4.2 %all-to-all-start = ((bf16[8,64,256]{2,1,0:T(8,128)(2,1)}), bf16[8,64,256]{2,1,0:T(8,128)(2,1)}, u32[]{:S(2)}, u32[]{:S(2)}) async-start(bf16[8,64,256]{2,1,0:T(8,128)(2,1)} %bitcast.119), calls=%async_computation | async-start | bytes 524288 | tf_op jit(solution)/shard_map/all_to_all | solution.py:526
  204.5 3.5 %order_blocks.1 = (bf16[4096,128]{1,0:T(8,128)(2,1)S(1)}, bf16[4096,256]{1,0:T(8,128)(2,1)S(1)}) custom-call(s32[1]{0:T(128)} %dynamic_slice.67.length_ref, s32[256]{0:T(256)S(1)} %multiply_add_fusion.where_ref, bf16[64,16,256]{2,1,0:T(8,128)(2,1)S(1)} %bitcast.103, bf16[64,16,256]{2,1,0:T(8,128)(2,1)S(1)} %bitcast.106, bf16[64,16,256]{2,1,0:T(8,128)(2,1)S(1)} %bitcast.107, ...), custom_call_target="tpu_custom_call" | custom-call | tf_op jit(solution)/shard_map/order_blocks/pallas_call | solution.py:319
  208.1 22.2 %attend.1 = bf16[512,1024]{1,0:T(8,128)(2,1)S(1)} custom-call(s32[1]{0:T(128)} %bitcast.half_ref, bf16[8,256,128]{2,1,0:T(8,128)(2,1)S(1)} %copy-done.2, bf16[8,256,128]{2,1,0:T(8,128)(2,1)S(1)} %copy-done.3, bf16[4096,128]{1,0:T(8,128)(2,1)S(1)} %get-tuple-element.91.refs_2_, bf16[4096,256]{1,0:T(8,128)(2,1)S(1)} %get-tuple-element.92.refs_3_, ...), custom_call_target="tpu_custom_call" | custom-call | flops 19327352832 | bytes 5636096 | tf_op jit(solution)/shard_map/attend/pallas_call | solution.py:391
  230.3 8.1 %fusion.4 = bf16[512,4096]{1,0:T(8,128)(2,1)S(1)} fusion(bf16[512,1024]{1,0:T(8,128)(2,1)S(1)} %attend.1, bf16[1024,8192]{1,0:T(8,128)(2,1)} %param.23), kind=kOutput, calls=%fused_computation.5 | convolution fusion | flops 4297064448 | bytes 13631488 | tf_op jit(solution)/shard_map/dot_general | solution.py:537
  238.5 2.6 collective-permute-start.18
  241.1 8.1 %fusion.7 = bf16[512,4096]{1,0:T(8,128)(2,1)S(1)} fusion(bf16[512,1024]{1,0:T(8,128)(2,1)S(1)} %attend.1, bf16[1024,8192]{1,0:T(8,128)(2,1)} %param.23), kind=kOutput, calls=%fused_computation.6 | convolution fusion | flops 4297064448 | bytes 13631488 | tf_op jit(solution)/shard_map/dot_general | solution.py:537
  253.5 2.5 collective-permute-done.17
  258.3 8.9 %collective-permute-done.22 = bf16[64,4096]{1,0:T(8,128)(2,1)S(1)} collective-permute-done((bf16[64,4096]{1,0:T(8,128)(2,1)S(1)}, bf16[64,4096]{1,0:T(8,128)(2,1)S(1)}, u32[]{:S(2)}, u32[]{:S(2)}) %collective-permute-start.22) | collective-permute-done | bytes 524320 | tf_op jit(solution)/shard_map/ppermute | solution.py:224
  269.6 4.7 %collective-permute-done.20 = bf16[64,4096]{1,0:T(8,128)(2,1)S(1)} collective-permute-done((bf16[64,4096]{1,0:T(8,128)(2,1)S(1)}, bf16[64,4096]{1,0:T(8,128)(2,1)S(1)}, u32[]{:S(2)}, u32[]{:S(2)}) %collective-permute-start.20) | collective-permute-done | bytes 524320 | tf_op jit(solution)/shard_map/ppermute | solution.py:224
  274.3 4.2 %collective-permute-done.19 = bf16[64,4096]{1,0:T(8,128)(2,1)S(1)} collective-permute-done((bf16[64,4096]{1,0:T(8,128)(2,1)S(1)}, bf16[64,4096]{1,0:T(8,128)(2,1)S(1)}, u32[]{:S(2)}, u32[]{:S(2)}) %collective-permute-start.19) | collective-permute-done | bytes 524320 | tf_op jit(solution)/shard_map/ppermute | solution.py:224
  280.8 3.3 %collective-permute-done.25 = bf16[64,4096]{1,0:T(8,128)(2,1)S(1)} collective-permute-done((bf16[64,4096]{1,0:T(8,128)(2,1)S(1)}, bf16[64,4096]{1,0:T(8,128)(2,1)S(1)}, u32[]{:S(2)}, u32[]{:S(2)}) %collective-permute-start.25) | collective-permute-done | bytes 524320 | tf_op jit(solution)/shard_map/ppermute | solution.py:224
  286.4 3.3 %collective-permute-done.23 = bf16[64,4096]{1,0:T(8,128)(2,1)S(1)} collective-permute-done((bf16[64,4096]{1,0:T(8,128)(2,1)S(1)}, bf16[64,4096]{1,0:T(8,128)(2,1)S(1)}, u32[]{:S(2)}, u32[]{:S(2)}) %collective-permute-start.23) | collective-permute-done | bytes 524320 | tf_op jit(solution)/shard_map/ppermute | solution.py:224
  289.8 3.1 %collective-permute-done.26 = bf16[64,4096]{1,0:T(8,128)(2,1)S(1)} collective-permute-done((bf16[64,4096]{1,0:T(8,128)(2,1)S(1)}, bf16[64,4096]{1,0:T(8,128)(2,1)S(1)}, u32[]{:S(2)}, u32[]{:S(2)}) %collective-permute-start.26) | collective-permute-done | bytes 524320 | tf_op jit(solution)/shard_map/ppermute | solution.py:224
  293.3 5.9 %collective-permute-done.29 = bf16[64,4096]{1,0:T(8,128)(2,1)S(1)} collective-permute-done((bf16[64,4096]{1,0:T(8,128)(2,1)S(1)}, bf16[64,4096]{1,0:T(8,128)(2,1)S(1)}, u32[]{:S(2)}, u32[]{:S(2)}) %collective-permute-start.29) | collective-permute-done | bytes 524320 | tf_op jit(solution)/shard_map/ppermute | solution.py:224
  299.4 3.3 %collective-permute-done.27 = bf16[64,4096]{1,0:T(8,128)(2,1)S(1)} collective-permute-done((bf16[64,4096]{1,0:T(8,128)(2,1)S(1)}, bf16[64,4096]{1,0:T(8,128)(2,1)S(1)}, u32[]{:S(2)}, u32[]{:S(2)}) %collective-permute-start.27) | collective-permute-done | bytes 524320 | tf_op jit(solution)/shard_map/ppermute | solution.py:224
  307.0 5.1 %collective-permute-done.30 = bf16[64,4096]{1,0:T(8,128)(2,1)S(1)} collective-permute-done((bf16[64,4096]{1,0:T(8,128)(2,1)S(1)}, bf16[64,4096]{1,0:T(8,128)(2,1)S(1)}, u32[]{:S(2)}, u32[]{:S(2)}) %collective-permute-start.30) | collective-permute-done | bytes 524320 | tf_op jit(solution)/shard_map/ppermute | solution.py:224
  (128 shorter events, 52.9 us)
Async XLA Ops:
  4.5 6.2 %collective-permute-start.6 = (bf16[64,8192]{1,0:T(8,128)(2,1)S(1)}, bf16[64,8192]{1,0:T(8,128)(2,1)}, u32[]{:S(2)}, u32[]{:S(2)}) collective-permute-start(bf16[64,8192]{1,0:T(8,128)(2,1)S(1)} %fusion.12.refs_0_), channel_id=1, source_target_pairs={{0,1},{1,0},{2,3},{3,2},{4,8},{5,9},{6,10},{7,11},{8,4},{9,5},{10,... | collective-permute-start | bytes 3145736 | tf_op jit(solution)/shard_map/ppermute | solution.py:65
  5.0 33.4 %collective-permute-start = (bf16[64,8192]{1,0:T(8,128)(2,1)S(1)}, bf16[64,8192]{1,0:T(8,128)(2,1)}, u32[]{:S(2)}, u32[]{:S(2)}) collective-permute-start(bf16[64,8192]{1,0:T(8,128)(2,1)S(1)} %fusion.12.refs_0_), channel_id=1, source_target_pairs={{0,4},{2,6},{4,0},{6,2},{8,12},{10,14},{12,8},{14,10},{1,5},{3,7},... | collective-permute-start | bytes 3145736 | tf_op jit(solution)/shard_map/ppermute | solution.py:54
  9.1 29.3 %collective-permute-start.8 = (bf16[64,8192]{1,0:T(8,128)(2,1)S(1)}, bf16[64,8192]{1,0:T(8,128)(2,1)}, u32[]{:S(2)}, u32[]{:S(2)}) collective-permute-start(bf16[64,8192]{1,0:T(8,128)(2,1)S(1)} %fusion.12.refs_0_), channel_id=1, source_target_pairs={{0,2},{2,0},{4,6},{6,4},{8,10},{10,8},{12,14},{14,12},{1,3},{3,1},... | collective-permute-start | bytes 3145736 | tf_op jit(solution)/shard_map/ppermute | solution.py:54
  10.6 44.5 %collective-permute-start.7 = (bf16[64,8192]{1,0:T(8,128)(2,1)}, bf16[64,8192]{1,0:T(8,128)(2,1)}, u32[]{:S(2)}, u32[]{:S(2)}) collective-permute-start(bf16[64,8192]{1,0:T(8,128)(2,1)} %collective-permute-done.6), channel_id=1, source_target_pairs={{0,4},{2,6},{4,0},{6,2},{8,12},{10,14},{12,8},{14,10},{1,5},{3,7},... | collective-permute-start | bytes 3145736 | tf_op jit(solution)/shard_map/ppermute | solution.py:54
  38.2 27.6 %collective-permute-start.2 = (bf16[32,16,2048]{2,1,0:T(8,128)(2,1)S(1)}, bf16[32,16,2048]{2,1,0:T(8,128)(2,1)}, u32[]{:S(2)}, u32[]{:S(2)}) collective-permute-start(bf16[32,16,2048]{2,1,0:T(8,128)(2,1)S(1)} %pick_blocks.1), channel_id=1, source_target_pairs={{0,1},{1,0},{2,3},{3,2},{4,5},{5,4},{6,7},{7,6},{8,9},{9,8},{10,11... | collective-permute-start | bytes 6291464 | tf_op jit(solution)/shard_map/ppermute | solution.py:458
  38.4 25.8 %collective-permute-start.9 = (bf16[64,8192]{1,0:T(8,128)(2,1)}, bf16[64,8192]{1,0:T(8,128)(2,1)S(1)}, u32[]{:S(2)}, u32[]{:S(2)}) collective-permute-start(bf16[64,8192]{1,0:T(8,128)(2,1)} %collective-permute-done.refs_1_), channel_id=1, source_target_pairs={{0,2},{2,0},{4,6},{6,4},{8,10},{10,8},{12,14},{14,12},{1,3},{3,1},... | collective-permute-start | bytes 3145736 | tf_op jit(solution)/shard_map/ppermute | solution.py:54
  40.0 32.2 %collective-permute-start.1 = (bf16[64,8192]{1,0:T(8,128)(2,1)}, bf16[64,8192]{1,0:T(8,128)(2,1)}, u32[]{:S(2)}, u32[]{:S(2)}) collective-permute-start(bf16[64,8192]{1,0:T(8,128)(2,1)} %collective-permute-done.refs_1_), channel_id=1, source_target_pairs={{0,1},{1,0},{2,3},{3,2},{4,8},{5,9},{6,10},{7,11},{8,4},{9,5},{10,... | collective-permute-start | bytes 3145736 | tf_op jit(solution)/shard_map/ppermute | solution.py:65
  64.2 25.1 %collective-permute-start.10 = (bf16[64,8192]{1,0:T(8,128)(2,1)}, bf16[64,8192]{1,0:T(8,128)(2,1)}, u32[]{:S(2)}, u32[]{:S(2)}) collective-permute-start(bf16[64,8192]{1,0:T(8,128)(2,1)} %broadcast_select_fusion.refs_0_), channel_id=1, source_target_pairs={{0,2},{2,0},{4,6},{6,4},{8,10},{10,8},{12,14},{14,12},{1,3},{3,1},... | collective-permute-start | bytes 3145736 | tf_op jit(solution)/shard_map/ppermute | solution.py:54
  72.2 36.5 %collective-permute-start.3 = (bf16[64,8192]{1,0:T(8,128)(2,1)}, bf16[64,8192]{1,0:T(8,128)(2,1)}, u32[]{:S(2)}, u32[]{:S(2)}) collective-permute-start(bf16[64,8192]{1,0:T(8,128)(2,1)} %collective-permute-done.1), channel_id=1, source_target_pairs={{0,4},{2,6},{4,0},{6,2},{8,12},{10,14},{12,8},{14,10},{1,5},{3,7},... | collective-permute-start | bytes 3145736 | tf_op jit(solution)/shard_map/ppermute | solution.py:54
  76.9 36.4 %collective-permute-start.4 = (bf16[2,32,16,256]{3,2,1,0:T(8,128)(2,1)S(1)}, bf16[2,32,16,256]{3,2,1,0:T(8,128)(2,1)S(1)}, u32[]{:S(2)}, u32[]{:S(2)}) collective-permute-start(bf16[2,32,16,256]{3,2,1,0:T(8,128)(2,1)S(1)} %get-tuple-element.59), channel_id=1, source_target_pairs={{0,8},{2,10},{4,12},{6,14},{8,0},{10,2},{12,4},{14,6},{1,9},{3,11}... | collective-permute-start | bytes 1572872 | tf_op jit(solution)/shard_map/ppermute | solution.py:54
  79.9 41.6 %collective-permute-start.5 = (bf16[2,32,16,256]{3,2,1,0:T(8,128)(2,1)}, bf16[2,32,16,256]{3,2,1,0:T(8,128)(2,1)S(1)}, u32[]{:S(2)}, u32[]{:S(2)}) collective-permute-start(bf16[2,32,16,256]{3,2,1,0:T(8,128)(2,1)} %get-tuple-element.61), channel_id=1, source_target_pairs={{0,12},{2,14},{4,8},{6,10},{8,4},{10,6},{12,0},{14,2},{1,13},{3,15... | collective-permute-start | bytes 1572872 | tf_op jit(solution)/shard_map/ppermute | solution.py:54
  89.3 38.6 %collective-permute-start.11 = (bf16[2,32,16,256]{3,2,1,0:T(8,128)(2,1)}, bf16[2,32,16,256]{3,2,1,0:T(8,128)(2,1)S(1)}, u32[]{:S(2)}, u32[]{:S(2)}) collective-permute-start(bf16[2,32,16,256]{3,2,1,0:T(8,128)(2,1)} %get-tuple-element.65), channel_id=1, source_target_pairs={{0,2},{2,0},{4,6},{6,4},{8,10},{10,8},{12,14},{14,12},{1,3},{3,1},... | collective-permute-start | bytes 1572872 | tf_op jit(solution)/shard_map/ppermute | solution.py:54
  110.1 55.4 %collective-permute-start.12 = (bf16[64,8192]{1,0:T(8,128)(2,1)S(1)}, bf16[64,8192]{1,0:T(8,128)(2,1)S(1)}, u32[]{:S(2)}, u32[]{:S(2)}) collective-permute-start(bf16[64,8192]{1,0:T(8,128)(2,1)S(1)} %broadcast_select_fusion.1.refs_1_), channel_id=1, source_target_pairs={{0,2},{2,0},{4,6},{6,4},{8,10},{10,8},{12,14},{14,12},{1,3},{3,1},... | collective-permute-start | bytes 3145736 | tf_op jit(solution)/shard_map/ppermute | solution.py:54
  113.2 91.2 %collective-permute-start.13 = (bf16[2,32,16,256]{3,2,1,0:T(8,128)(2,1)}, bf16[2,32,16,256]{3,2,1,0:T(8,128)(2,1)S(1)}, u32[]{:S(2)}, u32[]{:S(2)}) collective-permute-start(bf16[2,32,16,256]{3,2,1,0:T(8,128)(2,1)} %get-tuple-element.72), channel_id=1, source_target_pairs={{0,4},{2,6},{4,0},{6,2},{8,12},{10,14},{12,8},{14,10},{1,5},{3,7},... | collective-permute-start | bytes 1572872 | tf_op jit(solution)/shard_map/ppermute | solution.py:54
  113.3 91.1 %collective-permute-start.14 = (bf16[2,32,16,256]{3,2,1,0:T(8,128)(2,1)}, bf16[2,32,16,256]{3,2,1,0:T(8,128)(2,1)S(1)}, u32[]{:S(2)}, u32[]{:S(2)}) collective-permute-start(bf16[2,32,16,256]{3,2,1,0:T(8,128)(2,1)} %get-tuple-element.74), channel_id=1, source_target_pairs={{0,6},{2,4},{4,2},{6,0},{8,14},{10,12},{12,10},{14,8},{1,7},{3,5},... | collective-permute-start | bytes 1572872 | tf_op jit(solution)/shard_map/ppermute | solution.py:54
  121.5 82.9 %collective-permute-start.15 = (bf16[2,32,16,256]{3,2,1,0:T(8,128)(2,1)}, bf16[2,32,16,256]{3,2,1,0:T(8,128)(2,1)}, u32[]{:S(2)}, u32[]{:S(2)}) collective-permute-start(bf16[2,32,16,256]{3,2,1,0:T(8,128)(2,1)} %get-tuple-element.76), channel_id=1, source_target_pairs={{0,10},{2,8},{4,14},{6,12},{8,2},{10,0},{12,6},{14,4},{1,11},{3,9}... | collective-permute-start | bytes 1572872 | tf_op jit(solution)/shard_map/ppermute | solution.py:54
  127.9 76.5 %collective-permute-start.16 = (bf16[2,32,16,256]{3,2,1,0:T(8,128)(2,1)}, bf16[2,32,16,256]{3,2,1,0:T(8,128)(2,1)}, u32[]{:S(2)}, u32[]{:S(2)}) collective-permute-start(bf16[2,32,16,256]{3,2,1,0:T(8,128)(2,1)} %get-tuple-element.78), channel_id=1, source_target_pairs={{0,14},{2,12},{4,10},{6,8},{8,6},{10,4},{12,2},{14,0},{1,15},{3,13... | collective-permute-start | bytes 1572872 | tf_op jit(solution)/shard_map/ppermute | solution.py:54
  184.0 20.4 %all-to-all-start = ((bf16[8,64,256]{2,1,0:T(8,128)(2,1)}), bf16[8,64,256]{2,1,0:T(8,128)(2,1)}, u32[]{:S(2)}, u32[]{:S(2)}) async-start(bf16[8,64,256]{2,1,0:T(8,128)(2,1)} %bitcast.119), calls=%async_computation | async-start | bytes 524288 | tf_op jit(solution)/shard_map/all_to_all | solution.py:526
  238.5 15.0 %collective-permute-start.18 = (bf16[64,4096]{1,0:T(8,128)(2,1)S(1)}, bf16[64,4096]{1,0:T(8,128)(2,1)S(1)}, u32[]{:S(2)}, u32[]{:S(2)}) collective-permute-start(bf16[64,4096]{1,0:T(8,128)(2,1)S(1)} %get-tuple-element.98), channel_id=1, source_target_pairs={{0,2},{4,0},{8,4},{12,8},{14,12},{10,14},{6,10},{2,6},{1,3},{5,1},... | collective-permute-start | bytes 1572872 | tf_op jit(solution)/shard_map/ppermute | solution.py:224
  241.1 14.9 %collective-permute-start.17 = (bf16[64,4096]{1,0:T(8,128)(2,1)S(1)}, bf16[64,4096]{1,0:T(8,128)(2,1)S(1)}, u32[]{:S(2)}, u32[]{:S(2)}) collective-permute-start(bf16[64,4096]{1,0:T(8,128)(2,1)S(1)} %get-tuple-element.97), channel_id=1, source_target_pairs={{0,4},{4,8},{8,12},{12,14},{14,10},{10,6},{6,2},{2,0},{1,5},{5,9},... | collective-permute-start | bytes 1572872 | tf_op jit(solution)/shard_map/ppermute | solution.py:224
  249.3 17.9 %collective-permute-start.22 = (bf16[64,4096]{1,0:T(8,128)(2,1)S(1)}, bf16[64,4096]{1,0:T(8,128)(2,1)S(1)}, u32[]{:S(2)}, u32[]{:S(2)}) collective-permute-start(bf16[64,4096]{1,0:T(8,128)(2,1)S(1)} %get-tuple-element.100), channel_id=1, source_target_pairs={{0,4},{4,8},{8,12},{12,14},{14,10},{10,6},{6,2},{2,0},{1,5},{5,9},... | collective-permute-start | bytes 1572872 | tf_op jit(solution)/shard_map/ppermute | solution.py:224
  250.5 16.7 %collective-permute-start.21 = (bf16[64,4096]{1,0:T(8,128)(2,1)S(1)}, bf16[64,4096]{1,0:T(8,128)(2,1)S(1)}, u32[]{:S(2)}, u32[]{:S(2)}) collective-permute-start(bf16[64,4096]{1,0:T(8,128)(2,1)S(1)} %get-tuple-element.99), channel_id=1, source_target_pairs={{0,2},{4,0},{8,4},{12,8},{14,12},{10,14},{6,10},{2,6},{1,3},{5,1},... | collective-permute-start | bytes 1572872 | tf_op jit(solution)/shard_map/ppermute | solution.py:224
  256.2 18.0 %collective-permute-start.20 = (bf16[64,4096]{1,0:T(8,128)(2,1)S(1)}, bf16[64,4096]{1,0:T(8,128)(2,1)S(1)}, u32[]{:S(2)}, u32[]{:S(2)}) collective-permute-start(bf16[64,4096]{1,0:T(8,128)(2,1)S(1)} %get-tuple-element.102), channel_id=1, source_target_pairs={{0,2},{4,0},{8,4},{12,8},{14,12},{10,14},{6,10},{2,6},{1,3},{5,1},... | collective-permute-start | bytes 1572872 | tf_op jit(solution)/shard_map/ppermute | solution.py:224
  256.9 21.6 %collective-permute-start.19 = (bf16[64,4096]{1,0:T(8,128)(2,1)S(1)}, bf16[64,4096]{1,0:T(8,128)(2,1)S(1)}, u32[]{:S(2)}, u32[]{:S(2)}) collective-permute-start(bf16[64,4096]{1,0:T(8,128)(2,1)S(1)} %get-tuple-element.101), channel_id=1, source_target_pairs={{0,4},{4,8},{8,12},{12,14},{14,10},{10,6},{6,2},{2,0},{1,5},{5,9},... | collective-permute-start | bytes 1572872 | tf_op jit(solution)/shard_map/ppermute | solution.py:224
  267.5 16.6 %collective-permute-start.25 = (bf16[64,4096]{1,0:T(8,128)(2,1)S(1)}, bf16[64,4096]{1,0:T(8,128)(2,1)S(1)}, u32[]{:S(2)}, u32[]{:S(2)}) collective-permute-start(bf16[64,4096]{1,0:T(8,128)(2,1)S(1)} %get-tuple-element.104), channel_id=1, source_target_pairs={{0,4},{4,8},{8,12},{12,14},{14,10},{10,6},{6,2},{2,0},{1,5},{5,9},... | collective-permute-start | bytes 1572872 | tf_op jit(solution)/shard_map/ppermute | solution.py:224
  267.6 16.5 %collective-permute-start.24 = (bf16[64,4096]{1,0:T(8,128)(2,1)S(1)}, bf16[64,4096]{1,0:T(8,128)(2,1)S(1)}, u32[]{:S(2)}, u32[]{:S(2)}) collective-permute-start(bf16[64,4096]{1,0:T(8,128)(2,1)S(1)} %get-tuple-element.103), channel_id=1, source_target_pairs={{0,2},{4,0},{8,4},{12,8},{14,12},{10,14},{6,10},{2,6},{1,3},{5,1},... | collective-permute-start | bytes 1572872 | tf_op jit(solution)/shard_map/ppermute | solution.py:224
  278.7 11.0 %collective-permute-start.23 = (bf16[64,4096]{1,0:T(8,128)(2,1)S(1)}, bf16[64,4096]{1,0:T(8,128)(2,1)S(1)}, u32[]{:S(2)}, u32[]{:S(2)}) collective-permute-start(bf16[64,4096]{1,0:T(8,128)(2,1)S(1)} %get-tuple-element.105), channel_id=1, source_target_pairs={{0,4},{4,8},{8,12},{12,14},{14,10},{10,6},{6,2},{2,0},{1,5},{5,9},... | collective-permute-start | bytes 1572872 | tf_op jit(solution)/shard_map/ppermute | solution.py:224
  278.8 14.2 %collective-permute-start.26 = (bf16[64,4096]{1,0:T(8,128)(2,1)S(1)}, bf16[64,4096]{1,0:T(8,128)(2,1)S(1)}, u32[]{:S(2)}, u32[]{:S(2)}) collective-permute-start(bf16[64,4096]{1,0:T(8,128)(2,1)S(1)} %get-tuple-element.106), channel_id=1, source_target_pairs={{0,2},{4,0},{8,4},{12,8},{14,12},{10,14},{6,10},{2,6},{1,3},{5,1},... | collective-permute-start | bytes 1572872 | tf_op jit(solution)/shard_map/ppermute | solution.py:224
  284.4 14.9 %collective-permute-start.29 = (bf16[64,4096]{1,0:T(8,128)(2,1)S(1)}, bf16[64,4096]{1,0:T(8,128)(2,1)S(1)}, u32[]{:S(2)}, u32[]{:S(2)}) collective-permute-start(bf16[64,4096]{1,0:T(8,128)(2,1)S(1)} %get-tuple-element.107), channel_id=1, source_target_pairs={{0,2},{4,0},{8,4},{12,8},{14,12},{10,14},{6,10},{2,6},{1,3},{5,1},... | collective-permute-start | bytes 1572872 | tf_op jit(solution)/shard_map/ppermute | solution.py:224
  286.1 16.7 %collective-permute-start.28 = (bf16[64,4096]{1,0:T(8,128)(2,1)S(1)}, bf16[64,4096]{1,0:T(8,128)(2,1)S(1)}, u32[]{:S(2)}, u32[]{:S(2)}) collective-permute-start(bf16[64,4096]{1,0:T(8,128)(2,1)S(1)} %get-tuple-element.108), channel_id=1, source_target_pairs={{0,4},{4,8},{8,12},{12,14},{14,10},{10,6},{6,2},{2,0},{1,5},{5,9},... | collective-permute-start | bytes 1572872 | tf_op jit(solution)/shard_map/ppermute | solution.py:224
  293.0 9.6 %collective-permute-start.27 = (bf16[64,4096]{1,0:T(8,128)(2,1)S(1)}, bf16[64,4096]{1,0:T(8,128)(2,1)S(1)}, u32[]{:S(2)}, u32[]{:S(2)}) collective-permute-start(bf16[64,4096]{1,0:T(8,128)(2,1)S(1)} %fusion.24), channel_id=1, source_target_pairs={{0,4},{4,8},{8,12},{12,14},{14,10},{10,6},{6,2},{2,0},{1,5},{5,9},... | collective-permute-start | bytes 1572872 | tf_op jit(solution)/shard_map/ppermute | solution.py:224
  302.8 9.2 %collective-permute-start.30 = (bf16[64,4096]{1,0:T(8,128)(2,1)S(1)}, bf16[64,4096]{1,0:T(8,128)(2,1)S(1)}, u32[]{:S(2)}, u32[]{:S(2)}) collective-permute-start(bf16[64,4096]{1,0:T(8,128)(2,1)S(1)} %fusion.13), channel_id=1, source_target_pairs={{0,2},{4,0},{8,4},{12,8},{14,12},{10,14},{6,10},{2,6},{1,3},{5,1},... | collective-permute-start | bytes 1572872 | tf_op jit(solution)/shard_map/ppermute | solution.py:224
  (19 other events, 448.8 us)

commit v16 on v15

--- a/solution.py
+++ b/solution.py
@@ -92,8 +92,8 @@
     exchange(2, far_first_y, far_second)
     exchange(7, arrived[4], far_first_y)
     exchange(3, arrived[4], far_first_y)
-    exchange(1, far_first_y)
-    near = [after(own, far_second, arrived[4], arrived[6], arrived[1]), beside, own_y, beside_y]
+    exchange(1, arrived[4], far_first_y)
+    near = [after(own, far_second, arrived[4], arrived[6]), beside, own_y, beside_y]
     far = [far_first, far_second, far_first_y, far_second_y]
     return near, far, [arrived[apart] for apart in range(LINE_MODELS)]
 
@@ -455,7 +455,8 @@
             for pool in (my_pool, 1 - my_pool)
         )
         pool_blocks = kv_pool[0]
-        got = lax.ppermute(pick_blocks(pool_blocks, others), "pool", [(0, 1), (1, 0)])
+        picked, normed = lax.optimization_barrier((pick_blocks(pool_blocks, others), normed))
+        got = lax.ppermute(picked, "pool", [(0, 1), (1, 0)])
         slots = jnp.stack([mine, jnp.arange(capacity, dtype=jnp.int32)])
         outgoing = pack_blocks((pool_blocks, got), slots, (models ^ my_model) * q_local // group_size)
         my_z, my_y = my_model // 2, my_model % 2
@@ -543,9 +544,13 @@
     ]
 
     order = [m for m in range(0, n_model, 2)] + [m for m in range(n_model - 1, 0, -2)]
-    spot = jnp.array([order.index(m) for m in range(n_model)], jnp.int32)[my_model]
-    places = jnp.array(order, jnp.int32)[(spot + models) % n_model]
-    places = (places + n_model - upper_half * (n_model // 2)) % n_model
+    half = n_model // 2
+    spot = jnp.where(my_model % 2 == 0, my_model // 2, n_model - 1 - my_model // 2)
+    places = []
+    for offset in range(n_model):
+        index = (spot + offset) % n_model
+        owner = jnp.where(index < half, 2 * index, 2 * (n_model - 1 - index) + 1)
+        places.append((owner + n_model - upper_half * half) % n_model)
     scatters = [
         RingScatter(
             share.reshape(n_model, row_count, -1), places, order, 1 if chunk % 2 == 0 else -1

time: 316 us -> 303 us (0.959)
  waiting for transfers between devices: 120 us -> 136 us
  between operations: 16.5 us -> 1.22 us
  starting transfers between devices: 68.5 us -> 59.6 us
    all_to_all x1, waiting for transfers between devices: 0.01 us -> 7.65 us  [on_device(): pairs = lax.all_to_all(pairs, 'mp', split_axis=0, concat_axis=0, tiled=True)]
    ppermute x14, starting transfers between devices: 48 us -> 41.1 us  [swap(): lax.ppermute(block, 'mp', [(index, index ^ mask) for index in range(LINE_...]
    ppermute x14, waiting for transfers between devices: 46.3 us -> 52.1 us  [step(): self.moving[way] = lax.ppermute(block, 'mp', pairs)]
  transfers between devices with their start and end apart: 32 -> 32, of which waited for: 17 -> 15; matrix products, arithmetic and copies ran while one was open for 9% -> 7% of each run, Pallas kernels for 12% -> 12%
where the time goes in v16:
time: 303 us; the launch traced here: 302 us
  waiting for transfers between devices  136 us (45%)
  Pallas kernels  62.6 us (21%)
  starting transfers between devices  59.6 us (20%)
  other arithmetic  17.1 us (6%)
  matrix products  16.2 us (5%)
  local copies, waits for them, and re-layouts  9.56 us (3%)
    ppermute x14, waiting for transfers between devices, swap(): lax.ppermute(block, 'mp', [(index, index ^ mask) for index in range(LINE_...  76.1 us
    ppermute x14, waiting for transfers between devices, step(): self.moving[way] = lax.ppermute(block, 'mp', pairs)  52.1 us
    ppermute x14, starting transfers between devices, swap(): lax.ppermute(block, 'mp', [(index, index ^ mask) for index in range(LINE_...  41.1 us
    pallas_call x2, Pallas kernels, project(): pl.pallas_call(project_kernel, grid=(width // depth,), out_shape=out_shap...  31.3 us
    pallas_call x1, Pallas kernels, attend(): pl.pallas_call(functools.partial(attend_kernel, span), grid=(heads,), out...  22.8 us
    dot_general x2, matrix products, on_device(): jnp.dot(mixed, w_out[:, chunk * width:(chunk + 1) * width], preferred_ele...  16.2 us
    ppermute x14, starting transfers between devices, step(): self.moving[way] = lax.ppermute(block, 'mp', pairs)  13.6 us
    all_to_all x1, waiting for transfers between devices, on_device(): pairs = lax.all_to_all(pairs, 'mp', split_axis=0, concat_axis=0, tiled=True)  7.65 us
  transfers between devices with their start and end apart: 32, of which 15 were waited for; matrix products, arithmetic and copies ran while one was open for 7% of the time, Pallas kernels for 12%

profile of v16, /device:TPU:0, one launch (start us, length us, event | category | flops | bytes accessed | tf_op | source)
XLA Modules:
  0.0 302.2 jit_solution(7452695845308018951)
XLA Ops:
  5.5 2.2 copy-done
  9.8 2.7 collective-permute-start
  14.1 22.2 %collective-permute-done.refs_1_ = bf16[64,8192]{1,0:T(8,128)(2,1)} collective-permute-done((bf16[64,8192]{1,0:T(8,128)(2,1)S(1)}, bf16[64,8192]{1,0:T(8,128)(2,1)}, u32[]{:S(2)}, u32[]{:S(2)}) %collective-permute-start) | collective-permute-done | bytes 1048608 | tf_op jit(solution)/shard_map/ppermute | solution.py:54
  36.3 3.3 %collective-permute-start.9 = (bf16[64,8192]{1,0:T(8,128)(2,1)}, bf16[64,8192]{1,0:T(8,128)(2,1)}, u32[]{:S(2)}, u32[]{:S(2)}) collective-permute-start(bf16[64,8192]{1,0:T(8,128)(2,1)} %collective-permute-done.8), channel_id=1, source_target_pairs={{0,4},{2,6},{4,0},{6,2},{8,12},{10,14},{12,8},{14,10},{1,5},{3,7},... | collective-permute-start | bytes 3145736 | tf_op jit(solution)/shard_map/ppermute | solution.py:54
  41.9 2.2 copy-done.1
  44.1 4.0 %pack_blocks.1 = (bf16[2,32,16,256]{3,2,1,0:T(8,128)(2,1)S(1)}, bf16[2,32,16,256]{3,2,1,0:T(8,128)(2,1)}, bf16[2,32,16,256]{3,2,1,0:T(8,128)(2,1)}, bf16[2,32,16...) custom-call(s32[2,32]{1,0:T(2,128)S(1)} %pad_add_fusion.slots_ref, ...), custom_call_target="tpu_custom_call" | custom-call | tf_op jit(solution)/shard_map/pack_blocks/pallas_call | solution.py:274
  48.1 14.9 %collective-permute-start.3 = (bf16[64,8192]{1,0:T(8,128)(2,1)}, bf16[64,8192]{1,0:T(8,128)(2,1)S(1)}, u32[]{:S(2)}, u32[]{:S(2)}) collective-permute-start(bf16[64,8192]{1,0:T(8,128)(2,1)} %collective-permute-done.1), channel_id=1, source_target_pairs={{0,4},{2,6},{4,0},{6,2},{8,12},{10,14},{12,8},{14,10},{1,5},{3,7},... | collective-permute-start | bytes 3145736 | tf_op jit(solution)/shard_map/ppermute | solution.py:54
  69.5 27.2 %collective-permute-done.3 = bf16[64,8192]{1,0:T(8,128)(2,1)S(1)} collective-permute-done((bf16[64,8192]{1,0:T(8,128)(2,1)}, bf16[64,8192]{1,0:T(8,128)(2,1)S(1)}, u32[]{:S(2)}, u32[]{:S(2)}) %collective-permute-start.3) | collective-permute-done | bytes 1048608 | tf_op jit(solution)/shard_map/ppermute | solution.py:54
  104.0 6.1 %collective-permute-done.5 = bf16[2,32,16,256]{3,2,1,0:T(8,128)(2,1)S(1)} collective-permute-done((bf16[2,32,16,256]{3,2,1,0:T(8,128)(2,1)S(1)}, bf16[2,32,16,256]{3,2,1,0:T(8,128)(2,1)S(1)}, u32[]{:S(2)}, u32[]{:S(2)}) %collective-permute-start.5) | collective-permute-done | bytes 524320 | tf_op jit(solution)/shard_map/ppermute | solution.py:54
  113.6 2.5 collective-permute-start.15
  116.1 15.7 %project.2 = (bf16[8,256,128]{2,1,0:T(8,128)(2,1)}, bf16[256,128]{1,0:T(8,128)(2,1)}, bf16[256,256]{1,0:T(8,128)(2,1)}, bf16[256,256]{1,0:T(8,128)(2,1)}) custom-call(s32[4]{0:T(128)} %add_multiply_fusion.starts_ref, bf16[64,8192]{1,0:T(8,128)(2,1)} %copy-done.10, bf16[64,8192]{1,0:T(8,128)(2,1)} %collective-permute-done.refs_1_, ...), custom_call_target="tpu_custom_call" | custom-call | flops 5368709120 | bytes 26476544 | tf_op jit(solution)/shard_map/project/pallas_call | solution.py:177
  131.8 20.6 %collective-permute-done.11.refs_3_ = bf16[64,8192]{1,0:T(8,128)(2,1)} collective-permute-done((bf16[64,8192]{1,0:T(8,128)(2,1)}, bf16[64,8192]{1,0:T(8,128)(2,1)}, u32[]{:S(2)}, u32[]{:S(2)}) %collective-permute-start.11) | collective-permute-done | bytes 1048608 | tf_op jit(solution)/shard_map/ppermute | solution.py:54
  152.4 5.4 %collective-permute-start.16 = (bf16[2,32,16,256]{3,2,1,0:T(8,128)(2,1)}, bf16[2,32,16,256]{3,2,1,0:T(8,128)(2,1)}, u32[]{:S(2)}, u32[]{:S(2)}) collective-permute-start(bf16[2,32,16,256]{3,2,1,0:T(8,128)(2,1)} %get-tuple-element.82), channel_id=1, source_target_pairs={{0,14},{2,12},{4,10},{6,8},{8,6},{10,4},{12,2},{14,0},{1,15},{3,13... | collective-permute-start | bytes 1572872 | tf_op jit(solution)/shard_map/ppermute | solution.py:54
  157.8 15.6 %project.3 = (bf16[8,256,128]{2,1,0:T(8,128)(2,1)}, bf16[256,128]{1,0:T(8,128)(2,1)}, bf16[256,256]{1,0:T(8,128)(2,1)}, bf16[256,256]{1,0:T(8,128)(2,1)}) custom-call(s32[4]{0:T(128)} %add_multiply_fusion.1.starts_ref, bf16[64,8192]{1,0:T(8,128)(2,1)} %copy-done.11, bf16[64,8192]{1,0:T(8,128)(2,1)} %broadcast_select_fusion.1.refs_1_, ...), custom_call_target="tpu_custom_call" | custom-call | flops 5368709120 | bytes 26476544 | tf_op jit(solution)/shard_map/project/pallas_call | solution.py:177
  175.3 4.2 %all-to-all-start = ((bf16[8,64,256]{2,1,0:T(8,128)(2,1)}), bf16[8,64,256]{2,1,0:T(8,128)(2,1)}, u32[]{:S(2)}, u32[]{:S(2)}) async-start(bf16[8,64,256]{2,1,0:T(8,128)(2,1)} %bitcast.108), calls=%async_computation | async-start | bytes 524288 | tf_op jit(solution)/shard_map/all_to_all | solution.py:527
  180.0 7.6 %all-to-all-done = bf16[8,64,256]{2,1,0:T(8,128)(2,1)} async-done(((bf16[8,64,256]{2,1,0:T(8,128)(2,1)}), bf16[8,64,256]{2,1,0:T(8,128)(2,1)}, u32[]{:S(2)}, u32[]{:S(2)}) %all-to-all-start) | async-done | bytes 262176 | tf_op jit(solution)/shard_map/all_to_all | solution.py:527
  187.6 3.7 %order_blocks.1 = (bf16[4096,128]{1,0:T(8,128)(2,1)S(1)}, bf16[4096,256]{1,0:T(8,128)(2,1)S(1)}) custom-call(s32[1]{0:T(128)} %dynamic_slice.64.length_ref, s32[256]{0:T(256)S(1)} %multiply_add_fusion.where_ref, bf16[64,16,256]{2,1,0:T(8,128)(2,1)S(1)} %bitcast.92, bf16[64,16,256]{2,1,0:T(8,128)(2,1)S(1)} %bitcast.95, bf16[64,16,256]{2,1,0:T(8,128)(2,1)S(1)} %bitcast.96, ...), custom_call_target="tpu_custom_call" | custom-call | tf_op jit(solution)/shard_map/order_blocks/pallas_call | solution.py:319
  191.4 22.8 %attend.1 = bf16[512,1024]{1,0:T(8,128)(2,1)S(1)} custom-call(s32[1]{0:T(128)} %bitcast.half_ref, bf16[8,256,128]{2,1,0:T(8,128)(2,1)S(1)} %copy-done.4, bf16[8,256,128]{2,1,0:T(8,128)(2,1)S(1)} %copy-done.5, bf16[4096,128]{1,0:T(8,128)(2,1)S(1)} %get-tuple-element.95.refs_2_, bf16[4096,256]{1,0:T(8,128)(2,1)S(1)} %get-tuple-element.96.refs_3_, ...), custom_call_target="tpu_custom_call" | custom-call | flops 19327352832 | bytes 5636096 | tf_op jit(solution)/shard_map/attend/pallas_call | solution.py:391
  214.2 8.1 %fusion.4 = bf16[512,4096]{1,0:T(8,128)(2,1)S(1)} fusion(bf16[512,1024]{1,0:T(8,128)(2,1)S(1)} %attend.1, bf16[1024,8192]{1,0:T(8,128)(2,1)} %param.21), kind=kOutput, calls=%fused_computation.4 | convolution fusion | flops 4297064448 | bytes 13631488 | tf_op jit(solution)/shard_map/dot_general | solution.py:538
  222.5 2.0 collective-permute-start.17
  224.5 8.1 %fusion.7 = bf16[512,4096]{1,0:T(8,128)(2,1)S(1)} fusion(bf16[512,1024]{1,0:T(8,128)(2,1)S(1)} %attend.1, bf16[1024,8192]{1,0:T(8,128)(2,1)} %param.21), kind=kOutput, calls=%fused_computation.5 | convolution fusion | flops 4297064448 | bytes 13631488 | tf_op jit(solution)/shard_map/dot_general | solution.py:538
  232.7 2.0 collective-permute-start.21
  234.7 2.6 collective-permute-done.18
  239.7 8.9 %collective-permute-done.22 = bf16[64,4096]{1,0:T(8,128)(2,1)S(1)} collective-permute-done((bf16[64,4096]{1,0:T(8,128)(2,1)S(1)}, bf16[64,4096]{1,0:T(8,128)(2,1)S(1)}, u32[]{:S(2)}, u32[]{:S(2)}) %collective-permute-start.22) | collective-permute-done | bytes 524320 | tf_op jit(solution)/shard_map/ppermute | solution.py:224
  248.9 2.0 collective-permute-start.25
  250.9 8.8 %collective-permute-done.20 = bf16[64,4096]{1,0:T(8,128)(2,1)S(1)} collective-permute-done((bf16[64,4096]{1,0:T(8,128)(2,1)S(1)}, bf16[64,4096]{1,0:T(8,128)(2,1)S(1)}, u32[]{:S(2)}, u32[]{:S(2)}) %collective-permute-start.20) | collective-permute-done | bytes 524320 | tf_op jit(solution)/shard_map/ppermute | solution.py:224
  260.1 2.0 collective-permute-start.23
  262.2 8.9 %collective-permute-done.25 = bf16[64,4096]{1,0:T(8,128)(2,1)S(1)} collective-permute-done((bf16[64,4096]{1,0:T(8,128)(2,1)S(1)}, bf16[64,4096]{1,0:T(8,128)(2,1)S(1)}, u32[]{:S(2)}, u32[]{:S(2)}) %collective-permute-start.25) | collective-permute-done | bytes 524320 | tf_op jit(solution)/shard_map/ppermute | solution.py:224
  273.4 5.8 %collective-permute-done.23 = bf16[64,4096]{1,0:T(8,128)(2,1)S(1)} collective-permute-done((bf16[64,4096]{1,0:T(8,128)(2,1)S(1)}, bf16[64,4096]{1,0:T(8,128)(2,1)S(1)}, u32[]{:S(2)}, u32[]{:S(2)}) %collective-permute-start.23) | collective-permute-done | bytes 524320 | tf_op jit(solution)/shard_map/ppermute | solution.py:224
  279.7 2.3 collective-permute-done.29
  282.1 8.4 %collective-permute-done.27 = bf16[64,4096]{1,0:T(8,128)(2,1)S(1)} collective-permute-done((bf16[64,4096]{1,0:T(8,128)(2,1)S(1)}, bf16[64,4096]{1,0:T(8,128)(2,1)S(1)}, u32[]{:S(2)}, u32[]{:S(2)}) %collective-permute-start.27) | collective-permute-done | bytes 524320 | tf_op jit(solution)/shard_map/ppermute | solution.py:224
  293.6 6.3 %collective-permute-done.30 = bf16[64,4096]{1,0:T(8,128)(2,1)S(1)} collective-permute-done((bf16[64,4096]{1,0:T(8,128)(2,1)S(1)}, bf16[64,4096]{1,0:T(8,128)(2,1)S(1)}, u32[]{:S(2)}, u32[]{:S(2)}) %collective-permute-start.30) | collective-permute-done | bytes 524320 | tf_op jit(solution)/shard_map/ppermute | solution.py:224
  (124 shorter events, 41.8 us)
Async XLA Ops:
  9.3 32.6 %collective-permute-start.2 = (bf16[32,16,2048]{2,1,0:T(8,128)(2,1)S(1)}, bf16[32,16,2048]{2,1,0:T(8,128)(2,1)}, u32[]{:S(2)}, u32[]{:S(2)}) collective-permute-start(bf16[32,16,2048]{2,1,0:T(8,128)(2,1)S(1)} %pick_blocks.1), channel_id=1, source_target_pairs={{0,1},{1,0},{2,3},{3,2},{4,5},{5,4},{6,7},{7,6},{8,9},{9,8},{10,11... | collective-permute-start | bytes 6291464 | tf_op jit(solution)/shard_map/ppermute | solution.py:459
  9.8 26.5 %collective-permute-start = (bf16[64,8192]{1,0:T(8,128)(2,1)S(1)}, bf16[64,8192]{1,0:T(8,128)(2,1)}, u32[]{:S(2)}, u32[]{:S(2)}) collective-permute-start(bf16[64,8192]{1,0:T(8,128)(2,1)S(1)} %fusion.12.refs_0_), channel_id=1, source_target_pairs={{0,4},{2,6},{4,0},{6,2},{8,12},{10,14},{12,8},{14,10},{1,5},{3,7},... | collective-permute-start | bytes 3145736 | tf_op jit(solution)/shard_map/ppermute | solution.py:54
  12.4 23.9 %collective-permute-start.8 = (bf16[64,8192]{1,0:T(8,128)(2,1)S(1)}, bf16[64,8192]{1,0:T(8,128)(2,1)}, u32[]{:S(2)}, u32[]{:S(2)}) collective-permute-start(bf16[64,8192]{1,0:T(8,128)(2,1)S(1)} %fusion.12.refs_0_), channel_id=1, source_target_pairs={{0,1},{1,0},{2,3},{3,2},{4,8},{5,9},{6,10},{7,11},{8,4},{9,5},{10,... | collective-permute-start | bytes 3145736 | tf_op jit(solution)/shard_map/ppermute | solution.py:65
  12.6 27.7 %collective-permute-start.6 = (bf16[64,8192]{1,0:T(8,128)(2,1)S(1)}, bf16[64,8192]{1,0:T(8,128)(2,1)}, u32[]{:S(2)}, u32[]{:S(2)}) collective-permute-start(bf16[64,8192]{1,0:T(8,128)(2,1)S(1)} %fusion.12.refs_0_), channel_id=1, source_target_pairs={{0,2},{2,0},{4,6},{6,4},{8,10},{10,8},{12,14},{14,12},{1,3},{3,1},... | collective-permute-start | bytes 3145736 | tf_op jit(solution)/shard_map/ppermute | solution.py:54
  36.3 11.8 %collective-permute-start.1 = (bf16[64,8192]{1,0:T(8,128)(2,1)}, bf16[64,8192]{1,0:T(8,128)(2,1)}, u32[]{:S(2)}, u32[]{:S(2)}) collective-permute-start(bf16[64,8192]{1,0:T(8,128)(2,1)} %collective-permute-done.refs_1_), channel_id=1, source_target_pairs={{0,1},{1,0},{2,3},{3,2},{4,8},{5,9},{6,10},{7,11},{8,4},{9,5},{10,... | collective-permute-start | bytes 3145736 | tf_op jit(solution)/shard_map/ppermute | solution.py:65
  36.3 29.3 %collective-permute-start.9 = (bf16[64,8192]{1,0:T(8,128)(2,1)}, bf16[64,8192]{1,0:T(8,128)(2,1)}, u32[]{:S(2)}, u32[]{:S(2)}) collective-permute-start(bf16[64,8192]{1,0:T(8,128)(2,1)} %collective-permute-done.8), channel_id=1, source_target_pairs={{0,4},{2,6},{4,0},{6,2},{8,12},{10,14},{12,8},{14,10},{1,5},{3,7},... | collective-permute-start | bytes 3145736 | tf_op jit(solution)/shard_map/ppermute | solution.py:54
  40.3 26.7 %collective-permute-start.7 = (bf16[64,8192]{1,0:T(8,128)(2,1)}, bf16[64,8192]{1,0:T(8,128)(2,1)S(1)}, u32[]{:S(2)}, u32[]{:S(2)}) collective-permute-start(bf16[64,8192]{1,0:T(8,128)(2,1)} %collective-permute-done.refs_1_), channel_id=1, source_target_pairs={{0,2},{2,0},{4,6},{6,4},{8,10},{10,8},{12,14},{14,12},{1,3},{3,1},... | collective-permute-start | bytes 3145736 | tf_op jit(solution)/shard_map/ppermute | solution.py:54
  48.1 48.5 %collective-permute-start.3 = (bf16[64,8192]{1,0:T(8,128)(2,1)}, bf16[64,8192]{1,0:T(8,128)(2,1)S(1)}, u32[]{:S(2)}, u32[]{:S(2)}) collective-permute-start(bf16[64,8192]{1,0:T(8,128)(2,1)} %collective-permute-done.1), channel_id=1, source_target_pairs={{0,4},{2,6},{4,0},{6,2},{8,12},{10,14},{12,8},{14,10},{1,5},{3,7},... | collective-permute-start | bytes 3145736 | tf_op jit(solution)/shard_map/ppermute | solution.py:54
  63.1 40.9 %collective-permute-start.4 = (bf16[2,32,16,256]{3,2,1,0:T(8,128)(2,1)S(1)}, bf16[2,32,16,256]{3,2,1,0:T(8,128)(2,1)S(1)}, u32[]{:S(2)}, u32[]{:S(2)}) collective-permute-start(bf16[2,32,16,256]{3,2,1,0:T(8,128)(2,1)S(1)} %get-tuple-element.63), channel_id=1, source_target_pairs={{0,8},{2,10},{4,12},{6,14},{8,0},{10,2},{12,4},{14,6},{1,9},{3,11}... | collective-permute-start | bytes 1572872 | tf_op jit(solution)/shard_map/ppermute | solution.py:54
  64.1 45.9 %collective-permute-start.5 = (bf16[2,32,16,256]{3,2,1,0:T(8,128)(2,1)S(1)}, bf16[2,32,16,256]{3,2,1,0:T(8,128)(2,1)S(1)}, u32[]{:S(2)}, u32[]{:S(2)}) collective-permute-start(bf16[2,32,16,256]{3,2,1,0:T(8,128)(2,1)S(1)} %get-tuple-element.65), channel_id=1, source_target_pairs={{0,12},{2,14},{4,8},{6,10},{8,4},{10,6},{12,0},{14,2},{1,13},{3,15... | collective-permute-start | bytes 1572872 | tf_op jit(solution)/shard_map/ppermute | solution.py:54
  68.0 29.8 %collective-permute-start.10 = (bf16[64,8192]{1,0:T(8,128)(2,1)S(1)}, bf16[64,8192]{1,0:T(8,128)(2,1)S(1)}, u32[]{:S(2)}, u32[]{:S(2)}) collective-permute-start(bf16[64,8192]{1,0:T(8,128)(2,1)S(1)} %broadcast_select_fusion.refs_0_), channel_id=1, source_target_pairs={{0,2},{2,0},{4,6},{6,4},{8,10},{10,8},{12,14},{14,12},{1,3},{3,1},... | collective-permute-start | bytes 3145736 | tf_op jit(solution)/shard_map/ppermute | solution.py:54
  97.8 54.6 %collective-permute-start.11 = (bf16[64,8192]{1,0:T(8,128)(2,1)}, bf16[64,8192]{1,0:T(8,128)(2,1)}, u32[]{:S(2)}, u32[]{:S(2)}) collective-permute-start(bf16[64,8192]{1,0:T(8,128)(2,1)} %broadcast_select_fusion.1.refs_1_), channel_id=1, source_target_pairs={{0,2},{2,0},{4,6},{6,4},{8,10},{10,8},{12,14},{14,12},{1,3},{3,1},... | collective-permute-start | bytes 3145736 | tf_op jit(solution)/shard_map/ppermute | solution.py:54
  110.1 69.9 %collective-permute-start.12 = (bf16[2,32,16,256]{3,2,1,0:T(8,128)(2,1)}, bf16[2,32,16,256]{3,2,1,0:T(8,128)(2,1)S(1)}, u32[]{:S(2)}, u32[]{:S(2)}) collective-permute-start(bf16[2,32,16,256]{3,2,1,0:T(8,128)(2,1)} %get-tuple-element.74), channel_id=1, source_target_pairs={{0,2},{2,0},{4,6},{6,4},{8,10},{10,8},{12,14},{14,12},{1,3},{3,1},... | collective-permute-start | bytes 1572872 | tf_op jit(solution)/shard_map/ppermute | solution.py:54
  111.6 68.4 %collective-permute-start.13 = (bf16[2,32,16,256]{3,2,1,0:T(8,128)(2,1)}, bf16[2,32,16,256]{3,2,1,0:T(8,128)(2,1)S(1)}, u32[]{:S(2)}, u32[]{:S(2)}) collective-permute-start(bf16[2,32,16,256]{3,2,1,0:T(8,128)(2,1)} %get-tuple-element.76), channel_id=1, source_target_pairs={{0,4},{2,6},{4,0},{6,2},{8,12},{10,14},{12,8},{14,10},{1,5},{3,7},... | collective-permute-start | bytes 1572872 | tf_op jit(solution)/shard_map/ppermute | solution.py:54
  111.6 68.4 %collective-permute-start.14 = (bf16[2,32,16,256]{3,2,1,0:T(8,128)(2,1)}, bf16[2,32,16,256]{3,2,1,0:T(8,128)(2,1)S(1)}, u32[]{:S(2)}, u32[]{:S(2)}) collective-permute-start(bf16[2,32,16,256]{3,2,1,0:T(8,128)(2,1)} %copy-done.3), channel_id=1, source_target_pairs={{0,6},{2,4},{4,2},{6,0},{8,14},{10,12},{12,10},{14,8},{1,7},{3,5},... | collective-permute-start | bytes 1572872 | tf_op jit(solution)/shard_map/ppermute | solution.py:54
  113.6 66.4 %collective-permute-start.15 = (bf16[2,32,16,256]{3,2,1,0:T(8,128)(2,1)}, bf16[2,32,16,256]{3,2,1,0:T(8,128)(2,1)}, u32[]{:S(2)}, u32[]{:S(2)}) collective-permute-start(bf16[2,32,16,256]{3,2,1,0:T(8,128)(2,1)} %copy-done.2), channel_id=1, source_target_pairs={{0,10},{2,8},{4,14},{6,12},{8,2},{10,0},{12,6},{14,4},{1,11},{3,9}... | collective-permute-start | bytes 1572872 | tf_op jit(solution)/shard_map/ppermute | solution.py:54
  152.4 27.6 %collective-permute-start.16 = (bf16[2,32,16,256]{3,2,1,0:T(8,128)(2,1)}, bf16[2,32,16,256]{3,2,1,0:T(8,128)(2,1)}, u32[]{:S(2)}, u32[]{:S(2)}) collective-permute-start(bf16[2,32,16,256]{3,2,1,0:T(8,128)(2,1)} %get-tuple-element.82), channel_id=1, source_target_pairs={{0,14},{2,12},{4,10},{6,8},{8,6},{10,4},{12,2},{14,0},{1,15},{3,13... | collective-permute-start | bytes 1572872 | tf_op jit(solution)/shard_map/ppermute | solution.py:54
  175.3 12.3 %all-to-all-start = ((bf16[8,64,256]{2,1,0:T(8,128)(2,1)}), bf16[8,64,256]{2,1,0:T(8,128)(2,1)}, u32[]{:S(2)}, u32[]{:S(2)}) async-start(bf16[8,64,256]{2,1,0:T(8,128)(2,1)} %bitcast.108), calls=%async_computation | async-start | bytes 524288 | tf_op jit(solution)/shard_map/all_to_all | solution.py:527
  222.4 14.9 %collective-permute-start.18 = (bf16[64,4096]{1,0:T(8,128)(2,1)S(1)}, bf16[64,4096]{1,0:T(8,128)(2,1)S(1)}, u32[]{:S(2)}, u32[]{:S(2)}) collective-permute-start(bf16[64,4096]{1,0:T(8,128)(2,1)S(1)} %get-tuple-element.102), channel_id=1, source_target_pairs={{0,2},{4,0},{8,4},{12,8},{14,12},{10,14},{6,10},{2,6},{1,3},{5,1},... | collective-permute-start | bytes 1572872 | tf_op jit(solution)/shard_map/ppermute | solution.py:224
  222.5 14.9 %collective-permute-start.17 = (bf16[64,4096]{1,0:T(8,128)(2,1)S(1)}, bf16[64,4096]{1,0:T(8,128)(2,1)S(1)}, u32[]{:S(2)}, u32[]{:S(2)}) collective-permute-start(bf16[64,4096]{1,0:T(8,128)(2,1)S(1)} %get-tuple-element.101), channel_id=1, source_target_pairs={{0,4},{4,8},{8,12},{12,14},{14,10},{10,6},{6,2},{2,0},{1,5},{5,9},... | collective-permute-start | bytes 1572872 | tf_op jit(solution)/shard_map/ppermute | solution.py:224
  232.6 16.0 %collective-permute-start.22 = (bf16[64,4096]{1,0:T(8,128)(2,1)S(1)}, bf16[64,4096]{1,0:T(8,128)(2,1)S(1)}, u32[]{:S(2)}, u32[]{:S(2)}) collective-permute-start(bf16[64,4096]{1,0:T(8,128)(2,1)S(1)} %get-tuple-element.104), channel_id=1, source_target_pairs={{0,4},{4,8},{8,12},{12,14},{14,10},{10,6},{6,2},{2,0},{1,5},{5,9},... | collective-permute-start | bytes 1572872 | tf_op jit(solution)/shard_map/ppermute | solution.py:224
  232.7 15.9 %collective-permute-start.21 = (bf16[64,4096]{1,0:T(8,128)(2,1)S(1)}, bf16[64,4096]{1,0:T(8,128)(2,1)S(1)}, u32[]{:S(2)}, u32[]{:S(2)}) collective-permute-start(bf16[64,4096]{1,0:T(8,128)(2,1)S(1)} %get-tuple-element.103), channel_id=1, source_target_pairs={{0,2},{4,0},{8,4},{12,8},{14,12},{10,14},{6,10},{2,6},{1,3},{5,1},... | collective-permute-start | bytes 1572872 | tf_op jit(solution)/shard_map/ppermute | solution.py:224
  237.6 22.1 %collective-permute-start.20 = (bf16[64,4096]{1,0:T(8,128)(2,1)S(1)}, bf16[64,4096]{1,0:T(8,128)(2,1)S(1)}, u32[]{:S(2)}, u32[]{:S(2)}) collective-permute-start(bf16[64,4096]{1,0:T(8,128)(2,1)S(1)} %get-tuple-element.106), channel_id=1, source_target_pairs={{0,2},{4,0},{8,4},{12,8},{14,12},{10,14},{6,10},{2,6},{1,3},{5,1},... | collective-permute-start | bytes 1572872 | tf_op jit(solution)/shard_map/ppermute | solution.py:224
  239.1 20.7 %collective-permute-start.19 = (bf16[64,4096]{1,0:T(8,128)(2,1)S(1)}, bf16[64,4096]{1,0:T(8,128)(2,1)S(1)}, u32[]{:S(2)}, u32[]{:S(2)}) collective-permute-start(bf16[64,4096]{1,0:T(8,128)(2,1)S(1)} %get-tuple-element.105), channel_id=1, source_target_pairs={{0,4},{4,8},{8,12},{12,14},{14,10},{10,6},{6,2},{2,0},{1,5},{5,9},... | collective-permute-start | bytes 1572872 | tf_op jit(solution)/shard_map/ppermute | solution.py:224
  248.9 22.2 %collective-permute-start.25 = (bf16[64,4096]{1,0:T(8,128)(2,1)S(1)}, bf16[64,4096]{1,0:T(8,128)(2,1)S(1)}, u32[]{:S(2)}, u32[]{:S(2)}) collective-permute-start(bf16[64,4096]{1,0:T(8,128)(2,1)S(1)} %get-tuple-element.108), channel_id=1, source_target_pairs={{0,4},{4,8},{8,12},{12,14},{14,10},{10,6},{6,2},{2,0},{1,5},{5,9},... | collective-permute-start | bytes 1572872 | tf_op jit(solution)/shard_map/ppermute | solution.py:224
  250.9 20.2 %collective-permute-start.24 = (bf16[64,4096]{1,0:T(8,128)(2,1)S(1)}, bf16[64,4096]{1,0:T(8,128)(2,1)S(1)}, u32[]{:S(2)}, u32[]{:S(2)}) collective-permute-start(bf16[64,4096]{1,0:T(8,128)(2,1)S(1)} %get-tuple-element.107), channel_id=1, source_target_pairs={{0,2},{4,0},{8,4},{12,8},{14,12},{10,14},{6,10},{2,6},{1,3},{5,1},... | collective-permute-start | bytes 1572872 | tf_op jit(solution)/shard_map/ppermute | solution.py:224
  260.1 19.2 %collective-permute-start.23 = (bf16[64,4096]{1,0:T(8,128)(2,1)S(1)}, bf16[64,4096]{1,0:T(8,128)(2,1)S(1)}, u32[]{:S(2)}, u32[]{:S(2)}) collective-permute-start(bf16[64,4096]{1,0:T(8,128)(2,1)S(1)} %get-tuple-element.109), channel_id=1, source_target_pairs={{0,4},{4,8},{8,12},{12,14},{14,10},{10,6},{6,2},{2,0},{1,5},{5,9},... | collective-permute-start | bytes 1572872 | tf_op jit(solution)/shard_map/ppermute | solution.py:224
  262.1 17.3 %collective-permute-start.26 = (bf16[64,4096]{1,0:T(8,128)(2,1)S(1)}, bf16[64,4096]{1,0:T(8,128)(2,1)S(1)}, u32[]{:S(2)}, u32[]{:S(2)}) collective-permute-start(bf16[64,4096]{1,0:T(8,128)(2,1)S(1)} %get-tuple-element.110), channel_id=1, source_target_pairs={{0,2},{4,0},{8,4},{12,8},{14,12},{10,14},{6,10},{2,6},{1,3},{5,1},... | collective-permute-start | bytes 1572872 | tf_op jit(solution)/shard_map/ppermute | solution.py:224
  271.3 10.7 %collective-permute-start.29 = (bf16[64,4096]{1,0:T(8,128)(2,1)S(1)}, bf16[64,4096]{1,0:T(8,128)(2,1)S(1)}, u32[]{:S(2)}, u32[]{:S(2)}) collective-permute-start(bf16[64,4096]{1,0:T(8,128)(2,1)S(1)} %get-tuple-element.111), channel_id=1, source_target_pairs={{0,2},{4,0},{8,4},{12,8},{14,12},{10,14},{6,10},{2,6},{1,3},{5,1},... | collective-permute-start | bytes 1572872 | tf_op jit(solution)/shard_map/ppermute | solution.py:224
  272.8 17.9 %collective-permute-start.28 = (bf16[64,4096]{1,0:T(8,128)(2,1)S(1)}, bf16[64,4096]{1,0:T(8,128)(2,1)S(1)}, u32[]{:S(2)}, u32[]{:S(2)}) collective-permute-start(bf16[64,4096]{1,0:T(8,128)(2,1)S(1)} %get-tuple-element.112), channel_id=1, source_target_pairs={{0,4},{4,8},{8,12},{12,14},{14,10},{10,6},{6,2},{2,0},{1,5},{5,9},... | collective-permute-start | bytes 1572872 | tf_op jit(solution)/shard_map/ppermute | solution.py:224
  279.4 11.1 %collective-permute-start.27 = (bf16[64,4096]{1,0:T(8,128)(2,1)S(1)}, bf16[64,4096]{1,0:T(8,128)(2,1)S(1)}, u32[]{:S(2)}, u32[]{:S(2)}) collective-permute-start(bf16[64,4096]{1,0:T(8,128)(2,1)S(1)} %fusion.24), channel_id=1, source_target_pairs={{0,4},{4,8},{8,12},{12,14},{14,10},{10,6},{6,2},{2,0},{1,5},{5,9},... | collective-permute-start | bytes 1572872 | tf_op jit(solution)/shard_map/ppermute | solution.py:224
  290.7 9.2 %collective-permute-start.30 = (bf16[64,4096]{1,0:T(8,128)(2,1)S(1)}, bf16[64,4096]{1,0:T(8,128)(2,1)S(1)}, u32[]{:S(2)}, u32[]{:S(2)}) collective-permute-start(bf16[64,4096]{1,0:T(8,128)(2,1)S(1)} %fusion.13), channel_id=1, source_target_pairs={{0,2},{4,0},{8,4},{12,8},{14,12},{10,14},{6,10},{2,6},{1,3},{5,1},... | collective-permute-start | bytes 1572872 | tf_op jit(solution)/shard_map/ppermute | solution.py:224
  (20 other events, 373.0 us)

commit v17 on v16

--- a/solution.py
+++ b/solution.py
@@ -91,8 +91,8 @@
     exchange(5, far_first_y, far_second)
     exchange(2, far_first_y, far_second)
     exchange(7, arrived[4], far_first_y)
-    exchange(3, arrived[4], far_first_y)
-    exchange(1, arrived[4], far_first_y)
+    exchange(3, far_second_y)
+    exchange(1, far_second_y)
     near = [after(own, far_second, arrived[4], arrived[6]), beside, own_y, beside_y]
     far = [far_first, far_second, far_first_y, far_second_y]
     return near, far, [arrived[apart] for apart in range(LINE_MODELS)]

time: 303 us -> 300 us (0.990)
  waiting for transfers between devices: 136 us -> 116 us
  starting transfers between devices: 59.6 us -> 76.1 us
    all_to_all x1, starting transfers between devices: 4.22 us -> 24.5 us  [on_device(): pairs = lax.all_to_all(pairs, 'mp', split_axis=0, concat_axis=0, tiled=True)]
    ppermute x14, waiting for transfers between devices: 76.1 us -> 56.3 us  [swap(): lax.ppermute(block, 'mp', [(index, index ^ mask) for index in range(LINE_...]
    ppermute x14, starting transfers between devices: 41.1 us -> 36.3 us  [swap(): lax.ppermute(block, 'mp', [(index, index ^ mask) for index in range(LINE_...]
where the time goes in v17:
time: 300 us; the launch traced here: 299 us
  waiting for transfers between devices  116 us (39%)
  starting transfers between devices  76.1 us (25%)
  Pallas kernels  62.7 us (21%)
  other arithmetic  17.1 us (6%)
  matrix products  16.2 us (5%)
  local copies, waits for them, and re-layouts  9.56 us (3%)
    ppermute x14, waiting for transfers between devices, swap(): lax.ppermute(block, 'mp', [(index, index ^ mask) for index in range(LINE_...  56.3 us
    ppermute x14, waiting for transfers between devices, step(): self.moving[way] = lax.ppermute(block, 'mp', pairs)  51.9 us
    ppermute x14, starting transfers between devices, swap(): lax.ppermute(block, 'mp', [(index, index ^ mask) for index in range(LINE_...  36.3 us
    pallas_call x2, Pallas kernels, project(): pl.pallas_call(project_kernel, grid=(width // depth,), out_shape=out_shap...  31.3 us
    all_to_all x1, starting transfers between devices, on_device(): pairs = lax.all_to_all(pairs, 'mp', split_axis=0, concat_axis=0, tiled=True)  24.5 us
    pallas_call x1, Pallas kernels, attend(): pl.pallas_call(functools.partial(attend_kernel, span), grid=(heads,), out...  22.9 us
    dot_general x2, matrix products, on_device(): jnp.dot(mixed, w_out[:, chunk * width:(chunk + 1) * width], preferred_ele...  16.2 us
    ppermute x14, starting transfers between devices, step(): self.moving[way] = lax.ppermute(block, 'mp', pairs)  14.6 us
  transfers between devices with their start and end apart: 32, of which 15 were waited for; matrix products, arithmetic and copies ran while one was open for 7% of the time, Pallas kernels for 12%

profile of v17, /device:TPU:0, one launch (start us, length us, event | category | flops | bytes accessed | tf_op | source)
XLA Modules:
  0.0 299.0 jit_solution(16656362252703178294)
XLA Ops:
  5.5 2.2 copy-done
  9.8 2.7 collective-permute-start
  14.1 22.2 %collective-permute-done.refs_1_ = bf16[64,8192]{1,0:T(8,128)(2,1)} collective-permute-done((bf16[64,8192]{1,0:T(8,128)(2,1)S(1)}, bf16[64,8192]{1,0:T(8,128)(2,1)}, u32[]{:S(2)}, u32[]{:S(2)}) %collective-permute-start) | collective-permute-done | bytes 1048608 | tf_op jit(solution)/shard_map/ppermute | solution.py:54
  36.3 3.3 %collective-permute-start.9 = (bf16[64,8192]{1,0:T(8,128)(2,1)}, bf16[64,8192]{1,0:T(8,128)(2,1)}, u32[]{:S(2)}, u32[]{:S(2)}) collective-permute-start(bf16[64,8192]{1,0:T(8,128)(2,1)} %collective-permute-done.8), channel_id=1, source_target_pairs={{0,4},{2,6},{4,0},{6,2},{8,12},{10,14},{12,8},{14,10},{1,5},{3,7},... | collective-permute-start | bytes 3145736 | tf_op jit(solution)/shard_map/ppermute | solution.py:54
  41.9 2.2 copy-done.1
  44.1 4.1 %pack_blocks.1 = (bf16[2,32,16,256]{3,2,1,0:T(8,128)(2,1)S(1)}, bf16[2,32,16,256]{3,2,1,0:T(8,128)(2,1)}, bf16[2,32,16,256]{3,2,1,0:T(8,128)(2,1)}, bf16[2,32,16...) custom-call(s32[2,32]{1,0:T(2,128)S(1)} %pad_add_fusion.slots_ref, ...), custom_call_target="tpu_custom_call" | custom-call | tf_op jit(solution)/shard_map/pack_blocks/pallas_call | solution.py:274
  48.3 14.8 %collective-permute-start.3 = (bf16[64,8192]{1,0:T(8,128)(2,1)}, bf16[64,8192]{1,0:T(8,128)(2,1)S(1)}, u32[]{:S(2)}, u32[]{:S(2)}) collective-permute-start(bf16[64,8192]{1,0:T(8,128)(2,1)} %collective-permute-done.1), channel_id=1, source_target_pairs={{0,4},{2,6},{4,0},{6,2},{8,12},{10,14},{12,8},{14,10},{1,5},{3,7},... | collective-permute-start | bytes 3145736 | tf_op jit(solution)/shard_map/ppermute | solution.py:54
  69.4 27.2 %collective-permute-done.3 = bf16[64,8192]{1,0:T(8,128)(2,1)S(1)} collective-permute-done((bf16[64,8192]{1,0:T(8,128)(2,1)}, bf16[64,8192]{1,0:T(8,128)(2,1)S(1)}, u32[]{:S(2)}, u32[]{:S(2)}) %collective-permute-start.3) | collective-permute-done | bytes 1048608 | tf_op jit(solution)/shard_map/ppermute | solution.py:54
  104.0 6.1 %collective-permute-done.5 = bf16[2,32,16,256]{3,2,1,0:T(8,128)(2,1)S(1)} collective-permute-done((bf16[2,32,16,256]{3,2,1,0:T(8,128)(2,1)S(1)}, bf16[2,32,16,256]{3,2,1,0:T(8,128)(2,1)S(1)}, u32[]{:S(2)}, u32[]{:S(2)}) %collective-permute-start.5) | collective-permute-done | bytes 524320 | tf_op jit(solution)/shard_map/ppermute | solution.py:54
  110.1 3.0 collective-permute-start.15
  113.0 2.3 collective-permute-start.16
  115.3 15.6 %project.2 = (bf16[8,256,128]{2,1,0:T(8,128)(2,1)}, bf16[256,128]{1,0:T(8,128)(2,1)}, bf16[256,256]{1,0:T(8,128)(2,1)}, bf16[256,256]{1,0:T(8,128)(2,1)}) custom-call(s32[4]{0:T(128)} %add_multiply_fusion.starts_ref, bf16[64,8192]{1,0:T(8,128)(2,1)} %copy-done.9, bf16[64,8192]{1,0:T(8,128)(2,1)} %collective-permute-done.refs_1_, ...), custom_call_target="tpu_custom_call" | custom-call | flops 5368709120 | bytes 26476544 | tf_op jit(solution)/shard_map/project/pallas_call | solution.py:177
  133.3 15.7 %project.3 = (bf16[8,256,128]{2,1,0:T(8,128)(2,1)}, bf16[256,128]{1,0:T(8,128)(2,1)}, bf16[256,256]{1,0:T(8,128)(2,1)}, bf16[256,256]{1,0:T(8,128)(2,1)}) custom-call(s32[4]{0:T(128)} %add_multiply_fusion.1.starts_ref, bf16[64,8192]{1,0:T(8,128)(2,1)} %copy-done.10, bf16[64,8192]{1,0:T(8,128)(2,1)} %broadcast_select_fusion.1.refs_1_, ...), custom_call_target="tpu_custom_call" | custom-call | flops 5368709120 | bytes 26476544 | tf_op jit(solution)/shard_map/project/pallas_call | solution.py:177
  149.1 1.8 maximum_select_fusion
  150.9 24.5 %all-to-all-start = ((bf16[8,64,256]{2,1,0:T(8,128)(2,1)}), bf16[8,64,256]{2,1,0:T(8,128)(2,1)}, u32[]{:S(2)}, u32[]{:S(2)}) async-start(bf16[8,64,256]{2,1,0:T(8,128)(2,1)} %bitcast.108), calls=%async_computation | async-start | bytes 524288 | tf_op jit(solution)/shard_map/all_to_all | solution.py:527
  175.7 8.1 %all-to-all-done = bf16[8,64,256]{2,1,0:T(8,128)(2,1)} async-done(((bf16[8,64,256]{2,1,0:T(8,128)(2,1)}), bf16[8,64,256]{2,1,0:T(8,128)(2,1)}, u32[]{:S(2)}, u32[]{:S(2)}) %all-to-all-start) | async-done | bytes 262176 | tf_op jit(solution)/shard_map/all_to_all | solution.py:527
  183.7 3.5 %order_blocks.1 = (bf16[4096,128]{1,0:T(8,128)(2,1)S(1)}, bf16[4096,256]{1,0:T(8,128)(2,1)S(1)}) custom-call(s32[1]{0:T(128)} %dynamic_slice.64.length_ref, s32[256]{0:T(256)S(1)} %multiply_add_fusion.where_ref, bf16[64,16,256]{2,1,0:T(8,128)(2,1)S(1)} %bitcast.92, bf16[64,16,256]{2,1,0:T(8,128)(2,1)} %bitcast.18.refs_1_, bf16[64,16,256]{2,1,0:T(8,128)(2,1)S(1)} %bitcast.95, ...), custom_call_target="tpu_custom_call" | custom-call | tf_op jit(solution)/shard_map/order_blocks/pallas_call | solution.py:319
  187.3 22.9 %attend.1 = bf16[512,1024]{1,0:T(8,128)(2,1)S(1)} custom-call(s32[1]{0:T(128)} %bitcast.half_ref, bf16[8,256,128]{2,1,0:T(8,128)(2,1)S(1)} %copy-done.3, bf16[8,256,128]{2,1,0:T(8,128)(2,1)S(1)} %copy-done.4, bf16[4096,128]{1,0:T(8,128)(2,1)S(1)} %get-tuple-element.95.refs_2_, bf16[4096,256]{1,0:T(8,128)(2,1)S(1)} %get-tuple-element.96.refs_3_, ...), custom_call_target="tpu_custom_call" | custom-call | flops 19327352832 | bytes 5636096 | tf_op jit(solution)/shard_map/attend/pallas_call | solution.py:391
  210.2 8.1 %fusion.4 = bf16[512,4096]{1,0:T(8,128)(2,1)S(1)} fusion(bf16[512,1024]{1,0:T(8,128)(2,1)S(1)} %attend.1, bf16[1024,8192]{1,0:T(8,128)(2,1)} %param.21), kind=kOutput, calls=%fused_computation.4 | convolution fusion | flops 4297064448 | bytes 13631488 | tf_op jit(solution)/shard_map/dot_general | solution.py:538
  218.5 2.0 collective-permute-start.17
  220.5 8.1 %fusion.7 = bf16[512,4096]{1,0:T(8,128)(2,1)S(1)} fusion(bf16[512,1024]{1,0:T(8,128)(2,1)S(1)} %attend.1, bf16[1024,8192]{1,0:T(8,128)(2,1)} %param.21), kind=kOutput, calls=%fused_computation.5 | convolution fusion | flops 4297064448 | bytes 13631488 | tf_op jit(solution)/shard_map/dot_general | solution.py:538
  228.8 2.0 collective-permute-start.21
  230.8 2.6 collective-permute-done.18
  235.7 8.9 %collective-permute-done.22 = bf16[64,4096]{1,0:T(8,128)(2,1)S(1)} collective-permute-done((bf16[64,4096]{1,0:T(8,128)(2,1)S(1)}, bf16[64,4096]{1,0:T(8,128)(2,1)S(1)}, u32[]{:S(2)}, u32[]{:S(2)}) %collective-permute-start.22) | collective-permute-done | bytes 524320 | tf_op jit(solution)/shard_map/ppermute | solution.py:224
  244.9 2.0 collective-permute-start.25
  247.0 8.8 %collective-permute-done.20 = bf16[64,4096]{1,0:T(8,128)(2,1)S(1)} collective-permute-done((bf16[64,4096]{1,0:T(8,128)(2,1)S(1)}, bf16[64,4096]{1,0:T(8,128)(2,1)S(1)}, u32[]{:S(2)}, u32[]{:S(2)}) %collective-permute-start.20) | collective-permute-done | bytes 524320 | tf_op jit(solution)/shard_map/ppermute | solution.py:224
  256.1 2.0 collective-permute-start.23
  258.2 8.9 %collective-permute-done.25 = bf16[64,4096]{1,0:T(8,128)(2,1)S(1)} collective-permute-done((bf16[64,4096]{1,0:T(8,128)(2,1)S(1)}, bf16[64,4096]{1,0:T(8,128)(2,1)S(1)}, u32[]{:S(2)}, u32[]{:S(2)}) %collective-permute-start.25) | collective-permute-done | bytes 524320 | tf_op jit(solution)/shard_map/ppermute | solution.py:224
  269.4 6.6 %collective-permute-done.23 = bf16[64,4096]{1,0:T(8,128)(2,1)S(1)} collective-permute-done((bf16[64,4096]{1,0:T(8,128)(2,1)S(1)}, bf16[64,4096]{1,0:T(8,128)(2,1)S(1)}, u32[]{:S(2)}, u32[]{:S(2)}) %collective-permute-start.23) | collective-permute-done | bytes 524320 | tf_op jit(solution)/shard_map/ppermute | solution.py:224
  276.7 10.5 %collective-permute-done.27 = bf16[64,4096]{1,0:T(8,128)(2,1)S(1)} collective-permute-done((bf16[64,4096]{1,0:T(8,128)(2,1)S(1)}, bf16[64,4096]{1,0:T(8,128)(2,1)S(1)}, u32[]{:S(2)}, u32[]{:S(2)}) %collective-permute-start.27) | collective-permute-done | bytes 524320 | tf_op jit(solution)/shard_map/ppermute | solution.py:224
  287.5 1.8 collective-permute-start.30
  291.4 5.3 %collective-permute-done.30 = bf16[64,4096]{1,0:T(8,128)(2,1)S(1)} collective-permute-done((bf16[64,4096]{1,0:T(8,128)(2,1)S(1)}, bf16[64,4096]{1,0:T(8,128)(2,1)S(1)}, u32[]{:S(2)}, u32[]{:S(2)}) %collective-permute-start.30) | collective-permute-done | bytes 524320 | tf_op jit(solution)/shard_map/ppermute | solution.py:224
  (122 shorter events, 38.1 us)
Async XLA Ops:
  9.3 32.7 %collective-permute-start.2 = (bf16[32,16,2048]{2,1,0:T(8,128)(2,1)S(1)}, bf16[32,16,2048]{2,1,0:T(8,128)(2,1)}, u32[]{:S(2)}, u32[]{:S(2)}) collective-permute-start(bf16[32,16,2048]{2,1,0:T(8,128)(2,1)S(1)} %pick_blocks.1), channel_id=1, source_target_pairs={{0,1},{1,0},{2,3},{3,2},{4,5},{5,4},{6,7},{7,6},{8,9},{9,8},{10,11... | collective-permute-start | bytes 6291464 | tf_op jit(solution)/shard_map/ppermute | solution.py:459
  9.8 26.5 %collective-permute-start = (bf16[64,8192]{1,0:T(8,128)(2,1)S(1)}, bf16[64,8192]{1,0:T(8,128)(2,1)}, u32[]{:S(2)}, u32[]{:S(2)}) collective-permute-start(bf16[64,8192]{1,0:T(8,128)(2,1)S(1)} %fusion.12.refs_0_), channel_id=1, source_target_pairs={{0,4},{2,6},{4,0},{6,2},{8,12},{10,14},{12,8},{14,10},{1,5},{3,7},... | collective-permute-start | bytes 3145736 | tf_op jit(solution)/shard_map/ppermute | solution.py:54
  12.4 23.9 %collective-permute-start.8 = (bf16[64,8192]{1,0:T(8,128)(2,1)S(1)}, bf16[64,8192]{1,0:T(8,128)(2,1)}, u32[]{:S(2)}, u32[]{:S(2)}) collective-permute-start(bf16[64,8192]{1,0:T(8,128)(2,1)S(1)} %fusion.12.refs_0_), channel_id=1, source_target_pairs={{0,1},{1,0},{2,3},{3,2},{4,8},{5,9},{6,10},{7,11},{8,4},{9,5},{10,... | collective-permute-start | bytes 3145736 | tf_op jit(solution)/shard_map/ppermute | solution.py:65
  12.6 27.7 %collective-permute-start.6 = (bf16[64,8192]{1,0:T(8,128)(2,1)S(1)}, bf16[64,8192]{1,0:T(8,128)(2,1)}, u32[]{:S(2)}, u32[]{:S(2)}) collective-permute-start(bf16[64,8192]{1,0:T(8,128)(2,1)S(1)} %fusion.12.refs_0_), channel_id=1, source_target_pairs={{0,2},{2,0},{4,6},{6,4},{8,10},{10,8},{12,14},{14,12},{1,3},{3,1},... | collective-permute-start | bytes 3145736 | tf_op jit(solution)/shard_map/ppermute | solution.py:54
  36.3 12.0 %collective-permute-start.1 = (bf16[64,8192]{1,0:T(8,128)(2,1)}, bf16[64,8192]{1,0:T(8,128)(2,1)}, u32[]{:S(2)}, u32[]{:S(2)}) collective-permute-start(bf16[64,8192]{1,0:T(8,128)(2,1)} %collective-permute-done.refs_1_), channel_id=1, source_target_pairs={{0,1},{1,0},{2,3},{3,2},{4,8},{5,9},{6,10},{7,11},{8,4},{9,5},{10,... | collective-permute-start | bytes 3145736 | tf_op jit(solution)/shard_map/ppermute | solution.py:65
  36.3 29.3 %collective-permute-start.9 = (bf16[64,8192]{1,0:T(8,128)(2,1)}, bf16[64,8192]{1,0:T(8,128)(2,1)}, u32[]{:S(2)}, u32[]{:S(2)}) collective-permute-start(bf16[64,8192]{1,0:T(8,128)(2,1)} %collective-permute-done.8), channel_id=1, source_target_pairs={{0,4},{2,6},{4,0},{6,2},{8,12},{10,14},{12,8},{14,10},{1,5},{3,7},... | collective-permute-start | bytes 3145736 | tf_op jit(solution)/shard_map/ppermute | solution.py:54
  40.3 26.6 %collective-permute-start.7 = (bf16[64,8192]{1,0:T(8,128)(2,1)}, bf16[64,8192]{1,0:T(8,128)(2,1)S(1)}, u32[]{:S(2)}, u32[]{:S(2)}) collective-permute-start(bf16[64,8192]{1,0:T(8,128)(2,1)} %collective-permute-done.refs_1_), channel_id=1, source_target_pairs={{0,2},{2,0},{4,6},{6,4},{8,10},{10,8},{12,14},{14,12},{1,3},{3,1},... | collective-permute-start | bytes 3145736 | tf_op jit(solution)/shard_map/ppermute | solution.py:54
  48.3 48.4 %collective-permute-start.3 = (bf16[64,8192]{1,0:T(8,128)(2,1)}, bf16[64,8192]{1,0:T(8,128)(2,1)S(1)}, u32[]{:S(2)}, u32[]{:S(2)}) collective-permute-start(bf16[64,8192]{1,0:T(8,128)(2,1)} %collective-permute-done.1), channel_id=1, source_target_pairs={{0,4},{2,6},{4,0},{6,2},{8,12},{10,14},{12,8},{14,10},{1,5},{3,7},... | collective-permute-start | bytes 3145736 | tf_op jit(solution)/shard_map/ppermute | solution.py:54
  63.1 40.9 %collective-permute-start.4 = (bf16[2,32,16,256]{3,2,1,0:T(8,128)(2,1)S(1)}, bf16[2,32,16,256]{3,2,1,0:T(8,128)(2,1)S(1)}, u32[]{:S(2)}, u32[]{:S(2)}) collective-permute-start(bf16[2,32,16,256]{3,2,1,0:T(8,128)(2,1)S(1)} %get-tuple-element.63), channel_id=1, source_target_pairs={{0,8},{2,10},{4,12},{6,14},{8,0},{10,2},{12,4},{14,6},{1,9},{3,11}... | collective-permute-start | bytes 1572872 | tf_op jit(solution)/shard_map/ppermute | solution.py:54
  64.1 45.9 %collective-permute-start.5 = (bf16[2,32,16,256]{3,2,1,0:T(8,128)(2,1)S(1)}, bf16[2,32,16,256]{3,2,1,0:T(8,128)(2,1)S(1)}, u32[]{:S(2)}, u32[]{:S(2)}) collective-permute-start(bf16[2,32,16,256]{3,2,1,0:T(8,128)(2,1)S(1)} %get-tuple-element.65), channel_id=1, source_target_pairs={{0,12},{2,14},{4,8},{6,10},{8,4},{10,6},{12,0},{14,2},{1,13},{3,15... | collective-permute-start | bytes 1572872 | tf_op jit(solution)/shard_map/ppermute | solution.py:54
  67.9 29.9 %collective-permute-start.10 = (bf16[64,8192]{1,0:T(8,128)(2,1)S(1)}, bf16[64,8192]{1,0:T(8,128)(2,1)S(1)}, u32[]{:S(2)}, u32[]{:S(2)}) collective-permute-start(bf16[64,8192]{1,0:T(8,128)(2,1)S(1)} %broadcast_select_fusion.refs_0_), channel_id=1, source_target_pairs={{0,2},{2,0},{4,6},{6,4},{8,10},{10,8},{12,14},{14,12},{1,3},{3,1},... | collective-permute-start | bytes 3145736 | tf_op jit(solution)/shard_map/ppermute | solution.py:54
  97.8 34.0 %collective-permute-start.11 = (bf16[64,8192]{1,0:T(8,128)(2,1)}, bf16[64,8192]{1,0:T(8,128)(2,1)}, u32[]{:S(2)}, u32[]{:S(2)}) collective-permute-start(bf16[64,8192]{1,0:T(8,128)(2,1)} %broadcast_select_fusion.1.refs_1_), channel_id=1, source_target_pairs={{0,2},{2,0},{4,6},{6,4},{8,10},{10,8},{12,14},{14,12},{1,3},{3,1},... | collective-permute-start | bytes 3145736 | tf_op jit(solution)/shard_map/ppermute | solution.py:54
  110.1 65.6 %collective-permute-start.13 = (bf16[2,32,16,256]{3,2,1,0:T(8,128)(2,1)}, bf16[2,32,16,256]{3,2,1,0:T(8,128)(2,1)S(1)}, u32[]{:S(2)}, u32[]{:S(2)}) collective-permute-start(bf16[2,32,16,256]{3,2,1,0:T(8,128)(2,1)} %get-tuple-element.76), channel_id=1, source_target_pairs={{0,4},{2,6},{4,0},{6,2},{8,12},{10,14},{12,8},{14,10},{1,5},{3,7},... | collective-permute-start | bytes 1572872 | tf_op jit(solution)/shard_map/ppermute | solution.py:54
  110.1 65.6 %collective-permute-start.15 = (bf16[2,32,16,256]{3,2,1,0:T(8,128)(2,1)}, bf16[2,32,16,256]{3,2,1,0:T(8,128)(2,1)S(1)}, u32[]{:S(2)}, u32[]{:S(2)}) collective-permute-start(bf16[2,32,16,256]{3,2,1,0:T(8,128)(2,1)} %get-tuple-element.80), channel_id=1, source_target_pairs={{0,10},{2,8},{4,14},{6,12},{8,2},{10,0},{12,6},{14,4},{1,11},{3,9}... | collective-permute-start | bytes 1572872 | tf_op jit(solution)/shard_map/ppermute | solution.py:54
  113.0 62.6 %collective-permute-start.16 = (bf16[2,32,16,256]{3,2,1,0:T(8,128)(2,1)}, bf16[2,32,16,256]{3,2,1,0:T(8,128)(2,1)S(1)}, u32[]{:S(2)}, u32[]{:S(2)}) collective-permute-start(bf16[2,32,16,256]{3,2,1,0:T(8,128)(2,1)} %copy-done.2), channel_id=1, source_target_pairs={{0,14},{2,12},{4,10},{6,8},{8,6},{10,4},{12,2},{14,0},{1,15},{3,13... | collective-permute-start | bytes 1572872 | tf_op jit(solution)/shard_map/ppermute | solution.py:54
  131.8 51.9 %collective-permute-start.12 = (bf16[2,32,16,256]{3,2,1,0:T(8,128)(2,1)}, bf16[2,32,16,256]{3,2,1,0:T(8,128)(2,1)}, u32[]{:S(2)}, u32[]{:S(2)}) collective-permute-start(bf16[2,32,16,256]{3,2,1,0:T(8,128)(2,1)} %get-tuple-element.74), channel_id=1, source_target_pairs={{0,2},{2,0},{4,6},{6,4},{8,10},{10,8},{12,14},{14,12},{1,3},{3,1},... | collective-permute-start | bytes 1572872 | tf_op jit(solution)/shard_map/ppermute | solution.py:54
  133.3 50.4 %collective-permute-start.14 = (bf16[2,32,16,256]{3,2,1,0:T(8,128)(2,1)}, bf16[2,32,16,256]{3,2,1,0:T(8,128)(2,1)}, u32[]{:S(2)}, u32[]{:S(2)}) collective-permute-start(bf16[2,32,16,256]{3,2,1,0:T(8,128)(2,1)} %get-tuple-element.78), channel_id=1, source_target_pairs={{0,6},{2,4},{4,2},{6,0},{8,14},{10,12},{12,10},{14,8},{1,7},{3,5},... | collective-permute-start | bytes 1572872 | tf_op jit(solution)/shard_map/ppermute | solution.py:54
  150.9 32.9 %all-to-all-start = ((bf16[8,64,256]{2,1,0:T(8,128)(2,1)}), bf16[8,64,256]{2,1,0:T(8,128)(2,1)}, u32[]{:S(2)}, u32[]{:S(2)}) async-start(bf16[8,64,256]{2,1,0:T(8,128)(2,1)} %bitcast.108), calls=%async_computation | async-start | bytes 524288 | tf_op jit(solution)/shard_map/all_to_all | solution.py:527
  218.4 14.9 %collective-permute-start.18 = (bf16[64,4096]{1,0:T(8,128)(2,1)S(1)}, bf16[64,4096]{1,0:T(8,128)(2,1)S(1)}, u32[]{:S(2)}, u32[]{:S(2)}) collective-permute-start(bf16[64,4096]{1,0:T(8,128)(2,1)S(1)} %get-tuple-element.102), channel_id=1, source_target_pairs={{0,2},{4,0},{8,4},{12,8},{14,12},{10,14},{6,10},{2,6},{1,3},{5,1},... | collective-permute-start | bytes 1572872 | tf_op jit(solution)/shard_map/ppermute | solution.py:224
  218.5 14.9 %collective-permute-start.17 = (bf16[64,4096]{1,0:T(8,128)(2,1)S(1)}, bf16[64,4096]{1,0:T(8,128)(2,1)S(1)}, u32[]{:S(2)}, u32[]{:S(2)}) collective-permute-start(bf16[64,4096]{1,0:T(8,128)(2,1)S(1)} %get-tuple-element.101), channel_id=1, source_target_pairs={{0,4},{4,8},{8,12},{12,14},{14,10},{10,6},{6,2},{2,0},{1,5},{5,9},... | collective-permute-start | bytes 1572872 | tf_op jit(solution)/shard_map/ppermute | solution.py:224
  228.7 16.0 %collective-permute-start.22 = (bf16[64,4096]{1,0:T(8,128)(2,1)S(1)}, bf16[64,4096]{1,0:T(8,128)(2,1)S(1)}, u32[]{:S(2)}, u32[]{:S(2)}) collective-permute-start(bf16[64,4096]{1,0:T(8,128)(2,1)S(1)} %get-tuple-element.104), channel_id=1, source_target_pairs={{0,4},{4,8},{8,12},{12,14},{14,10},{10,6},{6,2},{2,0},{1,5},{5,9},... | collective-permute-start | bytes 1572872 | tf_op jit(solution)/shard_map/ppermute | solution.py:224
  228.8 15.9 %collective-permute-start.21 = (bf16[64,4096]{1,0:T(8,128)(2,1)S(1)}, bf16[64,4096]{1,0:T(8,128)(2,1)S(1)}, u32[]{:S(2)}, u32[]{:S(2)}) collective-permute-start(bf16[64,4096]{1,0:T(8,128)(2,1)S(1)} %get-tuple-element.103), channel_id=1, source_target_pairs={{0,2},{4,0},{8,4},{12,8},{14,12},{10,14},{6,10},{2,6},{1,3},{5,1},... | collective-permute-start | bytes 1572872 | tf_op jit(solution)/shard_map/ppermute | solution.py:224
  233.7 22.1 %collective-permute-start.20 = (bf16[64,4096]{1,0:T(8,128)(2,1)S(1)}, bf16[64,4096]{1,0:T(8,128)(2,1)S(1)}, u32[]{:S(2)}, u32[]{:S(2)}) collective-permute-start(bf16[64,4096]{1,0:T(8,128)(2,1)S(1)} %get-tuple-element.106), channel_id=1, source_target_pairs={{0,2},{4,0},{8,4},{12,8},{14,12},{10,14},{6,10},{2,6},{1,3},{5,1},... | collective-permute-start | bytes 1572872 | tf_op jit(solution)/shard_map/ppermute | solution.py:224
  235.1 20.7 %collective-permute-start.19 = (bf16[64,4096]{1,0:T(8,128)(2,1)S(1)}, bf16[64,4096]{1,0:T(8,128)(2,1)S(1)}, u32[]{:S(2)}, u32[]{:S(2)}) collective-permute-start(bf16[64,4096]{1,0:T(8,128)(2,1)S(1)} %get-tuple-element.105), channel_id=1, source_target_pairs={{0,4},{4,8},{8,12},{12,14},{14,10},{10,6},{6,2},{2,0},{1,5},{5,9},... | collective-permute-start | bytes 1572872 | tf_op jit(solution)/shard_map/ppermute | solution.py:224
  244.9 22.2 %collective-permute-start.25 = (bf16[64,4096]{1,0:T(8,128)(2,1)S(1)}, bf16[64,4096]{1,0:T(8,128)(2,1)S(1)}, u32[]{:S(2)}, u32[]{:S(2)}) collective-permute-start(bf16[64,4096]{1,0:T(8,128)(2,1)S(1)} %get-tuple-element.108), channel_id=1, source_target_pairs={{0,4},{4,8},{8,12},{12,14},{14,10},{10,6},{6,2},{2,0},{1,5},{5,9},... | collective-permute-start | bytes 1572872 | tf_op jit(solution)/shard_map/ppermute | solution.py:224
  246.9 20.2 %collective-permute-start.24 = (bf16[64,4096]{1,0:T(8,128)(2,1)S(1)}, bf16[64,4096]{1,0:T(8,128)(2,1)S(1)}, u32[]{:S(2)}, u32[]{:S(2)}) collective-permute-start(bf16[64,4096]{1,0:T(8,128)(2,1)S(1)} %get-tuple-element.107), channel_id=1, source_target_pairs={{0,2},{4,0},{8,4},{12,8},{14,12},{10,14},{6,10},{2,6},{1,3},{5,1},... | collective-permute-start | bytes 1572872 | tf_op jit(solution)/shard_map/ppermute | solution.py:224
  256.1 19.9 %collective-permute-start.23 = (bf16[64,4096]{1,0:T(8,128)(2,1)S(1)}, bf16[64,4096]{1,0:T(8,128)(2,1)S(1)}, u32[]{:S(2)}, u32[]{:S(2)}) collective-permute-start(bf16[64,4096]{1,0:T(8,128)(2,1)S(1)} %get-tuple-element.109), channel_id=1, source_target_pairs={{0,4},{4,8},{8,12},{12,14},{14,10},{10,6},{6,2},{2,0},{1,5},{5,9},... | collective-permute-start | bytes 1572872 | tf_op jit(solution)/shard_map/ppermute | solution.py:224
  258.1 18.0 %collective-permute-start.26 = (bf16[64,4096]{1,0:T(8,128)(2,1)S(1)}, bf16[64,4096]{1,0:T(8,128)(2,1)S(1)}, u32[]{:S(2)}, u32[]{:S(2)}) collective-permute-start(bf16[64,4096]{1,0:T(8,128)(2,1)S(1)} %get-tuple-element.110), channel_id=1, source_target_pairs={{0,2},{4,0},{8,4},{12,8},{14,12},{10,14},{6,10},{2,6},{1,3},{5,1},... | collective-permute-start | bytes 1572872 | tf_op jit(solution)/shard_map/ppermute | solution.py:224
  267.4 9.2 %collective-permute-start.29 = (bf16[64,4096]{1,0:T(8,128)(2,1)S(1)}, bf16[64,4096]{1,0:T(8,128)(2,1)S(1)}, u32[]{:S(2)}, u32[]{:S(2)}) collective-permute-start(bf16[64,4096]{1,0:T(8,128)(2,1)S(1)} %get-tuple-element.111), channel_id=1, source_target_pairs={{0,2},{4,0},{8,4},{12,8},{14,12},{10,14},{6,10},{2,6},{1,3},{5,1},... | collective-permute-start | bytes 1572872 | tf_op jit(solution)/shard_map/ppermute | solution.py:224
  268.8 18.6 %collective-permute-start.28 = (bf16[64,4096]{1,0:T(8,128)(2,1)S(1)}, bf16[64,4096]{1,0:T(8,128)(2,1)S(1)}, u32[]{:S(2)}, u32[]{:S(2)}) collective-permute-start(bf16[64,4096]{1,0:T(8,128)(2,1)S(1)} %get-tuple-element.112), channel_id=1, source_target_pairs={{0,4},{4,8},{8,12},{12,14},{14,10},{10,6},{6,2},{2,0},{1,5},{5,9},... | collective-permute-start | bytes 1572872 | tf_op jit(solution)/shard_map/ppermute | solution.py:224
  276.2 11.1 %collective-permute-start.27 = (bf16[64,4096]{1,0:T(8,128)(2,1)S(1)}, bf16[64,4096]{1,0:T(8,128)(2,1)S(1)}, u32[]{:S(2)}, u32[]{:S(2)}) collective-permute-start(bf16[64,4096]{1,0:T(8,128)(2,1)S(1)} %fusion.24), channel_id=1, source_target_pairs={{0,4},{4,8},{8,12},{12,14},{14,10},{10,6},{6,2},{2,0},{1,5},{5,9},... | collective-permute-start | bytes 1572872 | tf_op jit(solution)/shard_map/ppermute | solution.py:224
  287.5 9.2 %collective-permute-start.30 = (bf16[64,4096]{1,0:T(8,128)(2,1)S(1)}, bf16[64,4096]{1,0:T(8,128)(2,1)S(1)}, u32[]{:S(2)}, u32[]{:S(2)}) collective-permute-start(bf16[64,4096]{1,0:T(8,128)(2,1)S(1)} %fusion.13), channel_id=1, source_target_pairs={{0,2},{4,0},{8,4},{12,8},{14,12},{10,14},{6,10},{2,6},{1,3},{5,1},... | collective-permute-start | bytes 1572872 | tf_op jit(solution)/shard_map/ppermute | solution.py:224
  (19 other events, 457.0 us)
